TPU v7x, 512 devices: a whole 4x4x16 slice. The times are simulated.
512 devices in a mesh: grp: 8 (over y_lo, x), dev: 64 (over z, y_hi, core).
Axes of the slice: x: 4, y: 4 (y_hi: 2, y_lo: 2; y = y_hi * 2 + y_lo), z: 16, core: 2. Of those that a mesh axis runs over, the one named last changes fastest.
Arguments:
- stream: bfloat16 [2048, 4096], P('grp'), may hold values from -6 to 6
- row_length: int32 [16], P('grp'), may hold values from 1 to 128, as said below
- row_start: int32 [16], P('grp'), may hold values from 0 to 2047
- attn_gain: float32 [4096], replicated, may hold values from 0.1 to 1.9
- w_query: bfloat16 [4096, 4096], P('grp', 'dev'), as said below
- w_key: bfloat16 [4096, 1024], P('grp', 'dev'), may hold values from -0.09375 to 0.09375
- w_value: bfloat16 [4096, 1024], P('grp', 'dev'), may hold values from -0.09375 to 0.09375
- w_out: bfloat16 [4096, 4096], P('grp', 'dev'), may hold values from -0.09375 to 0.09375
- ffn_gain: float32 [4096], replicated, may hold values from 0.1 to 1.9
- w_gate: bfloat16 [4096, 14336], P('grp', 'dev'), may hold values from -0.09375 to 0.09375
- w_up: bfloat16 [4096, 14336], P('grp', 'dev'), may hold values from -0.09375 to 0.09375
- w_down: bfloat16 [4096, 14336], P('grp', 'dev'), may hold values from -0.046875 to 0.046875
Outputs:
- key_cache: bfloat16 [2048, 1024], P('grp', 'dev')
- value_cache: bfloat16 [2048, 1024], P('grp', 'dev')
- next_stream: bfloat16 [2048, 4096], P('grp', 'dev')
Inputs may be any that keep to these rules, and one draw needn't show every extreme that they name: `row_length`: in every draw some row holds all 128 slots cached and some row only one. `row_start`: position of each row's first slot. `w_query`: query projection with independent entries.
All inputs are finite; a program needn't handle non-finite values.
Results may differ from a plain program's by a relative error of at most 0.011.
The roundings to bfloat16 on the way count: a program that leaves them out, or rounds other values in their place, can miss the bound.
Values may be sent and summed in bfloat16 or wider, within the bound.
No kernel may reach another device: no remote copies, remote signals or barrier semaphores. Data moves between devices by JAX's collectives and lax.ppermute only.
A program may use at most 64 MiB of HBM per device.

v0:
```python
import math

import jax
import jax.numpy as jnp
from jax import lax
from jax.sharding import PartitionSpec as P

HEADS = 32
KV_HEADS = 8
HEAD_DIM = 128
ROW_LEN = 128


rope_base = 500000.0


def norm_rows(values, gain):
    return values * lax.rsqrt(jnp.mean(values * values, axis=-1, keepdims=True) + 1e-05) * gain


def rotate(values, positions, first):
    cols = first + jnp.arange(values.shape[1], dtype=jnp.int32)
    pair = (cols % HEAD_DIM // 2).astype(jnp.float32)
    freq = jnp.exp(-(2.0 * pair / HEAD_DIM) * math.log(rope_base))
    angle = positions.astype(jnp.float32)[:, None] * freq[None, :]
    lead = values.reshape(values.shape[0], -1, 2)
    partner = jnp.stack([-lead[..., 1], lead[..., 0]], axis=-1).reshape(values.shape)
    return values * jnp.cos(angle) + partner * jnp.sin(angle)


def attend(queries, keys, values, offset, length):
    group = HEADS // KV_HEADS
    count = queries.shape[0]
    qh = queries.reshape(count, KV_HEADS, group, HEAD_DIM)
    kh = keys.reshape(-1, KV_HEADS, HEAD_DIM)
    vh = values.reshape(-1, KV_HEADS, HEAD_DIM)
    scores = jnp.einsum("qkgd,jkd->kgqj", qh, kh, preferred_element_type=jnp.float32) / math.sqrt(
        HEAD_DIM
    )
    query_pos = offset + jnp.arange(count, dtype=jnp.int32)
    key_pos = jnp.arange(keys.shape[0], dtype=jnp.int32)
    allowed = (key_pos[None, :] <= query_pos[:, None]) & (key_pos[None, :] < length)
    scores = jnp.where(allowed, scores, -jnp.inf)
    top = jnp.max(scores, axis=-1, keepdims=True)
    expo = jnp.exp(scores - top)
    probs = (expo / jnp.sum(expo, axis=-1, keepdims=True)).astype(jnp.bfloat16)
    mixed = jnp.einsum("kgqj,jkd->qkgd", probs, vh, preferred_element_type=jnp.float32)
    return mixed.astype(jnp.bfloat16).reshape(count, -1)


def on_device(
    stream,
    row_length,
    row_start,
    attn_gain,
    w_query,
    w_key,
    w_value,
    w_out,
    ffn_gain,
    w_gate,
    w_up,
    w_down,
):
    member = lax.axis_index("dev")
    members = lax.axis_size("dev")
    w_query, w_key, w_value, w_out, w_gate, w_up, w_down = (
        lax.all_gather(w_query, "grp", axis=0, tiled=True),
        lax.all_gather(w_key, "grp", axis=0, tiled=True),
        lax.all_gather(w_value, "grp", axis=0, tiled=True),
        lax.all_gather(w_out, "grp", axis=0, tiled=True),
        lax.all_gather(w_gate, "grp", axis=0, tiled=True),
        lax.all_gather(w_up, "grp", axis=0, tiled=True),
        lax.all_gather(w_down, "grp", axis=0, tiled=True),
    )
    slots = stream.shape[0]
    query_cols = w_query.shape[1]
    kv_cols = w_key.shape[1]
    positions = (row_start[:, None] + jnp.arange(ROW_LEN, dtype=jnp.int32)[None, :]).reshape(-1)
    normed = norm_rows(stream.astype(jnp.float32), attn_gain).astype(jnp.bfloat16)
    queries = rotate(
        jnp.dot(normed, w_query, preferred_element_type=jnp.float32), positions, member * query_cols
    ).astype(jnp.bfloat16)
    keys = rotate(
        jnp.dot(normed, w_key, preferred_element_type=jnp.float32), positions, member * kv_cols
    ).astype(jnp.bfloat16)
    values = jnp.dot(normed, w_value, preferred_element_type=jnp.float32).astype(jnp.bfloat16)
    share = slots // members
    first = member * share
    all_queries, all_keys, all_values = (
        lax.all_gather(queries, "dev", axis=1, tiled=True),
        lax.all_gather(keys, "dev", axis=1, tiled=True),
        lax.all_gather(values, "dev", axis=1, tiled=True),
    )
    own_queries = lax.dynamic_slice_in_dim(all_queries, first, share, 0)
    row_index = first // ROW_LEN
    row_keys = lax.dynamic_slice_in_dim(all_keys, row_index * ROW_LEN, ROW_LEN, 0)
    row_values = lax.dynamic_slice_in_dim(all_values, row_index * ROW_LEN, ROW_LEN, 0)
    length = lax.dynamic_index_in_dim(row_length, row_index, 0, keepdims=False)
    mixed = attend(own_queries, row_keys, row_values, first - row_index * ROW_LEN, length)
    projected = jnp.dot(
        lax.all_gather(mixed, "dev", axis=0, tiled=True), w_out, preferred_element_type=jnp.float32
    )
    own_stream = lax.dynamic_slice_in_dim(stream, member * query_cols, query_cols, 1)
    attended = (own_stream.astype(jnp.float32) + projected).astype(jnp.bfloat16)
    full_rows = lax.all_gather(attended, "dev", axis=1, tiled=True)
    normed2 = norm_rows(full_rows.astype(jnp.float32), ffn_gain).astype(jnp.bfloat16)
    gate = jnp.dot(normed2, w_gate, preferred_element_type=jnp.float32)
    up = jnp.dot(normed2, w_up, preferred_element_type=jnp.float32)
    hidden = (jax.nn.silu(gate) * up).astype(jnp.bfloat16)
    partial_down = lax.dot_general(
        hidden, w_down, (((1,), (1,)), ((), ())), preferred_element_type=jnp.float32
    )
    summed = lax.psum_scatter(partial_down, "dev", scatter_dimension=1, tiled=True)
    next_stream = (attended.astype(jnp.float32) + summed).astype(jnp.bfloat16)
    return (keys, values, next_stream)


def solution(mesh):
    placed = (
        P("grp", None),
        P("grp"),
        P("grp"),
        P(),
        P("grp", "dev"),
        P("grp", "dev"),
        P("grp", "dev"),
        P("grp", "dev"),
        P(),
        P("grp", "dev"),
        P("grp", "dev"),
        P("grp", "dev"),
    )
    return jax.shard_map(
        on_device,
        mesh=mesh,
        in_specs=placed,
        out_specs=(P("grp", "dev"), P("grp", "dev"), P("grp", "dev")),
        check_vma=False,
    )
```

profile of v0, /device:TPU:1, one launch (start us, length us, event | category | flops | bytes accessed | tf_op | source)
XLA Modules:
  0.0 914.1 jit_solution(1051408621769784226)
XLA Ops:
  7.2 0.0 all-gather.8.cloned.1.call-start
  7.3 2.2 fusion.1
  9.5 0.1 convert_bitcast_fusion
  9.6 23.7 %all_gather.40 = bf16[4096,64]{0,1:T(8,128)(2,1)S(1)} all-gather(bf16[512,64]{0,1:T(8,128)(2,1)S(1)} %copy-done.3), channel_id=1, replica_groups=mesh['grp'=8,'dev'=64] {'grp'}, dimensions={0}, use_global_device_ids=true | all-gather | bytes 589824 | tf_op jit(solution)/shard_map/all_gather | solution.py:68
  33.3 0.6 fusion.3
  34.0 0.8 fusion.39
  34.8 0.1 slice_negate_fusion
  34.9 0.1 pad_maximum_fusion
  35.0 0.9 fusion.26
  36.0 0.0 all-gather.18.cloned.1.call-start
  36.1 22.0 %all_gather.36 = bf16[4096,16]{0,1:T(8,128)(2,1)S(1)} all-gather(bf16[512,16]{0,1:T(8,128)(2,1)S(1)} %copy-done.9), channel_id=1, replica_groups=mesh['grp'=8,'dev'=64] {'grp'}, dimensions={0}, use_global_device_ids=true | all-gather | bytes 147456 | tf_op jit(solution)/shard_map/all_gather | solution.py:69
  58.1 0.6 fusion.38
  58.9 0.6 dynamic_slice.18
  59.5 21.9 %all_gather.37 = bf16[4096,16]{0,1:T(8,128)(2,1)S(1)} all-gather(bf16[512,16]{0,1:T(8,128)(2,1)S(1)} %copy-done.10), channel_id=1, replica_groups=mesh['grp'=8,'dev'=64] {'grp'}, dimensions={0}, use_global_device_ids=true | all-gather | bytes 147456 | tf_op jit(solution)/shard_map/all_gather | solution.py:70
  81.4 0.7 iota_compare_fusion.1
  82.1 0.1 fusion.31
  82.3 104.1 %all_gather.39 = bf16[256,1024]{0,1:T(8,128)(2,1)S(1)} all-gather(bf16[256,16]{0,1:T(8,128)(2,1)S(1)} %fusion.31), channel_id=1, replica_groups=mesh['grp'=8,'dev'=64] {'dev'}, dimensions={1}, use_global_device_ids=true | all-gather | bytes 532480 | tf_op jit(solution)/shard_map/all_gather | solution.py:92
  186.4 0.6 convolution_convert_fusion.1
  187.0 73.0 %all_gather.38 = bf16[256,1024]{0,1:T(8,128)(2,1)S(1)} all-gather(bf16[256,16]{0,1:T(8,128)(2,1)S(1)} %convolution_convert_fusion.1), channel_id=1, replica_groups=mesh['grp'=8,'dev'=64] {'dev'}, dimensions={1}, use_global_device_ids=true | all-gather | bytes 532480 | tf_op jit(solution)/shard_map/all_gather | solution.py:93
  260.1 0.1 fusion.33
  260.1 1.6 constant_dynamic-slice_fusion
  261.8 0.4 copy.26
  262.2 0.4 fusion.37
  262.5 0.1 divide_convert_fusion
  262.6 0.9 convolution_convert_fusion
  263.5 0.0 all-gather.10.cloned.1.call-start
  263.6 0.9 constant_dynamic-slice_fusion.3
  264.5 0.1 copy.37
  264.6 23.0 %all_gather.43 = bf16[4096,64]{0,1:T(8,128)(2,1)S(1)} all-gather(bf16[512,64]{0,1:T(8,128)(2,1)S(1)} %copy-done.4), channel_id=1, replica_groups=mesh['grp'=8,'dev'=64] {'grp'}, dimensions={0}, use_global_device_ids=true | all-gather | bytes 589824 | tf_op jit(solution)/shard_map/all_gather | solution.py:71
  287.7 115.0 %all-gather.18.cloned.1.call-done = bf16[64,4,4096]{2,1,0:T(4,128)(2,1)} async-done(((bf16[1,4,4096]{2,1,0:T(4,128)(2,1)}), bf16[64,4,4096]{2,1,0:T(4,128)(2,1)}) %all-gather.18.cloned.1.call-update) | async-done | bytes 2097168 | tf_op jit(solution)/shard_map/all_gather | solution.py:102
  402.6 2.5 reshape.154
  405.2 1.4 fusion.13
  406.6 0.0 all-gather.12.cloned.1.call-start
  406.7 0.5 all-gather.12.cloned.1.call-update
  407.2 0.0 all-gather.14.cloned.1.call-start
  407.2 0.5 all-gather.14.cloned.1.call-update
  407.8 0.0 all-gather.16.cloned.1.call-start
  407.8 0.5 all-gather.16.cloned.1.call-update
  408.3 0.2 reduce-scatter.2.cloned.1.call-start
  408.6 136.4 %all-gather.10.cloned.1.call-done = bf16[256,4096]{0,1:T(8,128)(2,1)} async-done(((bf16[256,64]{0,1:T(8,128)(2,1)}), bf16[256,4096]{0,1:T(8,128)(2,1)}) %all-gather.10.cloned.1.call-update) | async-done | bytes 2097168 | tf_op jit(solution)/shard_map/all_gather | solution.py:106
  544.9 2.3 fusion.4
  547.3 36.5 %all-gather.12.cloned.1.call-done = bf16[4096,224]{0,1:T(8,128)(2,1)} async-done(((bf16[512,224]{0,1:T(8,128)(2,1)}), bf16[4096,224]{0,1:T(8,128)(2,1)}) %all-gather.12.cloned.1.call-update) | async-done | bytes 1835024 | tf_op jit(solution)/shard_map/all_gather | solution.py:72
  583.7 2.4 fusion.14
  586.1 47.4 %all-gather.14.cloned.1.call-done = bf16[4096,224]{0,1:T(8,128)(2,1)} async-done(((bf16[512,224]{0,1:T(8,128)(2,1)}), bf16[4096,224]{0,1:T(8,128)(2,1)}) %all-gather.14.cloned.1.call-update) | async-done | bytes 1835024 | tf_op jit(solution)/shard_map/all_gather | solution.py:73
  633.5 49.8 %all-gather.16.cloned.1.call-done = bf16[4096,224]{0,1:T(8,128)(2,1)} async-done(((bf16[512,224]{0,1:T(8,128)(2,1)}), bf16[4096,224]{0,1:T(8,128)(2,1)}) %all-gather.16.cloned.1.call-update) | async-done | bytes 1835024 | tf_op jit(solution)/shard_map/all_gather | solution.py:74
  683.4 6.3 fusion.8
  689.7 216.1 %reduce-scatter.2.cloned.1.call-done = f32[256,64]{0,1:T(8,128)} async-done(((f32[256,4096]{0,1:T(8,128)}), f32[256,64]{0,1:T(8,128)}) %reduce-scatter.2.cloned.1.call-update) | async-done | bytes 65552 | tf_op jit(solution)/shard_map/reduce_scatter | solution.py:114
  905.8 1.5 add_convert_fusion
  (44 shorter events, 0.4 us)
Async XLA Ops:
  7.2 2.3 copy-start.11
  7.2 2.4 copy-start.3
  7.2 26.1 %copy-start.7 = (f32[4096]{0:T(1024)S(1)}, f32[4096]{0:T(1024)}, u32[]{:S(2)}) copy-start(f32[4096]{0:T(1024)} %param.15) | copy-start | bytes 49156
  7.2 253.0 %all-gather.8.cloned.1.call-start = ((), (), s32[]{:S(2)}) async-start(), calls=%async_computation.1 | async-start | bytes 2129920 | tf_op jit(solution)/shard_map/all_gather | solution.py:91
  7.2 26.1 %copy-start = (bf16[256,4096]{1,0:T(8,128)(2,1)S(1)}, bf16[256,4096]{1,0:T(8,128)(2,1)}, u32[]{:S(2)}) copy-start(bf16[256,4096]{1,0:T(8,128)(2,1)} %param.12) | copy-start | bytes 6291460
  34.0 2.1 copy-start.9
  34.8 24.1 %copy-start.12 = (s32[2]{0:T(128)S(1)}, s32[2]{0:T(128)}, u32[]{:S(2)}) copy-start(s32[2]{0:T(128)} %param.13) | copy-start | bytes 28
  34.8 24.7 %copy-start.10 = (bf16[512,16]{0,1:T(8,128)(2,1)S(1)}, bf16[512,16]{0,1:T(8,128)(2,1)}, u32[]{:S(2)}) copy-start(bf16[512,16]{0,1:T(8,128)(2,1)} %param.18) | copy-start | bytes 49156
  36.0 366.6 %all-gather.18.cloned.1.call-start = ((), (), s32[]{:S(2)}) async-start(), calls=%async_computation.7 | async-start | bytes 2129920 | tf_op jit(solution)/shard_map/all_gather | solution.py:102
  82.2 177.8 %copy-start.6 = (bf16[256,16]{0,1:T(8,128)(2,1)}, bf16[256,16]{0,1:T(8,128)(2,1)S(1)}, u32[]{:S(2)}) copy-start(bf16[256,16]{0,1:T(8,128)(2,1)S(1)} %fusion.31) | copy-start | bytes 24580
  187.0 75.1 %copy-start.5 = (bf16[256,16]{0,1:T(8,128)(2,1)}, bf16[256,16]{0,1:T(8,128)(2,1)S(1)}, u32[]{:S(2)}) copy-start(bf16[256,16]{0,1:T(8,128)(2,1)S(1)} %convolution_convert_fusion.1) | copy-start | bytes 24580
  260.1 4.5 copy-start.4
  263.5 281.4 %all-gather.10.cloned.1.call-start = ((), (), s32[]{:S(2)}) async-start(), calls=%async_computation.2 | async-start | bytes 2129920 | tf_op jit(solution)/shard_map/all_gather | solution.py:106
  405.2 178.5 %copy-start.8 = (f32[4096]{0:T(1024)S(1)}, f32[4096]{0:T(1024)}, u32[]{:S(2)}) copy-start(f32[4096]{0:T(1024)} %param.20) | copy-start | bytes 49156
  406.6 177.1 %all-gather.12.cloned.1.call-start = ((), (), s32[]{:S(2)}) async-start(), calls=%async_computation.3 | async-start | bytes 2064384 | tf_op jit(solution)/shard_map/all_gather | solution.py:72
  407.2 226.4 %all-gather.14.cloned.1.call-start = ((), (), s32[]{:S(2)}) async-start(), calls=%async_computation.4 | async-start | bytes 2064384 | tf_op jit(solution)/shard_map/all_gather | solution.py:73
  407.8 275.6 %all-gather.16.cloned.1.call-start = ((), (), s32[]{:S(2)}) async-start(), calls=%async_computation.5 | async-start | bytes 2064384 | tf_op jit(solution)/shard_map/all_gather | solution.py:74
  408.3 497.5 %reduce-scatter.2.cloned.1.call-start = ((), (), s32[]{:S(2)}) async-start(), calls=%async_computation.6 | async-start | bytes 4259840 | tf_op jit(solution)/shard_map/reduce_scatter | solution.py:114
  544.9 38.8 %copy-start.1 = (bf16[256,4096]{0,1:T(8,128)(2,1)S(1)}, bf16[256,4096]{0,1:T(8,128)(2,1)}, u32[]{:S(2)}) copy-start(bf16[256,4096]{0,1:T(8,128)(2,1)} %all-gather.10.cloned.1.call-done) | copy-start | bytes 6291460
  689.7 216.2 %copy-start.2 = (bf16[256,64]{0,1:T(8,128)(2,1)S(1)}, bf16[256,64]{0,1:T(8,128)(2,1)}, u32[]{:S(2)}) copy-start(bf16[256,64]{0,1:T(8,128)(2,1)} %fusion.13) | copy-start | bytes 98308
Sparse Core Ops, SparseCore 0:
  36.1 155.1 all-gather.7
  263.7 138.9 all-gather.17
  406.7 138.1 all-gather.9
  546.9 36.8 all-gather.11
  585.7 47.8 all-gather.13
  635.5 47.8 all-gather.15
  689.8 215.9 reduce-scatter.1
where the time goes:
time: 925 us; the launch traced here: 914 us
  waiting for transfers between devices  603 us (65%)
  blocking collectives  268 us (29%)
  between operations  14.4 us (2%)
  matrix products  13.3 us (1%)
    reduce_scatter x1, waiting for transfers between devices, on_device(): lax.psum_scatter(partial_down, 'dev', scatter_dimension=1, tiled=True)  216 us
    all_gather x1, waiting for transfers between devices, on_device(): full_rows = lax.all_gather(attended, 'dev', axis=1, tiled=True)  136 us
    all_gather x1, waiting for transfers between devices, on_device(): lax.all_gather(mixed, 'dev', axis=0, tiled=True)  115 us
    all_gather x1, blocking collectives, on_device(): lax.all_gather(keys, 'dev', axis=1, tiled=True)  104 us
    all_gather x1, blocking collectives, on_device(): lax.all_gather(values, 'dev', axis=1, tiled=True)  73 us
    all_gather x1, waiting for transfers between devices, on_device(): lax.all_gather(w_down, 'grp', axis=0, tiled=True)  49.8 us
    all_gather x1, waiting for transfers between devices, on_device(): lax.all_gather(w_up, 'grp', axis=0, tiled=True)  47.4 us
    all_gather x1, waiting for transfers between devices, on_device(): lax.all_gather(w_gate, 'grp', axis=0, tiled=True)  36.5 us
  transfers between devices with their start and end apart: 7, of which 6 were waited for; matrix products, arithmetic and copies ran while one was open for 1% of the time, Pallas kernels for 0%

commit v1 on v0

v1 whole, which is shorter than its diff:
```python
import functools
import math

import jax
import jax.numpy as jnp
from jax import lax
from jax.experimental import pallas as pl
from jax.experimental.pallas import tpu as pltpu
from jax.sharding import PartitionSpec as P

HEADS = 32
KV_HEADS = 8
HEAD_DIM = 128
ROW_LEN = 128
D = 4096
ROPE_BASE = 500000.0

GROUPS = 8
MEMBERS = 64
DEPTH = 16
HALF = 64
QC = 64
KC = 16
FC = 224
BAND = 256
RUN = 512

COLUMNS = [[4 * z + q for z in range(DEPTH)] for q in range(4)]
QUADS = [[4 * z + q for q in range(4)] for z in range(DEPTH)]
OCTETS = [[8 * z + m for m in range(8)] for z in range(8)]

BF = jnp.bfloat16
F32 = jnp.float32
VMEM = pl.BlockSpec(memory_space=pltpu.VMEM)
SMEM = pl.BlockSpec(memory_space=pltpu.SMEM)


def nt(a, b):
    return lax.dot_general(a, b, (((1,), (1,)), ((), ())), preferred_element_type=F32)


def params(mib):
    return pltpu.CompilerParams(vmem_limit_bytes=mib * 2**20)


def cost(flops, nbytes):
    return pl.CostEstimate(flops=flops, bytes_accessed=nbytes, transcendentals=0)


def project_kernel(at, stream, gain, weights, cos, sin, send, keys, values, own):
    x = stream[...].astype(F32)
    scale = lax.rsqrt(jnp.mean(x * x, axis=-1, keepdims=True) + 1e-05)
    total = jnp.zeros((256, 96), F32)
    for g in range(GROUPS):
        cols = pl.ds(g * RUN, RUN)
        part = stream[:, cols].astype(F32) * scale * gain[:, cols]
        total = total + nt(part.astype(BF), weights[g, 0:96, :])
    total = jnp.concatenate([total, jnp.zeros((256, 32), F32)], axis=1)
    lane = lax.broadcasted_iota(jnp.int32, (256, 128), 1)
    partner = jnp.where(lane % 2 == 0, -pltpu.roll(total, 127, 1), pltpu.roll(total, 1, 1))
    turned = jnp.where(lane < QC + KC, total * cos[...] + partner * sin[...], total)
    turned = turned.astype(BF).astype(F32)
    flipped = turned.T
    keys[...] = flipped[QC : QC + KC, :].astype(BF)
    values[...] = flipped[QC + KC : QC + 2 * KC, :].astype(BF)
    lane = lax.broadcasted_iota(jnp.int32, (HALF, 128), 1)
    for zl in range(2):
        for yhi in range(2):
            for c in range(2):
                first = turned[c * 128 : c * 128 + HALF, :]
                second = turned[c * 128 + HALF : c * 128 + 128, :]
                mine = second if yhi else first
                chunk = jnp.where(lane < QC, mine, jnp.where(lane < 96, first, pltpu.roll(second, 32, 1)))
                send[zl * 4 + yhi * 2 + c] = chunk.astype(BF)
    rows = pl.ds(pl.multiple_of(at[0] * 128 + at[1] * HALF, HALF), HALF)
    own[...] = stream[rows, pl.ds(pl.multiple_of(at[2] * BAND, BAND), BAND)]


def attend_kernel(at, got, out):
    lane = lax.broadcasted_iota(jnp.int32, (HALF, 128), 1)
    pieces = [got[m].astype(F32) for m in range(8)]

    def gather(start):
        full = jnp.zeros((HALF, 128), F32)
        for m in range(8):
            full = jnp.where(lane // KC == m, pltpu.roll(pieces[m], (KC * m - start) % 128, 1), full)
        return full.astype(BF)

    keys = jnp.concatenate([gather(QC), gather(96)], axis=0)
    values = jnp.concatenate([gather(QC + KC), gather(96 + KC)], axis=0)
    slot = lax.broadcasted_iota(jnp.int32, (HALF, 128), 0) + at[1] * HALF
    allowed = (lane <= slot) & (lane < at[4])
    for a in range(2):
        low = got[at[3] * 4 + a * 2].astype(F32)
        high = got[at[3] * 4 + a * 2 + 1].astype(F32)
        queries = jnp.where(lane < QC, low, pltpu.roll(high, QC, 1)).astype(BF)
        scores = nt(queries, keys) / math.sqrt(HEAD_DIM)
        scores = jnp.where(allowed, scores, -jnp.inf)
        expo = jnp.exp(scores - jnp.max(scores, axis=-1, keepdims=True))
        probs = (expo / jnp.sum(expo, axis=-1, keepdims=True)).astype(BF)
        mixed = jnp.dot(probs, values, preferred_element_type=F32).astype(BF)
        for z in range(DEPTH):
            out[z, :, a * 128 : a * 128 + 128] = mixed


def output_kernel(at, got, mine, core, far, cross, own, out):
    parts = []
    for w in (mine, core, far, cross):
        total = jnp.zeros((HALF, QC), F32)
        for g in range(GROUPS):
            total = total + nt(got[2 * g], w[g, :, 0:BAND]) + nt(got[2 * g + 1], w[g, :, BAND:RUN])
        parts.append(total)
    blocks = []
    for j in range(4):
        picked = parts[0]
        for k in range(1, 4):
            picked = jnp.where(jnp.bitwise_xor(at[5], j) == k, parts[k], picked)
        blocks.append(picked)
    projected = jnp.concatenate(blocks, axis=1)
    attended = (own[...].astype(F32) + projected).astype(BF)
    for z in range(DEPTH):
        out[z] = attended


def hidden_kernel(got, gain, mine, core, out, normed, totals):
    g = pl.program_id(0)

    @pl.when(g == 0)
    def _():
        squares = jnp.zeros((HALF, 1), F32)
        for z in range(DEPTH):
            x = got[z].astype(F32)
            squares = squares + jnp.sum(x * x, axis=-1, keepdims=True)
        scale = lax.rsqrt(squares * (1.0 / D) + 1e-05)
        for z in range(DEPTH):
            x = got[z].astype(F32) * scale * gain[:, z * BAND : (z + 1) * BAND]
            normed[z // 2, :, (z % 2) * BAND : (z % 2 + 1) * BAND] = x.astype(BF)
        totals[...] = jnp.zeros_like(totals)

    x = normed[g]
    for i, w in enumerate((mine, core)):
        totals[i, 0] += nt(x, w[0, 0:FC, :])
        totals[i, 1] += nt(x, w[0, FC : 2 * FC, :])

    @pl.when(g == GROUPS - 1)
    def _():
        for i in range(2):
            gate = totals[i, 0]
            out[i] = (gate / (1.0 + jnp.exp(-gate)) * totals[i, 1]).astype(BF)


def down_kernel(hidden, mine, core, out):
    total = jnp.dot(hidden[0], mine[0], preferred_element_type=F32)
    total = total + jnp.dot(hidden[1], core[0], preferred_element_type=F32)
    out[0] = total[:, 0:BAND].astype(out.dtype)
    out[1] = total[:, BAND:RUN].astype(out.dtype)


def finish_kernel(got, attended, out):
    total = got[0].astype(F32)
    for z in range(1, DEPTH):
        total = total + got[z].astype(F32)
    result = (attended[0].astype(F32) + total).T
    for q in range(4):
        out[q] = result[q * QC : (q + 1) * QC, :].astype(BF)


def project(at, stream, gain, weights, cos, sin):
    return pl.pallas_call(
        project_kernel,
        out_shape=(
            jax.ShapeDtypeStruct((8, HALF, 128), BF),
            jax.ShapeDtypeStruct((KC, 256), BF),
            jax.ShapeDtypeStruct((KC, 256), BF),
            jax.ShapeDtypeStruct((HALF, BAND), BF),
        ),
        in_specs=[SMEM] + [VMEM] * 5,
        out_specs=(VMEM,) * 4,
        compiler_params=params(32),
        name="project",
    )(at, stream, gain, weights, cos, sin)


def attend(at, got):
    return pl.pallas_call(
        attend_kernel,
        out_shape=jax.ShapeDtypeStruct((DEPTH, HALF, BAND), BF),
        in_specs=[SMEM, VMEM],
        out_specs=VMEM,
        compiler_params=params(16),
        name="attend",
    )(at, got)


def output(at, got, weights, own):
    return pl.pallas_call(
        output_kernel,
        out_shape=jax.ShapeDtypeStruct((DEPTH, HALF, BAND), BF),
        in_specs=[SMEM] + [VMEM] * 6,
        out_specs=VMEM,
        compiler_params=params(24),
        name="output",
    )(at, got, *weights, own)


def hidden_units(got, gain, mine, core):
    block = pl.BlockSpec((1, 2 * FC, RUN), lambda g: (g, 0, 0))
    return pl.pallas_call(
        hidden_kernel,
        grid=(GROUPS,),
        out_shape=jax.ShapeDtypeStruct((2, HALF, FC), BF),
        in_specs=[
            pl.BlockSpec((DEPTH, HALF, BAND), lambda g: (0, 0, 0)),
            pl.BlockSpec((1, D), lambda g: (0, 0)),
            block,
            block,
        ],
        out_specs=pl.BlockSpec((2, HALF, FC), lambda g: (0, 0, 0)),
        scratch_shapes=[pltpu.VMEM((GROUPS, HALF, RUN), BF), pltpu.VMEM((2, 2, HALF, FC), F32)],
        compiler_params=params(24),
        cost_estimate=cost(2 * HALF * D * 4 * FC, 8 * 2**20),
        name="hidden",
    )(got, gain, mine, core)


def down(hidden, mine, core, dtype):
    block = pl.BlockSpec((1, FC, RUN), lambda g: (g, 0, 0))
    return pl.pallas_call(
        down_kernel,
        grid=(GROUPS,),
        out_shape=jax.ShapeDtypeStruct((DEPTH, HALF, BAND), dtype),
        in_specs=[pl.BlockSpec((2, HALF, FC), lambda g: (0, 0, 0)), block, block],
        out_specs=pl.BlockSpec((2, HALF, BAND), lambda g: (g, 0, 0)),
        compiler_params=params(24),
        cost_estimate=cost(2 * HALF * D * 2 * FC, 5 * 2**20),
        name="down",
    )(hidden, mine, core)


def finish(got, attended):
    return pl.pallas_call(
        finish_kernel,
        out_shape=jax.ShapeDtypeStruct((4, QC, HALF), BF),
        in_specs=[VMEM, VMEM],
        out_specs=VMEM,
        compiler_params=params(16),
        name="finish",
    )(got, attended)


def swap(x, bits):
    return lax.ppermute(x, "dev", [(d, d ^ bits) for d in range(MEMBERS)])


def trade(x, groups):
    return lax.all_to_all(x, "dev", 0, 0, axis_index_groups=groups, tiled=True)


def on_device(
    stream,
    row_length,
    row_start,
    attn_gain,
    w_query,
    w_key,
    w_value,
    w_out,
    ffn_gain,
    w_gate,
    w_up,
    w_down,
):
    member = lax.axis_index("dev")
    core, yhi, z, quad = member % 2, member // 2 % 2, member // 4, member % 4
    length = jnp.where(core == 0, row_length[0], row_length[1])
    at = jnp.stack([core, yhi, z, z % 2, length, quad]).astype(jnp.int32)

    first = jnp.concatenate([w_query.T, w_key.T, w_value.T, w_out.T], axis=0)
    first = lax.all_to_all(jnp.broadcast_to(first[None], (GROUPS, 160, RUN)), "grp", 0, 0, tiled=True)
    out_own = first[:, 96:160, :]
    out_weights = (out_own, swap(out_own, 1), swap(out_own, 2), swap(out_own, 3))

    widen = lax.all_gather(jnp.concatenate([w_gate.T, w_up.T], axis=0), "grp", axis=0)
    narrow = lax.all_gather(w_down.T, "grp", axis=0)
    widen_core = swap(widen, 1)
    narrow_core = swap(narrow, 1)

    lane = jnp.arange(128, dtype=jnp.int32)
    column = jnp.where(lane < QC, member * QC + lane, member * KC + lane - QC)
    pair = (column % HEAD_DIM // 2).astype(F32)
    freq = jnp.exp(-(2.0 * pair / HEAD_DIM) * math.log(ROPE_BASE))
    positions = (row_start[:, None] + jnp.arange(ROW_LEN, dtype=jnp.int32)[None, :]).reshape(-1)
    angle = positions.astype(F32)[:, None] * freq[None, :]

    send, keys, values, own = project(
        at, stream, attn_gain.reshape(1, D), first, jnp.cos(angle), jnp.sin(angle)
    )
    mixed = trade(attend(at, trade(send, OCTETS)), COLUMNS)
    attended = output(at, mixed, out_weights, own)
    full = trade(attended, COLUMNS)
    far = swap(full, 2)
    gain = ffn_gain.reshape(1, D)
    hidden = hidden_units(full, gain, widen, widen_core)
    far_hidden = hidden_units(far, gain, widen, widen_core)
    far_sum = swap(down(far_hidden, narrow, narrow_core, BF), 2)
    total = down(hidden, narrow, narrow_core, F32)
    total = (total + far_sum.astype(F32)).astype(BF)
    blocks = trade(finish(trade(total, COLUMNS), attended), QUADS)
    next_stream = blocks.reshape(2, 2, QC, HALF).transpose(1, 0, 3, 2).reshape(256, QC)
    return (keys.T, values.T, next_stream)


def solution(mesh):
    placed = (
        P("grp", None),
        P("grp"),
        P("grp"),
        P(),
        P("grp", "dev"),
        P("grp", "dev"),
        P("grp", "dev"),
        P("grp", "dev"),
        P(),
        P("grp", "dev"),
        P("grp", "dev"),
        P("grp", "dev"),
    )
    return jax.shard_map(
        on_device,
        mesh=mesh,
        in_specs=placed,
        out_specs=(P("grp", "dev"), P("grp", "dev"), P("grp", "dev")),
        check_vma=False,
    )
```

time: 925 us -> 277 us (0.30); the launches traced: 914 us -> 276 us
  waiting for transfers between devices: 603 us -> 78.5 us
  blocking collectives: 268 us -> 92.4 us
  starting transfers between devices: 0.46 us -> 52.3 us
  Pallas kernels: 0 us -> 24.8 us
  matrix products: 13.3 us -> 0 us
    all_gather x6 -> x2, waiting for transfers between devices: 385 us -> 0.04 us  [the longest x1 0.02 us: on_device(): lax.all_gather(jnp.concatenate([w_gate.T, w_up.T], axis=0), 'grp', axis=0)]
    all_gather x6 -> x0, blocking collectives: 268 us -> none  [the longest x1 104 us: on_device(): lax.all_gather(keys, 'dev', axis=1, tiled=True)]
    reduce_scatter x1 -> x0, waiting for transfers between devices: 216 us -> none  [on_device(): lax.psum_scatter(partial_down, 'dev', scatter_dimension=1, tiled=True)]
    all_to_all x0 -> x3, blocking collectives: none -> 92.4 us  [trade(): return lax.all_to_all(x, 'dev', 0, 0, axis_index_groups=groups, tiled=True)]
    ppermute x0 -> x7, waiting for transfers between devices: none -> 45.5 us  [swap(): return lax.ppermute(x, 'dev', [(d, d ^ bits) for d in range(MEMBERS)])]
    all_to_all x0 -> x3, starting transfers between devices: none -> 33 us  [the longest x2 27.1 us: trade(): return lax.all_to_all(x, 'dev', 0, 0, axis_index_groups=groups, tiled=True)]
    all_to_all x0 -> x3, waiting for transfers between devices: none -> 32.3 us  [the longest x2 20.1 us: trade(): return lax.all_to_all(x, 'dev', 0, 0, axis_index_groups=groups, tiled=True)]
    pallas_call x0 -> x8, Pallas kernels: none -> 24.8 us  [the longest x2 13.4 us: hidden_units(): pl.pallas_call(hidden_kernel, grid=(GROUPS,), out_shape=jax.ShapeDtypeStr...]
  transfers between devices with their start and end apart: 7 -> 12, of which waited for: 6 -> 6; matrix products, arithmetic and copies ran while one was open for 1% -> 2% of each run, Pallas kernels for 0% -> 8%
where the time goes in v1:
time: 277 us; the launch traced here: 276 us
  blocking collectives  92.4 us (33%)
  waiting for transfers between devices  78.5 us (28%)
  starting transfers between devices  52.3 us (19%)
  Pallas kernels  24.8 us (9%)
  between operations  15.6 us (6%)
  local copies, waits for them, and re-layouts  7.84 us (3%)
  other arithmetic  4.24 us (2%)
    all_to_all x3, blocking collectives, trade(): return lax.all_to_all(x, 'dev', 0, 0, axis_index_groups=groups, tiled=True)  92.4 us
    ppermute x7, waiting for transfers between devices, swap(): return lax.ppermute(x, 'dev', [(d, d ^ bits) for d in range(MEMBERS)])  45.5 us
    all_to_all x2, starting transfers between devices, trade(): return lax.all_to_all(x, 'dev', 0, 0, axis_index_groups=groups, tiled=True)  27.1 us
    all_to_all x2, waiting for transfers between devices, trade(): return lax.all_to_all(x, 'dev', 0, 0, axis_index_groups=groups, tiled=True)  20.1 us
    ppermute x7, starting transfers between devices, swap(): return lax.ppermute(x, 'dev', [(d, d ^ bits) for d in range(MEMBERS)])  19.2 us
    pallas_call x2, Pallas kernels, hidden_units(): pl.pallas_call(hidden_kernel, grid=(GROUPS,), out_shape=jax.ShapeDtypeStr...  13.4 us
    all_to_all x1, waiting for transfers between devices, on_device(): lax.all_to_all(jnp.broadcast_to(first[None], (GROUPS, 160, RUN)), 'grp',...  12.1 us
    all_to_all x1, starting transfers between devices, on_device(): lax.all_to_all(jnp.broadcast_to(first[None], (GROUPS, 160, RUN)), 'grp',...  5.99 us
  transfers between devices with their start and end apart: 12, of which 6 were waited for; matrix products, arithmetic and copies ran while one was open for 2% of the time, Pallas kernels for 8%

profile of v1, /device:TPU:1, one launch (start us, length us, event | category | flops | bytes accessed | tf_op | source)
XLA Modules:
  0.0 275.7 jit_solution(4072885693368929758)
XLA Ops:
  7.2 0.0 all-gather.5.cloned.1.call-start
  7.2 1.9 pad_maximum_fusion
  9.1 0.0 all-gather.5.cloned.1.call-update
  9.1 0.9 pad_maximum_fusion.1
  10.1 1.2 broadcast_in_dim.2
  11.2 6.0 %all-to-all-start = ((bf16[8,160,512]{2,1,0:T(8,128)(2,1)}), bf16[8,160,512]{2,1,0:T(8,128)(2,1)S(1)}, u32[]{:S(2)}, u32[]{:S(2)}) async-start(bf16[8,160,512]{2,1,0:T(8,128)(2,1)} %broadcast_in_dim.2), calls=%async_computation | async-start | bytes 2621440 | tf_op jit(solution)/shard_map/all_to_all | solution.py:279
  17.2 0.0 all-gather.7.cloned.1.call-start
  17.3 0.7 all-gather.7.cloned.1.call-update
  18.1 0.1 convert_bitcast_fusion
  18.2 1.2 multiply_sine_fusion
  19.3 1.4 fusion.1
  22.0 0.6 stack.27.at
  22.6 12.1 %all-to-all-done.weights = bf16[8,160,512]{2,1,0:T(8,128)(2,1)S(1)} async-done(((bf16[8,160,512]{2,1,0:T(8,128)(2,1)}), bf16[8,160,512]{2,1,0:T(8,128)(2,1)S(1)}, u32[]{:S(2)}, u32[]{:S(2)}) %all-to-all-start) | async-done | bytes 1310752 | tf_op jit(solution)/shard_map/all_to_all | solution.py:279
  34.8 0.9 copy-done.4
  35.7 0.6 copy-done.9
  36.3 2.4 project.1
  38.7 34.5 %all_to_all.30.got = bf16[8,64,128]{2,1,0:T(8,128)(2,1)S(1)} all-to-all(bf16[8,64,128]{2,1,0:T(8,128)(2,1)S(1)} %get-tuple-element.9), channel_id=1, replica_groups={{0,1,2,3,4,5,6,7},{8,9,10,11,12,13,14,15},{16,17,18,19,20,21,22,23},{24..., dimensions={0} | all-to-all | bytes 262144 | tf_op jit(solution)/shard_map/all_to_all | solution.py:256
  73.2 2.3 attend.1
  75.5 15.0 %all-to-all-start.2 = ((bf16[16,64,256]{2,1,0:T(8,128)(2,1)}), bf16[16,64,256]{2,1,0:T(8,128)(2,1)S(1)}, u32[]{:S(2)}, u32[]{:S(2)}) async-start(bf16[16,64,256]{2,1,0:T(8,128)(2,1)} %attend.1), calls=%async_computation.2 | async-start | bytes 1048576 | tf_op jit(solution)/shard_map/all_to_all | solution.py:256
  90.6 0.0 all-gather.5.cloned.1.call-done
  90.6 2.9 %collective-permute-start.3 = (bf16[8,448,512]{2,1,0:T(8,128)(2,1)}, bf16[8,448,512]{2,1,0:T(8,128)(2,1)}, u32[]{:S(2)}, u32[]{:S(2)}) collective-permute-start(bf16[8,448,512]{2,1,0:T(8,128)(2,1)} %bitcast.28), channel_id=1, source_target_pairs={{0,1},{1,0},{2,3},{3,2},{4,5},{5,4},{6,7},{7,6},{8,9},{9,8},{10,11... | collective-permute-start | bytes 11010056 | tf_op jit(solution)/shard_map/ppermute | solution.py:252
  93.5 2.2 collective-permute-start.2
  95.7 4.5 %collective-permute-start.1 = (bf16[8,64,512]{2,1,0:T(8,128)(2,1)S(1)}, bf16[8,64,512]{2,1,0:T(8,128)(2,1)S(1)}, u32[]{:S(2)}, u32[]{:S(2)}) collective-permute-start(bf16[8,64,512]{2,1,0:T(8,128)(2,1)S(1)} %slice.12.mine), channel_id=1, source_target_pairs={{0,2},{1,3},{2,0},{3,1},{4,6},{5,7},{6,4},{7,5},{8,10},{9,11},{10,... | collective-permute-start | bytes 1572872 | tf_op jit(solution)/shard_map/ppermute | solution.py:252
  100.2 2.7 collective-permute-start
  102.9 24.0 %collective-permute-done.2.cross = bf16[8,64,512]{2,1,0:T(8,128)(2,1)S(1)} collective-permute-done((bf16[8,64,512]{2,1,0:T(8,128)(2,1)S(1)}, bf16[8,64,512]{2,1,0:T(8,128)(2,1)S(1)}, u32[]{:S(2)}, u32[]{:S(2)}) %collective-permute-start.2) | collective-permute-done | bytes 524320 | tf_op jit(solution)/shard_map/ppermute | solution.py:252
  126.9 11.2 %collective-permute-done.1.far = bf16[8,64,512]{2,1,0:T(8,128)(2,1)S(1)} collective-permute-done((bf16[8,64,512]{2,1,0:T(8,128)(2,1)S(1)}, bf16[8,64,512]{2,1,0:T(8,128)(2,1)S(1)}, u32[]{:S(2)}, u32[]{:S(2)}) %collective-permute-start.1) | collective-permute-done | bytes 524320 | tf_op jit(solution)/shard_map/ppermute | solution.py:252
  138.2 2.2 output.1.attended
  140.3 12.0 %all-to-all-start.3 = ((bf16[16,64,256]{2,1,0:T(8,128)(2,1)}), bf16[16,64,256]{2,1,0:T(8,128)(2,1)S(1)}, u32[]{:S(2)}, u32[]{:S(2)}) async-start(bf16[16,64,256]{2,1,0:T(8,128)(2,1)} %output.1.attended), calls=%async_computation.3 | async-start | bytes 1048576 | tf_op jit(solution)/shard_map/all_to_all | solution.py:256
  152.4 0.0 all-gather.7.cloned.1.call-done
  152.4 2.6 collective-permute-start.4
  155.0 20.1 %all-to-all-done.3.got = bf16[16,64,256]{2,1,0:T(8,128)(2,1)S(1)} async-done(((bf16[16,64,256]{2,1,0:T(8,128)(2,1)}), bf16[16,64,256]{2,1,0:T(8,128)(2,1)S(1)}, u32[]{:S(2)}, u32[]{:S(2)}) %all-to-all-start.3) | async-done | bytes 524320 | tf_op jit(solution)/shard_map/all_to_all | solution.py:256
  175.2 2.1 collective-permute-start.5
  177.3 9.3 %collective-permute-done.5.got = bf16[16,64,256]{2,1,0:T(8,128)(2,1)S(1)} collective-permute-done((bf16[16,64,256]{2,1,0:T(8,128)(2,1)S(1)}, bf16[16,64,256]{2,1,0:T(8,128)(2,1)S(1)}, u32[]{:S(2)}, u32[]{:S(2)}) %collective-permute-start.5) | collective-permute-done | bytes 524320 | tf_op jit(solution)/shard_map/ppermute | solution.py:252
  186.6 2.0 copy-done
  188.6 6.8 %hidden.3 = bf16[2,64,224]{2,1,0:T(8,128)(2,1)S(1)} custom-call(bf16[16,64,256]{2,1,0:T(8,128)(2,1)S(1)} %collective-permute-done.5.got, f32[1,4096]{1,0:T(1,128)S(1)} %bitcast.34, bf16[8,448,512]{2,1,0:T(8,128)(2,1)S(1)} %bitcast.29, bf16[8,448,512]{2,1,0:T(8,128)(2,1)} %collective-permute-done.3.core), custom_call_target="tpu_custom_call" | custom-call | flops 469762048 | bytes 8388608 | tf_op jit(solution)/shard_map/hidden/pallas_call | solution.py:208
  195.4 1.7 down.3
  197.1 2.1 collective-permute-start.6
  199.3 6.6 %hidden.2 = bf16[2,64,224]{2,1,0:T(8,128)(2,1)S(1)} custom-call(bf16[16,64,256]{2,1,0:T(8,128)(2,1)S(1)} %all-to-all-done.3.got, f32[1,4096]{1,0:T(1,128)S(1)} %bitcast.35, bf16[8,448,512]{2,1,0:T(8,128)(2,1)S(1)} %bitcast.30, bf16[8,448,512]{2,1,0:T(8,128)(2,1)} %collective-permute-done.3.core), custom_call_target="tpu_custom_call" | custom-call | flops 469762048 | bytes 8388608 | tf_op jit(solution)/shard_map/hidden/pallas_call | solution.py:208
  205.9 1.6 down.2
  207.5 1.0 collective-permute-done.6
  208.5 0.1 add_convert_fusion
  208.7 43.0 %all_to_all.31.got = bf16[16,64,256]{2,1,0:T(8,128)(2,1)S(1)} all-to-all(bf16[16,64,256]{2,1,0:T(8,128)(2,1)S(1)} %add_convert_fusion), channel_id=1, replica_groups={{0,4,8,12,16,20,24,28,32,36,40,44,48,52,56,60},{1,5,9,13,17,21,25,29,33..., dimensions={0} | all-to-all | bytes 1048576 | tf_op jit(solution)/shard_map/all_to_all | solution.py:256
  251.7 1.2 finish.1
  252.9 0.1 reshape.82
  253.0 14.9 %all_to_all.32 = bf16[4,2,2048]{2,1,0:T(2,128)(2,1)S(1)} all-to-all(bf16[4,2,2048]{2,1,0:T(2,128)(2,1)S(1)} %reshape.82), channel_id=1, replica_groups={{0,1,2,3},{4,5,6,7},{8,9,10,11},{12,13,14,15},{16,17,18,19},{20,21,22,2..., dimensions={0} | all-to-all | bytes 65536 | tf_op jit(solution)/shard_map/all_to_all | solution.py:256
  267.9 0.1 reshape.83
  268.0 0.1 copy.15
  268.1 0.7 reshape.79
  (27 shorter events, 0.1 us)
Async XLA Ops:
  7.2 83.4 %all-gather.5.cloned.1.call-start = ((), (), s32[]{:S(2)}) async-start(), calls=%async_computation.6 | async-start | bytes 4128768 | tf_op jit(solution)/shard_map/all_gather | solution.py:283
  11.2 6.8 %copy-start.11 = (s32[2]{0:T(128)S(1)}, s32[2]{0:T(128)}, u32[]{:S(2)}) copy-start(s32[2]{0:T(128)} %param.14) | copy-start | bytes 28
  11.2 23.5 %copy-start.3 = (bf16[256,4096]{1,0:T(8,128)(2,1)S(1)}, bf16[256,4096]{1,0:T(8,128)(2,1)}, u32[]{:S(2)}) copy-start(bf16[256,4096]{1,0:T(8,128)(2,1)} %stream.1) | copy-start | bytes 6291460
  11.2 23.5 %copy-start.8 = (f32[4096]{0:T(1024)S(1)}, f32[4096]{0:T(1024)}, u32[]{:S(2)}) copy-start(f32[4096]{0:T(1024)} %param.15) | copy-start | bytes 49156
  11.2 23.5 %all-to-all-start = ((bf16[8,160,512]{2,1,0:T(8,128)(2,1)}), bf16[8,160,512]{2,1,0:T(8,128)(2,1)S(1)}, u32[]{:S(2)}, u32[]{:S(2)}) async-start(bf16[8,160,512]{2,1,0:T(8,128)(2,1)} %broadcast_in_dim.2), calls=%async_computation | async-start | bytes 2621440 | tf_op jit(solution)/shard_map/all_to_all | solution.py:279
  17.2 135.1 %all-gather.7.cloned.1.call-start = ((), (), s32[]{:S(2)}) async-start(), calls=%async_computation.7 | async-start | bytes 2064384 | tf_op jit(solution)/shard_map/all_gather | solution.py:284
  34.8 0.9 copy-start.4
  35.7 0.6 copy-start.9
  38.7 34.5 %copy-start.6 = (bf16[64,256]{1,0:T(8,128)(2,1)}, bf16[64,256]{1,0:T(8,128)(2,1)S(1)}, u32[]{:S(2)}) copy-start(bf16[64,256]{1,0:T(8,128)(2,1)S(1)} %get-tuple-element.10.own) | copy-start | bytes 98308
  38.7 99.4 %copy-start.10 = (s32[6]{0:T(128)S(1)}, s32[6]{0:T(128)}, u32[]{:S(2)}) copy-start(s32[6]{0:T(128)} %stack.27.at) | copy-start | bytes 76
  75.5 62.7 %copy-start.7 = (bf16[64,256]{1,0:T(8,128)(2,1)S(1)}, bf16[64,256]{1,0:T(8,128)(2,1)}, u32[]{:S(2)}) copy-start(bf16[64,256]{1,0:T(8,128)(2,1)} %copy-done.6) | copy-start | bytes 98308
  75.5 62.6 %all-to-all-start.2 = ((bf16[16,64,256]{2,1,0:T(8,128)(2,1)}), bf16[16,64,256]{2,1,0:T(8,128)(2,1)S(1)}, u32[]{:S(2)}, u32[]{:S(2)}) async-start(bf16[16,64,256]{2,1,0:T(8,128)(2,1)} %attend.1), calls=%async_computation.2 | async-start | bytes 1048576 | tf_op jit(solution)/shard_map/all_to_all | solution.py:256
  90.6 96.0 %collective-permute-start.3 = (bf16[8,448,512]{2,1,0:T(8,128)(2,1)}, bf16[8,448,512]{2,1,0:T(8,128)(2,1)}, u32[]{:S(2)}, u32[]{:S(2)}) collective-permute-start(bf16[8,448,512]{2,1,0:T(8,128)(2,1)} %bitcast.28), channel_id=1, source_target_pairs={{0,1},{1,0},{2,3},{3,2},{4,5},{5,4},{6,7},{7,6},{8,9},{9,8},{10,11... | collective-permute-start | bytes 11010056 | tf_op jit(solution)/shard_map/ppermute | solution.py:252
  93.5 33.4 %collective-permute-start.2 = (bf16[8,64,512]{2,1,0:T(8,128)(2,1)S(1)}, bf16[8,64,512]{2,1,0:T(8,128)(2,1)S(1)}, u32[]{:S(2)}, u32[]{:S(2)}) collective-permute-start(bf16[8,64,512]{2,1,0:T(8,128)(2,1)S(1)} %slice.12.mine), channel_id=1, source_target_pairs={{0,3},{1,2},{2,1},{3,0},{4,7},{5,6},{6,5},{7,4},{8,11},{9,10},{10,... | collective-permute-start | bytes 1572872 | tf_op jit(solution)/shard_map/ppermute | solution.py:252
  95.7 42.4 %collective-permute-start.1 = (bf16[8,64,512]{2,1,0:T(8,128)(2,1)S(1)}, bf16[8,64,512]{2,1,0:T(8,128)(2,1)S(1)}, u32[]{:S(2)}, u32[]{:S(2)}) collective-permute-start(bf16[8,64,512]{2,1,0:T(8,128)(2,1)S(1)} %slice.12.mine), channel_id=1, source_target_pairs={{0,2},{1,3},{2,0},{3,1},{4,6},{5,7},{6,4},{7,5},{8,10},{9,11},{10,... | collective-permute-start | bytes 1572872 | tf_op jit(solution)/shard_map/ppermute | solution.py:252
  100.2 37.9 %collective-permute-start = (bf16[8,64,512]{2,1,0:T(8,128)(2,1)S(1)}, bf16[8,64,512]{2,1,0:T(8,128)(2,1)S(1)}, u32[]{:S(2)}, u32[]{:S(2)}) collective-permute-start(bf16[8,64,512]{2,1,0:T(8,128)(2,1)S(1)} %slice.12.mine), channel_id=1, source_target_pairs={{0,1},{1,0},{2,3},{3,2},{4,5},{5,4},{6,7},{7,6},{8,9},{9,8},{10,11... | collective-permute-start | bytes 1572872 | tf_op jit(solution)/shard_map/ppermute | solution.py:252
  138.2 48.4 %copy-start.5 = (f32[4096]{0:T(1024)S(1)}, f32[4096]{0:T(1024)}, u32[]{:S(2)}) copy-start(f32[4096]{0:T(1024)} %param.20) | copy-start | bytes 49156
  140.3 34.8 %all-to-all-start.3 = ((bf16[16,64,256]{2,1,0:T(8,128)(2,1)}), bf16[16,64,256]{2,1,0:T(8,128)(2,1)S(1)}, u32[]{:S(2)}, u32[]{:S(2)}) async-start(bf16[16,64,256]{2,1,0:T(8,128)(2,1)} %output.1.attended), calls=%async_computation.3 | async-start | bytes 1048576 | tf_op jit(solution)/shard_map/all_to_all | solution.py:256
  152.4 43.0 %collective-permute-start.4 = (bf16[8,224,512]{2,1,0:T(8,128)(2,1)}, bf16[8,224,512]{2,1,0:T(8,128)(2,1)S(1)}, u32[]{:S(2)}, u32[]{:S(2)}) collective-permute-start(bf16[8,224,512]{2,1,0:T(8,128)(2,1)} %bitcast.31), channel_id=1, source_target_pairs={{0,1},{1,0},{2,3},{3,2},{4,5},{5,4},{6,7},{7,6},{8,9},{9,8},{10,11... | collective-permute-start | bytes 5505032 | tf_op jit(solution)/shard_map/ppermute | solution.py:252
  175.2 11.4 %collective-permute-start.5 = (bf16[16,64,256]{2,1,0:T(8,128)(2,1)S(1)}, bf16[16,64,256]{2,1,0:T(8,128)(2,1)S(1)}, u32[]{:S(2)}, u32[]{:S(2)}) collective-permute-start(bf16[16,64,256]{2,1,0:T(8,128)(2,1)S(1)} %all-to-all-done.3.got), channel_id=1, source_target_pairs={{0,2},{1,3},{2,0},{3,1},{4,6},{5,7},{6,4},{7,5},{8,10},{9,11},{10,... | collective-permute-start | bytes 1572872 | tf_op jit(solution)/shard_map/ppermute | solution.py:252
  186.6 2.0 copy-start
  188.6 6.8 %copy-start.2 = (bf16[1792,512]{1,0:T(8,128)(2,1)S(1)}, bf16[1792,512]{1,0:T(8,128)(2,1)}, u32[]{:S(2)}) copy-start(bf16[1792,512]{1,0:T(8,128)(2,1)} %all-gather.7.cloned.1.call-done) | copy-start | bytes 5505028
  195.4 3.9 %copy-start.1 = (bf16[3584,512]{1,0:T(8,128)(2,1)S(1)}, bf16[3584,512]{1,0:T(8,128)(2,1)}, u32[]{:S(2)}) copy-start(bf16[3584,512]{1,0:T(8,128)(2,1)} %all-gather.5.cloned.1.call-done) | copy-start | bytes 11010052
  197.1 11.4 %collective-permute-start.6 = (bf16[16,64,256]{2,1,0:T(8,128)(2,1)S(1)}, bf16[16,64,256]{2,1,0:T(8,128)(2,1)S(1)}, u32[]{:S(2)}, u32[]{:S(2)}) collective-permute-start(bf16[16,64,256]{2,1,0:T(8,128)(2,1)S(1)} %down.3), channel_id=1, source_target_pairs={{0,2},{1,3},{2,0},{3,1},{4,6},{5,7},{6,4},{7,5},{8,10},{9,11},{10,... | collective-permute-start | bytes 1572872 | tf_op jit(solution)/shard_map/ppermute | solution.py:252
Sparse Core Ops, SparseCore 0:
  10.1 61.9 all-gather.4
  74.1 46.0 all-gather.6

commit v2 on v1

--- a/solution.py
+++ b/solution.py
@@ -1,4 +1,3 @@
-import functools
 import math
 
 import jax
@@ -26,7 +25,6 @@
 RUN = 512
 
 COLUMNS = [[4 * z + q for z in range(DEPTH)] for q in range(4)]
-QUADS = [[4 * z + q for q in range(4)] for z in range(DEPTH)]
 OCTETS = [[8 * z + m for m in range(8)] for z in range(8)]
 
 BF = jnp.bfloat16
@@ -99,8 +97,7 @@
         expo = jnp.exp(scores - jnp.max(scores, axis=-1, keepdims=True))
         probs = (expo / jnp.sum(expo, axis=-1, keepdims=True)).astype(BF)
         mixed = jnp.dot(probs, values, preferred_element_type=F32).astype(BF)
-        for z in range(DEPTH):
-            out[z, :, a * 128 : a * 128 + 128] = mixed
+        out[:, a * 128 : a * 128 + 128] = mixed
 
 
 def output_kernel(at, got, mine, core, far, cross, own, out):
@@ -118,11 +115,10 @@
         blocks.append(picked)
     projected = jnp.concatenate(blocks, axis=1)
     attended = (own[...].astype(F32) + projected).astype(BF)
-    for z in range(DEPTH):
-        out[z] = attended
-
-
-def hidden_kernel(got, gain, mine, core, out, normed, totals):
+    out[...] = attended
+
+
+def hidden_kernel(at, got, gain, mine, core, out, kept, normed, totals):
     g = pl.program_id(0)
 
     @pl.when(g == 0)
@@ -138,31 +134,69 @@
         totals[...] = jnp.zeros_like(totals)
 
     x = normed[g]
-    for i, w in enumerate((mine, core)):
-        totals[i, 0] += nt(x, w[0, 0:FC, :])
-        totals[i, 1] += nt(x, w[0, FC : 2 * FC, :])
+    totals[0] += nt(mine[0, 0], x)
+    totals[1] += nt(core[0, 0], x)
 
     @pl.when(g == GROUPS - 1)
     def _():
         for i in range(2):
-            gate = totals[i, 0]
-            out[i] = (gate / (1.0 + jnp.exp(-gate)) * totals[i, 1]).astype(BF)
-
-
-def down_kernel(hidden, mine, core, out):
-    total = jnp.dot(hidden[0], mine[0], preferred_element_type=F32)
-    total = total + jnp.dot(hidden[1], core[0], preferred_element_type=F32)
-    out[0] = total[:, 0:BAND].astype(out.dtype)
-    out[1] = total[:, BAND:RUN].astype(out.dtype)
-
-
-def finish_kernel(got, attended, out):
+            gate = totals[i, 0:FC, :]
+            units = gate / (1.0 + jnp.exp(-gate)) * totals[i, FC : 2 * FC, :]
+            out[i] = units.T.astype(BF)
+        kept[...] = got[at[2], :, pl.ds(pl.multiple_of(at[1] * 128, 128), 128)]
+
+
+def down_kernel(at, near, far, far_near, far_far, mine, core, out, units):
+    g = pl.program_id(0)
+
+    @pl.when(g == 0)
+    def _():
+        own = pl.ds(pl.multiple_of(at[1] * HALF, HALF), HALF)
+        other = pl.ds(pl.multiple_of((1 - at[1]) * HALF, HALF), HALF)
+        for i in range(2):
+            units[i, own, :] = near[i]
+            units[i, other, :] = far[i]
+            units[2 + i, own, :] = far_far[i]
+            units[2 + i, other, :] = far_near[i]
+
+    total = jnp.dot(units[0], mine[0, 0, :, 0:BAND], preferred_element_type=F32)
+    total = total + jnp.dot(units[1], core[0, 0, :, 0:BAND], preferred_element_type=F32)
+    total = total + jnp.dot(units[2], mine[0, 0, :, BAND:RUN], preferred_element_type=F32)
+    total = total + jnp.dot(units[3], core[0, 0, :, BAND:RUN], preferred_element_type=F32)
+    out[0] = total[:, 0:128].astype(BF)
+    out[1] = total[:, 128:256].astype(BF)
+
+
+def finish_kernel(at, got, near, far, keep, give):
     total = got[0].astype(F32)
     for z in range(1, DEPTH):
         total = total + got[z].astype(F32)
-    result = (attended[0].astype(F32) + total).T
-    for q in range(4):
-        out[q] = result[q * QC : (q + 1) * QC, :].astype(BF)
+    low = at[1] == 0
+    first = jnp.where(low, near[...].astype(F32), far[...].astype(F32))
+    second = jnp.where(low, far[...].astype(F32), near[...].astype(F32))
+    result = (jnp.concatenate([first, second], axis=0) + total).T
+    head, tail = result[0:QC, :], result[QC : 2 * QC, :]
+    keep[...] = jnp.where(at[0] == 0, head, tail).astype(BF)
+    give[...] = jnp.where(at[0] == 0, tail, head).astype(BF)
+
+
+def pack_kernel(query, key, value, out_part, out):
+    for g in range(GROUPS):
+        out[g, 0:QC, :] = query[...]
+        out[g, QC : QC + KC, :] = key[...]
+        out[g, QC + KC : QC + 2 * KC, :] = value[...]
+        out[g, 96:160, :] = out_part[...]
+
+
+def pack(*parts):
+    return pl.pallas_call(
+        pack_kernel,
+        out_shape=jax.ShapeDtypeStruct((GROUPS, 160, RUN), BF),
+        in_specs=[VMEM] * 4,
+        out_specs=VMEM,
+        compiler_params=params(16),
+        name="pack",
+    )(*parts)
 
 
 def project(at, stream, gain, weights, cos, sin):
@@ -184,7 +218,7 @@
 def attend(at, got):
     return pl.pallas_call(
         attend_kernel,
-        out_shape=jax.ShapeDtypeStruct((DEPTH, HALF, BAND), BF),
+        out_shape=jax.ShapeDtypeStruct((HALF, BAND), BF),
         in_specs=[SMEM, VMEM],
         out_specs=VMEM,
         compiler_params=params(16),
@@ -195,7 +229,7 @@
 def output(at, got, weights, own):
     return pl.pallas_call(
         output_kernel,
-        out_shape=jax.ShapeDtypeStruct((DEPTH, HALF, BAND), BF),
+        out_shape=jax.ShapeDtypeStruct((HALF, BAND), BF),
         in_specs=[SMEM] + [VMEM] * 6,
         out_specs=VMEM,
         compiler_params=params(24),
@@ -203,57 +237,83 @@
     )(at, got, *weights, own)
 
 
-def hidden_units(got, gain, mine, core):
-    block = pl.BlockSpec((1, 2 * FC, RUN), lambda g: (g, 0, 0))
+def weights_at(g, at, part):
+    return (g % 4, jnp.bitwise_xor(g // 4, at[6]), part, 0)
+
+
+def hidden_units(at, got, gain, mine, core):
+    block = pl.BlockSpec((1, 1, 2 * FC, RUN), lambda g, at: weights_at(g, at, 0))
     return pl.pallas_call(
         hidden_kernel,
-        grid=(GROUPS,),
-        out_shape=jax.ShapeDtypeStruct((2, HALF, FC), BF),
-        in_specs=[
-            pl.BlockSpec((DEPTH, HALF, BAND), lambda g: (0, 0, 0)),
-            pl.BlockSpec((1, D), lambda g: (0, 0)),
-            block,
-            block,
-        ],
-        out_specs=pl.BlockSpec((2, HALF, FC), lambda g: (0, 0, 0)),
-        scratch_shapes=[pltpu.VMEM((GROUPS, HALF, RUN), BF), pltpu.VMEM((2, 2, HALF, FC), F32)],
+        grid_spec=pltpu.PrefetchScalarGridSpec(
+            num_scalar_prefetch=1,
+            grid=(GROUPS,),
+            in_specs=[
+                pl.BlockSpec((DEPTH, HALF, BAND), lambda g, at: (0, 0, 0)),
+                pl.BlockSpec((1, D), lambda g, at: (0, 0)),
+                block,
+                block,
+            ],
+            out_specs=(
+                pl.BlockSpec((2, HALF, FC), lambda g, at: (0, 0, 0)),
+                pl.BlockSpec((HALF, 128), lambda g, at: (0, 0)),
+            ),
+            scratch_shapes=[pltpu.VMEM((GROUPS, HALF, RUN), BF), pltpu.VMEM((2, 2 * FC, HALF), F32)],
+        ),
+        out_shape=(jax.ShapeDtypeStruct((2, HALF, FC), BF), jax.ShapeDtypeStruct((HALF, 128), BF)),
         compiler_params=params(24),
         cost_estimate=cost(2 * HALF * D * 4 * FC, 8 * 2**20),
         name="hidden",
-    )(got, gain, mine, core)
-
-
-def down(hidden, mine, core, dtype):
-    block = pl.BlockSpec((1, FC, RUN), lambda g: (g, 0, 0))
+    )(at, got, gain, mine, core)
+
+
+def down(at, units, mine, core):
+    block = pl.BlockSpec((1, 1, FC, RUN), lambda g, at: weights_at(g, at, 2))
     return pl.pallas_call(
         down_kernel,
-        grid=(GROUPS,),
-        out_shape=jax.ShapeDtypeStruct((DEPTH, HALF, BAND), dtype),
-        in_specs=[pl.BlockSpec((2, HALF, FC), lambda g: (0, 0, 0)), block, block],
-        out_specs=pl.BlockSpec((2, HALF, BAND), lambda g: (g, 0, 0)),
+        grid_spec=pltpu.PrefetchScalarGridSpec(
+            num_scalar_prefetch=1,
+            grid=(GROUPS,),
+            in_specs=[pl.BlockSpec((2, HALF, FC), lambda g, at: (0, 0, 0))] * 4 + [block, block],
+            out_specs=pl.BlockSpec((2, 128, 128), lambda g, at: (g, 0, 0)),
+            scratch_shapes=[pltpu.VMEM((4, 128, FC), BF)],
+        ),
+        out_shape=jax.ShapeDtypeStruct((DEPTH, 128, 128), BF),
         compiler_params=params(24),
-        cost_estimate=cost(2 * HALF * D * 2 * FC, 5 * 2**20),
+        cost_estimate=cost(4 * HALF * D * 2 * FC, 5 * 2**20),
         name="down",
-    )(hidden, mine, core)
-
-
-def finish(got, attended):
+    )(at, *units, mine, core)
+
+
+def finish(at, got, near, far):
     return pl.pallas_call(
         finish_kernel,
-        out_shape=jax.ShapeDtypeStruct((4, QC, HALF), BF),
-        in_specs=[VMEM, VMEM],
-        out_specs=VMEM,
+        out_shape=(jax.ShapeDtypeStruct((QC, 128), BF),) * 2,
+        in_specs=[SMEM] + [VMEM] * 3,
+        out_specs=(VMEM, VMEM),
         compiler_params=params(16),
         name="finish",
-    )(got, attended)
+    )(at, got, near, far)
 
 
 def swap(x, bits):
     return lax.ppermute(x, "dev", [(d, d ^ bits) for d in range(MEMBERS)])
 
 
+def swap_groups(x):
+    return lax.ppermute(x, "grp", [(g, g ^ 4) for g in range(GROUPS)])
+
+
 def trade(x, groups):
     return lax.all_to_all(x, "dev", 0, 0, axis_index_groups=groups, tiled=True)
+
+
+def collect(x):
+    return lax.all_gather(x, "dev", axis=0, axis_index_groups=COLUMNS)
+
+
+def after(x, other):
+    return lax.optimization_barrier((x, other))[0]
 
 
 def on_device(
@@ -272,18 +332,24 @@
 ):
     member = lax.axis_index("dev")
     core, yhi, z, quad = member % 2, member // 2 % 2, member // 4, member % 4
+    ylo = lax.axis_index("grp") // 4
     length = jnp.where(core == 0, row_length[0], row_length[1])
-    at = jnp.stack([core, yhi, z, z % 2, length, quad]).astype(jnp.int32)
-
-    first = jnp.concatenate([w_query.T, w_key.T, w_value.T, w_out.T], axis=0)
-    first = lax.all_to_all(jnp.broadcast_to(first[None], (GROUPS, 160, RUN)), "grp", 0, 0, tiled=True)
-    out_own = first[:, 96:160, :]
-    out_weights = (out_own, swap(out_own, 1), swap(out_own, 2), swap(out_own, 3))
-
-    widen = lax.all_gather(jnp.concatenate([w_gate.T, w_up.T], axis=0), "grp", axis=0)
-    narrow = lax.all_gather(w_down.T, "grp", axis=0)
-    widen_core = swap(widen, 1)
-    narrow_core = swap(narrow, 1)
+    at = jnp.stack([core, yhi, z, z % 2, length, quad, ylo]).astype(jnp.int32)
+
+    first = pack(w_query.T, w_key.T, w_value.T, w_out.T)
+    first = lax.all_to_all(first, "grp", 0, 0, tiled=True)
+
+    bands = w_down.T.reshape(FC, 2, 2, 128)
+    low, high = bands[:, :, 0].reshape(FC, BAND), bands[:, :, 1].reshape(FC, BAND)
+    kept = jnp.where(yhi == 0, low, high)
+    given = swap(jnp.where(yhi == 0, high, low), 2)
+    narrow = jnp.concatenate([kept, given], axis=1)
+    wide = jnp.concatenate([w_gate.T, w_up.T], axis=0)
+    ff = jnp.stack(
+        [jnp.concatenate([wide, narrow], axis=0), jnp.concatenate([swap_groups(wide), swap_groups(narrow)], axis=0)]
+    )
+    ff = lax.all_gather(ff, "grp", axis=0, axis_index_groups=[[0, 1, 2, 3], [4, 5, 6, 7]])
+    ff_core = swap(ff, 1)
 
     lane = jnp.arange(128, dtype=jnp.int32)
     column = jnp.where(lane < QC, member * QC + lane, member * KC + lane - QC)
@@ -295,19 +361,23 @@
     send, keys, values, own = project(
         at, stream, attn_gain.reshape(1, D), first, jnp.cos(angle), jnp.sin(angle)
     )
-    mixed = trade(attend(at, trade(send, OCTETS)), COLUMNS)
+    got = trade(send, OCTETS)
+    out_own = after(first, got)[:, 96:160, :]
+    out_weights = (out_own, swap(out_own, 1), swap(out_own, 2), swap(out_own, 3))
+    mixed = collect(attend(at, got))
     attended = output(at, mixed, out_weights, own)
-    full = trade(attended, COLUMNS)
-    far = swap(full, 2)
+    full = collect(attended)
+    far_full = swap(full, 2)
     gain = ffn_gain.reshape(1, D)
-    hidden = hidden_units(full, gain, widen, widen_core)
-    far_hidden = hidden_units(far, gain, widen, widen_core)
-    far_sum = swap(down(far_hidden, narrow, narrow_core, BF), 2)
-    total = down(hidden, narrow, narrow_core, F32)
-    total = (total + far_sum.astype(F32)).astype(BF)
-    blocks = trade(finish(trade(total, COLUMNS), attended), QUADS)
-    next_stream = blocks.reshape(2, 2, QC, HALF).transpose(1, 0, 3, 2).reshape(256, QC)
-    return (keys.T, values.T, next_stream)
+    near, near_kept = hidden_units(at, full, gain, ff, ff_core)
+    far_near = swap(near, 2)
+    far, far_kept = hidden_units(at, far_full, gain, ff, ff_core)
+    far_far = swap(far, 2)
+    sums = trade(down(at, (near, far, far_near, far_far), ff, ff_core), COLUMNS)
+    keep, give = finish(at, sums, near_kept, far_kept)
+    give = swap(give, 1)
+    rows = jnp.where(core == 0, jnp.concatenate([keep, give], axis=1), jnp.concatenate([give, keep], axis=1))
+    return (keys.T, values.T, rows.T)
 
 
 def solution(mesh):

time: 277 us -> 304 us (1.097)
  waiting for transfers between devices: 78.5 us -> 111 us
  blocking collectives: 92.4 us -> 86.7 us
  starting transfers between devices: 52.3 us -> 56.5 us
    all_gather x2 -> x1, waiting for transfers between devices: 0.04 us -> 71.9 us  [on_device(): lax.all_gather(ff, 'grp', axis=0, axis_index_groups=[[0, 1, 2, 3], [4, 5,...]
    all_to_all x3 -> x2, blocking collectives: 92.4 us -> 36.9 us  [trade(): return lax.all_to_all(x, 'dev', 0, 0, axis_index_groups=groups, tiled=True)]
    all_gather x0 -> x2, blocking collectives: none -> 49.7 us  [collect(): return lax.all_gather(x, 'dev', axis=0, axis_index_groups=COLUMNS)]
    ppermute x7 -> x9, waiting for transfers between devices: 45.5 us -> 12 us  [swap(): return lax.ppermute(x, 'dev', [(d, d ^ bits) for d in range(MEMBERS)])]
    all_to_all x3 -> x1, starting transfers between devices: 33 us -> 4.32 us  [on_device(): first = lax.all_to_all(first, 'grp', 0, 0, tiled=True)]
    ppermute x7 -> x9, starting transfers between devices: 19.2 us -> 46.4 us  [swap(): return lax.ppermute(x, 'dev', [(d, d ^ bits) for d in range(MEMBERS)])]
    all_to_all x3 -> x1, waiting for transfers between devices: 32.3 us -> 16.2 us  [on_device(): first = lax.all_to_all(first, 'grp', 0, 0, tiled=True)]
    ppermute x0 -> x2, waiting for transfers between devices: none -> 10.8 us  [swap_groups(): return lax.ppermute(x, 'grp', [(g, g ^ 4) for g in range(GROUPS)])]
  transfers between devices with their start and end apart: 12 -> 13, of which waited for: 6 -> 6; matrix products, arithmetic and copies ran while one was open for 2% -> 0% of each run, Pallas kernels for 8% -> 4%
where the time goes in v2:
time: 304 us; the launch traced here: 303 us
  waiting for transfers between devices  111 us (37%)
  blocking collectives  86.7 us (29%)
  starting transfers between devices  56.5 us (19%)
  Pallas kernels  26.1 us (9%)
  between operations  15.7 us (5%)
  local copies, waits for them, and re-layouts  4.91 us (2%)
    all_gather x1, waiting for transfers between devices, on_device(): lax.all_gather(ff, 'grp', axis=0, axis_index_groups=[[0, 1, 2, 3], [4, 5,...  71.9 us
    all_gather x2, blocking collectives, collect(): return lax.all_gather(x, 'dev', axis=0, axis_index_groups=COLUMNS)  49.7 us
    ppermute x9, starting transfers between devices, swap(): return lax.ppermute(x, 'dev', [(d, d ^ bits) for d in range(MEMBERS)])  46.4 us
    all_to_all x2, blocking collectives, trade(): return lax.all_to_all(x, 'dev', 0, 0, axis_index_groups=groups, tiled=True)  36.9 us
    all_to_all x1, waiting for transfers between devices, on_device(): first = lax.all_to_all(first, 'grp', 0, 0, tiled=True)  16.2 us
    pallas_call x2, Pallas kernels, hidden_units(): pl.pallas_call(hidden_kernel, grid_spec=pltpu.PrefetchScalarGridSpec(num_...  14.5 us
    ppermute x9, waiting for transfers between devices, swap(): return lax.ppermute(x, 'dev', [(d, d ^ bits) for d in range(MEMBERS)])  12 us
    ppermute x2, waiting for transfers between devices, swap_groups(): return lax.ppermute(x, 'grp', [(g, g ^ 4) for g in range(GROUPS)])  10.8 us
  transfers between devices with their start and end apart: 13, of which 6 were waited for; matrix products, arithmetic and copies ran while one was open for 0% of the time, Pallas kernels for 4%

profile of v2, /device:TPU:1, one launch (start us, length us, event | category | flops | bytes accessed | tf_op | source)
XLA Modules:
  0.0 303.5 jit_solution(15476429128839403017)
XLA Ops:
  7.2 0.0 all-gather.5.cloned.1.call-start
  7.3 1.1 reshape.78
  8.4 0.3 fusion.2
  8.7 0.2 broadcast_select_fusion
  9.0 5.7 %collective-permute-start.3 = (bf16[224,256]{1,0:T(8,128)(2,1)S(1)}, bf16[224,256]{1,0:T(8,128)(2,1)S(1)}, u32[]{:S(2)}, u32[]{:S(2)}) collective-permute-start(bf16[224,256]{1,0:T(8,128)(2,1)S(1)} %bitcast.65), channel_id=1, source_target_pairs={{0,2},{1,3},{2,0},{3,1},{4,6},{5,7},{6,4},{7,5},{8,10},{9,11},{10,... | collective-permute-start | bytes 344072 | tf_op jit(solution)/shard_map/ppermute | solution.py:300
  14.7 2.3 collective-permute-start.4
  17.0 0.0 collective-permute-done.3
  17.1 3.4 %collective-permute-start.5 = (bf16[224,512]{1,0:T(8,128)(2,1)S(1)}, bf16[224,512]{1,0:T(8,128)(2,1)S(1)}, u32[]{:S(2)}, u32[]{:S(2)}) collective-permute-start(bf16[224,512]{1,0:T(8,128)(2,1)S(1)} %constant_dynamic-update-slice_fusion), channel_id=1, source_target_pairs={{0,256},{64,320},{128,384},{192,448},{256,0},{320,64},{384,128},{4... | collective-permute-start | bytes 688136 | tf_op jit(solution)/shard_map/ppermute | solution.py:304
  20.5 10.8 %collective-permute-done.5 = bf16[224,512]{1,0:T(8,128)(2,1)S(1)} collective-permute-done((bf16[224,512]{1,0:T(8,128)(2,1)S(1)}, bf16[224,512]{1,0:T(8,128)(2,1)S(1)}, u32[]{:S(2)}, u32[]{:S(2)}) %collective-permute-start.5) | collective-permute-done | bytes 229408 | tf_op jit(solution)/shard_map/ppermute | solution.py:304
  31.3 0.0 collective-permute-done.4
  31.4 1.2 pad_maximum_fusion
  32.6 0.0 all-gather.5.cloned.1.call-update
  32.6 71.9 %all-gather.5.cloned.1.call-done = bf16[8,672,512]{2,1,0:T(8,128)(2,1)} async-done(((bf16[2,672,512]{2,1,0:T(8,128)(2,1)}), bf16[8,672,512]{2,1,0:T(8,128)(2,1)}) %all-gather.5.cloned.1.call-update) | async-done | bytes 5505040 | tf_op jit(solution)/shard_map/all_gather | solution.py:351
  104.5 2.6 collective-permute-start.6
  107.2 0.1 pack.1
  107.3 1.1 copy-done
  108.4 4.3 %all-to-all-start = ((bf16[8,160,512]{2,1,0:T(8,128)(2,1)}), bf16[8,160,512]{2,1,0:T(8,128)(2,1)S(1)}, u32[]{:S(2)}, u32[]{:S(2)}) async-start(bf16[8,160,512]{2,1,0:T(8,128)(2,1)} %copy-done), calls=%async_computation | async-start | bytes 2621440 | tf_op jit(solution)/shard_map/all_to_all | solution.py:340
  112.7 0.6 fusion.3
  114.5 0.1 stack.40.at
  114.7 0.1 convert_bitcast_fusion
  114.7 0.5 multiply_sine_fusion
  115.3 16.2 %all-to-all-done.weights = bf16[8,160,512]{2,1,0:T(8,128)(2,1)S(1)} async-done(((bf16[8,160,512]{2,1,0:T(8,128)(2,1)}), bf16[8,160,512]{2,1,0:T(8,128)(2,1)S(1)}, u32[]{:S(2)}, u32[]{:S(2)}) %all-to-all-start) | async-done | bytes 1310752 | tf_op jit(solution)/shard_map/all_to_all | solution.py:340
  131.4 1.6 copy-done.1
  133.0 2.4 project.1
  135.5 11.3 %all_to_all.15.got = bf16[8,64,128]{2,1,0:T(8,128)(2,1)S(1)} all-to-all(bf16[8,64,128]{2,1,0:T(8,128)(2,1)S(1)} %get-tuple-element.16), channel_id=1, replica_groups={{0,1,2,3,4,5,6,7},{8,9,10,11,12,13,14,15},{16,17,18,19,20,21,22,23},{24..., dimensions={0} | all-to-all | bytes 262144 | tf_op jit(solution)/shard_map/all_to_all | solution.py:308
  146.8 3.3 %collective-permute-start.2 = (bf16[8,64,512]{2,1,0:T(8,128)(2,1)S(1)}, bf16[8,64,512]{2,1,0:T(8,128)(2,1)S(1)}, u32[]{:S(2)}, u32[]{:S(2)}) collective-permute-start(bf16[8,64,512]{2,1,0:T(8,128)(2,1)S(1)} %slice.17.mine), channel_id=1, source_target_pairs={{0,3},{1,2},{2,1},{3,0},{4,7},{5,6},{6,5},{7,4},{8,11},{9,10},{10,... | collective-permute-start | bytes 1572872 | tf_op jit(solution)/shard_map/ppermute | solution.py:300
  150.2 4.2 %collective-permute-start.1 = (bf16[8,64,512]{2,1,0:T(8,128)(2,1)S(1)}, bf16[8,64,512]{2,1,0:T(8,128)(2,1)S(1)}, u32[]{:S(2)}, u32[]{:S(2)}) collective-permute-start(bf16[8,64,512]{2,1,0:T(8,128)(2,1)S(1)} %slice.17.mine), channel_id=1, source_target_pairs={{0,2},{1,3},{2,0},{3,1},{4,6},{5,7},{6,4},{7,5},{8,10},{9,11},{10,... | collective-permute-start | bytes 1572872 | tf_op jit(solution)/shard_map/ppermute | solution.py:300
  154.4 1.9 collective-permute-start
  156.3 1.4 attend.1
  157.7 27.0 %all-gather = bf16[1024,256]{1,0:T(8,128)(2,1)S(1)} all-gather(bf16[64,256]{1,0:T(8,128)(2,1)S(1)} %attend.1), channel_id=2, replica_groups={{0,4,8,12,16,20,24,28,32,36,40,44,48,52,56,60},{1,5,9,13,17,21,25,29,33..., dimensions={0}, use_global_device_ids=true | all-gather | bytes 557056 | tf_op jit(solution)/shard_map/all_gather | solution.py:312
  184.8 0.0 copy-start.2
  184.8 1.3 output.1
  186.1 22.7 %all-gather.1 = bf16[1024,256]{1,0:T(8,128)(2,1)S(1)} all-gather(bf16[64,256]{1,0:T(8,128)(2,1)S(1)} %output.1), channel_id=3, replica_groups={{0,4,8,12,16,20,24,28,32,36,40,44,48,52,56,60},{1,5,9,13,17,21,25,29,33..., dimensions={0}, use_global_device_ids=true | all-gather | bytes 557056 | tf_op jit(solution)/shard_map/all_gather | solution.py:312
  208.8 2.0 collective-permute-start.7
  210.8 9.4 %collective-permute-done.7.got = bf16[16,64,256]{2,1,0:T(8,128)(2,1)S(1)} collective-permute-done((bf16[16,64,256]{2,1,0:T(8,128)(2,1)S(1)}, bf16[16,64,256]{2,1,0:T(8,128)(2,1)S(1)}, u32[]{:S(2)}, u32[]{:S(2)}) %collective-permute-start.7) | collective-permute-done | bytes 524320 | tf_op jit(solution)/shard_map/ppermute | solution.py:300
  220.2 0.0 collective-permute-done.6.core
  220.2 7.2 %hidden.3 = (bf16[2,64,224]{2,1,0:T(8,128)(2,1)S(1)}, bf16[64,128]{1,0:T(8,128)(2,1)S(1)}) custom-call(s32[7]{0:T(128)S(1)} %stack.40.at, bf16[16,64,256]{2,1,0:T(8,128)(2,1)S(1)} %collective-permute-done.7.got, f32[1,4096]{1,0:T(1,128)S(1)} %bitcast.51, bf16[4,2,672,512]{3,2,1,0:T(8,128)(2,1)S(1)} %bitcast.45, ...), custom_call_target="tpu_custom_call" | custom-call | flops 469762048 | bytes 8388608 | tf_op jit(solution)/shard_map/hidden/pallas_call | solution.py:246
  227.5 2.0 collective-permute-start.9
  229.5 7.2 %hidden.2 = (bf16[2,64,224]{2,1,0:T(8,128)(2,1)S(1)}, bf16[64,128]{1,0:T(8,128)(2,1)S(1)}) custom-call(s32[7]{0:T(128)S(1)} %stack.40.at, bf16[16,64,256]{2,1,0:T(8,128)(2,1)S(1)} %bitcast.49, f32[1,4096]{1,0:T(1,128)S(1)} %bitcast.52, bf16[4,2,672,512]{3,2,1,0:T(8,128)(2,1)S(1)} %bitcast.46, bf16[4,2,672,512]{3,2,1,0:T(8,128)(2,1)} %collective-permute-done.6.core), custom_call_target="tpu_custom_call" | custom-call | flops 469762048 | bytes 8388608 | tf_op jit(solution)/shard_map/hidden/pallas_call | solution.py:246
  236.8 4.8 %collective-permute-start.8 = (bf16[2,64,224]{2,1,0:T(8,128)(2,1)S(1)}, bf16[2,64,224]{2,1,0:T(8,128)(2,1)S(1)}, u32[]{:S(2)}, u32[]{:S(2)}) collective-permute-start(bf16[2,64,224]{2,1,0:T(8,128)(2,1)S(1)} %get-tuple-element.19.near), channel_id=1, source_target_pairs={{0,2},{1,3},{2,0},{3,1},{4,6},{5,7},{6,4},{7,5},{8,10},{9,11},{10,... | collective-permute-start | bytes 172040 | tf_op jit(solution)/shard_map/ppermute | solution.py:300
  241.6 0.0 collective-permute-done.9.far_far
  241.6 1.7 collective-permute-done.8.far_near
  243.3 5.7 %down.1 = bf16[16,128,128]{2,1,0:T(8,128)(2,1)S(1)} custom-call(s32[7]{0:T(128)S(1)} %stack.40.at, bf16[2,64,224]{2,1,0:T(8,128)(2,1)S(1)} %get-tuple-element.19.near, bf16[2,64,224]{2,1,0:T(8,128)(2,1)S(1)} %get-tuple-element.20.far, bf16[2,64,224]{2,1,0:T(8,128)(2,1)S(1)} %collective-permute-done.8.far_near, ...), custom_call_target="tpu_custom_call" | custom-call | flops 469762048 | bytes 5242880 | tf_op jit(solution)/shard_map/down/pallas_call | solution.py:272
  249.0 25.7 %all_to_all.16.got = bf16[16,128,128]{2,1,0:T(8,128)(2,1)S(1)} all-to-all(bf16[16,128,128]{2,1,0:T(8,128)(2,1)S(1)} %down.1), channel_id=1, replica_groups={{0,4,8,12,16,20,24,28,32,36,40,44,48,52,56,60},{1,5,9,13,17,21,25,29,33..., dimensions={0} | all-to-all | bytes 1048576 | tf_op jit(solution)/shard_map/all_to_all | solution.py:308
  274.6 0.7 finish.1
  275.3 19.9 %collective-permute-start.10 = (bf16[64,128]{1,0:T(8,128)(2,1)S(1)}, bf16[64,128]{1,0:T(8,128)(2,1)S(1)}, u32[]{:S(2)}, u32[]{:S(2)}) collective-permute-start(bf16[64,128]{1,0:T(8,128)(2,1)S(1)} %get-tuple-element.24), channel_id=1, source_target_pairs={{0,1},{1,0},{2,3},{3,2},{4,5},{5,4},{6,7},{7,6},{8,9},{9,8},{10,11... | collective-permute-start | bytes 49160 | tf_op jit(solution)/shard_map/ppermute | solution.py:300
  295.2 0.8 collective-permute-done.10
  296.0 0.6 fusion
  (37 shorter events, 0.3 us)
Async XLA Ops:
  7.2 7.5 %copy-start.8 = (bf16[512,224]{0,1:T(8,128)(2,1)S(1)}, bf16[512,224]{0,1:T(8,128)(2,1)}, u32[]{:S(2)}) copy-start(bf16[512,224]{0,1:T(8,128)(2,1)} %param.22) | copy-start | bytes 688132
  7.2 7.5 %copy-start.9 = (bf16[512,224]{0,1:T(8,128)(2,1)S(1)}, bf16[512,224]{0,1:T(8,128)(2,1)}, u32[]{:S(2)}) copy-start(bf16[512,224]{0,1:T(8,128)(2,1)} %param.21) | copy-start | bytes 688132
  7.2 97.4 %all-gather.5.cloned.1.call-start = ((), (), s32[]{:S(2)}) async-start(), calls=%async_computation.3 | async-start | bytes 6881280 | tf_op jit(solution)/shard_map/all_gather | solution.py:351
  9.0 8.1 %collective-permute-start.3 = (bf16[224,256]{1,0:T(8,128)(2,1)S(1)}, bf16[224,256]{1,0:T(8,128)(2,1)S(1)}, u32[]{:S(2)}, u32[]{:S(2)}) collective-permute-start(bf16[224,256]{1,0:T(8,128)(2,1)S(1)} %bitcast.65), channel_id=1, source_target_pairs={{0,2},{1,3},{2,0},{3,1},{4,6},{5,7},{6,4},{7,5},{8,10},{9,11},{10,... | collective-permute-start | bytes 344072 | tf_op jit(solution)/shard_map/ppermute | solution.py:300
  14.7 16.6 %collective-permute-start.4 = (bf16[448,512]{1,0:T(8,128)(2,1)S(1)}, bf16[448,512]{1,0:T(8,128)(2,1)S(1)}, u32[]{:S(2)}, u32[]{:S(2)}) collective-permute-start(bf16[448,512]{1,0:T(8,128)(2,1)S(1)} %pad_maximum_fusion.1), channel_id=1, source_target_pairs={{0,256},{64,320},{128,384},{192,448},{256,0},{320,64},{384,128},{4... | collective-permute-start | bytes 1376264 | tf_op jit(solution)/shard_map/ppermute | solution.py:304
  17.1 14.2 %collective-permute-start.5 = (bf16[224,512]{1,0:T(8,128)(2,1)S(1)}, bf16[224,512]{1,0:T(8,128)(2,1)S(1)}, u32[]{:S(2)}, u32[]{:S(2)}) collective-permute-start(bf16[224,512]{1,0:T(8,128)(2,1)S(1)} %constant_dynamic-update-slice_fusion), channel_id=1, source_target_pairs={{0,256},{64,320},{128,384},{192,448},{256,0},{320,64},{384,128},{4... | collective-permute-start | bytes 688136 | tf_op jit(solution)/shard_map/ppermute | solution.py:304
  32.6 74.6 %copy-start.3 = (bf16[512,64]{0,1:T(8,128)(2,1)S(1)}, bf16[512,64]{0,1:T(8,128)(2,1)}, u32[]{:S(2)}) copy-start(bf16[512,64]{0,1:T(8,128)(2,1)} %param.16) | copy-start | bytes 196612
  32.6 74.6 %copy-start.4 = (bf16[512,64]{0,1:T(8,128)(2,1)S(1)}, bf16[512,64]{0,1:T(8,128)(2,1)}, u32[]{:S(2)}) copy-start(bf16[512,64]{0,1:T(8,128)(2,1)} %param.19) | copy-start | bytes 196612
  32.6 74.6 %copy-start.5 = (bf16[512,16]{0,1:T(8,128)(2,1)S(1)}, bf16[512,16]{0,1:T(8,128)(2,1)}, u32[]{:S(2)}) copy-start(bf16[512,16]{0,1:T(8,128)(2,1)} %param.17) | copy-start | bytes 49156
  32.6 74.6 %copy-start.6 = (bf16[512,16]{0,1:T(8,128)(2,1)S(1)}, bf16[512,16]{0,1:T(8,128)(2,1)}, u32[]{:S(2)}) copy-start(bf16[512,16]{0,1:T(8,128)(2,1)} %param.18) | copy-start | bytes 49156
  104.5 115.7 %collective-permute-start.6 = (bf16[4,2,672,512]{3,2,1,0:T(8,128)(2,1)}, bf16[4,2,672,512]{3,2,1,0:T(8,128)(2,1)}, u32[]{:S(2)}, u32[]{:S(2)}) collective-permute-start(bf16[4,2,672,512]{3,2,1,0:T(8,128)(2,1)} %bitcast.42), channel_id=1, source_target_pairs={{0,1},{1,0},{2,3},{3,2},{4,5},{5,4},{6,7},{7,6},{8,9},{9,8},{10,11... | collective-permute-start | bytes 16515080 | tf_op jit(solution)/shard_map/ppermute | solution.py:300
  107.3 1.1 copy-start
  108.4 4.3 %copy-start.10 = (s32[2]{0:T(128)S(1)}, s32[2]{0:T(128)}, u32[]{:S(2)}) copy-start(s32[2]{0:T(128)} %param.13) | copy-start | bytes 28
  108.4 6.3 %copy-start.11 = (s32[2]{0:T(128)S(1)}, s32[2]{0:T(128)}, u32[]{:S(2)}) copy-start(s32[2]{0:T(128)} %param.14) | copy-start | bytes 28
  108.4 23.0 %copy-start.7 = (f32[4096]{0:T(1024)S(1)}, f32[4096]{0:T(1024)}, u32[]{:S(2)}) copy-start(f32[4096]{0:T(1024)} %param.15) | copy-start | bytes 49156
  108.4 111.8 %slice-start = ((s8[5505024]{0:T(1024)(128)(4,1)}), s8[1310720]{0:T(1024)(128)(4,1)S(1)}, s32[]{:S(2)}) async-start(s8[5505024]{0:T(1024)(128)(4,1)} %bitcast.43), calls=%async_computation.4 | async-start | bytes 2621440
  108.4 23.0 %all-to-all-start = ((bf16[8,160,512]{2,1,0:T(8,128)(2,1)}), bf16[8,160,512]{2,1,0:T(8,128)(2,1)S(1)}, u32[]{:S(2)}, u32[]{:S(2)}) async-start(bf16[8,160,512]{2,1,0:T(8,128)(2,1)} %copy-done), calls=%async_computation | async-start | bytes 2621440 | tf_op jit(solution)/shard_map/all_to_all | solution.py:340
  131.4 1.6 copy-start.1
  133.0 87.2 %slice-start.1 = ((s8[5505024]{0:T(1024)(128)(4,1)}), s8[4194304]{0:T(1024)(128)(4,1)S(1)}, s32[]{:S(2)}) async-start(s8[5505024]{0:T(1024)(128)(4,1)} %bitcast.43), calls=%async_computation.5 | async-start | bytes 8388608
  146.8 38.0 %collective-permute-start.2 = (bf16[8,64,512]{2,1,0:T(8,128)(2,1)S(1)}, bf16[8,64,512]{2,1,0:T(8,128)(2,1)S(1)}, u32[]{:S(2)}, u32[]{:S(2)}) collective-permute-start(bf16[8,64,512]{2,1,0:T(8,128)(2,1)S(1)} %slice.17.mine), channel_id=1, source_target_pairs={{0,3},{1,2},{2,1},{3,0},{4,7},{5,6},{6,5},{7,4},{8,11},{9,10},{10,... | collective-permute-start | bytes 1572872 | tf_op jit(solution)/shard_map/ppermute | solution.py:300
  150.2 34.6 %collective-permute-start.1 = (bf16[8,64,512]{2,1,0:T(8,128)(2,1)S(1)}, bf16[8,64,512]{2,1,0:T(8,128)(2,1)S(1)}, u32[]{:S(2)}, u32[]{:S(2)}) collective-permute-start(bf16[8,64,512]{2,1,0:T(8,128)(2,1)S(1)} %slice.17.mine), channel_id=1, source_target_pairs={{0,2},{1,3},{2,0},{3,1},{4,6},{5,7},{6,4},{7,5},{8,10},{9,11},{10,... | collective-permute-start | bytes 1572872 | tf_op jit(solution)/shard_map/ppermute | solution.py:300
  154.4 30.4 %collective-permute-start = (bf16[8,64,512]{2,1,0:T(8,128)(2,1)S(1)}, bf16[8,64,512]{2,1,0:T(8,128)(2,1)S(1)}, u32[]{:S(2)}, u32[]{:S(2)}) collective-permute-start(bf16[8,64,512]{2,1,0:T(8,128)(2,1)S(1)} %slice.17.mine), channel_id=1, source_target_pairs={{0,1},{1,0},{2,3},{3,2},{4,5},{5,4},{6,7},{7,6},{8,9},{9,8},{10,11... | collective-permute-start | bytes 1572872 | tf_op jit(solution)/shard_map/ppermute | solution.py:300
  184.8 35.4 %copy-start.2 = (f32[4096]{0:T(1024)S(1)}, f32[4096]{0:T(1024)}, u32[]{:S(2)}) copy-start(f32[4096]{0:T(1024)} %param.20) | copy-start | bytes 49156
  208.8 11.4 %collective-permute-start.7 = (bf16[16,64,256]{2,1,0:T(8,128)(2,1)S(1)}, bf16[16,64,256]{2,1,0:T(8,128)(2,1)S(1)}, u32[]{:S(2)}, u32[]{:S(2)}) collective-permute-start(bf16[16,64,256]{2,1,0:T(8,128)(2,1)S(1)} %bitcast.48), channel_id=1, source_target_pairs={{0,2},{1,3},{2,0},{3,1},{4,6},{5,7},{6,4},{7,5},{8,10},{9,11},{10,... | collective-permute-start | bytes 1572872 | tf_op jit(solution)/shard_map/ppermute | solution.py:300
  227.5 14.1 %collective-permute-start.9 = (bf16[2,64,224]{2,1,0:T(8,128)(2,1)S(1)}, bf16[2,64,224]{2,1,0:T(8,128)(2,1)S(1)}, u32[]{:S(2)}, u32[]{:S(2)}) collective-permute-start(bf16[2,64,224]{2,1,0:T(8,128)(2,1)S(1)} %get-tuple-element.20.far), channel_id=1, source_target_pairs={{0,2},{1,3},{2,0},{3,1},{4,6},{5,7},{6,4},{7,5},{8,10},{9,11},{10,... | collective-permute-start | bytes 172040 | tf_op jit(solution)/shard_map/ppermute | solution.py:300
  236.8 6.5 %collective-permute-start.8 = (bf16[2,64,224]{2,1,0:T(8,128)(2,1)S(1)}, bf16[2,64,224]{2,1,0:T(8,128)(2,1)S(1)}, u32[]{:S(2)}, u32[]{:S(2)}) collective-permute-start(bf16[2,64,224]{2,1,0:T(8,128)(2,1)S(1)} %get-tuple-element.19.near), channel_id=1, source_target_pairs={{0,2},{1,3},{2,0},{3,1},{4,6},{5,7},{6,4},{7,5},{8,10},{9,11},{10,... | collective-permute-start | bytes 172040 | tf_op jit(solution)/shard_map/ppermute | solution.py:300
  275.3 20.7 %collective-permute-start.10 = (bf16[64,128]{1,0:T(8,128)(2,1)S(1)}, bf16[64,128]{1,0:T(8,128)(2,1)S(1)}, u32[]{:S(2)}, u32[]{:S(2)}) collective-permute-start(bf16[64,128]{1,0:T(8,128)(2,1)S(1)} %get-tuple-element.24), channel_id=1, source_target_pairs={{0,1},{1,0},{2,3},{3,2},{4,5},{5,4},{6,7},{7,6},{8,9},{9,8},{10,11... | collective-permute-start | bytes 49160 | tf_op jit(solution)/shard_map/ppermute | solution.py:300
Sparse Core Ops, SparseCore 0:
  32.7 71.7 all-gather.4

commit v3 on v2

v3 whole, which is shorter than its diff:
```python
import math

import jax
import jax.numpy as jnp
from jax import lax
from jax.experimental import pallas as pl
from jax.experimental.pallas import tpu as pltpu
from jax.sharding import PartitionSpec as P

HEADS = 32
KV_HEADS = 8
HEAD_DIM = 128
ROW_LEN = 128
D = 4096
ROPE_BASE = 500000.0

GROUPS = 8
MEMBERS = 64
DEPTH = 16
HALF = 64
QC = 64
KC = 16
FC = 224
BAND = 256
RUN = 512

COLUMNS = [[4 * z + q for z in range(DEPTH)] for q in range(4)]
OCTETS = [[8 * z + m for m in range(8)] for z in range(8)]

BF = jnp.bfloat16
F32 = jnp.float32
VMEM = pl.BlockSpec(memory_space=pltpu.VMEM)
HBM = pl.BlockSpec(memory_space=pltpu.HBM)
ANY = pl.BlockSpec(memory_space=pl.ANY)
SMEM = pl.BlockSpec(memory_space=pltpu.SMEM)


def nt(a, b):
    return lax.dot_general(a, b, (((1,), (1,)), ((), ())), preferred_element_type=F32)


def whole(*shape):
    return pl.BlockSpec(shape, lambda i: (0,) * len(shape))


def params(mib):
    return pltpu.CompilerParams(vmem_limit_bytes=mib * 2**20)


def cost(flops, nbytes):
    return pl.CostEstimate(flops=flops, bytes_accessed=nbytes, transcendentals=0)


def project_kernel(after, normed, weights, cos, sin, send, keys, values):
    total = jnp.zeros((256, 96), F32)
    for g in range(GROUPS):
        total = total + nt(normed[g], weights[g, 0:96, :])
    total = jnp.concatenate([total, jnp.zeros((256, 32), F32)], axis=1)
    lane = lax.broadcasted_iota(jnp.int32, (256, 128), 1)
    partner = jnp.where(lane % 2 == 0, -pltpu.roll(total, 127, 1), pltpu.roll(total, 1, 1))
    turned = jnp.where(lane < QC + KC, total * cos[...] + partner * sin[...], total)
    turned = turned.astype(BF).astype(F32)
    flipped = turned.T
    keys[...] = flipped[QC : QC + KC, :].astype(BF)
    values[...] = flipped[QC + KC : QC + 2 * KC, :].astype(BF)
    lane = lax.broadcasted_iota(jnp.int32, (HALF, 128), 1)
    for zl in range(2):
        for yhi in range(2):
            for c in range(2):
                first = turned[c * 128 : c * 128 + HALF, :]
                second = turned[c * 128 + HALF : c * 128 + 128, :]
                mine = second if yhi else first
                chunk = jnp.where(lane < QC, mine, jnp.where(lane < 96, first, pltpu.roll(second, 32, 1)))
                send[zl * 4 + yhi * 2 + c] = chunk.astype(BF)


def attend_kernel(at, lengths, got, out):
    lane = lax.broadcasted_iota(jnp.int32, (HALF, 128), 1)
    pieces = [got[m].astype(F32) for m in range(8)]

    def gather(start):
        full = jnp.zeros((HALF, 128), F32)
        for m in range(8):
            full = jnp.where(lane // KC == m, pltpu.roll(pieces[m], (KC * m - start) % 128, 1), full)
        return full.astype(BF)

    keys = jnp.concatenate([gather(QC), gather(96)], axis=0)
    values = jnp.concatenate([gather(QC + KC), gather(96 + KC)], axis=0)
    slot = lax.broadcasted_iota(jnp.int32, (HALF, 128), 0) + at[1] * HALF
    allowed = (lane <= slot) & (lane < lengths[at[0]])
    for a in range(2):
        low = got[at[3] * 4 + a * 2].astype(F32)
        high = got[at[3] * 4 + a * 2 + 1].astype(F32)
        queries = jnp.where(lane < QC, low, pltpu.roll(high, QC, 1)).astype(BF)
        scores = nt(queries, keys) / math.sqrt(HEAD_DIM)
        scores = jnp.where(allowed, scores, -jnp.inf)
        expo = jnp.exp(scores - jnp.max(scores, axis=-1, keepdims=True))
        probs = (expo / jnp.sum(expo, axis=-1, keepdims=True)).astype(BF)
        mixed = jnp.dot(probs, values, preferred_element_type=F32).astype(BF)
        out[:, a * 128 : a * 128 + 128] = mixed


def output_kernel(at, got, mine, core, far, cross, own, out):
    parts = []
    for w in (mine, core, far, cross):
        total = jnp.zeros((HALF, QC), F32)
        for g in range(GROUPS):
            total = total + nt(got[2 * g], w[g, :, 0:BAND]) + nt(got[2 * g + 1], w[g, :, BAND:RUN])
        parts.append(total)
    blocks = []
    for j in range(4):
        picked = parts[0]
        for k in range(1, 4):
            picked = jnp.where(jnp.bitwise_xor(at[5], j) == k, parts[k], picked)
        blocks.append(picked)
    projected = jnp.concatenate(blocks, axis=1)
    attended = (own[...].astype(F32) + projected).astype(BF)
    out[...] = attended


def hidden_kernel(at, after, got, gain, mine, core, out, kept):
    squares = jnp.zeros((HALF, 1), F32)
    for z in range(DEPTH):
        x = got[z].astype(F32)
        squares = squares + jnp.sum(x * x, axis=-1, keepdims=True)
    scale = lax.rsqrt(squares * (1.0 / D) + 1e-05)
    kept[...] = got[at[2], :, pl.ds(pl.multiple_of(at[1] * 128, 128), 128)]
    totals = [jnp.zeros((HALF, FC), F32) for _ in range(4)]
    for g in range(GROUPS):
        parts = []
        for z in (2 * g, 2 * g + 1):
            part = got[z].astype(F32) * scale * gain[:, z * BAND : (z + 1) * BAND]
            parts.append(part.astype(BF))
        x = jnp.concatenate(parts, axis=1)
        side = jnp.bitwise_xor(g // 4, at[6])
        for i, w in enumerate((mine, core)):
            totals[2 * i] = totals[2 * i] + nt(x, w[g % 4, side, 0:FC, :])
            totals[2 * i + 1] = totals[2 * i + 1] + nt(x, w[g % 4, side, FC : 2 * FC, :])
    for i in range(2):
        gate = totals[2 * i]
        out[i] = (gate / (1.0 + jnp.exp(-gate)) * totals[2 * i + 1]).astype(BF)


def down_kernel(at, near, far, far_near, far_far, mine, core, out, units):
    own = pl.ds(pl.multiple_of(at[1] * HALF, HALF), HALF)
    other = pl.ds(pl.multiple_of((1 - at[1]) * HALF, HALF), HALF)
    for i in range(2):
        units[i, own, :] = near[i]
        units[i, other, :] = far[i]
        units[2 + i, own, :] = far_far[i]
        units[2 + i, other, :] = far_near[i]
    for g in range(GROUPS):
        side = jnp.bitwise_xor(g // 4, at[6])
        total = jnp.zeros((128, BAND), F32)
        for i, w in enumerate((mine, core)):
            total = total + jnp.dot(units[i], w[g % 4, side, 2 * FC : 3 * FC, 0:BAND], preferred_element_type=F32)
            total = total + jnp.dot(units[2 + i], w[g % 4, side, 2 * FC : 3 * FC, BAND:RUN], preferred_element_type=F32)
        out[2 * g] = total[:, 0:128].astype(BF)
        out[2 * g + 1] = total[:, 128:256].astype(BF)


def finish_kernel(at, got, near, far, keep, give):
    total = got[0].astype(F32)
    for z in range(1, DEPTH):
        total = total + got[z].astype(F32)
    low = at[1] == 0
    first = jnp.where(low, near[...].astype(F32), far[...].astype(F32))
    second = jnp.where(low, far[...].astype(F32), near[...].astype(F32))
    result = (jnp.concatenate([first, second], axis=0) + total).T
    head, tail = result[0:QC, :], result[QC : 2 * QC, :]
    keep[...] = jnp.where(at[0] == 0, head, tail).astype(BF)
    give[...] = jnp.where(at[0] == 0, tail, head).astype(BF)


def pack_kernel(query, key, value, out_part, out, token, held, sems):
    token[...] = jnp.zeros_like(token)
    spans = ((query, 0, QC), (key, QC, KC), (value, QC + KC, KC), (out_part, 96, QC))
    reads = [
        pltpu.make_async_copy(ref, held.at[pl.ds(start, rows), :], sems.at[i])
        for i, (ref, start, rows) in enumerate(spans)
    ]
    for copy in reads:
        copy.start()
    for copy in reads:
        copy.wait()
    writes = [pltpu.make_async_copy(held, out.at[g], sems.at[4 + g]) for g in range(GROUPS)]
    for copy in writes:
        copy.start()
    for copy in writes:
        copy.wait()


def prepare_kernel(at, after, tables, gate, up, narrow, stream, gain, wide, keep, give, normed, own):
    wide[0:FC, :] = gate[...]
    wide[FC : 2 * FC, :] = up[...]
    low = at[1] == 0
    for i in range(2):
        even = narrow[:, 2 * i * 128 : (2 * i + 1) * 128]
        odd = narrow[:, (2 * i + 1) * 128 : (2 * i + 2) * 128]
        keep[:, i * 128 : (i + 1) * 128] = jnp.where(low, even, odd)
        give[:, i * 128 : (i + 1) * 128] = jnp.where(low, odd, even)
    x = stream[...].astype(F32)
    scale = lax.rsqrt(jnp.mean(x * x, axis=-1, keepdims=True) + 1e-05)
    for g in range(GROUPS):
        cols = pl.ds(g * RUN, RUN)
        normed[g] = (stream[:, cols].astype(F32) * scale * gain[:, cols]).astype(BF)
    rows = pl.ds(pl.multiple_of(at[0] * 128 + at[1] * HALF, HALF), HALF)
    own[...] = stream[rows, pl.ds(pl.multiple_of(at[2] * BAND, BAND), BAND)]


def prepare(at, after, tables, gate, up, narrow, stream, gain):
    half = jax.ShapeDtypeStruct((FC, BAND), BF)
    return pl.pallas_call(
        prepare_kernel,
        out_shape=(
            jax.ShapeDtypeStruct((2 * FC, RUN), BF),
            half,
            half,
            jax.ShapeDtypeStruct((GROUPS, 256, RUN), BF),
            jax.ShapeDtypeStruct((HALF, BAND), BF),
        ),
        in_specs=[SMEM, ANY, ANY] + [VMEM] * 5,
        out_specs=(VMEM,) * 5,
        compiler_params=params(24),
        name="prepare",
    )(at, after, tables, gate, up, narrow, stream, gain)


def join_kernel(after, wide, keep, got, wide_lo, keep_lo, got_lo, out, token, sems):
    token[...] = jnp.zeros_like(token)
    copies = []
    for i, parts in enumerate(((wide, keep, got), (wide_lo, keep_lo, got_lo))):
        spans = (
            out.at[i, pl.ds(0, 2 * FC), :],
            out.at[i, pl.ds(2 * FC, FC), pl.ds(0, BAND)],
            out.at[i, pl.ds(2 * FC, FC), pl.ds(BAND, BAND)],
        )
        for k, (part, span) in enumerate(zip(parts, spans)):
            copies.append(pltpu.make_async_copy(part, span, sems.at[3 * i + k]))
    for copy in copies:
        copy.start()
    for copy in copies:
        copy.wait()


def join(after, *parts):
    return pl.pallas_call(
        join_kernel,
        out_shape=(jax.ShapeDtypeStruct((2, 3 * FC, RUN), BF), jax.ShapeDtypeStruct((8, 128), F32)),
        in_specs=[ANY] + [HBM] * 6,
        out_specs=(HBM, VMEM),
        scratch_shapes=[pltpu.SemaphoreType.DMA((6,))],
        compiler_params=params(57),
        name="join",
    )(after, *parts)


def pack(*parts):
    return pl.pallas_call(
        pack_kernel,
        out_shape=(jax.ShapeDtypeStruct((GROUPS, 160, RUN), BF), jax.ShapeDtypeStruct((8, 128), F32)),
        in_specs=[HBM] * 4,
        out_specs=(HBM, VMEM),
        scratch_shapes=[pltpu.VMEM((160, RUN), BF), pltpu.SemaphoreType.DMA((4 + GROUPS,))],
        compiler_params=params(60),
        name="pack",
    )(*parts)


def project(after, normed, weights, cos, sin):
    return pl.pallas_call(
        project_kernel,
        out_shape=(
            jax.ShapeDtypeStruct((8, HALF, 128), BF),
            jax.ShapeDtypeStruct((KC, 256), BF),
            jax.ShapeDtypeStruct((KC, 256), BF),
        ),
        in_specs=[ANY] + [VMEM] * 4,
        out_specs=(VMEM,) * 3,
        compiler_params=params(24),
        name="project",
    )(after, normed, weights, cos, sin)


def attend(at, lengths, got):
    return pl.pallas_call(
        attend_kernel,
        out_shape=jax.ShapeDtypeStruct((HALF, BAND), BF),
        in_specs=[SMEM, SMEM, VMEM],
        out_specs=VMEM,
        compiler_params=params(16),
        name="attend",
    )(at, lengths, got)


def output(at, got, weights, own):
    return pl.pallas_call(
        output_kernel,
        out_shape=jax.ShapeDtypeStruct((HALF, BAND), BF),
        in_specs=[SMEM] + [VMEM] * 6,
        out_specs=VMEM,
        compiler_params=params(24),
        name="output",
    )(at, got, *weights, own)


def hidden_units(at, after, got, gain, mine, core):
    return pl.pallas_call(
        hidden_kernel,
        out_shape=(jax.ShapeDtypeStruct((2, HALF, FC), BF), jax.ShapeDtypeStruct((HALF, 128), BF)),
        in_specs=[SMEM, ANY] + [VMEM] * 4,
        out_specs=(VMEM, VMEM),
        compiler_params=params(16),
        cost_estimate=cost(2 * HALF * D * 4 * FC, 8 * 2**20),
        name="hidden",
    )(at, after, got, gain, mine, core)


def down(at, units, mine, core):
    return pl.pallas_call(
        down_kernel,
        out_shape=jax.ShapeDtypeStruct((DEPTH, 128, 128), BF),
        in_specs=[SMEM] + [VMEM] * 6,
        out_specs=VMEM,
        scratch_shapes=[pltpu.VMEM((4, 128, FC), BF)],
        compiler_params=params(16),
        cost_estimate=cost(4 * HALF * D * 2 * FC, 5 * 2**20),
        name="down",
    )(at, *units, mine, core)


def finish(at, got, near, far):
    return pl.pallas_call(
        finish_kernel,
        out_shape=(jax.ShapeDtypeStruct((QC, 128), BF),) * 2,
        in_specs=[SMEM] + [VMEM] * 3,
        out_specs=(VMEM, VMEM),
        compiler_params=params(16),
        name="finish",
    )(at, got, near, far)


def swap(x, bits):
    return lax.ppermute(x, "dev", [(d, d ^ bits) for d in range(MEMBERS)])


def swap_groups(x):
    return lax.ppermute(x, "grp", [(g, g ^ 4) for g in range(GROUPS)])


def swap_both(x):
    pairs = [(g * MEMBERS + d, (g ^ 4) * MEMBERS + (d ^ 2)) for g in range(GROUPS) for d in range(MEMBERS)]
    return lax.ppermute(x, ("grp", "dev"), pairs)


def trade(x, groups):
    return lax.all_to_all(x, "dev", 0, 0, axis_index_groups=groups, tiled=True)


def collect(x):
    return lax.all_gather(x, "dev", axis=0, axis_index_groups=COLUMNS)


def after(x, other):
    return lax.optimization_barrier((x, other))[0]


def on_device(
    stream,
    row_length,
    row_start,
    attn_gain,
    w_query,
    w_key,
    w_value,
    w_out,
    ffn_gain,
    w_gate,
    w_up,
    w_down,
):
    member = lax.axis_index("dev")
    core, yhi, z, quad = member % 2, member // 2 % 2, member // 4, member % 4
    ylo = lax.axis_index("grp") // 4
    at = jnp.stack([core, yhi, z, z % 2, z // 2, quad, ylo]).astype(jnp.int32)

    packed, token = pack(w_query.T, w_key.T, w_value.T, w_out.T)
    first = lax.all_to_all(packed, "grp", 0, 0, tiled=True)

    lane = jnp.arange(128, dtype=jnp.int32)
    column = jnp.where(lane < QC, member * QC + lane, member * KC + lane - QC)
    pair = (column % HEAD_DIM // 2).astype(F32)
    freq = jnp.exp(-(2.0 * pair / HEAD_DIM) * math.log(ROPE_BASE))
    positions = (row_start[:, None] + jnp.arange(ROW_LEN, dtype=jnp.int32)[None, :]).reshape(-1)
    angle = positions.astype(F32)[:, None] * freq[None, :]
    cos, sin = jnp.cos(angle), jnp.sin(angle)

    wide, keep, give, normed, own = prepare(
        at, token, cos, w_gate.T, w_up.T, w_down.T, stream, attn_gain.reshape(1, D)
    )
    ff, token = join(first, wide, keep, swap(give, 2), swap_groups(wide), swap_groups(keep), swap_both(give))
    ff_all = lax.all_gather(ff, "grp", axis=0, axis_index_groups=[[0, 1, 2, 3], [4, 5, 6, 7]])

    send, keys, values = project(token, normed, first, cos, sin)
    got = trade(send, OCTETS)
    out_own = after(first, got)[:, 96:160, :]
    out_weights = (out_own, swap(out_own, 1), swap(out_own, 2), swap(out_own, 3))
    mixed = collect(attend(at, row_length, got))
    attended = output(at, mixed, out_weights, own)
    ff = after(ff_all, attended)
    ff_core = swap(ff, 1)
    full = collect(attended)
    far_full = swap(full, 2)
    gain = ffn_gain.reshape(1, D)
    near, near_kept = hidden_units(at, at, full, gain, ff, ff_core)
    far_near = swap(near, 2)
    far, far_kept = hidden_units(at, far_near, far_full, gain, ff, ff_core)
    far_far = swap(far, 2)
    sums = trade(down(at, (near, far, far_near, far_far), ff, ff_core), COLUMNS)
    keep, give = finish(at, sums, near_kept, far_kept)
    give = swap(give, 1)
    rows = jnp.where(core == 0, jnp.concatenate([keep, give], axis=1), jnp.concatenate([give, keep], axis=1))
    return (keys.T, values.T, rows.T)


def solution(mesh):
    placed = (
        P("grp", None),
        P("grp"),
        P("grp"),
        P(),
        P("grp", "dev"),
        P("grp", "dev"),
        P("grp", "dev"),
        P("grp", "dev"),
        P(),
        P("grp", "dev"),
        P("grp", "dev"),
        P("grp", "dev"),
    )
    return jax.shard_map(
        on_device,
        mesh=mesh,
        in_specs=placed,
        out_specs=(P("grp", "dev"), P("grp", "dev"), P("grp", "dev")),
        check_vma=False,
    )
```

time: 304 us -> 269 us (0.88)
  waiting for transfers between devices: 111 us -> 31.1 us
  Pallas kernels: 26.1 us -> 60.3 us
  blocking collectives: 86.7 us -> 94.7 us
  local copies, waits for them, and re-layouts: 4.91 us -> 12.8 us
  starting transfers between devices: 56.5 us -> 53.4 us
    all_gather x1, waiting for transfers between devices: 71.9 us -> 8.18 us  [on_device(): lax.all_gather(ff, 'grp', axis=0, axis_index_groups=[[0, 1, 2, 3], [4, 5,...]
    pallas_call x4 -> x6, Pallas kernels: 20.2 us -> 55.5 us  [the longest x1 43.4 us: join(): pl.pallas_call(join_kernel, out_shape=(jax.ShapeDtypeStruct((2, 3 * FC, R...]
    all_to_all x1, waiting for transfers between devices: 16.2 us -> 0.01 us  [on_device(): first = lax.all_to_all(packed, 'grp', 0, 0, tiled=True)]
    all_gather x2, blocking collectives: 49.7 us -> 60 us  [collect(): return lax.all_gather(x, 'dev', axis=0, axis_index_groups=COLUMNS)]
    unnamed x30 -> x46, local copies, waits for them, and re-layouts: 2.76 us -> 12.7 us
    ppermute x9, starting transfers between devices: 46.4 us -> 37.2 us  [swap(): return lax.ppermute(x, 'dev', [(d, d ^ bits) for d in range(MEMBERS)])]
    ppermute x0 -> x1, starting transfers between devices: none -> 4.68 us  [swap_both(): return lax.ppermute(x, ('grp', 'dev'), pairs)]
  transfers between devices with their start and end apart: 13 -> 14, of which waited for: 6 -> 6; matrix products, arithmetic and copies ran while one was open for 0% -> 1% of each run, Pallas kernels for 4% -> 3%
where the time goes in v3:
time: 269 us
  blocking collectives  94.7 us (35%)
  Pallas kernels  60.3 us (22%)
  starting transfers between devices  53.4 us (20%)
  waiting for transfers between devices  31.1 us (12%)
  between operations  14.4 us (5%)
  local copies, waits for them, and re-layouts  12.8 us (5%)
    all_gather x2, blocking collectives, collect(): return lax.all_gather(x, 'dev', axis=0, axis_index_groups=COLUMNS)  60 us
    pallas_call x1, Pallas kernels, join(): pl.pallas_call(join_kernel, out_shape=(jax.ShapeDtypeStruct((2, 3 * FC, R...  43.4 us
    ppermute x9, starting transfers between devices, swap(): return lax.ppermute(x, 'dev', [(d, d ^ bits) for d in range(MEMBERS)])  37.2 us
    all_to_all x2, blocking collectives, trade(): return lax.all_to_all(x, 'dev', 0, 0, axis_index_groups=groups, tiled=True)  34.7 us
    ppermute x9, waiting for transfers between devices, swap(): return lax.ppermute(x, 'dev', [(d, d ^ bits) for d in range(MEMBERS)])  13 us
    unnamed x46, local copies, waits for them, and re-layouts  12.7 us
    ppermute x2, waiting for transfers between devices, swap_groups(): return lax.ppermute(x, 'grp', [(g, g ^ 4) for g in range(GROUPS)])  9.9 us
    all_gather x1, waiting for transfers between devices, on_device(): lax.all_gather(ff, 'grp', axis=0, axis_index_groups=[[0, 1, 2, 3], [4, 5,...  8.18 us
  transfers between devices with their start and end apart: 14, of which 6 were waited for; matrix products, arithmetic and copies ran while one was open for 1% of the time, Pallas kernels for 3%

profile of v3, /device:TPU:1, one launch (start us, length us, event | category | flops | bytes accessed | tf_op | source)
XLA Modules:
  0.0 268.5 jit_solution(4857947064313456086)
XLA Ops:
  7.2 2.9 %pack.1 = (bf16[8,160,512]{2,1,0:T(8,128)(2,1)}, f32[8,128]{1,0:T(8,128)}) custom-call(bf16[64,512]{1,0:T(8,128)(2,1)} %bitcast.38, bf16[16,512]{1,0:T(8,128)(2,1)} %bitcast.40, bf16[16,512]{1,0:T(8,128)(2,1)} %bitcast.41, bf16[64,512]{1,0:T(8,128)(2,1)} %bitcast.39), custom_call_target="tpu_custom_call" | custom-call | tf_op jit(solution)/shard_map/pack/pallas_call | solution.py:259
  10.1 5.9 %all-to-all-start = ((bf16[8,160,512]{2,1,0:T(8,128)(2,1)}), bf16[8,160,512]{2,1,0:T(8,128)(2,1)S(1)}, u32[]{:S(2)}, u32[]{:S(2)}) async-start(bf16[8,160,512]{2,1,0:T(8,128)(2,1)} %get-tuple-element.23), calls=%async_computation | async-start | bytes 2621440 | tf_op jit(solution)/shard_map/all_to_all | solution.py:388
  16.1 0.1 stack.31.at.after
  16.3 1.2 multiply_sine_fusion
  17.5 0.9 copy-done.8
  18.4 0.9 copy-done.9
  19.4 0.9 copy-done.10
  20.3 0.7 copy-done.15
  21.0 1.8 prepare.1
  22.8 1.3 copy-done.4
  24.2 0.6 copy-done.13
  24.8 3.5 %collective-permute-start.1 = (bf16[448,512]{1,0:T(8,128)(2,1)S(1)}, bf16[448,512]{1,0:T(8,128)(2,1)}, u32[]{:S(2)}, u32[]{:S(2)}) collective-permute-start(bf16[448,512]{1,0:T(8,128)(2,1)S(1)} %get-tuple-element.25.wide), channel_id=1, source_target_pairs={{0,256},{64,320},{128,384},{192,448},{256,0},{320,64},{384,128},{4... | collective-permute-start | bytes 1376264 | tf_op jit(solution)/shard_map/ppermute | solution.py:348
  28.3 2.0 collective-permute-start.2
  30.3 4.7 %collective-permute-start.3 = (bf16[224,256]{1,0:T(8,128)(2,1)S(1)}, bf16[224,256]{1,0:T(8,128)(2,1)S(1)}, u32[]{:S(2)}, u32[]{:S(2)}) collective-permute-start(bf16[224,256]{1,0:T(8,128)(2,1)S(1)} %get-tuple-element.27), channel_id=1, source_target_pairs={{0,258},{1,259},{2,256},{3,257},{4,262},{5,263},{6,260},{7,261},{8... | collective-permute-start | bytes 344072 | tf_op jit(solution)/shard_map/ppermute | solution.py:353
  35.0 2.3 collective-permute-start
  37.3 9.9 %collective-permute-done.2.keep_lo = bf16[224,256]{1,0:T(8,128)(2,1)S(1)} collective-permute-done((bf16[224,256]{1,0:T(8,128)(2,1)S(1)}, bf16[224,256]{1,0:T(8,128)(2,1)S(1)}, u32[]{:S(2)}, u32[]{:S(2)}) %collective-permute-start.2) | collective-permute-done | bytes 114720 | tf_op jit(solution)/shard_map/ppermute | solution.py:348
  47.2 2.2 collective-permute-done.got
  49.5 0.6 copy-done.21
  50.1 1.1 copy-done.1
  51.2 43.4 %join.1 = (bf16[2,672,512]{2,1,0:T(8,128)(2,1)}, f32[8,128]{1,0:T(8,128)}) custom-call(bf16[8,160,512]{2,1,0:T(8,128)(2,1)} %copy-done.1, bf16[448,512]{1,0:T(8,128)(2,1)} %copy-done.7, bf16[224,256]{1,0:T(8,128)(2,1)} %copy-done.11, bf16[224,256]{1,0:T(8,128)(2,1)} %copy-done.21, bf16[448,512]{1,0:T(8,128)(2,1)} %collective-permute-done.1.wide_lo, ...), custom_call_target="tpu_custom_call" | custom-call | tf_op jit(solution)/shard_map/join/pallas_call | solution.py:247
  94.7 1.3 copy-done.2
  96.0 0.9 copy-done.6
  96.9 0.7 copy-done.17
  97.6 1.4 project.1
  99.0 10.2 %all_to_all.15.got = bf16[8,64,128]{2,1,0:T(8,128)(2,1)S(1)} all-to-all(bf16[8,64,128]{2,1,0:T(8,128)(2,1)S(1)} %get-tuple-element.32), channel_id=1, replica_groups={{0,1,2,3,4,5,6,7},{8,9,10,11,12,13,14,15},{16,17,18,19,20,21,22,23},{24..., dimensions={0} | all-to-all | bytes 262144 | tf_op jit(solution)/shard_map/all_to_all | solution.py:357
  109.2 3.3 %collective-permute-start.6 = (bf16[8,64,512]{2,1,0:T(8,128)(2,1)S(1)}, bf16[8,64,512]{2,1,0:T(8,128)(2,1)S(1)}, u32[]{:S(2)}, u32[]{:S(2)}) collective-permute-start(bf16[8,64,512]{2,1,0:T(8,128)(2,1)S(1)} %slice.3.mine), channel_id=1, source_target_pairs={{0,3},{1,2},{2,1},{3,0},{4,7},{5,6},{6,5},{7,4},{8,11},{9,10},{10,... | collective-permute-start | bytes 1572872 | tf_op jit(solution)/shard_map/ppermute | solution.py:344
  112.6 4.2 %collective-permute-start.5 = (bf16[8,64,512]{2,1,0:T(8,128)(2,1)S(1)}, bf16[8,64,512]{2,1,0:T(8,128)(2,1)S(1)}, u32[]{:S(2)}, u32[]{:S(2)}) collective-permute-start(bf16[8,64,512]{2,1,0:T(8,128)(2,1)S(1)} %slice.3.mine), channel_id=1, source_target_pairs={{0,2},{1,3},{2,0},{3,1},{4,6},{5,7},{6,4},{7,5},{8,10},{9,11},{10,... | collective-permute-start | bytes 1572872 | tf_op jit(solution)/shard_map/ppermute | solution.py:344
  116.8 1.9 collective-permute-start.4
  118.8 1.4 attend.1
  120.2 33.8 %all-gather = bf16[1024,256]{1,0:T(8,128)(2,1)S(1)} all-gather(bf16[64,256]{1,0:T(8,128)(2,1)S(1)} %attend.1), channel_id=2, replica_groups={{0,4,8,12,16,20,24,28,32,36,40,44,48,52,56,60},{1,5,9,13,17,21,25,29,33..., dimensions={0}, use_global_device_ids=true | all-gather | bytes 557056 | tf_op jit(solution)/shard_map/all_gather | solution.py:361
  154.0 1.3 output.1
  155.3 8.2 %all-gather.5.cloned.1.call-done = bf16[8,672,512]{2,1,0:T(8,128)(2,1)} async-done(((bf16[2,672,512]{2,1,0:T(8,128)(2,1)}), bf16[8,672,512]{2,1,0:T(8,128)(2,1)}) %all-gather.5.cloned.1.call-update) | async-done | bytes 5505040 | tf_op jit(solution)/shard_map/all_gather | solution.py:402
  163.4 2.6 collective-permute-start.7
  166.1 26.2 %all-gather.1 = bf16[1024,256]{1,0:T(8,128)(2,1)S(1)} all-gather(bf16[64,256]{1,0:T(8,128)(2,1)S(1)} %output.1), channel_id=3, replica_groups={{0,4,8,12,16,20,24,28,32,36,40,44,48,52,56,60},{1,5,9,13,17,21,25,29,33..., dimensions={0}, use_global_device_ids=true | all-gather | bytes 557056 | tf_op jit(solution)/shard_map/all_gather | solution.py:361
  192.2 4.6 %collective-permute-start.9 = (bf16[16,64,256]{2,1,0:T(8,128)(2,1)S(1)}, bf16[16,64,256]{2,1,0:T(8,128)(2,1)S(1)}, u32[]{:S(2)}, u32[]{:S(2)}) collective-permute-start(bf16[16,64,256]{2,1,0:T(8,128)(2,1)S(1)} %bitcast.29), channel_id=1, source_target_pairs={{0,2},{1,3},{2,0},{3,1},{4,6},{5,7},{6,4},{7,5},{8,10},{9,11},{10,... | collective-permute-start | bytes 1572872 | tf_op jit(solution)/shard_map/ppermute | solution.py:344
  196.9 2.6 copy-done
  199.5 3.0 %hidden.2 = (bf16[2,64,224]{2,1,0:T(8,128)(2,1)S(1)}, bf16[64,128]{1,0:T(8,128)(2,1)S(1)}) custom-call(s32[7]{0:T(128)S(1)} %stack.31.at.after, s32[7]{0:T(128)S(1)} %stack.31.at.after, bf16[16,64,256]{2,1,0:T(8,128)(2,1)S(1)} %bitcast.30, f32[1,4096]{1,0:T(1,128)S(1)} %bitcast.35, bf16[4,2,672,512]{3,2,1,0:T(8,128)(2,1)S(1)} %bitcast.26, ...), custom_call_target="tpu_custom_call" | custom-call | flops 469762048 | bytes 8388608 | tf_op jit(solution)/shard_map/hidden/pallas_call | solution.py:308
  202.5 2.1 collective-permute-start.8
  204.7 5.4 %collective-permute-done.8.after.far_near = bf16[2,64,224]{2,1,0:T(8,128)(2,1)S(1)} collective-permute-done((bf16[2,64,224]{2,1,0:T(8,128)(2,1)S(1)}, bf16[2,64,224]{2,1,0:T(8,128)(2,1)S(1)}, u32[]{:S(2)}, u32[]{:S(2)}) %collective-permute-start.8) | collective-permute-done | bytes 57376 | tf_op jit(solution)/shard_map/ppermute | solution.py:344
  210.1 3.0 %hidden.3 = (bf16[2,64,224]{2,1,0:T(8,128)(2,1)S(1)}, bf16[64,128]{1,0:T(8,128)(2,1)S(1)}) custom-call(s32[7]{0:T(128)S(1)} %stack.31.at.after, bf16[2,64,224]{2,1,0:T(8,128)(2,1)S(1)} %collective-permute-done.8.after.far_near, bf16[16,64,256]{2,1,0:T(8,128)(2,1)S(1)} %collective-permute-done.9.got, f32[1,4096]{1,0:T(1,128)S(1)} %bitcast.36, ...), custom_call_target="tpu_custom_call" | custom-call | flops 469762048 | bytes 8388608 | tf_op jit(solution)/shard_map/hidden/pallas_call | solution.py:308
  213.1 2.0 collective-permute-start.10
  215.1 4.5 %collective-permute-done.10.far_far = bf16[2,64,224]{2,1,0:T(8,128)(2,1)S(1)} collective-permute-done((bf16[2,64,224]{2,1,0:T(8,128)(2,1)S(1)}, bf16[2,64,224]{2,1,0:T(8,128)(2,1)S(1)}, u32[]{:S(2)}, u32[]{:S(2)}) %collective-permute-start.10) | collective-permute-done | bytes 57376 | tf_op jit(solution)/shard_map/ppermute | solution.py:344
  219.7 1.3 down.1
  220.9 24.5 %all_to_all.16.got = bf16[16,128,128]{2,1,0:T(8,128)(2,1)S(1)} all-to-all(bf16[16,128,128]{2,1,0:T(8,128)(2,1)S(1)} %down.1), channel_id=1, replica_groups={{0,4,8,12,16,20,24,28,32,36,40,44,48,52,56,60},{1,5,9,13,17,21,25,29,33..., dimensions={0} | all-to-all | bytes 1048576 | tf_op jit(solution)/shard_map/all_to_all | solution.py:357
  245.5 0.7 finish.1
  246.1 14.1 %collective-permute-start.11 = (bf16[64,128]{1,0:T(8,128)(2,1)S(1)}, bf16[64,128]{1,0:T(8,128)(2,1)S(1)}, u32[]{:S(2)}, u32[]{:S(2)}) collective-permute-start(bf16[64,128]{1,0:T(8,128)(2,1)S(1)} %get-tuple-element.42), channel_id=1, source_target_pairs={{0,1},{1,0},{2,3},{3,2},{4,5},{5,4},{6,7},{7,6},{8,9},{9,8},{10,11... | collective-permute-start | bytes 49160 | tf_op jit(solution)/shard_map/ppermute | solution.py:344
  260.3 0.8 collective-permute-done.11
  261.1 0.6 fusion
  (47 shorter events, 0.3 us)
Async XLA Ops:
  7.2 9.0 %copy-start.22 = (s32[2]{0:T(128)S(1)}, s32[2]{0:T(128)}, u32[]{:S(2)}) copy-start(s32[2]{0:T(128)} %param.14) | copy-start | bytes 28
  7.2 10.3 %copy-start.3 = (bf16[256,4096]{1,0:T(8,128)(2,1)S(1)}, bf16[256,4096]{1,0:T(8,128)(2,1)}, u32[]{:S(2)}) copy-start(bf16[256,4096]{1,0:T(8,128)(2,1)} %stream.1) | copy-start | bytes 6291460
  10.1 7.4 %copy-start.16 = (f32[8,128]{1,0:T(8,128)S(1)}, f32[8,128]{1,0:T(8,128)}, u32[]{:S(2)}) copy-start(f32[8,128]{1,0:T(8,128)} %get-tuple-element.24.after) | copy-start | bytes 12292
  10.1 40.0 %all-to-all-start = ((bf16[8,160,512]{2,1,0:T(8,128)(2,1)}), bf16[8,160,512]{2,1,0:T(8,128)(2,1)S(1)}, u32[]{:S(2)}, u32[]{:S(2)}) async-start(bf16[8,160,512]{2,1,0:T(8,128)(2,1)} %get-tuple-element.23), calls=%async_computation | async-start | bytes 2621440 | tf_op jit(solution)/shard_map/all_to_all | solution.py:388
  15.9 147.5 %all-gather.5.cloned.1.call-start = ((), (), s32[]{:S(2)}) async-start(), calls=%async_computation.3 | async-start | bytes 6881280 | tf_op jit(solution)/shard_map/all_gather | solution.py:402
  17.5 0.9 copy-start.8
  18.4 0.9 copy-start.9
  19.4 0.9 copy-start.10
  20.3 0.7 copy-start.15
  22.8 1.3 copy-start.4
  24.2 0.6 copy-start.13
  24.8 24.6 %copy-start.7 = (bf16[448,512]{1,0:T(8,128)(2,1)}, bf16[448,512]{1,0:T(8,128)(2,1)S(1)}, u32[]{:S(2)}) copy-start(bf16[448,512]{1,0:T(8,128)(2,1)S(1)} %get-tuple-element.25.wide) | copy-start | bytes 1376260
  24.8 24.6 %copy-start.11 = (bf16[224,256]{1,0:T(8,128)(2,1)}, bf16[224,256]{1,0:T(8,128)(2,1)S(1)}, u32[]{:S(2)}) copy-start(bf16[224,256]{1,0:T(8,128)(2,1)S(1)} %get-tuple-element.26.keep) | copy-start | bytes 344068
  24.8 69.9 %copy-start.5 = (bf16[8,256,512]{2,1,0:T(8,128)(2,1)S(1)}, bf16[8,256,512]{2,1,0:T(8,128)(2,1)}, u32[]{:S(2)}) copy-start(bf16[8,256,512]{2,1,0:T(8,128)(2,1)} %copy-done.4) | copy-start | bytes 6291460
  24.8 25.3 %collective-permute-start.1 = (bf16[448,512]{1,0:T(8,128)(2,1)S(1)}, bf16[448,512]{1,0:T(8,128)(2,1)}, u32[]{:S(2)}, u32[]{:S(2)}) collective-permute-start(bf16[448,512]{1,0:T(8,128)(2,1)S(1)} %get-tuple-element.25.wide), channel_id=1, source_target_pairs={{0,256},{64,320},{128,384},{192,448},{256,0},{320,64},{384,128},{4... | collective-permute-start | bytes 1376264 | tf_op jit(solution)/shard_map/ppermute | solution.py:348
  28.3 18.9 %collective-permute-start.2 = (bf16[224,256]{1,0:T(8,128)(2,1)S(1)}, bf16[224,256]{1,0:T(8,128)(2,1)S(1)}, u32[]{:S(2)}, u32[]{:S(2)}) collective-permute-start(bf16[224,256]{1,0:T(8,128)(2,1)S(1)} %get-tuple-element.26.keep), channel_id=1, source_target_pairs={{0,256},{64,320},{128,384},{192,448},{256,0},{320,64},{384,128},{4... | collective-permute-start | bytes 344072 | tf_op jit(solution)/shard_map/ppermute | solution.py:348
  30.3 16.9 %collective-permute-start.3 = (bf16[224,256]{1,0:T(8,128)(2,1)S(1)}, bf16[224,256]{1,0:T(8,128)(2,1)S(1)}, u32[]{:S(2)}, u32[]{:S(2)}) collective-permute-start(bf16[224,256]{1,0:T(8,128)(2,1)S(1)} %get-tuple-element.27), channel_id=1, source_target_pairs={{0,258},{1,259},{2,256},{3,257},{4,262},{5,263},{6,260},{7,261},{8... | collective-permute-start | bytes 344072 | tf_op jit(solution)/shard_map/ppermute | solution.py:353
  35.0 14.4 %collective-permute-start = (bf16[224,256]{1,0:T(8,128)(2,1)S(1)}, bf16[224,256]{1,0:T(8,128)(2,1)S(1)}, u32[]{:S(2)}, u32[]{:S(2)}) collective-permute-start(bf16[224,256]{1,0:T(8,128)(2,1)S(1)} %get-tuple-element.27), channel_id=1, source_target_pairs={{0,2},{1,3},{2,0},{3,1},{4,6},{5,7},{6,4},{7,5},{8,10},{9,11},{10,... | collective-permute-start | bytes 344072 | tf_op jit(solution)/shard_map/ppermute | solution.py:344
  47.2 2.2 copy-start.19
  47.2 2.2 copy-start.20
  49.5 0.6 copy-start.21
  50.1 1.1 copy-start.1
  94.6 1.3 copy-start.2
  96.0 0.9 copy-start.6
  96.9 0.7 copy-start.17
  97.6 21.2 %copy-start.18 = (s32[2]{0:T(128)S(1)}, s32[2]{0:T(128)}, u32[]{:S(2)}) copy-start(s32[2]{0:T(128)} %lengths.1) | copy-start | bytes 28
  97.6 56.4 %copy-start.14 = (bf16[64,256]{1,0:T(8,128)(2,1)S(1)}, bf16[64,256]{1,0:T(8,128)(2,1)}, u32[]{:S(2)}) copy-start(bf16[64,256]{1,0:T(8,128)(2,1)} %copy-done.13) | copy-start | bytes 98308
  109.2 87.7 %copy-start.12 = (f32[4096]{0:T(1024)S(1)}, f32[4096]{0:T(1024)}, u32[]{:S(2)}) copy-start(f32[4096]{0:T(1024)} %param.20) | copy-start | bytes 49156
  109.2 44.7 %collective-permute-start.6 = (bf16[8,64,512]{2,1,0:T(8,128)(2,1)S(1)}, bf16[8,64,512]{2,1,0:T(8,128)(2,1)S(1)}, u32[]{:S(2)}, u32[]{:S(2)}) collective-permute-start(bf16[8,64,512]{2,1,0:T(8,128)(2,1)S(1)} %slice.3.mine), channel_id=1, source_target_pairs={{0,3},{1,2},{2,1},{3,0},{4,7},{5,6},{6,5},{7,4},{8,11},{9,10},{10,... | collective-permute-start | bytes 1572872 | tf_op jit(solution)/shard_map/ppermute | solution.py:344
  112.6 41.4 %collective-permute-start.5 = (bf16[8,64,512]{2,1,0:T(8,128)(2,1)S(1)}, bf16[8,64,512]{2,1,0:T(8,128)(2,1)S(1)}, u32[]{:S(2)}, u32[]{:S(2)}) collective-permute-start(bf16[8,64,512]{2,1,0:T(8,128)(2,1)S(1)} %slice.3.mine), channel_id=1, source_target_pairs={{0,2},{1,3},{2,0},{3,1},{4,6},{5,7},{6,4},{7,5},{8,10},{9,11},{10,... | collective-permute-start | bytes 1572872 | tf_op jit(solution)/shard_map/ppermute | solution.py:344
  116.8 37.1 %collective-permute-start.4 = (bf16[8,64,512]{2,1,0:T(8,128)(2,1)S(1)}, bf16[8,64,512]{2,1,0:T(8,128)(2,1)S(1)}, u32[]{:S(2)}, u32[]{:S(2)}) collective-permute-start(bf16[8,64,512]{2,1,0:T(8,128)(2,1)S(1)} %slice.3.mine), channel_id=1, source_target_pairs={{0,1},{1,0},{2,3},{3,2},{4,5},{5,4},{6,7},{7,6},{8,9},{9,8},{10,11... | collective-permute-start | bytes 1572872 | tf_op jit(solution)/shard_map/ppermute | solution.py:344
  163.4 33.4 %collective-permute-start.7 = (bf16[4,2,672,512]{3,2,1,0:T(8,128)(2,1)}, bf16[4,2,672,512]{3,2,1,0:T(8,128)(2,1)S(1)}, u32[]{:S(2)}, u32[]{:S(2)}) collective-permute-start(bf16[4,2,672,512]{3,2,1,0:T(8,128)(2,1)} %bitcast.25), channel_id=1, source_target_pairs={{0,1},{1,0},{2,3},{3,2},{4,5},{5,4},{6,7},{7,6},{8,9},{9,8},{10,11... | collective-permute-start | bytes 16515080 | tf_op jit(solution)/shard_map/ppermute | solution.py:344
  192.2 12.4 %collective-permute-start.9 = (bf16[16,64,256]{2,1,0:T(8,128)(2,1)S(1)}, bf16[16,64,256]{2,1,0:T(8,128)(2,1)S(1)}, u32[]{:S(2)}, u32[]{:S(2)}) collective-permute-start(bf16[16,64,256]{2,1,0:T(8,128)(2,1)S(1)} %bitcast.29), channel_id=1, source_target_pairs={{0,2},{1,3},{2,0},{3,1},{4,6},{5,7},{6,4},{7,5},{8,10},{9,11},{10,... | collective-permute-start | bytes 1572872 | tf_op jit(solution)/shard_map/ppermute | solution.py:344
  196.9 2.6 copy-start
  202.5 7.6 %collective-permute-start.8 = (bf16[2,64,224]{2,1,0:T(8,128)(2,1)S(1)}, bf16[2,64,224]{2,1,0:T(8,128)(2,1)S(1)}, u32[]{:S(2)}, u32[]{:S(2)}) collective-permute-start(bf16[2,64,224]{2,1,0:T(8,128)(2,1)S(1)} %get-tuple-element.37.near), channel_id=1, source_target_pairs={{0,2},{1,3},{2,0},{3,1},{4,6},{5,7},{6,4},{7,5},{8,10},{9,11},{10,... | collective-permute-start | bytes 172040 | tf_op jit(solution)/shard_map/ppermute | solution.py:344
  213.1 6.5 %collective-permute-start.10 = (bf16[2,64,224]{2,1,0:T(8,128)(2,1)S(1)}, bf16[2,64,224]{2,1,0:T(8,128)(2,1)S(1)}, u32[]{:S(2)}, u32[]{:S(2)}) collective-permute-start(bf16[2,64,224]{2,1,0:T(8,128)(2,1)S(1)} %get-tuple-element.38.far), channel_id=1, source_target_pairs={{0,2},{1,3},{2,0},{3,1},{4,6},{5,7},{6,4},{7,5},{8,10},{9,11},{10,... | collective-permute-start | bytes 172040 | tf_op jit(solution)/shard_map/ppermute | solution.py:344
  246.1 14.9 %collective-permute-start.11 = (bf16[64,128]{1,0:T(8,128)(2,1)S(1)}, bf16[64,128]{1,0:T(8,128)(2,1)S(1)}, u32[]{:S(2)}, u32[]{:S(2)}) collective-permute-start(bf16[64,128]{1,0:T(8,128)(2,1)S(1)} %get-tuple-element.42), channel_id=1, source_target_pairs={{0,1},{1,0},{2,3},{3,2},{4,5},{5,4},{6,7},{7,6},{8,9},{9,8},{10,11... | collective-permute-start | bytes 49160 | tf_op jit(solution)/shard_map/ppermute | solution.py:344
Sparse Core Ops, SparseCore 0:
  94.8 68.5 all-gather.4

commit v4 on v3

--- a/solution.py
+++ b/solution.py
@@ -51,7 +51,7 @@
     return pl.CostEstimate(flops=flops, bytes_accessed=nbytes, transcendentals=0)
 
 
-def project_kernel(after, normed, weights, cos, sin, send, keys, values):
+def project_kernel(normed, weights, cos, sin, send, keys, values):
     total = jnp.zeros((256, 96), F32)
     for g in range(GROUPS):
         total = total + nt(normed[g], weights[g, 0:96, :])
@@ -118,55 +118,57 @@
     out[...] = attended
 
 
-def hidden_kernel(at, after, got, gain, mine, core, out, kept):
-    squares = jnp.zeros((HALF, 1), F32)
-    for z in range(DEPTH):
-        x = got[z].astype(F32)
-        squares = squares + jnp.sum(x * x, axis=-1, keepdims=True)
-    scale = lax.rsqrt(squares * (1.0 / D) + 1e-05)
-    kept[...] = got[at[2], :, pl.ds(pl.multiple_of(at[1] * 128, 128), 128)]
-    totals = [jnp.zeros((HALF, FC), F32) for _ in range(4)]
+def hidden_kernel(at, near, far, gain, mine, core, out, kept):
+    low = at[1] == 0
+    lanes = pl.ds(pl.multiple_of(at[1] * 128, 128), 128)
+    near_kept, far_kept = near[at[2], :, lanes], far[at[2], :, lanes]
+    kept[0:HALF, :] = jnp.where(low, near_kept, far_kept)
+    kept[HALF : 2 * HALF, :] = jnp.where(low, far_kept, near_kept)
+    scales = []
+    for got in (near, far):
+        squares = jnp.zeros((HALF, 1), F32)
+        for z in range(DEPTH):
+            x = got[z].astype(F32)
+            squares = squares + jnp.sum(x * x, axis=-1, keepdims=True)
+        scales.append(lax.rsqrt(squares * (1.0 / D) + 1e-05))
+    totals = [jnp.zeros((2 * HALF, FC), F32) for _ in range(4)]
     for g in range(GROUPS):
-        parts = []
-        for z in (2 * g, 2 * g + 1):
-            part = got[z].astype(F32) * scale * gain[:, z * BAND : (z + 1) * BAND]
-            parts.append(part.astype(BF))
-        x = jnp.concatenate(parts, axis=1)
+        rows = []
+        for got, scale in zip((near, far), scales):
+            parts = []
+            for z in (2 * g, 2 * g + 1):
+                part = got[z].astype(F32) * scale * gain[:, z * BAND : (z + 1) * BAND]
+                parts.append(part.astype(BF))
+            rows.append(jnp.concatenate(parts, axis=1))
+        x = jnp.concatenate(rows, axis=0)
         side = jnp.bitwise_xor(g // 4, at[6])
         for i, w in enumerate((mine, core)):
             totals[2 * i] = totals[2 * i] + nt(x, w[g % 4, side, 0:FC, :])
             totals[2 * i + 1] = totals[2 * i + 1] + nt(x, w[g % 4, side, FC : 2 * FC, :])
     for i in range(2):
         gate = totals[2 * i]
-        out[i] = (gate / (1.0 + jnp.exp(-gate)) * totals[2 * i + 1]).astype(BF)
-
-
-def down_kernel(at, near, far, far_near, far_far, mine, core, out, units):
-    own = pl.ds(pl.multiple_of(at[1] * HALF, HALF), HALF)
-    other = pl.ds(pl.multiple_of((1 - at[1]) * HALF, HALF), HALF)
-    for i in range(2):
-        units[i, own, :] = near[i]
-        units[i, other, :] = far[i]
-        units[2 + i, own, :] = far_far[i]
-        units[2 + i, other, :] = far_near[i]
+        units = (gate / (1.0 + jnp.exp(-gate)) * totals[2 * i + 1]).astype(BF)
+        first, second = units[0:HALF, :], units[HALF : 2 * HALF, :]
+        out[i, 0:HALF, :] = jnp.where(low, first, second)
+        out[i, HALF : 2 * HALF, :] = jnp.where(low, second, first)
+
+
+def down_kernel(at, units, far_units, mine, core, out):
     for g in range(GROUPS):
         side = jnp.bitwise_xor(g // 4, at[6])
         total = jnp.zeros((128, BAND), F32)
         for i, w in enumerate((mine, core)):
             total = total + jnp.dot(units[i], w[g % 4, side, 2 * FC : 3 * FC, 0:BAND], preferred_element_type=F32)
-            total = total + jnp.dot(units[2 + i], w[g % 4, side, 2 * FC : 3 * FC, BAND:RUN], preferred_element_type=F32)
+            total = total + jnp.dot(far_units[i], w[g % 4, side, 2 * FC : 3 * FC, BAND:RUN], preferred_element_type=F32)
         out[2 * g] = total[:, 0:128].astype(BF)
         out[2 * g + 1] = total[:, 128:256].astype(BF)
 
 
-def finish_kernel(at, got, near, far, keep, give):
-    total = got[0].astype(F32)
-    for z in range(1, DEPTH):
+def finish_kernel(at, got, kept, keep, give):
+    total = kept[...].astype(F32)
+    for z in range(DEPTH):
         total = total + got[z].astype(F32)
-    low = at[1] == 0
-    first = jnp.where(low, near[...].astype(F32), far[...].astype(F32))
-    second = jnp.where(low, far[...].astype(F32), near[...].astype(F32))
-    result = (jnp.concatenate([first, second], axis=0) + total).T
+    result = total.T
     head, tail = result[0:QC, :], result[QC : 2 * QC, :]
     keep[...] = jnp.where(at[0] == 0, head, tail).astype(BF)
     give[...] = jnp.where(at[0] == 0, tail, head).astype(BF)
@@ -190,14 +192,17 @@
         copy.wait()
 
 
-def prepare_kernel(at, after, tables, gate, up, narrow, stream, gain, wide, keep, give, normed, own):
+def prepare_kernel(at, after, tables, gate, up, narrow, stream, gain, wide, give, normed, own):
     wide[0:FC, :] = gate[...]
     wide[FC : 2 * FC, :] = up[...]
     low = at[1] == 0
     for i in range(2):
         even = narrow[:, 2 * i * 128 : (2 * i + 1) * 128]
         odd = narrow[:, (2 * i + 1) * 128 : (2 * i + 2) * 128]
-        keep[:, i * 128 : (i + 1) * 128] = jnp.where(low, even, odd)
+        keep = jnp.where(low, even, odd)
+        for k in range(2):
+            lanes = slice(k * BAND + i * 128, k * BAND + (i + 1) * 128)
+            wide[2 * FC : 5 * FC // 2, lanes] = keep[k * FC // 2 : (k + 1) * FC // 2, :]
         give[:, i * 128 : (i + 1) * 128] = jnp.where(low, odd, even)
     x = stream[...].astype(F32)
     scale = lax.rsqrt(jnp.mean(x * x, axis=-1, keepdims=True) + 1e-05)
@@ -213,44 +218,34 @@
     return pl.pallas_call(
         prepare_kernel,
         out_shape=(
-            jax.ShapeDtypeStruct((2 * FC, RUN), BF),
-            half,
+            jax.ShapeDtypeStruct((5 * FC // 2, RUN), BF),
             half,
             jax.ShapeDtypeStruct((GROUPS, 256, RUN), BF),
             jax.ShapeDtypeStruct((HALF, BAND), BF),
         ),
         in_specs=[SMEM, ANY, ANY] + [VMEM] * 5,
-        out_specs=(VMEM,) * 5,
+        out_specs=(VMEM,) * 4,
         compiler_params=params(24),
         name="prepare",
     )(at, after, tables, gate, up, narrow, stream, gain)
 
 
-def join_kernel(after, wide, keep, got, wide_lo, keep_lo, got_lo, out, token, sems):
-    token[...] = jnp.zeros_like(token)
-    copies = []
-    for i, parts in enumerate(((wide, keep, got), (wide_lo, keep_lo, got_lo))):
-        spans = (
-            out.at[i, pl.ds(0, 2 * FC), :],
-            out.at[i, pl.ds(2 * FC, FC), pl.ds(0, BAND)],
-            out.at[i, pl.ds(2 * FC, FC), pl.ds(BAND, BAND)],
-        )
-        for k, (part, span) in enumerate(zip(parts, spans)):
-            copies.append(pltpu.make_async_copy(part, span, sems.at[3 * i + k]))
-    for copy in copies:
-        copy.start()
-    for copy in copies:
-        copy.wait()
+def join_kernel(after, wide, got, wide_lo, got_lo, out):
+    for i, (kept, given) in enumerate(((wide, got), (wide_lo, got_lo))):
+        out[i, 0 : 2 * FC, :] = kept[0 : 2 * FC, :]
+        for k in range(2):
+            rows = slice(2 * FC + k * FC // 2, 2 * FC + (k + 1) * FC // 2)
+            out[i, rows, 0:BAND] = kept[2 * FC : 5 * FC // 2, k * BAND : (k + 1) * BAND]
+        out[i, 2 * FC : 3 * FC, BAND:RUN] = given[...]
 
 
 def join(after, *parts):
     return pl.pallas_call(
         join_kernel,
-        out_shape=(jax.ShapeDtypeStruct((2, 3 * FC, RUN), BF), jax.ShapeDtypeStruct((8, 128), F32)),
-        in_specs=[ANY] + [HBM] * 6,
-        out_specs=(HBM, VMEM),
-        scratch_shapes=[pltpu.SemaphoreType.DMA((6,))],
-        compiler_params=params(57),
+        out_shape=jax.ShapeDtypeStruct((2, 3 * FC, RUN), BF),
+        in_specs=[ANY] + [VMEM] * 4,
+        out_specs=VMEM,
+        compiler_params=params(16),
         name="join",
     )(after, *parts)
 
@@ -267,7 +262,7 @@
     )(*parts)
 
 
-def project(after, normed, weights, cos, sin):
+def project(normed, weights, cos, sin):
     return pl.pallas_call(
         project_kernel,
         out_shape=(
@@ -275,11 +270,11 @@
             jax.ShapeDtypeStruct((KC, 256), BF),
             jax.ShapeDtypeStruct((KC, 256), BF),
         ),
-        in_specs=[ANY] + [VMEM] * 4,
+        in_specs=[VMEM] * 4,
         out_specs=(VMEM,) * 3,
         compiler_params=params(24),
         name="project",
-    )(after, normed, weights, cos, sin)
+    )(normed, weights, cos, sin)
 
 
 def attend(at, lengths, got):
@@ -304,40 +299,39 @@
     )(at, got, *weights, own)
 
 
-def hidden_units(at, after, got, gain, mine, core):
+def hidden_units(at, near, far, gain, mine, core):
     return pl.pallas_call(
         hidden_kernel,
-        out_shape=(jax.ShapeDtypeStruct((2, HALF, FC), BF), jax.ShapeDtypeStruct((HALF, 128), BF)),
-        in_specs=[SMEM, ANY] + [VMEM] * 4,
+        out_shape=(jax.ShapeDtypeStruct((2, 128, FC), BF), jax.ShapeDtypeStruct((128, 128), BF)),
+        in_specs=[SMEM] + [VMEM] * 5,
         out_specs=(VMEM, VMEM),
         compiler_params=params(16),
-        cost_estimate=cost(2 * HALF * D * 4 * FC, 8 * 2**20),
+        cost_estimate=cost(4 * HALF * D * 4 * FC, 8 * 2**20),
         name="hidden",
-    )(at, after, got, gain, mine, core)
-
-
-def down(at, units, mine, core):
+    )(at, near, far, gain, mine, core)
+
+
+def down(at, units, far_units, mine, core):
     return pl.pallas_call(
         down_kernel,
         out_shape=jax.ShapeDtypeStruct((DEPTH, 128, 128), BF),
-        in_specs=[SMEM] + [VMEM] * 6,
+        in_specs=[SMEM] + [VMEM] * 4,
         out_specs=VMEM,
-        scratch_shapes=[pltpu.VMEM((4, 128, FC), BF)],
         compiler_params=params(16),
         cost_estimate=cost(4 * HALF * D * 2 * FC, 5 * 2**20),
         name="down",
-    )(at, *units, mine, core)
-
-
-def finish(at, got, near, far):
+    )(at, units, far_units, mine, core)
+
+
+def finish(at, got, kept):
     return pl.pallas_call(
         finish_kernel,
         out_shape=(jax.ShapeDtypeStruct((QC, 128), BF),) * 2,
-        in_specs=[SMEM] + [VMEM] * 3,
+        in_specs=[SMEM] + [VMEM] * 2,
         out_specs=(VMEM, VMEM),
         compiler_params=params(16),
         name="finish",
-    )(at, got, near, far)
+    )(at, got, kept)
 
 
 def swap(x, bits):
@@ -395,15 +389,15 @@
     angle = positions.astype(F32)[:, None] * freq[None, :]
     cos, sin = jnp.cos(angle), jnp.sin(angle)
 
-    wide, keep, give, normed, own = prepare(
+    wide, give, normed, own = prepare(
         at, token, cos, w_gate.T, w_up.T, w_down.T, stream, attn_gain.reshape(1, D)
     )
-    ff, token = join(first, wide, keep, swap(give, 2), swap_groups(wide), swap_groups(keep), swap_both(give))
+    trades = (swap(give, 2), swap_groups(wide), swap_both(give))
+    send, keys, values = project(normed, first, cos, sin)
+    got = trade(send, OCTETS)
+    ff = join(got, wide, *trades)
     ff_all = lax.all_gather(ff, "grp", axis=0, axis_index_groups=[[0, 1, 2, 3], [4, 5, 6, 7]])
-
-    send, keys, values = project(token, normed, first, cos, sin)
-    got = trade(send, OCTETS)
-    out_own = after(first, got)[:, 96:160, :]
+    out_own = first[:, 96:160, :]
     out_weights = (out_own, swap(out_own, 1), swap(out_own, 2), swap(out_own, 3))
     mixed = collect(attend(at, row_length, got))
     attended = output(at, mixed, out_weights, own)
@@ -412,12 +406,9 @@
     full = collect(attended)
     far_full = swap(full, 2)
     gain = ffn_gain.reshape(1, D)
-    near, near_kept = hidden_units(at, at, full, gain, ff, ff_core)
-    far_near = swap(near, 2)
-    far, far_kept = hidden_units(at, far_near, far_full, gain, ff, ff_core)
-    far_far = swap(far, 2)
-    sums = trade(down(at, (near, far, far_near, far_far), ff, ff_core), COLUMNS)
-    keep, give = finish(at, sums, near_kept, far_kept)
+    units, kept = hidden_units(at, full, far_full, gain, ff, ff_core)
+    sums = trade(down(at, units, swap(units, 2), ff, ff_core), COLUMNS)
+    keep, give = finish(at, sums, kept)
     give = swap(give, 1)
     rows = jnp.where(core == 0, jnp.concatenate([keep, give], axis=1), jnp.concatenate([give, keep], axis=1))
     return (keys.T, values.T, rows.T)

time: 269 us -> 230 us (0.86)
  Pallas kernels: 60.3 us -> 16.5 us
  blocking collectives: 94.7 us -> 84.5 us
  waiting for transfers between devices: 31.1 us -> 40.1 us
  starting transfers between devices: 53.4 us -> 61 us
    pallas_call x4 -> x3, Pallas kernels: 51.3 us -> 7.78 us  [the longest x1 3.47 us: hidden_units(): pl.pallas_call(hidden_kernel, out_shape=(jax.ShapeDtypeStruct((2, 128, FC...]
    all_gather x1, waiting for transfers between devices: 8.18 us -> 20.5 us  [on_device(): lax.all_gather(ff, 'grp', axis=0, axis_index_groups=[[0, 1, 2, 3], [4, 5,...]
    all_to_all x2 -> x1, blocking collectives: 34.7 us -> 24.5 us  [trade(): return lax.all_to_all(x, 'dev', 0, 0, axis_index_groups=groups, tiled=True)]
    ppermute x2 -> x1, waiting for transfers between devices: 9.9 us -> 0.01 us  [swap_groups(): return lax.ppermute(x, 'grp', [(g, g ^ 4) for g in range(GROUPS)])]
    all_to_all x0 -> x1, starting transfers between devices: none -> 7.54 us  [trade(): return lax.all_to_all(x, 'dev', 0, 0, axis_index_groups=groups, tiled=True)]
    all_to_all x1, waiting for transfers between devices: 0.01 us -> 4.52 us  [on_device(): first = lax.all_to_all(packed, 'grp', 0, 0, tiled=True)]
    ppermute x9 -> x8, starting transfers between devices: 37.2 us -> 40.2 us  [swap(): return lax.ppermute(x, 'dev', [(d, d ^ bits) for d in range(MEMBERS)])]
    ppermute x2 -> x1, starting transfers between devices: 5.53 us -> 3.36 us  [swap_groups(): return lax.ppermute(x, 'grp', [(g, g ^ 4) for g in range(GROUPS)])]
  transfers between devices with their start and end apart: 14 -> 13, of which waited for: 6 -> 7; matrix products, arithmetic and copies ran while one was open for 1% -> 1% of each run, Pallas kernels for 3% -> 3%
where the time goes in v4:
time: 230 us; the launch traced here: 229 us
  blocking collectives  84.5 us (37%)
  starting transfers between devices  61 us (27%)
  waiting for transfers between devices  40.1 us (17%)
  Pallas kernels  16.5 us (7%)
  between operations  14.2 us (6%)
  local copies, waits for them, and re-layouts  10.6 us (5%)
    all_gather x2, blocking collectives, collect(): return lax.all_gather(x, 'dev', axis=0, axis_index_groups=COLUMNS)  59.9 us
    ppermute x8, starting transfers between devices, swap(): return lax.ppermute(x, 'dev', [(d, d ^ bits) for d in range(MEMBERS)])  40.2 us
    all_to_all x1, blocking collectives, trade(): return lax.all_to_all(x, 'dev', 0, 0, axis_index_groups=groups, tiled=True)  24.5 us
    all_gather x1, waiting for transfers between devices, on_device(): lax.all_gather(ff, 'grp', axis=0, axis_index_groups=[[0, 1, 2, 3], [4, 5,...  20.5 us
    ppermute x8, waiting for transfers between devices, swap(): return lax.ppermute(x, 'dev', [(d, d ^ bits) for d in range(MEMBERS)])  13.4 us
    unnamed x30, local copies, waits for them, and re-layouts  10.5 us
    all_to_all x1, starting transfers between devices, trade(): return lax.all_to_all(x, 'dev', 0, 0, axis_index_groups=groups, tiled=True)  7.54 us
    all_to_all x1, starting transfers between devices, on_device(): first = lax.all_to_all(packed, 'grp', 0, 0, tiled=True)  5.87 us
  transfers between devices with their start and end apart: 13, of which 7 were waited for; matrix products, arithmetic and copies ran while one was open for 1% of the time, Pallas kernels for 3%

profile of v4, /device:TPU:1, one launch (start us, length us, event | category | flops | bytes accessed | tf_op | source)
XLA Modules:
  0.0 228.8 jit_solution(13884230562026926929)
XLA Ops:
  7.2 2.7 %pack.1 = (bf16[8,160,512]{2,1,0:T(8,128)(2,1)}, f32[8,128]{1,0:T(8,128)}) custom-call(bf16[64,512]{1,0:T(8,128)(2,1)} %bitcast.36, bf16[16,512]{1,0:T(8,128)(2,1)} %bitcast.38, bf16[16,512]{1,0:T(8,128)(2,1)} %bitcast.39, bf16[64,512]{1,0:T(8,128)(2,1)} %bitcast.37), custom_call_target="tpu_custom_call" | custom-call | tf_op jit(solution)/shard_map/pack/pallas_call | solution.py:254
  9.9 0.0 copy-start.11
  9.9 5.9 %all-to-all-start = ((bf16[8,160,512]{2,1,0:T(8,128)(2,1)}), bf16[8,160,512]{2,1,0:T(8,128)(2,1)S(1)}, u32[]{:S(2)}, u32[]{:S(2)}) async-start(bf16[8,160,512]{2,1,0:T(8,128)(2,1)} %get-tuple-element.19), calls=%async_computation | async-start | bytes 2621440 | tf_op jit(solution)/shard_map/all_to_all | solution.py:382
  15.8 0.1 stack.31.at
  15.9 0.1 convert_bitcast_fusion
  15.9 1.2 multiply_sine_fusion
  17.1 1.6 copy-done.1
  18.7 0.9 copy-done.3
  19.7 0.9 copy-done.4
  20.6 0.9 copy-done.5
  21.6 0.7 copy-done.9
  22.3 1.9 prepare.1
  24.2 0.6 copy-done.7
  24.8 0.6 copy-done.13
  25.4 3.4 %collective-permute-start.5 = (bf16[560,512]{1,0:T(8,128)(2,1)}, bf16[560,512]{1,0:T(8,128)(2,1)}, u32[]{:S(2)}, u32[]{:S(2)}) collective-permute-start(bf16[560,512]{1,0:T(8,128)(2,1)} %get-tuple-element.24.wide), channel_id=1, source_target_pairs={{0,256},{64,320},{128,384},{192,448},{256,0},{320,64},{384,128},{4... | collective-permute-start | bytes 1720328 | tf_op jit(solution)/shard_map/ppermute | solution.py:342
  28.8 4.5 %all-to-all-done.weights = bf16[8,160,512]{2,1,0:T(8,128)(2,1)S(1)} async-done(((bf16[8,160,512]{2,1,0:T(8,128)(2,1)}), bf16[8,160,512]{2,1,0:T(8,128)(2,1)S(1)}, u32[]{:S(2)}, u32[]{:S(2)}) %all-to-all-start) | async-done | bytes 1310752 | tf_op jit(solution)/shard_map/all_to_all | solution.py:382
  33.3 0.9 copy-done.2
  34.2 1.4 project.1
  35.6 0.6 copy-done.6
  36.3 7.5 %all-to-all-start.1 = ((bf16[8,64,128]{2,1,0:T(8,128)(2,1)}), bf16[8,64,128]{2,1,0:T(8,128)(2,1)S(1)}, u32[]{:S(2)}, u32[]{:S(2)}) async-start(bf16[8,64,128]{2,1,0:T(8,128)(2,1)} %copy-done.6), calls=%async_computation.1 | async-start | bytes 262144 | tf_op jit(solution)/shard_map/all_to_all | solution.py:351
  43.8 4.0 %collective-permute-start.6 = (bf16[224,256]{1,0:T(8,128)(2,1)}, bf16[224,256]{1,0:T(8,128)(2,1)S(1)}, u32[]{:S(2)}, u32[]{:S(2)}) collective-permute-start(bf16[224,256]{1,0:T(8,128)(2,1)} %copy-done.13), channel_id=1, source_target_pairs={{0,258},{1,259},{2,256},{3,257},{4,262},{5,263},{6,260},{7,261},{8... | collective-permute-start | bytes 344072 | tf_op jit(solution)/shard_map/ppermute | solution.py:347
  47.9 2.8 %collective-permute-start.4 = (bf16[224,256]{1,0:T(8,128)(2,1)}, bf16[224,256]{1,0:T(8,128)(2,1)S(1)}, u32[]{:S(2)}, u32[]{:S(2)}) collective-permute-start(bf16[224,256]{1,0:T(8,128)(2,1)} %copy-done.13), channel_id=1, source_target_pairs={{0,2},{1,3},{2,0},{3,1},{4,6},{5,7},{6,4},{7,5},{8,10},{9,11},{10,... | collective-permute-start | bytes 344072 | tf_op jit(solution)/shard_map/ppermute | solution.py:338
  50.7 1.6 collective-permute-done.6.got_lo
  52.3 3.2 %collective-permute-done.4.got = bf16[224,256]{1,0:T(8,128)(2,1)S(1)} collective-permute-done((bf16[224,256]{1,0:T(8,128)(2,1)}, bf16[224,256]{1,0:T(8,128)(2,1)S(1)}, u32[]{:S(2)}, u32[]{:S(2)}) %collective-permute-start.4) | collective-permute-done | bytes 114720 | tf_op jit(solution)/shard_map/ppermute | solution.py:338
  55.5 2.4 %join.1 = bf16[2,672,512]{2,1,0:T(8,128)(2,1)} custom-call(bf16[8,64,128]{2,1,0:T(8,128)(2,1)S(1)} %all-to-all-done.1.got.after, bf16[560,512]{1,0:T(8,128)(2,1)} %get-tuple-element.24.wide, bf16[224,256]{1,0:T(8,128)(2,1)S(1)} %collective-permute-done.4.got, bf16[560,512]{1,0:T(8,128)(2,1)} %collective-permute-done.5.wide_lo, ...), custom_call_target="tpu_custom_call" | custom-call | tf_op jit(solution)/shard_map/join/pallas_call | solution.py:243
  58.0 0.0 all-gather.5.cloned.1.call-update
  58.0 0.0 copy-start.10
  58.0 4.2 %collective-permute-start.2 = (bf16[8,64,512]{2,1,0:T(8,128)(2,1)S(1)}, bf16[8,64,512]{2,1,0:T(8,128)(2,1)S(1)}, u32[]{:S(2)}, u32[]{:S(2)}) collective-permute-start(bf16[8,64,512]{2,1,0:T(8,128)(2,1)S(1)} %slice.4.mine), channel_id=1, source_target_pairs={{0,3},{1,2},{2,1},{3,0},{4,7},{5,6},{6,5},{7,4},{8,11},{9,10},{10,... | collective-permute-start | bytes 1572872 | tf_op jit(solution)/shard_map/ppermute | solution.py:338
  62.3 4.0 %collective-permute-start.1 = (bf16[8,64,512]{2,1,0:T(8,128)(2,1)S(1)}, bf16[8,64,512]{2,1,0:T(8,128)(2,1)S(1)}, u32[]{:S(2)}, u32[]{:S(2)}) collective-permute-start(bf16[8,64,512]{2,1,0:T(8,128)(2,1)S(1)} %slice.4.mine), channel_id=1, source_target_pairs={{0,2},{1,3},{2,0},{3,1},{4,6},{5,7},{6,4},{7,5},{8,10},{9,11},{10,... | collective-permute-start | bytes 1572872 | tf_op jit(solution)/shard_map/ppermute | solution.py:338
  66.2 1.9 collective-permute-start
  68.2 1.4 attend.1
  69.6 33.7 %all-gather = bf16[1024,256]{1,0:T(8,128)(2,1)S(1)} all-gather(bf16[64,256]{1,0:T(8,128)(2,1)S(1)} %attend.1), channel_id=2, replica_groups={{0,4,8,12,16,20,24,28,32,36,40,44,48,52,56,60},{1,5,9,13,17,21,25,29,33..., dimensions={0}, use_global_device_ids=true | all-gather | bytes 557056 | tf_op jit(solution)/shard_map/all_gather | solution.py:355
  103.3 1.3 output.1
  104.6 20.5 %all-gather.5.cloned.1.call-done = bf16[8,672,512]{2,1,0:T(8,128)(2,1)} async-done(((bf16[2,672,512]{2,1,0:T(8,128)(2,1)}), bf16[8,672,512]{2,1,0:T(8,128)(2,1)}) %all-gather.5.cloned.1.call-update) | async-done | bytes 5505040 | tf_op jit(solution)/shard_map/all_gather | solution.py:399
  125.1 2.6 %collective-permute-start.7 = (bf16[4,2,672,512]{3,2,1,0:T(8,128)(2,1)}, bf16[4,2,672,512]{3,2,1,0:T(8,128)(2,1)S(1)}, u32[]{:S(2)}, u32[]{:S(2)}) collective-permute-start(bf16[4,2,672,512]{3,2,1,0:T(8,128)(2,1)} %bitcast.25), channel_id=1, source_target_pairs={{0,1},{1,0},{2,3},{3,2},{4,5},{5,4},{6,7},{7,6},{8,9},{9,8},{10,11... | collective-permute-start | bytes 16515080 | tf_op jit(solution)/shard_map/ppermute | solution.py:338
  127.8 26.2 %all-gather.1 = bf16[1024,256]{1,0:T(8,128)(2,1)S(1)} all-gather(bf16[64,256]{1,0:T(8,128)(2,1)S(1)} %output.1), channel_id=3, replica_groups={{0,4,8,12,16,20,24,28,32,36,40,44,48,52,56,60},{1,5,9,13,17,21,25,29,33..., dimensions={0}, use_global_device_ids=true | all-gather | bytes 557056 | tf_op jit(solution)/shard_map/all_gather | solution.py:355
  153.9 4.6 %collective-permute-start.3 = (bf16[16,64,256]{2,1,0:T(8,128)(2,1)S(1)}, bf16[16,64,256]{2,1,0:T(8,128)(2,1)S(1)}, u32[]{:S(2)}, u32[]{:S(2)}) collective-permute-start(bf16[16,64,256]{2,1,0:T(8,128)(2,1)S(1)} %bitcast.28), channel_id=1, source_target_pairs={{0,2},{1,3},{2,0},{3,1},{4,6},{5,7},{6,4},{7,5},{8,10},{9,11},{10,... | collective-permute-start | bytes 1572872 | tf_op jit(solution)/shard_map/ppermute | solution.py:338
  158.6 6.8 %collective-permute-done.3.far = bf16[16,64,256]{2,1,0:T(8,128)(2,1)S(1)} collective-permute-done((bf16[16,64,256]{2,1,0:T(8,128)(2,1)S(1)}, bf16[16,64,256]{2,1,0:T(8,128)(2,1)S(1)}, u32[]{:S(2)}, u32[]{:S(2)}) %collective-permute-start.3) | collective-permute-done | bytes 524320 | tf_op jit(solution)/shard_map/ppermute | solution.py:338
  165.4 2.6 %copy-done = bf16[8,672,512]{2,1,0:T(8,128)(2,1)S(1)} copy-done((bf16[8,672,512]{2,1,0:T(8,128)(2,1)S(1)}, bf16[8,672,512]{2,1,0:T(8,128)(2,1)}, u32[]{:S(2)}) %copy-start) | copy-done | bytes 5505048
  167.9 3.5 %hidden.1 = (bf16[2,128,224]{2,1,0:T(8,128)(2,1)S(1)}, bf16[128,128]{1,0:T(8,128)(2,1)S(1)}) custom-call(s32[7]{0:T(128)S(1)} %stack.31.at, bf16[16,64,256]{2,1,0:T(8,128)(2,1)S(1)} %bitcast.29, bf16[16,64,256]{2,1,0:T(8,128)(2,1)S(1)} %collective-permute-done.3.far, f32[1,4096]{1,0:T(1,128)S(1)} %bitcast.35, bf16[4,2,672,512]{3,2,1,0:T(8,128)(2,1)S(1)} %bitcast.26, ...), custom_call_target="tpu_custom_call" | custom-call | flops 939524096 | bytes 8388608 | tf_op jit(solution)/shard_map/hidden/pallas_call | solution.py:303
  171.4 4.6 %collective-permute-start.8 = (bf16[2,128,224]{2,1,0:T(8,128)(2,1)S(1)}, bf16[2,128,224]{2,1,0:T(8,128)(2,1)S(1)}, u32[]{:S(2)}, u32[]{:S(2)}) collective-permute-start(bf16[2,128,224]{2,1,0:T(8,128)(2,1)S(1)} %get-tuple-element.27.units), channel_id=1, source_target_pairs={{0,2},{1,3},{2,0},{3,1},{4,6},{5,7},{6,4},{7,5},{8,10},{9,11},{10,... | collective-permute-start | bytes 344072 | tf_op jit(solution)/shard_map/ppermute | solution.py:338
  176.0 2.6 %collective-permute-done.8.far_units = bf16[2,128,224]{2,1,0:T(8,128)(2,1)S(1)} collective-permute-done((bf16[2,128,224]{2,1,0:T(8,128)(2,1)S(1)}, bf16[2,128,224]{2,1,0:T(8,128)(2,1)S(1)}, u32[]{:S(2)}, u32[]{:S(2)}) %collective-permute-start.8) | collective-permute-done | bytes 114720 | tf_op jit(solution)/shard_map/ppermute | solution.py:338
  178.6 1.2 down.1
  179.9 24.5 %all_to_all.15.got = bf16[16,128,128]{2,1,0:T(8,128)(2,1)S(1)} all-to-all(bf16[16,128,128]{2,1,0:T(8,128)(2,1)S(1)} %down.1), channel_id=1, replica_groups={{0,4,8,12,16,20,24,28,32,36,40,44,48,52,56,60},{1,5,9,13,17,21,25,29,33..., dimensions={0} | all-to-all | bytes 1048576 | tf_op jit(solution)/shard_map/all_to_all | solution.py:351
  204.4 0.7 finish.1
  205.1 15.4 %collective-permute-start.9 = (bf16[64,128]{1,0:T(8,128)(2,1)S(1)}, bf16[64,128]{1,0:T(8,128)(2,1)S(1)}, u32[]{:S(2)}, u32[]{:S(2)}) collective-permute-start(bf16[64,128]{1,0:T(8,128)(2,1)S(1)} %get-tuple-element.30), channel_id=1, source_target_pairs={{0,1},{1,0},{2,3},{3,2},{4,5},{5,4},{6,7},{7,6},{8,9},{9,8},{10,11... | collective-permute-start | bytes 49160 | tf_op jit(solution)/shard_map/ppermute | solution.py:338
  220.5 0.8 collective-permute-done.9
  221.3 0.6 fusion
  (27 shorter events, 0.1 us)
Async XLA Ops:
  7.2 8.7 %copy-start.14 = (s32[2]{0:T(128)S(1)}, s32[2]{0:T(128)}, u32[]{:S(2)}) copy-start(s32[2]{0:T(128)} %param.14) | copy-start | bytes 28
  9.9 7.3 %copy-start.11 = (f32[8,128]{1,0:T(8,128)S(1)}, f32[8,128]{1,0:T(8,128)}, u32[]{:S(2)}) copy-start(f32[8,128]{1,0:T(8,128)} %get-tuple-element.17.after) | copy-start | bytes 12292
  9.9 23.4 %all-to-all-start = ((bf16[8,160,512]{2,1,0:T(8,128)(2,1)}), bf16[8,160,512]{2,1,0:T(8,128)(2,1)S(1)}, u32[]{:S(2)}, u32[]{:S(2)}) async-start(bf16[8,160,512]{2,1,0:T(8,128)(2,1)} %get-tuple-element.19), calls=%async_computation | async-start | bytes 2621440 | tf_op jit(solution)/shard_map/all_to_all | solution.py:382
  17.1 1.6 copy-start.1
  18.7 0.9 copy-start.3
  19.7 0.9 copy-start.4
  20.6 0.9 copy-start.5
  21.5 0.7 copy-start.9
  24.2 0.6 copy-start.7
  24.8 0.6 copy-start.13
  25.4 30.1 %collective-permute-start.5 = (bf16[560,512]{1,0:T(8,128)(2,1)}, bf16[560,512]{1,0:T(8,128)(2,1)}, u32[]{:S(2)}, u32[]{:S(2)}) collective-permute-start(bf16[560,512]{1,0:T(8,128)(2,1)} %get-tuple-element.24.wide), channel_id=1, source_target_pairs={{0,256},{64,320},{128,384},{192,448},{256,0},{320,64},{384,128},{4... | collective-permute-start | bytes 1720328 | tf_op jit(solution)/shard_map/ppermute | solution.py:342
  33.3 0.9 copy-start.2
  35.6 0.6 copy-start.6
  36.3 19.2 %all-to-all-start.1 = ((bf16[8,64,128]{2,1,0:T(8,128)(2,1)}), bf16[8,64,128]{2,1,0:T(8,128)(2,1)S(1)}, u32[]{:S(2)}, u32[]{:S(2)}) async-start(bf16[8,64,128]{2,1,0:T(8,128)(2,1)} %copy-done.6), calls=%async_computation.1 | async-start | bytes 262144 | tf_op jit(solution)/shard_map/all_to_all | solution.py:351
  43.8 81.3 %all-gather.5.cloned.1.call-start = ((), (), s32[]{:S(2)}) async-start(), calls=%async_computation.3 | async-start | bytes 6881280 | tf_op jit(solution)/shard_map/all_gather | solution.py:399
  43.8 24.3 %copy-start.12 = (s32[2]{0:T(128)S(1)}, s32[2]{0:T(128)}, u32[]{:S(2)}) copy-start(s32[2]{0:T(128)} %lengths.1) | copy-start | bytes 28
  43.8 8.5 %collective-permute-start.6 = (bf16[224,256]{1,0:T(8,128)(2,1)}, bf16[224,256]{1,0:T(8,128)(2,1)S(1)}, u32[]{:S(2)}, u32[]{:S(2)}) collective-permute-start(bf16[224,256]{1,0:T(8,128)(2,1)} %copy-done.13), channel_id=1, source_target_pairs={{0,258},{1,259},{2,256},{3,257},{4,262},{5,263},{6,260},{7,261},{8... | collective-permute-start | bytes 344072 | tf_op jit(solution)/shard_map/ppermute | solution.py:347
  47.9 7.7 %collective-permute-start.4 = (bf16[224,256]{1,0:T(8,128)(2,1)}, bf16[224,256]{1,0:T(8,128)(2,1)S(1)}, u32[]{:S(2)}, u32[]{:S(2)}) collective-permute-start(bf16[224,256]{1,0:T(8,128)(2,1)} %copy-done.13), channel_id=1, source_target_pairs={{0,2},{1,3},{2,0},{3,1},{4,6},{5,7},{6,4},{7,5},{8,10},{9,11},{10,... | collective-permute-start | bytes 344072 | tf_op jit(solution)/shard_map/ppermute | solution.py:338
  58.0 45.4 %copy-start.8 = (bf16[64,256]{1,0:T(8,128)(2,1)S(1)}, bf16[64,256]{1,0:T(8,128)(2,1)}, u32[]{:S(2)}) copy-start(bf16[64,256]{1,0:T(8,128)(2,1)} %copy-done.7) | copy-start | bytes 98308
  58.0 107.3 %copy-start.10 = (f32[4096]{0:T(1024)S(1)}, f32[4096]{0:T(1024)}, u32[]{:S(2)}) copy-start(f32[4096]{0:T(1024)} %param.20) | copy-start | bytes 49156
  58.0 45.3 %collective-permute-start.2 = (bf16[8,64,512]{2,1,0:T(8,128)(2,1)S(1)}, bf16[8,64,512]{2,1,0:T(8,128)(2,1)S(1)}, u32[]{:S(2)}, u32[]{:S(2)}) collective-permute-start(bf16[8,64,512]{2,1,0:T(8,128)(2,1)S(1)} %slice.4.mine), channel_id=1, source_target_pairs={{0,3},{1,2},{2,1},{3,0},{4,7},{5,6},{6,5},{7,4},{8,11},{9,10},{10,... | collective-permute-start | bytes 1572872 | tf_op jit(solution)/shard_map/ppermute | solution.py:338
  62.3 41.1 %collective-permute-start.1 = (bf16[8,64,512]{2,1,0:T(8,128)(2,1)S(1)}, bf16[8,64,512]{2,1,0:T(8,128)(2,1)S(1)}, u32[]{:S(2)}, u32[]{:S(2)}) collective-permute-start(bf16[8,64,512]{2,1,0:T(8,128)(2,1)S(1)} %slice.4.mine), channel_id=1, source_target_pairs={{0,2},{1,3},{2,0},{3,1},{4,6},{5,7},{6,4},{7,5},{8,10},{9,11},{10,... | collective-permute-start | bytes 1572872 | tf_op jit(solution)/shard_map/ppermute | solution.py:338
  66.2 37.1 %collective-permute-start = (bf16[8,64,512]{2,1,0:T(8,128)(2,1)S(1)}, bf16[8,64,512]{2,1,0:T(8,128)(2,1)S(1)}, u32[]{:S(2)}, u32[]{:S(2)}) collective-permute-start(bf16[8,64,512]{2,1,0:T(8,128)(2,1)S(1)} %slice.4.mine), channel_id=1, source_target_pairs={{0,1},{1,0},{2,3},{3,2},{4,5},{5,4},{6,7},{7,6},{8,9},{9,8},{10,11... | collective-permute-start | bytes 1572872 | tf_op jit(solution)/shard_map/ppermute | solution.py:338
  125.1 40.2 %collective-permute-start.7 = (bf16[4,2,672,512]{3,2,1,0:T(8,128)(2,1)}, bf16[4,2,672,512]{3,2,1,0:T(8,128)(2,1)S(1)}, u32[]{:S(2)}, u32[]{:S(2)}) collective-permute-start(bf16[4,2,672,512]{3,2,1,0:T(8,128)(2,1)} %bitcast.25), channel_id=1, source_target_pairs={{0,1},{1,0},{2,3},{3,2},{4,5},{5,4},{6,7},{7,6},{8,9},{9,8},{10,11... | collective-permute-start | bytes 16515080 | tf_op jit(solution)/shard_map/ppermute | solution.py:338
  153.9 11.4 %collective-permute-start.3 = (bf16[16,64,256]{2,1,0:T(8,128)(2,1)S(1)}, bf16[16,64,256]{2,1,0:T(8,128)(2,1)S(1)}, u32[]{:S(2)}, u32[]{:S(2)}) collective-permute-start(bf16[16,64,256]{2,1,0:T(8,128)(2,1)S(1)} %bitcast.28), channel_id=1, source_target_pairs={{0,2},{1,3},{2,0},{3,1},{4,6},{5,7},{6,4},{7,5},{8,10},{9,11},{10,... | collective-permute-start | bytes 1572872 | tf_op jit(solution)/shard_map/ppermute | solution.py:338
  165.4 2.6 %copy-start = (bf16[8,672,512]{2,1,0:T(8,128)(2,1)S(1)}, bf16[8,672,512]{2,1,0:T(8,128)(2,1)}, u32[]{:S(2)}) copy-start(bf16[8,672,512]{2,1,0:T(8,128)(2,1)} %all-gather.5.cloned.1.call-done) | copy-start | bytes 16515076
  171.4 7.2 %collective-permute-start.8 = (bf16[2,128,224]{2,1,0:T(8,128)(2,1)S(1)}, bf16[2,128,224]{2,1,0:T(8,128)(2,1)S(1)}, u32[]{:S(2)}, u32[]{:S(2)}) collective-permute-start(bf16[2,128,224]{2,1,0:T(8,128)(2,1)S(1)} %get-tuple-element.27.units), channel_id=1, source_target_pairs={{0,2},{1,3},{2,0},{3,1},{4,6},{5,7},{6,4},{7,5},{8,10},{9,11},{10,... | collective-permute-start | bytes 344072 | tf_op jit(solution)/shard_map/ppermute | solution.py:338
  205.1 16.2 %collective-permute-start.9 = (bf16[64,128]{1,0:T(8,128)(2,1)S(1)}, bf16[64,128]{1,0:T(8,128)(2,1)S(1)}, u32[]{:S(2)}, u32[]{:S(2)}) collective-permute-start(bf16[64,128]{1,0:T(8,128)(2,1)S(1)} %get-tuple-element.30), channel_id=1, source_target_pairs={{0,1},{1,0},{2,3},{3,2},{4,5},{5,4},{6,7},{7,6},{8,9},{9,8},{10,11... | collective-permute-start | bytes 49160 | tf_op jit(solution)/shard_map/ppermute | solution.py:338
Sparse Core Ops, SparseCore 0:
  58.1 66.9 all-gather.4

commit v5 on v4

--- a/solution.py
+++ b/solution.py
@@ -118,33 +118,36 @@
     out[...] = attended
 
 
-def hidden_kernel(at, near, far, gain, mine, core, out, kept):
+def renorm(got, gain, out):
+    squares = jnp.zeros((HALF, 1), F32)
+    for z in range(DEPTH):
+        x = got[z].astype(F32)
+        squares = squares + jnp.sum(x * x, axis=-1, keepdims=True)
+    scale = lax.rsqrt(squares * (1.0 / D) + 1e-05)
+    for z in range(DEPTH):
+        x = got[z].astype(F32) * scale * gain[:, z * BAND : (z + 1) * BAND]
+        out[z // 2, :, (z % 2) * BAND : (z % 2 + 1) * BAND] = x.astype(BF)
+
+
+def near_kernel(got, gain, mine, mine_lo, out):
+    renorm(got, gain, out)
+
+
+def hidden_kernel(at, near, full, far, gain, mine, mine_lo, core, core_lo, out, kept, normed):
     low = at[1] == 0
     lanes = pl.ds(pl.multiple_of(at[1] * 128, 128), 128)
-    near_kept, far_kept = near[at[2], :, lanes], far[at[2], :, lanes]
+    near_kept, far_kept = full[at[2], :, lanes], far[at[2], :, lanes]
     kept[0:HALF, :] = jnp.where(low, near_kept, far_kept)
     kept[HALF : 2 * HALF, :] = jnp.where(low, far_kept, near_kept)
-    scales = []
-    for got in (near, far):
-        squares = jnp.zeros((HALF, 1), F32)
-        for z in range(DEPTH):
-            x = got[z].astype(F32)
-            squares = squares + jnp.sum(x * x, axis=-1, keepdims=True)
-        scales.append(lax.rsqrt(squares * (1.0 / D) + 1e-05))
+    renorm(far, gain, normed)
     totals = [jnp.zeros((2 * HALF, FC), F32) for _ in range(4)]
-    for g in range(GROUPS):
-        rows = []
-        for got, scale in zip((near, far), scales):
-            parts = []
-            for z in (2 * g, 2 * g + 1):
-                part = got[z].astype(F32) * scale * gain[:, z * BAND : (z + 1) * BAND]
-                parts.append(part.astype(BF))
-            rows.append(jnp.concatenate(parts, axis=1))
-        x = jnp.concatenate(rows, axis=0)
-        side = jnp.bitwise_xor(g // 4, at[6])
-        for i, w in enumerate((mine, core)):
-            totals[2 * i] = totals[2 * i] + nt(x, w[g % 4, side, 0:FC, :])
-            totals[2 * i + 1] = totals[2 * i + 1] + nt(x, w[g % 4, side, FC : 2 * FC, :])
+    for x in range(4):
+        for side, pair in enumerate(((mine, core), (mine_lo, core_lo))):
+            g = jnp.bitwise_xor(at[6], side) * 4 + x
+            rows = jnp.concatenate([near[g], normed[g]], axis=0)
+            for i, w in enumerate(pair):
+                totals[2 * i] = totals[2 * i] + nt(rows, w[x, 0:FC, :])
+                totals[2 * i + 1] = totals[2 * i + 1] + nt(rows, w[x, FC : 2 * FC, :])
     for i in range(2):
         gate = totals[2 * i]
         units = (gate / (1.0 + jnp.exp(-gate)) * totals[2 * i + 1]).astype(BF)
@@ -153,15 +156,16 @@
         out[i, HALF : 2 * HALF, :] = jnp.where(low, second, first)
 
 
-def down_kernel(at, units, far_units, mine, core, out):
-    for g in range(GROUPS):
-        side = jnp.bitwise_xor(g // 4, at[6])
-        total = jnp.zeros((128, BAND), F32)
-        for i, w in enumerate((mine, core)):
-            total = total + jnp.dot(units[i], w[g % 4, side, 2 * FC : 3 * FC, 0:BAND], preferred_element_type=F32)
-            total = total + jnp.dot(far_units[i], w[g % 4, side, 2 * FC : 3 * FC, BAND:RUN], preferred_element_type=F32)
-        out[2 * g] = total[:, 0:128].astype(BF)
-        out[2 * g + 1] = total[:, 128:256].astype(BF)
+def down_kernel(at, units, far_units, mine, mine_lo, core, core_lo, out):
+    for x in range(4):
+        for side, pair in enumerate(((mine, core), (mine_lo, core_lo))):
+            total = jnp.zeros((128, BAND), F32)
+            for i, w in enumerate(pair):
+                total = total + jnp.dot(units[i], w[x, 2 * FC : 3 * FC, 0:BAND], preferred_element_type=F32)
+                total = total + jnp.dot(far_units[i], w[x, 2 * FC : 3 * FC, BAND:RUN], preferred_element_type=F32)
+            z = (jnp.bitwise_xor(at[6], side) * 4 + x) * 2
+            out[z] = total[:, 0:128].astype(BF)
+            out[z + 1] = total[:, 128:256].astype(BF)
 
 
 def finish_kernel(at, got, kept, keep, give):
@@ -192,62 +196,84 @@
         copy.wait()
 
 
-def prepare_kernel(at, after, tables, gate, up, narrow, stream, gain, wide, give, normed, own):
-    wide[0:FC, :] = gate[...]
-    wide[FC : 2 * FC, :] = up[...]
+def divide_kernel(at, after, narrow, keep, give, held, sem):
+    copy = pltpu.make_async_copy(narrow, held, sem.at[0])
+    copy.start()
+    copy.wait()
     low = at[1] == 0
     for i in range(2):
-        even = narrow[:, 2 * i * 128 : (2 * i + 1) * 128]
-        odd = narrow[:, (2 * i + 1) * 128 : (2 * i + 2) * 128]
-        keep = jnp.where(low, even, odd)
-        for k in range(2):
-            lanes = slice(k * BAND + i * 128, k * BAND + (i + 1) * 128)
-            wide[2 * FC : 5 * FC // 2, lanes] = keep[k * FC // 2 : (k + 1) * FC // 2, :]
+        even = held[:, 2 * i * 128 : (2 * i + 1) * 128]
+        odd = held[:, (2 * i + 1) * 128 : (2 * i + 2) * 128]
+        keep[:, i * 128 : (i + 1) * 128] = jnp.where(low, even, odd)
         give[:, i * 128 : (i + 1) * 128] = jnp.where(low, odd, even)
-    x = stream[...].astype(F32)
+
+
+def divide(at, after, narrow):
+    half = jax.ShapeDtypeStruct((FC, BAND), BF)
+    return pl.pallas_call(
+        divide_kernel,
+        out_shape=(half, half),
+        in_specs=[SMEM, ANY, HBM],
+        out_specs=(VMEM,) * 2,
+        scratch_shapes=[pltpu.VMEM((FC, RUN), BF), pltpu.SemaphoreType.DMA((1,))],
+        compiler_params=params(57),
+        name="divide",
+    )(at, after, narrow)
+
+
+def norm_kernel(at, after, tables, stream, gain, normed, own, held, gains, sems):
+    copies = [
+        pltpu.make_async_copy(stream, held, sems.at[0]),
+        pltpu.make_async_copy(gain, gains, sems.at[1]),
+    ]
+    for copy in copies:
+        copy.start()
+    for copy in copies:
+        copy.wait()
+    x = held[...].astype(F32)
     scale = lax.rsqrt(jnp.mean(x * x, axis=-1, keepdims=True) + 1e-05)
     for g in range(GROUPS):
         cols = pl.ds(g * RUN, RUN)
-        normed[g] = (stream[:, cols].astype(F32) * scale * gain[:, cols]).astype(BF)
+        normed[g] = (held[:, cols].astype(F32) * scale * gains[:, cols]).astype(BF)
     rows = pl.ds(pl.multiple_of(at[0] * 128 + at[1] * HALF, HALF), HALF)
-    own[...] = stream[rows, pl.ds(pl.multiple_of(at[2] * BAND, BAND), BAND)]
-
-
-def prepare(at, after, tables, gate, up, narrow, stream, gain):
-    half = jax.ShapeDtypeStruct((FC, BAND), BF)
-    return pl.pallas_call(
-        prepare_kernel,
-        out_shape=(
-            jax.ShapeDtypeStruct((5 * FC // 2, RUN), BF),
-            half,
-            jax.ShapeDtypeStruct((GROUPS, 256, RUN), BF),
-            jax.ShapeDtypeStruct((HALF, BAND), BF),
-        ),
-        in_specs=[SMEM, ANY, ANY] + [VMEM] * 5,
-        out_specs=(VMEM,) * 4,
-        compiler_params=params(24),
-        name="prepare",
-    )(at, after, tables, gate, up, narrow, stream, gain)
-
-
-def join_kernel(after, wide, got, wide_lo, got_lo, out):
-    for i, (kept, given) in enumerate(((wide, got), (wide_lo, got_lo))):
-        out[i, 0 : 2 * FC, :] = kept[0 : 2 * FC, :]
-        for k in range(2):
-            rows = slice(2 * FC + k * FC // 2, 2 * FC + (k + 1) * FC // 2)
-            out[i, rows, 0:BAND] = kept[2 * FC : 5 * FC // 2, k * BAND : (k + 1) * BAND]
-        out[i, 2 * FC : 3 * FC, BAND:RUN] = given[...]
-
-
-def join(after, *parts):
+    own[...] = held[rows, pl.ds(pl.multiple_of(at[2] * BAND, BAND), BAND)]
+
+
+def norm(at, after, tables, stream, gain):
+    return pl.pallas_call(
+        norm_kernel,
+        out_shape=(jax.ShapeDtypeStruct((GROUPS, 256, RUN), BF), jax.ShapeDtypeStruct((HALF, BAND), BF)),
+        in_specs=[SMEM, ANY, ANY, HBM, HBM],
+        out_specs=(VMEM,) * 2,
+        scratch_shapes=[pltpu.VMEM((256, D), BF), pltpu.VMEM((1, D), F32), pltpu.SemaphoreType.DMA((2,))],
+        compiler_params=params(50),
+        name="norm",
+    )(at, after, tables, stream, gain)
+
+
+def join_kernel(after, gate, up, keep, got, out, sems):
+    copies = [
+        pltpu.make_async_copy(gate, out.at[pl.ds(0, FC), :], sems.at[0]),
+        pltpu.make_async_copy(up, out.at[pl.ds(FC, FC), :], sems.at[1]),
+    ]
+    for copy in copies:
+        copy.start()
+    out[2 * FC : 3 * FC, 0:BAND] = keep[...]
+    out[2 * FC : 3 * FC, BAND:RUN] = got[...]
+    for copy in copies:
+        copy.wait()
+
+
+def join(after, gate, up, keep, got):
     return pl.pallas_call(
         join_kernel,
-        out_shape=jax.ShapeDtypeStruct((2, 3 * FC, RUN), BF),
-        in_specs=[ANY] + [VMEM] * 4,
+        out_shape=jax.ShapeDtypeStruct((3 * FC, RUN), BF),
+        in_specs=[ANY, HBM, HBM, VMEM, VMEM],
         out_specs=VMEM,
+        scratch_shapes=[pltpu.SemaphoreType.DMA((2,))],
         compiler_params=params(16),
         name="join",
-    )(after, *parts)
+    )(after, gate, up, keep, got)
 
 
 def pack(*parts):
@@ -299,28 +325,40 @@
     )(at, got, *weights, own)
 
 
-def hidden_units(at, near, far, gain, mine, core):
+def near_half(got, gain, mine, mine_lo):
+    return pl.pallas_call(
+        near_kernel,
+        out_shape=jax.ShapeDtypeStruct((GROUPS, HALF, RUN), BF),
+        in_specs=[VMEM] * 4,
+        out_specs=VMEM,
+        compiler_params=params(16),
+        name="near_half",
+    )(got, gain, mine, mine_lo)
+
+
+def hidden_units(at, near, full, far, gain, weights):
     return pl.pallas_call(
         hidden_kernel,
         out_shape=(jax.ShapeDtypeStruct((2, 128, FC), BF), jax.ShapeDtypeStruct((128, 128), BF)),
-        in_specs=[SMEM] + [VMEM] * 5,
+        in_specs=[SMEM] + [VMEM] * 8,
         out_specs=(VMEM, VMEM),
+        scratch_shapes=[pltpu.VMEM((GROUPS, HALF, RUN), BF)],
         compiler_params=params(16),
         cost_estimate=cost(4 * HALF * D * 4 * FC, 8 * 2**20),
         name="hidden",
-    )(at, near, far, gain, mine, core)
-
-
-def down(at, units, far_units, mine, core):
+    )(at, near, full, far, gain, *weights)
+
+
+def down(at, units, far_units, weights):
     return pl.pallas_call(
         down_kernel,
         out_shape=jax.ShapeDtypeStruct((DEPTH, 128, 128), BF),
-        in_specs=[SMEM] + [VMEM] * 4,
+        in_specs=[SMEM] + [VMEM] * 6,
         out_specs=VMEM,
         compiler_params=params(16),
         cost_estimate=cost(4 * HALF * D * 2 * FC, 5 * 2**20),
         name="down",
-    )(at, units, far_units, mine, core)
+    )(at, units, far_units, *weights)
 
 
 def finish(at, got, kept):
@@ -342,9 +380,8 @@
     return lax.ppermute(x, "grp", [(g, g ^ 4) for g in range(GROUPS)])
 
 
-def swap_both(x):
-    pairs = [(g * MEMBERS + d, (g ^ 4) * MEMBERS + (d ^ 2)) for g in range(GROUPS) for d in range(MEMBERS)]
-    return lax.ppermute(x, ("grp", "dev"), pairs)
+def collect_x(x):
+    return lax.all_gather(x, "grp", axis=0, axis_index_groups=[[0, 1, 2, 3], [4, 5, 6, 7]])
 
 
 def trade(x, groups):
@@ -389,25 +426,27 @@
     angle = positions.astype(F32)[:, None] * freq[None, :]
     cos, sin = jnp.cos(angle), jnp.sin(angle)
 
-    wide, give, normed, own = prepare(
-        at, token, cos, w_gate.T, w_up.T, w_down.T, stream, attn_gain.reshape(1, D)
-    )
-    trades = (swap(give, 2), swap_groups(wide), swap_both(give))
+    keep, give = divide(at, token, w_down.T)
+    other = swap(give, 2)
+    normed, own = norm(at, give, cos, stream, attn_gain.reshape(1, D))
     send, keys, values = project(normed, first, cos, sin)
     got = trade(send, OCTETS)
-    ff = join(got, wide, *trades)
-    ff_all = lax.all_gather(ff, "grp", axis=0, axis_index_groups=[[0, 1, 2, 3], [4, 5, 6, 7]])
+    mine = join(send, w_gate.T, w_up.T, keep, other)
+    own_mixed = attend(at, row_length, got)
+    mine_lo = after(swap_groups(mine), own_mixed)
+    mine, mine_lo = collect_x(mine), collect_x(mine_lo)
     out_own = first[:, 96:160, :]
     out_weights = (out_own, swap(out_own, 1), swap(out_own, 2), swap(out_own, 3))
-    mixed = collect(attend(at, row_length, got))
+    mixed = collect(own_mixed)
     attended = output(at, mixed, out_weights, own)
-    ff = after(ff_all, attended)
-    ff_core = swap(ff, 1)
     full = collect(attended)
-    far_full = swap(full, 2)
+    far = swap(full, 2)
+    mine, mine_lo = after((mine, mine_lo), full)
+    weights = (mine, mine_lo, swap(mine, 1), swap(mine_lo, 1))
     gain = ffn_gain.reshape(1, D)
-    units, kept = hidden_units(at, full, far_full, gain, ff, ff_core)
-    sums = trade(down(at, units, swap(units, 2), ff, ff_core), COLUMNS)
+    near = near_half(full, gain, mine, mine_lo)
+    units, kept = hidden_units(at, near, full, far, gain, weights)
+    sums = trade(down(at, units, swap(units, 2), weights), COLUMNS)
     keep, give = finish(at, sums, kept)
     give = swap(give, 1)
     rows = jnp.where(core == 0, jnp.concatenate([keep, give], axis=1), jnp.concatenate([give, keep], axis=1))

time: 230 us -> 223 us (0.970)
  blocking collectives: 84.5 us -> 107 us
  waiting for transfers between devices: 40.1 us -> 19.5 us
  starting transfers between devices: 61 us -> 50.4 us
  Pallas kernels: 16.5 us -> 20.5 us
    all_to_all x1 -> x2, blocking collectives: 24.5 us -> 48.9 us  [trade(): return lax.all_to_all(x, 'dev', 0, 0, axis_index_groups=groups, tiled=True)]
    all_gather x1 -> x2, waiting for transfers between devices: 20.5 us -> 0.01 us  [collect_x(): lax.all_gather(x, 'grp', axis=0, axis_index_groups=[[0, 1, 2, 3], [4, 5,...]
    all_to_all x1 -> x0, starting transfers between devices: 7.54 us -> none  [trade(): return lax.all_to_all(x, 'dev', 0, 0, axis_index_groups=groups, tiled=True)]
    pallas_call x2 -> x4, Pallas kernels: 4.31 us -> 8.4 us  [the longest x1 3.38 us: norm(): pl.pallas_call(norm_kernel, out_shape=(jax.ShapeDtypeStruct((GROUPS, 256,...]
    ppermute x1 -> x0, starting transfers between devices: 4.02 us -> none  [swap_both(): return lax.ppermute(x, ('grp', 'dev'), pairs)]
    ppermute x8 -> x9, waiting for transfers between devices: 13.4 us -> 16.4 us  [swap(): return lax.ppermute(x, 'dev', [(d, d ^ bits) for d in range(MEMBERS)])]
    unnamed x30 -> x38, local copies, waits for them, and re-layouts: 10.5 us -> 8.15 us
    all_gather x2, blocking collectives: 59.9 us -> 57.6 us  [collect(): return lax.all_gather(x, 'dev', axis=0, axis_index_groups=COLUMNS)]
  transfers between devices with their start and end apart: 13 -> 13, of which waited for: 7 -> 5; matrix products, arithmetic and copies ran while one was open for 1% -> 1% of each run, Pallas kernels for 3% -> 5%
where the time goes in v5:
time: 223 us; the launch traced here: 222 us
  blocking collectives  107 us (48%)
  starting transfers between devices  50.4 us (23%)
  Pallas kernels  20.5 us (9%)
  waiting for transfers between devices  19.5 us (9%)
  between operations  14.4 us (6%)
  local copies, waits for them, and re-layouts  8.86 us (4%)
    all_gather x2, blocking collectives, collect(): return lax.all_gather(x, 'dev', axis=0, axis_index_groups=COLUMNS)  57.6 us
    all_to_all x2, blocking collectives, trade(): return lax.all_to_all(x, 'dev', 0, 0, axis_index_groups=groups, tiled=True)  48.9 us
    ppermute x9, starting transfers between devices, swap(): return lax.ppermute(x, 'dev', [(d, d ^ bits) for d in range(MEMBERS)])  42.2 us
    ppermute x9, waiting for transfers between devices, swap(): return lax.ppermute(x, 'dev', [(d, d ^ bits) for d in range(MEMBERS)])  16.4 us
    unnamed x38, local copies, waits for them, and re-layouts  8.15 us
    all_to_all x1, starting transfers between devices, on_device(): first = lax.all_to_all(packed, 'grp', 0, 0, tiled=True)  5.87 us
  transfers between devices with their start and end apart: 13, of which 5 were waited for; matrix products, arithmetic and copies ran while one was open for 1% of the time, Pallas kernels for 5%

profile of v5, /device:TPU:1, one launch (start us, length us, event | category | flops | bytes accessed | tf_op | source)
XLA Modules:
  0.0 222.2 jit_solution(640481928831379644)
XLA Ops:
  7.2 2.7 %pack.1 = (bf16[8,160,512]{2,1,0:T(8,128)(2,1)}, f32[8,128]{1,0:T(8,128)}) custom-call(bf16[64,512]{1,0:T(8,128)(2,1)} %bitcast.44, bf16[16,512]{1,0:T(8,128)(2,1)} %bitcast.46, bf16[16,512]{1,0:T(8,128)(2,1)} %bitcast.47, bf16[64,512]{1,0:T(8,128)(2,1)} %bitcast.45), custom_call_target="tpu_custom_call" | custom-call | tf_op jit(solution)/shard_map/pack/pallas_call | solution.py:280
  9.9 5.9 %all-to-all-start = ((bf16[8,160,512]{2,1,0:T(8,128)(2,1)}), bf16[8,160,512]{2,1,0:T(8,128)(2,1)S(1)}, u32[]{:S(2)}, u32[]{:S(2)}) async-start(bf16[8,160,512]{2,1,0:T(8,128)(2,1)} %get-tuple-element.22), calls=%async_computation | async-start | bytes 2621440 | tf_op jit(solution)/shard_map/all_to_all | solution.py:419
  15.8 0.0 all-gather.7.cloned.1.call-start
  15.9 0.7 stack.31.at
  16.6 2.3 %divide.1 = (bf16[224,256]{1,0:T(8,128)(2,1)}, bf16[224,256]{1,0:T(8,128)(2,1)}) custom-call(s32[7]{0:T(128)} %stack.31.at, f32[8,128]{1,0:T(8,128)} %get-tuple-element.19.after, bf16[224,512]{1,0:T(8,128)(2,1)} %bitcast.43), custom_call_target="tpu_custom_call" | custom-call | tf_op jit(solution)/shard_map/divide/pallas_call | solution.py:213
  18.9 4.5 %collective-permute-start.3 = (bf16[224,256]{1,0:T(8,128)(2,1)}, bf16[224,256]{1,0:T(8,128)(2,1)}, u32[]{:S(2)}, u32[]{:S(2)}) collective-permute-start(bf16[224,256]{1,0:T(8,128)(2,1)} %get-tuple-element.20.after), channel_id=1, source_target_pairs={{0,2},{1,3},{2,0},{3,1},{4,6},{5,7},{6,4},{7,5},{8,10},{9,11},{10,... | collective-permute-start | bytes 344072 | tf_op jit(solution)/shard_map/ppermute | solution.py:376
  23.5 0.1 convert_bitcast_fusion
  23.6 1.2 multiply_sine_fusion
  24.8 0.9 copy-done.9
  25.7 0.7 copy-done.13
  26.3 3.4 %norm.1 = (bf16[8,256,512]{2,1,0:T(8,128)(2,1)S(1)}, bf16[64,256]{1,0:T(8,128)(2,1)S(1)}) custom-call(s32[7]{0:T(128)S(1)} %copy-done.13, bf16[224,256]{1,0:T(8,128)(2,1)S(1)} %copy-done.9, f32[256,128]{1,0:T(8,128)S(1)} %get-tuple-element.36.tables.cos, bf16[256,4096]{1,0:T(8,128)(2,1)} %stream.1, f32[1,4096]{1,0:T(1,128)S(1)} %bitcast.42), custom_call_target="tpu_custom_call" | custom-call | tf_op jit(solution)/shard_map/norm/pallas_call | solution.py:243
  29.7 0.0 copy-start.11
  29.7 0.6 copy-done.11
  30.3 3.1 %all-to-all-done.weights = bf16[8,160,512]{2,1,0:T(8,128)(2,1)S(1)} async-done(((bf16[8,160,512]{2,1,0:T(8,128)(2,1)}), bf16[8,160,512]{2,1,0:T(8,128)(2,1)S(1)}, u32[]{:S(2)}, u32[]{:S(2)}) %all-to-all-start) | async-done | bytes 1310752 | tf_op jit(solution)/shard_map/all_to_all | solution.py:419
  33.4 0.9 copy-done.5
  34.3 1.4 project.1
  35.8 1.1 collective-permute-done.3.got
  36.9 2.3 %join.1 = bf16[672,512]{1,0:T(8,128)(2,1)} custom-call(bf16[8,64,128]{2,1,0:T(8,128)(2,1)S(1)} %get-tuple-element.25.after, bf16[224,512]{1,0:T(8,128)(2,1)S(1)} %bitcast.38, bf16[224,512]{1,0:T(8,128)(2,1)S(1)} %bitcast.39, bf16[224,256]{1,0:T(8,128)(2,1)S(1)} %copy-done.8, bf16[224,256]{1,0:T(8,128)(2,1)} %collective-permute-done.3.got), custom_call_target="tpu_custom_call" | custom-call | tf_op jit(solution)/shard_map/join/pallas_call | solution.py:268
  39.3 0.6 copy-done.4
  39.9 0.0 all-gather.7.cloned.1.call-update
  39.9 0.0 all-gather.9.cloned.1.call-start
  40.0 2.3 %collective-permute-start.4 = (bf16[672,512]{1,0:T(8,128)(2,1)}, bf16[672,512]{1,0:T(8,128)(2,1)S(1)}, u32[]{:S(2)}, u32[]{:S(2)}) collective-permute-start(bf16[672,512]{1,0:T(8,128)(2,1)} %join.1), channel_id=1, source_target_pairs={{0,256},{64,320},{128,384},{192,448},{256,0},{320,64},{384,128},{4... | collective-permute-start | bytes 2064392 | tf_op jit(solution)/shard_map/ppermute | solution.py:380
  42.3 19.6 %all_to_all.15.got = bf16[8,64,128]{2,1,0:T(8,128)(2,1)S(1)} all-to-all(bf16[8,64,128]{2,1,0:T(8,128)(2,1)} %copy-done.4), channel_id=1, replica_groups={{0,1,2,3,4,5,6,7},{8,9,10,11,12,13,14,15},{16,17,18,19,20,21,22,23},{24..., dimensions={0} | all-to-all | bytes 262144 | tf_op jit(solution)/shard_map/all_to_all | solution.py:388
  61.8 1.4 attend.1
  63.3 0.8 copy-done.17
  64.1 0.0 all-gather.9.cloned.1.call-update
  64.2 3.2 %collective-permute-start.2 = (bf16[8,64,512]{2,1,0:T(8,128)(2,1)S(1)}, bf16[8,64,512]{2,1,0:T(8,128)(2,1)S(1)}, u32[]{:S(2)}, u32[]{:S(2)}) collective-permute-start(bf16[8,64,512]{2,1,0:T(8,128)(2,1)S(1)} %slice.4.mine), channel_id=1, source_target_pairs={{0,3},{1,2},{2,1},{3,0},{4,7},{5,6},{6,5},{7,4},{8,11},{9,10},{10,... | collective-permute-start | bytes 1572872 | tf_op jit(solution)/shard_map/ppermute | solution.py:376
  67.4 4.4 %collective-permute-start.1 = (bf16[8,64,512]{2,1,0:T(8,128)(2,1)S(1)}, bf16[8,64,512]{2,1,0:T(8,128)(2,1)S(1)}, u32[]{:S(2)}, u32[]{:S(2)}) collective-permute-start(bf16[8,64,512]{2,1,0:T(8,128)(2,1)S(1)} %slice.4.mine), channel_id=1, source_target_pairs={{0,2},{1,3},{2,0},{3,1},{4,6},{5,7},{6,4},{7,5},{8,10},{9,11},{10,... | collective-permute-start | bytes 1572872 | tf_op jit(solution)/shard_map/ppermute | solution.py:376
  71.7 1.9 collective-permute-start
  73.7 32.8 %all-gather = bf16[1024,256]{1,0:T(8,128)(2,1)S(1)} all-gather(bf16[64,256]{1,0:T(8,128)(2,1)S(1)} %attend.1), channel_id=2, replica_groups={{0,4,8,12,16,20,24,28,32,36,40,44,48,52,56,60},{1,5,9,13,17,21,25,29,33..., dimensions={0}, use_global_device_ids=true | all-gather | bytes 557056 | tf_op jit(solution)/shard_map/all_gather | solution.py:392
  106.5 1.3 output.1
  107.8 24.8 %all-gather.1 = bf16[1024,256]{1,0:T(8,128)(2,1)S(1)} all-gather(bf16[64,256]{1,0:T(8,128)(2,1)S(1)} %output.1), channel_id=3, replica_groups={{0,4,8,12,16,20,24,28,32,36,40,44,48,52,56,60},{1,5,9,13,17,21,25,29,33..., dimensions={0}, use_global_device_ids=true | all-gather | bytes 557056 | tf_op jit(solution)/shard_map/all_gather | solution.py:392
  132.6 11.9 %collective-permute-start.6 = (bf16[4,672,512]{2,1,0:T(8,128)(2,1)}, bf16[4,672,512]{2,1,0:T(8,128)(2,1)S(1)}, u32[]{:S(2)}, u32[]{:S(2)}) collective-permute-start(bf16[4,672,512]{2,1,0:T(8,128)(2,1)} %bitcast.26), channel_id=1, source_target_pairs={{0,1},{1,0},{2,3},{3,2},{4,5},{5,4},{6,7},{7,6},{8,9},{9,8},{10,11... | collective-permute-start | bytes 8257544 | tf_op jit(solution)/shard_map/ppermute | solution.py:376
  144.6 1.9 collective-permute-start.7
  146.5 2.6 %collective-permute-start.5 = (bf16[16,64,256]{2,1,0:T(8,128)(2,1)S(1)}, bf16[16,64,256]{2,1,0:T(8,128)(2,1)S(1)}, u32[]{:S(2)}, u32[]{:S(2)}) collective-permute-start(bf16[16,64,256]{2,1,0:T(8,128)(2,1)S(1)} %bitcast.34), channel_id=1, source_target_pairs={{0,2},{1,3},{2,0},{3,1},{4,6},{5,7},{6,4},{7,5},{8,10},{9,11},{10,... | collective-permute-start | bytes 1572872 | tf_op jit(solution)/shard_map/ppermute | solution.py:376
  149.1 1.8 copy-done
  150.9 1.8 copy-done.2
  152.7 0.3 near_half.1.near
  153.0 9.9 %collective-permute-done.5.far = bf16[16,64,256]{2,1,0:T(8,128)(2,1)S(1)} collective-permute-done((bf16[16,64,256]{2,1,0:T(8,128)(2,1)S(1)}, bf16[16,64,256]{2,1,0:T(8,128)(2,1)S(1)}, u32[]{:S(2)}, u32[]{:S(2)}) %collective-permute-start.5) | collective-permute-done | bytes 524320 | tf_op jit(solution)/shard_map/ppermute | solution.py:376
  162.9 3.3 %hidden.1 = (bf16[2,128,224]{2,1,0:T(8,128)(2,1)S(1)}, bf16[128,128]{1,0:T(8,128)(2,1)S(1)}) custom-call(s32[7]{0:T(128)S(1)} %copy-done.14, bf16[8,64,512]{2,1,0:T(8,128)(2,1)S(1)} %near_half.1.near, bf16[16,64,256]{2,1,0:T(8,128)(2,1)S(1)} %bitcast.36, bf16[16,64,256]{2,1,0:T(8,128)(2,1)S(1)} %collective-permute-done.5.far, f32[1,4096]{1,0:T(1,128)S(1)} %bitcast.41, ...), custom_call_target="tpu_custom_call" | custom-call | flops 939524096 | bytes 8388608 | tf_op jit(solution)/shard_map/hidden/pallas_call | solution.py:340
  166.2 2.6 %collective-permute-start.8 = (bf16[2,128,224]{2,1,0:T(8,128)(2,1)S(1)}, bf16[2,128,224]{2,1,0:T(8,128)(2,1)S(1)}, u32[]{:S(2)}, u32[]{:S(2)}) collective-permute-start(bf16[2,128,224]{2,1,0:T(8,128)(2,1)S(1)} %get-tuple-element.31.units), channel_id=1, source_target_pairs={{0,2},{1,3},{2,0},{3,1},{4,6},{5,7},{6,4},{7,5},{8,10},{9,11},{10,... | collective-permute-start | bytes 344072 | tf_op jit(solution)/shard_map/ppermute | solution.py:376
  168.8 4.6 %collective-permute-done.8.far_units = bf16[2,128,224]{2,1,0:T(8,128)(2,1)S(1)} collective-permute-done((bf16[2,128,224]{2,1,0:T(8,128)(2,1)S(1)}, bf16[2,128,224]{2,1,0:T(8,128)(2,1)S(1)}, u32[]{:S(2)}, u32[]{:S(2)}) %collective-permute-start.8) | collective-permute-done | bytes 114720 | tf_op jit(solution)/shard_map/ppermute | solution.py:376
  173.4 1.3 down.1
  174.7 29.4 %all_to_all.16.got = bf16[16,128,128]{2,1,0:T(8,128)(2,1)S(1)} all-to-all(bf16[16,128,128]{2,1,0:T(8,128)(2,1)S(1)} %down.1), channel_id=1, replica_groups={{0,4,8,12,16,20,24,28,32,36,40,44,48,52,56,60},{1,5,9,13,17,21,25,29,33..., dimensions={0} | all-to-all | bytes 1048576 | tf_op jit(solution)/shard_map/all_to_all | solution.py:388
  204.1 0.7 finish.1
  204.7 9.2 %collective-permute-start.9 = (bf16[64,128]{1,0:T(8,128)(2,1)S(1)}, bf16[64,128]{1,0:T(8,128)(2,1)S(1)}, u32[]{:S(2)}, u32[]{:S(2)}) collective-permute-start(bf16[64,128]{1,0:T(8,128)(2,1)S(1)} %get-tuple-element.34), channel_id=1, source_target_pairs={{0,1},{1,0},{2,3},{3,2},{4,5},{5,4},{6,7},{7,6},{8,9},{9,8},{10,11... | collective-permute-start | bytes 49160 | tf_op jit(solution)/shard_map/ppermute | solution.py:376
  213.9 0.8 collective-permute-done.9
  214.7 0.6 fusion
  (39 shorter events, 0.1 us)
Async XLA Ops:
  7.2 16.3 %copy-start.18 = (s32[2]{0:T(128)S(1)}, s32[2]{0:T(128)}, u32[]{:S(2)}) copy-start(s32[2]{0:T(128)} %param.14) | copy-start | bytes 28
  7.2 17.6 %copy-start.15 = (f32[4096]{0:T(1024)S(1)}, f32[4096]{0:T(1024)}, u32[]{:S(2)}) copy-start(f32[4096]{0:T(1024)} %param.15) | copy-start | bytes 49156
  9.9 23.5 %all-to-all-start = ((bf16[8,160,512]{2,1,0:T(8,128)(2,1)}), bf16[8,160,512]{2,1,0:T(8,128)(2,1)S(1)}, u32[]{:S(2)}, u32[]{:S(2)}) async-start(bf16[8,160,512]{2,1,0:T(8,128)(2,1)} %get-tuple-element.22), calls=%async_computation | async-start | bytes 2621440 | tf_op jit(solution)/shard_map/all_to_all | solution.py:419
  15.8 116.8 %all-gather.7.cloned.1.call-start = ((), (), s32[]{:S(2)}) async-start(), calls=%async_computation.3 | async-start | bytes 3440640 | tf_op jit(solution)/shard_map/all_gather | solution.py:384
  18.9 18.0 %collective-permute-start.3 = (bf16[224,256]{1,0:T(8,128)(2,1)}, bf16[224,256]{1,0:T(8,128)(2,1)}, u32[]{:S(2)}, u32[]{:S(2)}) collective-permute-start(bf16[224,256]{1,0:T(8,128)(2,1)} %get-tuple-element.20.after), channel_id=1, source_target_pairs={{0,2},{1,3},{2,0},{3,1},{4,6},{5,7},{6,4},{7,5},{8,10},{9,11},{10,... | collective-permute-start | bytes 344072 | tf_op jit(solution)/shard_map/ppermute | solution.py:376
  24.8 0.9 copy-start.9
  25.7 0.7 copy-start.13
  29.7 0.6 copy-start.11
  33.4 0.9 copy-start.5
  34.3 2.6 %copy-start.6 = (bf16[512,224]{0,1:T(8,128)(2,1)S(1)}, bf16[512,224]{0,1:T(8,128)(2,1)}, u32[]{:S(2)}) copy-start(bf16[512,224]{0,1:T(8,128)(2,1)} %param.21) | copy-start | bytes 688132
  34.3 2.6 %copy-start.7 = (bf16[512,224]{0,1:T(8,128)(2,1)S(1)}, bf16[512,224]{0,1:T(8,128)(2,1)}, u32[]{:S(2)}) copy-start(bf16[512,224]{0,1:T(8,128)(2,1)} %param.22) | copy-start | bytes 688132
  34.3 2.6 %copy-start.8 = (bf16[224,256]{1,0:T(8,128)(2,1)S(1)}, bf16[224,256]{1,0:T(8,128)(2,1)}, u32[]{:S(2)}) copy-start(bf16[224,256]{1,0:T(8,128)(2,1)} %get-tuple-element.27.keep) | copy-start | bytes 344068
  34.3 27.5 %copy-start.14 = (s32[7]{0:T(128)S(1)}, s32[7]{0:T(128)}, u32[]{:S(2)}) copy-start(s32[7]{0:T(128)} %stack.31.at) | copy-start | bytes 88
  34.3 27.5 %copy-start.16 = (s32[2]{0:T(128)S(1)}, s32[2]{0:T(128)}, u32[]{:S(2)}) copy-start(s32[2]{0:T(128)} %lengths.1) | copy-start | bytes 28
  35.8 70.7 %copy-start.12 = (bf16[64,256]{1,0:T(8,128)(2,1)S(1)}, bf16[64,256]{1,0:T(8,128)(2,1)}, u32[]{:S(2)}) copy-start(bf16[64,256]{1,0:T(8,128)(2,1)} %copy-done.11) | copy-start | bytes 98308
  39.3 0.7 copy-start.4
  39.9 92.7 %all-gather.9.cloned.1.call-start = ((), (), s32[]{:S(2)}) async-start(), calls=%async_computation.4 | async-start | bytes 3440640 | tf_op jit(solution)/shard_map/all_gather | solution.py:384
  40.0 23.3 %collective-permute-start.4 = (bf16[672,512]{1,0:T(8,128)(2,1)}, bf16[672,512]{1,0:T(8,128)(2,1)S(1)}, u32[]{:S(2)}, u32[]{:S(2)}) collective-permute-start(bf16[672,512]{1,0:T(8,128)(2,1)} %join.1), channel_id=1, source_target_pairs={{0,256},{64,320},{128,384},{192,448},{256,0},{320,64},{384,128},{4... | collective-permute-start | bytes 2064392 | tf_op jit(solution)/shard_map/ppermute | solution.py:380
  63.3 0.9 copy-start.17
  63.3 85.8 %copy-start.10 = (f32[4096]{0:T(1024)S(1)}, f32[4096]{0:T(1024)}, u32[]{:S(2)}) copy-start(f32[4096]{0:T(1024)} %param.20) | copy-start | bytes 49156
  64.2 42.3 %collective-permute-start.2 = (bf16[8,64,512]{2,1,0:T(8,128)(2,1)S(1)}, bf16[8,64,512]{2,1,0:T(8,128)(2,1)S(1)}, u32[]{:S(2)}, u32[]{:S(2)}) collective-permute-start(bf16[8,64,512]{2,1,0:T(8,128)(2,1)S(1)} %slice.4.mine), channel_id=1, source_target_pairs={{0,3},{1,2},{2,1},{3,0},{4,7},{5,6},{6,5},{7,4},{8,11},{9,10},{10,... | collective-permute-start | bytes 1572872 | tf_op jit(solution)/shard_map/ppermute | solution.py:376
  67.4 39.1 %collective-permute-start.1 = (bf16[8,64,512]{2,1,0:T(8,128)(2,1)S(1)}, bf16[8,64,512]{2,1,0:T(8,128)(2,1)S(1)}, u32[]{:S(2)}, u32[]{:S(2)}) collective-permute-start(bf16[8,64,512]{2,1,0:T(8,128)(2,1)S(1)} %slice.4.mine), channel_id=1, source_target_pairs={{0,2},{1,3},{2,0},{3,1},{4,6},{5,7},{6,4},{7,5},{8,10},{9,11},{10,... | collective-permute-start | bytes 1572872 | tf_op jit(solution)/shard_map/ppermute | solution.py:376
  71.7 34.7 %collective-permute-start = (bf16[8,64,512]{2,1,0:T(8,128)(2,1)S(1)}, bf16[8,64,512]{2,1,0:T(8,128)(2,1)S(1)}, u32[]{:S(2)}, u32[]{:S(2)}) collective-permute-start(bf16[8,64,512]{2,1,0:T(8,128)(2,1)S(1)} %slice.4.mine), channel_id=1, source_target_pairs={{0,1},{1,0},{2,3},{3,2},{4,5},{5,4},{6,7},{7,6},{8,9},{9,8},{10,11... | collective-permute-start | bytes 1572872 | tf_op jit(solution)/shard_map/ppermute | solution.py:376
  132.6 30.3 %collective-permute-start.6 = (bf16[4,672,512]{2,1,0:T(8,128)(2,1)}, bf16[4,672,512]{2,1,0:T(8,128)(2,1)S(1)}, u32[]{:S(2)}, u32[]{:S(2)}) collective-permute-start(bf16[4,672,512]{2,1,0:T(8,128)(2,1)} %bitcast.26), channel_id=1, source_target_pairs={{0,1},{1,0},{2,3},{3,2},{4,5},{5,4},{6,7},{7,6},{8,9},{9,8},{10,11... | collective-permute-start | bytes 8257544 | tf_op jit(solution)/shard_map/ppermute | solution.py:376
  144.6 18.3 %collective-permute-start.7 = (bf16[4,672,512]{2,1,0:T(8,128)(2,1)}, bf16[4,672,512]{2,1,0:T(8,128)(2,1)S(1)}, u32[]{:S(2)}, u32[]{:S(2)}) collective-permute-start(bf16[4,672,512]{2,1,0:T(8,128)(2,1)} %bitcast.30), channel_id=1, source_target_pairs={{0,1},{1,0},{2,3},{3,2},{4,5},{5,4},{6,7},{7,6},{8,9},{9,8},{10,11... | collective-permute-start | bytes 8257544 | tf_op jit(solution)/shard_map/ppermute | solution.py:376
  146.5 16.4 %collective-permute-start.5 = (bf16[16,64,256]{2,1,0:T(8,128)(2,1)S(1)}, bf16[16,64,256]{2,1,0:T(8,128)(2,1)S(1)}, u32[]{:S(2)}, u32[]{:S(2)}) collective-permute-start(bf16[16,64,256]{2,1,0:T(8,128)(2,1)S(1)} %bitcast.34), channel_id=1, source_target_pairs={{0,2},{1,3},{2,0},{3,1},{4,6},{5,7},{6,4},{7,5},{8,10},{9,11},{10,... | collective-permute-start | bytes 1572872 | tf_op jit(solution)/shard_map/ppermute | solution.py:376
  149.1 1.8 copy-start
  150.9 1.8 copy-start.2
  152.7 10.2 %copy-start.1 = (bf16[2688,512]{1,0:T(8,128)(2,1)S(1)}, bf16[2688,512]{1,0:T(8,128)(2,1)}, u32[]{:S(2)}) copy-start(bf16[2688,512]{1,0:T(8,128)(2,1)} %all-gather.7.cloned.1.call-done) | copy-start | bytes 8257540
  153.0 20.4 %copy-start.3 = (bf16[2688,512]{1,0:T(8,128)(2,1)S(1)}, bf16[2688,512]{1,0:T(8,128)(2,1)}, u32[]{:S(2)}) copy-start(bf16[2688,512]{1,0:T(8,128)(2,1)} %all-gather.9.cloned.1.call-done) | copy-start | bytes 8257540
  166.2 7.2 %collective-permute-start.8 = (bf16[2,128,224]{2,1,0:T(8,128)(2,1)S(1)}, bf16[2,128,224]{2,1,0:T(8,128)(2,1)S(1)}, u32[]{:S(2)}, u32[]{:S(2)}) collective-permute-start(bf16[2,128,224]{2,1,0:T(8,128)(2,1)S(1)} %get-tuple-element.31.units), channel_id=1, source_target_pairs={{0,2},{1,3},{2,0},{3,1},{4,6},{5,7},{6,4},{7,5},{8,10},{9,11},{10,... | collective-permute-start | bytes 344072 | tf_op jit(solution)/shard_map/ppermute | solution.py:376
  204.7 10.0 %collective-permute-start.9 = (bf16[64,128]{1,0:T(8,128)(2,1)S(1)}, bf16[64,128]{1,0:T(8,128)(2,1)S(1)}, u32[]{:S(2)}, u32[]{:S(2)}) collective-permute-start(bf16[64,128]{1,0:T(8,128)(2,1)S(1)} %get-tuple-element.34), channel_id=1, source_target_pairs={{0,1},{1,0},{2,3},{3,2},{4,5},{5,4},{6,7},{7,6},{8,9},{9,8},{10,11... | collective-permute-start | bytes 49160 | tf_op jit(solution)/shard_map/ppermute | solution.py:376
Sparse Core Ops, SparseCore 0:
  40.1 46.0 all-gather.6
  88.3 44.2 all-gather.8

commit v6 on v5

--- a/solution.py
+++ b/solution.py
@@ -129,7 +129,7 @@
         out[z // 2, :, (z % 2) * BAND : (z % 2 + 1) * BAND] = x.astype(BF)
 
 
-def near_kernel(got, gain, mine, mine_lo, out):
+def near_kernel(got, gain, out):
     renorm(got, gain, out)
 
 
@@ -196,31 +196,6 @@
         copy.wait()
 
 
-def divide_kernel(at, after, narrow, keep, give, held, sem):
-    copy = pltpu.make_async_copy(narrow, held, sem.at[0])
-    copy.start()
-    copy.wait()
-    low = at[1] == 0
-    for i in range(2):
-        even = held[:, 2 * i * 128 : (2 * i + 1) * 128]
-        odd = held[:, (2 * i + 1) * 128 : (2 * i + 2) * 128]
-        keep[:, i * 128 : (i + 1) * 128] = jnp.where(low, even, odd)
-        give[:, i * 128 : (i + 1) * 128] = jnp.where(low, odd, even)
-
-
-def divide(at, after, narrow):
-    half = jax.ShapeDtypeStruct((FC, BAND), BF)
-    return pl.pallas_call(
-        divide_kernel,
-        out_shape=(half, half),
-        in_specs=[SMEM, ANY, HBM],
-        out_specs=(VMEM,) * 2,
-        scratch_shapes=[pltpu.VMEM((FC, RUN), BF), pltpu.SemaphoreType.DMA((1,))],
-        compiler_params=params(57),
-        name="divide",
-    )(at, after, narrow)
-
-
 def norm_kernel(at, after, tables, stream, gain, normed, own, held, gains, sems):
     copies = [
         pltpu.make_async_copy(stream, held, sems.at[0]),
@@ -251,29 +226,36 @@
     )(at, after, tables, stream, gain)
 
 
-def join_kernel(after, gate, up, keep, got, out, sems):
+def join_kernel(at, after, gate, up, narrow, got, out, held, sems):
     copies = [
-        pltpu.make_async_copy(gate, out.at[pl.ds(0, FC), :], sems.at[0]),
-        pltpu.make_async_copy(up, out.at[pl.ds(FC, FC), :], sems.at[1]),
+        pltpu.make_async_copy(narrow, held, sems.at[0]),
+        pltpu.make_async_copy(gate, out.at[pl.ds(0, FC), :], sems.at[1]),
+        pltpu.make_async_copy(up, out.at[pl.ds(FC, FC), :], sems.at[2]),
     ]
     for copy in copies:
         copy.start()
-    out[2 * FC : 3 * FC, 0:BAND] = keep[...]
-    out[2 * FC : 3 * FC, BAND:RUN] = got[...]
-    for copy in copies:
-        copy.wait()
-
-
-def join(after, gate, up, keep, got):
+    low = at[1] == 0
+    for k, source in ((1, got), (0, held)):
+        if k == 0:
+            copies[0].wait()
+        for i in range(2):
+            even = source[:, 2 * i * 128 : (2 * i + 1) * 128]
+            odd = source[:, (2 * i + 1) * 128 : (2 * i + 2) * 128]
+            out[2 * FC : 3 * FC, k * BAND + i * 128 : k * BAND + (i + 1) * 128] = jnp.where(low, even, odd)
+    copies[1].wait()
+    copies[2].wait()
+
+
+def join(at, after, gate, up, narrow, got):
     return pl.pallas_call(
         join_kernel,
         out_shape=jax.ShapeDtypeStruct((3 * FC, RUN), BF),
-        in_specs=[ANY, HBM, HBM, VMEM, VMEM],
+        in_specs=[SMEM, ANY, HBM, HBM, HBM, VMEM],
         out_specs=VMEM,
-        scratch_shapes=[pltpu.SemaphoreType.DMA((2,))],
-        compiler_params=params(16),
+        scratch_shapes=[pltpu.VMEM((FC, RUN), BF), pltpu.SemaphoreType.DMA((3,))],
+        compiler_params=params(48),
         name="join",
-    )(after, gate, up, keep, got)
+    )(at, after, gate, up, narrow, got)
 
 
 def pack(*parts):
@@ -325,15 +307,15 @@
     )(at, got, *weights, own)
 
 
-def near_half(got, gain, mine, mine_lo):
+def near_half(got, gain):
     return pl.pallas_call(
         near_kernel,
         out_shape=jax.ShapeDtypeStruct((GROUPS, HALF, RUN), BF),
-        in_specs=[VMEM] * 4,
+        in_specs=[VMEM] * 2,
         out_specs=VMEM,
         compiler_params=params(16),
         name="near_half",
-    )(got, gain, mine, mine_lo)
+    )(got, gain)
 
 
 def hidden_units(at, near, full, far, gain, weights):
@@ -426,25 +408,27 @@
     angle = positions.astype(F32)[:, None] * freq[None, :]
     cos, sin = jnp.cos(angle), jnp.sin(angle)
 
-    keep, give = divide(at, token, w_down.T)
-    other = swap(give, 2)
-    normed, own = norm(at, give, cos, stream, attn_gain.reshape(1, D))
+    normed, own = norm(at, token, cos, stream, attn_gain.reshape(1, D))
+    narrow = after(w_down.T, token)
+    other = swap(narrow, 2)
+
     send, keys, values = project(normed, first, cos, sin)
     got = trade(send, OCTETS)
-    mine = join(send, w_gate.T, w_up.T, keep, other)
-    own_mixed = attend(at, row_length, got)
-    mine_lo = after(swap_groups(mine), own_mixed)
-    mine, mine_lo = collect_x(mine), collect_x(mine_lo)
+    mine = join(at, send, w_gate.T, w_up.T, narrow, other)
+    mine_lo = swap_groups(after(mine, got))
     out_own = first[:, 96:160, :]
     out_weights = (out_own, swap(out_own, 1), swap(out_own, 2), swap(out_own, 3))
-    mixed = collect(own_mixed)
+    mixed = collect(attend(at, row_length, got))
     attended = output(at, mixed, out_weights, own)
+    mine, mine_lo = collect_x(mine), collect_x(after(mine_lo, attended))
+    mine = after(mine, attended)
+    core_mine = swap(mine, 1)
     full = collect(attended)
     far = swap(full, 2)
-    mine, mine_lo = after((mine, mine_lo), full)
-    weights = (mine, mine_lo, swap(mine, 1), swap(mine_lo, 1))
+    mine_lo = after(mine_lo, far)
+    weights = (mine, mine_lo, core_mine, swap(mine_lo, 1))
     gain = ffn_gain.reshape(1, D)
-    near = near_half(full, gain, mine, mine_lo)
+    near = near_half(full, gain)
     units, kept = hidden_units(at, near, full, far, gain, weights)
     sums = trade(down(at, units, swap(units, 2), weights), COLUMNS)
     keep, give = finish(at, sums, kept)

time: 223 us -> 222 us (level)
  blocking collectives: 107 us -> 101 us
  starting transfers between devices: 50.4 us -> 55.2 us
  waiting for transfers between devices: 19.5 us -> 21.8 us
    all_to_all x2, blocking collectives: 48.9 us -> 42.9 us  [trade(): return lax.all_to_all(x, 'dev', 0, 0, axis_index_groups=groups, tiled=True)]
    ppermute x9, starting transfers between devices: 42.2 us -> 47 us  [swap(): return lax.ppermute(x, 'dev', [(d, d ^ bits) for d in range(MEMBERS)])]
    ppermute x9, waiting for transfers between devices: 16.4 us -> 12.1 us  [swap(): return lax.ppermute(x, 'dev', [(d, d ^ bits) for d in range(MEMBERS)])]
    all_to_all x1, waiting for transfers between devices: 3.07 us -> 6.84 us  [on_device(): first = lax.all_to_all(packed, 'grp', 0, 0, tiled=True)]
    all_gather x2, waiting for transfers between devices: 0.01 us -> 2.79 us  [collect_x(): lax.all_gather(x, 'grp', axis=0, axis_index_groups=[[0, 1, 2, 3], [4, 5,...]
    pallas_call x1 -> x0, Pallas kernels: 2.34 us -> none  [divide(): pl.pallas_call(divide_kernel, out_shape=(half, half), in_specs=[SMEM, ANY...]
    unnamed x38 -> x32, local copies, waits for them, and re-layouts: 8.15 us -> 6.67 us
  transfers between devices with their start and end apart: 13 -> 13, of which waited for: 5 -> 6; matrix products, arithmetic and copies ran while one was open for 1% -> 1% of each run, Pallas kernels for 5% -> 4%
where the time goes in v6:
time: 222 us; the launch traced here: 221 us
  blocking collectives  101 us (45%)
  starting transfers between devices  55.2 us (25%)
  waiting for transfers between devices  21.8 us (10%)
  Pallas kernels  19.3 us (9%)
  between operations  14.4 us (6%)
  local copies, waits for them, and re-layouts  6.79 us (3%)
    all_gather x2, blocking collectives, collect(): return lax.all_gather(x, 'dev', axis=0, axis_index_groups=COLUMNS)  58.4 us
    ppermute x9, starting transfers between devices, swap(): return lax.ppermute(x, 'dev', [(d, d ^ bits) for d in range(MEMBERS)])  47 us
    all_to_all x2, blocking collectives, trade(): return lax.all_to_all(x, 'dev', 0, 0, axis_index_groups=groups, tiled=True)  42.9 us
    ppermute x9, waiting for transfers between devices, swap(): return lax.ppermute(x, 'dev', [(d, d ^ bits) for d in range(MEMBERS)])  12.1 us
    all_to_all x1, waiting for transfers between devices, on_device(): first = lax.all_to_all(packed, 'grp', 0, 0, tiled=True)  6.84 us
    unnamed x32, local copies, waits for them, and re-layouts  6.67 us
    all_to_all x1, starting transfers between devices, on_device(): first = lax.all_to_all(packed, 'grp', 0, 0, tiled=True)  5.87 us
  transfers between devices with their start and end apart: 13, of which 6 were waited for; matrix products, arithmetic and copies ran while one was open for 1% of the time, Pallas kernels for 4%

profile of v6, /device:TPU:1, one launch (start us, length us, event | category | flops | bytes accessed | tf_op | source)
XLA Modules:
  0.0 220.7 jit_solution(13088080217219556264)
XLA Ops:
  7.2 2.7 %pack.1 = (bf16[8,160,512]{2,1,0:T(8,128)(2,1)}, f32[8,128]{1,0:T(8,128)}) custom-call(bf16[64,512]{1,0:T(8,128)(2,1)} %bitcast.41, bf16[16,512]{1,0:T(8,128)(2,1)} %bitcast.43, bf16[16,512]{1,0:T(8,128)(2,1)} %bitcast.44, bf16[64,512]{1,0:T(8,128)(2,1)} %bitcast.42), custom_call_target="tpu_custom_call" | custom-call | tf_op jit(solution)/shard_map/pack/pallas_call | solution.py:262
  9.9 0.0 copy-start.12
  9.9 5.9 %all-to-all-start = ((bf16[8,160,512]{2,1,0:T(8,128)(2,1)}), bf16[8,160,512]{2,1,0:T(8,128)(2,1)S(1)}, u32[]{:S(2)}, u32[]{:S(2)}) async-start(bf16[8,160,512]{2,1,0:T(8,128)(2,1)} %get-tuple-element.21), calls=%async_computation | async-start | bytes 2621440 | tf_op jit(solution)/shard_map/all_to_all | solution.py:401
  15.8 0.0 all-gather.7.cloned.1.call-start
  15.8 4.5 %collective-permute-start.4 = (bf16[224,512]{1,0:T(8,128)(2,1)}, bf16[224,512]{1,0:T(8,128)(2,1)}, u32[]{:S(2)}, u32[]{:S(2)}) collective-permute-start(bf16[224,512]{1,0:T(8,128)(2,1)} %bitcast.20.narrow), channel_id=1, source_target_pairs={{0,2},{1,3},{2,0},{3,1},{4,6},{5,7},{6,4},{7,5},{8,10},{9,11},{10,... | collective-permute-start | bytes 688136 | tf_op jit(solution)/shard_map/ppermute | solution.py:358
  20.4 0.1 stack.31.at
  20.6 0.1 convert_bitcast_fusion
  20.6 1.2 multiply_sine_fusion
  21.8 0.7 copy-done.11
  22.5 3.4 %norm.1 = (bf16[8,256,512]{2,1,0:T(8,128)(2,1)S(1)}, bf16[64,256]{1,0:T(8,128)(2,1)S(1)}) custom-call(s32[7]{0:T(128)S(1)} %stack.31.at, f32[8,128]{1,0:T(8,128)S(1)} %copy-done.12, f32[256,128]{1,0:T(8,128)S(1)} %get-tuple-element.36.tables.cos, bf16[256,4096]{1,0:T(8,128)(2,1)} %stream.1, f32[1,4096]{1,0:T(1,128)S(1)} %bitcast.40), custom_call_target="tpu_custom_call" | custom-call | tf_op jit(solution)/shard_map/norm/pallas_call | solution.py:218
  25.9 0.0 copy-start.9
  25.9 0.6 copy-done.9
  26.5 6.8 %all-to-all-done.weights = bf16[8,160,512]{2,1,0:T(8,128)(2,1)S(1)} async-done(((bf16[8,160,512]{2,1,0:T(8,128)(2,1)}), bf16[8,160,512]{2,1,0:T(8,128)(2,1)S(1)}, u32[]{:S(2)}, u32[]{:S(2)}) %all-to-all-start) | async-done | bytes 1310752 | tf_op jit(solution)/shard_map/all_to_all | solution.py:401
  33.4 0.9 copy-done.5
  34.3 1.4 project.1
  35.7 2.0 collective-permute-done.4.got
  37.8 2.8 %join.1 = bf16[672,512]{1,0:T(8,128)(2,1)} custom-call(s32[7]{0:T(128)S(1)} %stack.31.at, bf16[8,64,128]{2,1,0:T(8,128)(2,1)S(1)} %get-tuple-element.24.after, bf16[224,512]{1,0:T(8,128)(2,1)S(1)} %bitcast.36, bf16[224,512]{1,0:T(8,128)(2,1)S(1)} %bitcast.37, bf16[224,512]{1,0:T(8,128)(2,1)} %bitcast.20.narrow, bf16[224,512]{1,0:T(8,128)(2,1)} %collective-permute-done.4.got), custom_call_target="tpu_custom_call" | custom-call | tf_op jit(solution)/shard_map/join/pallas_call | solution.py:250
  40.6 0.0 all-gather.7.cloned.1.call-update
  40.6 0.0 all-gather.9.cloned.1.call-start
  40.6 11.9 %all_to_all.15.got = bf16[8,64,128]{2,1,0:T(8,128)(2,1)S(1)} all-to-all(bf16[8,64,128]{2,1,0:T(8,128)(2,1)} %copy-done.4), channel_id=1, replica_groups={{0,1,2,3,4,5,6,7},{8,9,10,11,12,13,14,15},{16,17,18,19,20,21,22,23},{24..., dimensions={0} | all-to-all | bytes 262144 | tf_op jit(solution)/shard_map/all_to_all | solution.py:370
  52.5 2.2 collective-permute-start.5
  54.8 4.2 %collective-permute-start.2 = (bf16[8,64,512]{2,1,0:T(8,128)(2,1)S(1)}, bf16[8,64,512]{2,1,0:T(8,128)(2,1)S(1)}, u32[]{:S(2)}, u32[]{:S(2)}) collective-permute-start(bf16[8,64,512]{2,1,0:T(8,128)(2,1)S(1)} %slice.4.mine), channel_id=1, source_target_pairs={{0,3},{1,2},{2,1},{3,0},{4,7},{5,6},{6,5},{7,4},{8,11},{9,10},{10,... | collective-permute-start | bytes 1572872 | tf_op jit(solution)/shard_map/ppermute | solution.py:358
  59.0 3.6 %collective-permute-start.1 = (bf16[8,64,512]{2,1,0:T(8,128)(2,1)S(1)}, bf16[8,64,512]{2,1,0:T(8,128)(2,1)S(1)}, u32[]{:S(2)}, u32[]{:S(2)}) collective-permute-start(bf16[8,64,512]{2,1,0:T(8,128)(2,1)S(1)} %slice.4.mine), channel_id=1, source_target_pairs={{0,2},{1,3},{2,0},{3,1},{4,6},{5,7},{6,4},{7,5},{8,10},{9,11},{10,... | collective-permute-start | bytes 1572872 | tf_op jit(solution)/shard_map/ppermute | solution.py:358
  62.7 1.9 collective-permute-start
  64.6 1.4 attend.1
  66.0 33.1 %all-gather = bf16[1024,256]{1,0:T(8,128)(2,1)S(1)} all-gather(bf16[64,256]{1,0:T(8,128)(2,1)S(1)} %attend.1), channel_id=2, replica_groups={{0,4,8,12,16,20,24,28,32,36,40,44,48,52,56,60},{1,5,9,13,17,21,25,29,33..., dimensions={0}, use_global_device_ids=true | all-gather | bytes 557056 | tf_op jit(solution)/shard_map/all_gather | solution.py:374
  99.1 1.3 output.1
  100.4 0.8 copy-done.14
  101.3 0.0 all-gather.9.cloned.1.call-update
  101.3 25.4 %all-gather.1 = bf16[1024,256]{1,0:T(8,128)(2,1)S(1)} all-gather(bf16[64,256]{1,0:T(8,128)(2,1)S(1)} %output.1), channel_id=3, replica_groups={{0,4,8,12,16,20,24,28,32,36,40,44,48,52,56,60},{1,5,9,13,17,21,25,29,33..., dimensions={0}, use_global_device_ids=true | all-gather | bytes 557056 | tf_op jit(solution)/shard_map/all_gather | solution.py:374
  126.7 4.0 %collective-permute-start.3 = (bf16[16,64,256]{2,1,0:T(8,128)(2,1)S(1)}, bf16[16,64,256]{2,1,0:T(8,128)(2,1)}, u32[]{:S(2)}, u32[]{:S(2)}) collective-permute-start(bf16[16,64,256]{2,1,0:T(8,128)(2,1)S(1)} %bitcast.32), channel_id=1, source_target_pairs={{0,2},{1,3},{2,0},{3,1},{4,6},{5,7},{6,4},{7,5},{8,10},{9,11},{10,... | collective-permute-start | bytes 1572872 | tf_op jit(solution)/shard_map/ppermute | solution.py:358
  130.7 0.0 all-gather.7.cloned.1.call-done
  130.7 10.3 %collective-permute-start.6 = (bf16[4,672,512]{2,1,0:T(8,128)(2,1)}, bf16[4,672,512]{2,1,0:T(8,128)(2,1)S(1)}, u32[]{:S(2)}, u32[]{:S(2)}) collective-permute-start(bf16[4,672,512]{2,1,0:T(8,128)(2,1)} %bitcast.26), channel_id=1, source_target_pairs={{0,1},{1,0},{2,3},{3,2},{4,5},{5,4},{6,7},{7,6},{8,9},{9,8},{10,11... | collective-permute-start | bytes 8257544 | tf_op jit(solution)/shard_map/ppermute | solution.py:358
  141.0 2.8 %all-gather.9.cloned.1.call-done = bf16[2688,512]{1,0:T(8,128)(2,1)} async-done(((bf16[672,512]{1,0:T(8,128)(2,1)}), bf16[2688,512]{1,0:T(8,128)(2,1)}) %all-gather.9.cloned.1.call-update) | async-done | bytes 2752528 | tf_op jit(solution)/shard_map/all_gather | solution.py:366
  143.8 6.2 %collective-permute-start.7 = (bf16[4,672,512]{2,1,0:T(8,128)(2,1)}, bf16[4,672,512]{2,1,0:T(8,128)(2,1)S(1)}, u32[]{:S(2)}, u32[]{:S(2)}) collective-permute-start(bf16[4,672,512]{2,1,0:T(8,128)(2,1)} %bitcast.29), channel_id=1, source_target_pairs={{0,1},{1,0},{2,3},{3,2},{4,5},{5,4},{6,7},{7,6},{8,9},{9,8},{10,11... | collective-permute-start | bytes 8257544 | tf_op jit(solution)/shard_map/ppermute | solution.py:358
  150.0 0.3 near_half.1.near
  150.4 4.5 %collective-permute-done.7.core_lo = bf16[4,672,512]{2,1,0:T(8,128)(2,1)S(1)} collective-permute-done((bf16[4,672,512]{2,1,0:T(8,128)(2,1)}, bf16[4,672,512]{2,1,0:T(8,128)(2,1)S(1)}, u32[]{:S(2)}, u32[]{:S(2)}) %collective-permute-start.7) | collective-permute-done | bytes 2752544 | tf_op jit(solution)/shard_map/ppermute | solution.py:358
  154.9 1.8 copy-done
  156.7 1.8 copy-done.2
  158.5 4.0 %hidden.1 = (bf16[2,128,224]{2,1,0:T(8,128)(2,1)S(1)}, bf16[128,128]{1,0:T(8,128)(2,1)S(1)}) custom-call(s32[7]{0:T(128)S(1)} %stack.31.at, bf16[8,64,512]{2,1,0:T(8,128)(2,1)S(1)} %near_half.1.near, bf16[16,64,256]{2,1,0:T(8,128)(2,1)S(1)} %bitcast.34, bf16[16,64,256]{2,1,0:T(8,128)(2,1)} %collective-permute-done.3.far, f32[1,4096]{1,0:T(1,128)S(1)} %bitcast.39, ...), custom_call_target="tpu_custom_call" | custom-call | flops 939524096 | bytes 8388608 | tf_op jit(solution)/shard_map/hidden/pallas_call | solution.py:322
  162.5 3.4 %collective-permute-start.8 = (bf16[2,128,224]{2,1,0:T(8,128)(2,1)S(1)}, bf16[2,128,224]{2,1,0:T(8,128)(2,1)S(1)}, u32[]{:S(2)}, u32[]{:S(2)}) collective-permute-start(bf16[2,128,224]{2,1,0:T(8,128)(2,1)S(1)} %get-tuple-element.31.units), channel_id=1, source_target_pairs={{0,2},{1,3},{2,0},{3,1},{4,6},{5,7},{6,4},{7,5},{8,10},{9,11},{10,... | collective-permute-start | bytes 344072 | tf_op jit(solution)/shard_map/ppermute | solution.py:358
  165.8 4.7 %collective-permute-done.8.far_units = bf16[2,128,224]{2,1,0:T(8,128)(2,1)S(1)} collective-permute-done((bf16[2,128,224]{2,1,0:T(8,128)(2,1)S(1)}, bf16[2,128,224]{2,1,0:T(8,128)(2,1)S(1)}, u32[]{:S(2)}, u32[]{:S(2)}) %collective-permute-start.8) | collective-permute-done | bytes 114720 | tf_op jit(solution)/shard_map/ppermute | solution.py:358
  170.6 1.2 down.1
  171.9 31.0 %all_to_all.16.got = bf16[16,128,128]{2,1,0:T(8,128)(2,1)S(1)} all-to-all(bf16[16,128,128]{2,1,0:T(8,128)(2,1)S(1)} %down.1), channel_id=1, replica_groups={{0,4,8,12,16,20,24,28,32,36,40,44,48,52,56,60},{1,5,9,13,17,21,25,29,33..., dimensions={0} | all-to-all | bytes 1048576 | tf_op jit(solution)/shard_map/all_to_all | solution.py:370
  202.8 0.7 finish.1
  203.5 8.9 %collective-permute-start.9 = (bf16[64,128]{1,0:T(8,128)(2,1)S(1)}, bf16[64,128]{1,0:T(8,128)(2,1)S(1)}, u32[]{:S(2)}, u32[]{:S(2)}) collective-permute-start(bf16[64,128]{1,0:T(8,128)(2,1)S(1)} %get-tuple-element.34), channel_id=1, source_target_pairs={{0,1},{1,0},{2,3},{3,2},{4,5},{5,4},{6,7},{7,6},{8,9},{9,8},{10,11... | collective-permute-start | bytes 49160 | tf_op jit(solution)/shard_map/ppermute | solution.py:358
  212.4 0.8 collective-permute-done.9
  213.2 0.6 fusion
  (32 shorter events, 0.1 us)
Async XLA Ops:
  7.2 13.4 %copy-start.15 = (s32[2]{0:T(128)S(1)}, s32[2]{0:T(128)}, u32[]{:S(2)}) copy-start(s32[2]{0:T(128)} %param.14) | copy-start | bytes 28
  9.9 11.9 %copy-start.12 = (f32[8,128]{1,0:T(8,128)S(1)}, f32[8,128]{1,0:T(8,128)}, u32[]{:S(2)}) copy-start(f32[8,128]{1,0:T(8,128)} %get-tuple-element.19.after) | copy-start | bytes 12292
  9.9 23.5 %all-to-all-start = ((bf16[8,160,512]{2,1,0:T(8,128)(2,1)}), bf16[8,160,512]{2,1,0:T(8,128)(2,1)S(1)}, u32[]{:S(2)}, u32[]{:S(2)}) async-start(bf16[8,160,512]{2,1,0:T(8,128)(2,1)} %get-tuple-element.21), calls=%async_computation | async-start | bytes 2621440 | tf_op jit(solution)/shard_map/all_to_all | solution.py:401
  15.8 115.0 %all-gather.7.cloned.1.call-start = ((), (), s32[]{:S(2)}) async-start(), calls=%async_computation.3 | async-start | bytes 3440640 | tf_op jit(solution)/shard_map/all_gather | solution.py:366
  15.8 21.9 %collective-permute-start.4 = (bf16[224,512]{1,0:T(8,128)(2,1)}, bf16[224,512]{1,0:T(8,128)(2,1)}, u32[]{:S(2)}, u32[]{:S(2)}) collective-permute-start(bf16[224,512]{1,0:T(8,128)(2,1)} %bitcast.20.narrow), channel_id=1, source_target_pairs={{0,2},{1,3},{2,0},{3,1},{4,6},{5,7},{6,4},{7,5},{8,10},{9,11},{10,... | collective-permute-start | bytes 688136 | tf_op jit(solution)/shard_map/ppermute | solution.py:358
  21.8 0.7 copy-start.11
  25.9 0.6 copy-start.9
  33.4 0.9 copy-start.5
  34.3 3.5 %copy-start.6 = (bf16[512,224]{0,1:T(8,128)(2,1)S(1)}, bf16[512,224]{0,1:T(8,128)(2,1)}, u32[]{:S(2)}) copy-start(bf16[512,224]{0,1:T(8,128)(2,1)} %param.21) | copy-start | bytes 688132
  34.3 3.5 %copy-start.7 = (bf16[512,224]{0,1:T(8,128)(2,1)S(1)}, bf16[512,224]{0,1:T(8,128)(2,1)}, u32[]{:S(2)}) copy-start(bf16[512,224]{0,1:T(8,128)(2,1)} %param.22) | copy-start | bytes 688132
  35.7 2.0 copy-start.4
  35.7 28.9 %copy-start.13 = (s32[2]{0:T(128)S(1)}, s32[2]{0:T(128)}, u32[]{:S(2)}) copy-start(s32[2]{0:T(128)} %lengths.1) | copy-start | bytes 28
  35.7 63.4 %copy-start.10 = (bf16[64,256]{1,0:T(8,128)(2,1)S(1)}, bf16[64,256]{1,0:T(8,128)(2,1)}, u32[]{:S(2)}) copy-start(bf16[64,256]{1,0:T(8,128)(2,1)} %copy-done.9) | copy-start | bytes 98308
  40.6 103.2 %all-gather.9.cloned.1.call-start = ((), (), s32[]{:S(2)}) async-start(), calls=%async_computation.4 | async-start | bytes 3440640 | tf_op jit(solution)/shard_map/all_gather | solution.py:366
  52.5 97.5 %copy-start.8 = (f32[4096]{0:T(1024)S(1)}, f32[4096]{0:T(1024)}, u32[]{:S(2)}) copy-start(f32[4096]{0:T(1024)} %param.20) | copy-start | bytes 49156
  52.5 47.9 %collective-permute-start.5 = (bf16[672,512]{1,0:T(8,128)(2,1)}, bf16[672,512]{1,0:T(8,128)(2,1)S(1)}, u32[]{:S(2)}, u32[]{:S(2)}) collective-permute-start(bf16[672,512]{1,0:T(8,128)(2,1)} %join.1), channel_id=1, source_target_pairs={{0,256},{64,320},{128,384},{192,448},{256,0},{320,64},{384,128},{4... | collective-permute-start | bytes 2064392 | tf_op jit(solution)/shard_map/ppermute | solution.py:362
  54.8 44.3 %collective-permute-start.2 = (bf16[8,64,512]{2,1,0:T(8,128)(2,1)S(1)}, bf16[8,64,512]{2,1,0:T(8,128)(2,1)S(1)}, u32[]{:S(2)}, u32[]{:S(2)}) collective-permute-start(bf16[8,64,512]{2,1,0:T(8,128)(2,1)S(1)} %slice.4.mine), channel_id=1, source_target_pairs={{0,3},{1,2},{2,1},{3,0},{4,7},{5,6},{6,5},{7,4},{8,11},{9,10},{10,... | collective-permute-start | bytes 1572872 | tf_op jit(solution)/shard_map/ppermute | solution.py:358
  59.0 40.1 %collective-permute-start.1 = (bf16[8,64,512]{2,1,0:T(8,128)(2,1)S(1)}, bf16[8,64,512]{2,1,0:T(8,128)(2,1)S(1)}, u32[]{:S(2)}, u32[]{:S(2)}) collective-permute-start(bf16[8,64,512]{2,1,0:T(8,128)(2,1)S(1)} %slice.4.mine), channel_id=1, source_target_pairs={{0,2},{1,3},{2,0},{3,1},{4,6},{5,7},{6,4},{7,5},{8,10},{9,11},{10,... | collective-permute-start | bytes 1572872 | tf_op jit(solution)/shard_map/ppermute | solution.py:358
  62.7 36.4 %collective-permute-start = (bf16[8,64,512]{2,1,0:T(8,128)(2,1)S(1)}, bf16[8,64,512]{2,1,0:T(8,128)(2,1)S(1)}, u32[]{:S(2)}, u32[]{:S(2)}) collective-permute-start(bf16[8,64,512]{2,1,0:T(8,128)(2,1)S(1)} %slice.4.mine), channel_id=1, source_target_pairs={{0,1},{1,0},{2,3},{3,2},{4,5},{5,4},{6,7},{7,6},{8,9},{9,8},{10,11... | collective-permute-start | bytes 1572872 | tf_op jit(solution)/shard_map/ppermute | solution.py:358
  100.4 0.9 copy-start.14
  126.7 14.3 %collective-permute-start.3 = (bf16[16,64,256]{2,1,0:T(8,128)(2,1)S(1)}, bf16[16,64,256]{2,1,0:T(8,128)(2,1)}, u32[]{:S(2)}, u32[]{:S(2)}) collective-permute-start(bf16[16,64,256]{2,1,0:T(8,128)(2,1)S(1)} %bitcast.32), channel_id=1, source_target_pairs={{0,2},{1,3},{2,0},{3,1},{4,6},{5,7},{6,4},{7,5},{8,10},{9,11},{10,... | collective-permute-start | bytes 1572872 | tf_op jit(solution)/shard_map/ppermute | solution.py:358
  130.7 19.6 %collective-permute-start.6 = (bf16[4,672,512]{2,1,0:T(8,128)(2,1)}, bf16[4,672,512]{2,1,0:T(8,128)(2,1)S(1)}, u32[]{:S(2)}, u32[]{:S(2)}) collective-permute-start(bf16[4,672,512]{2,1,0:T(8,128)(2,1)} %bitcast.26), channel_id=1, source_target_pairs={{0,1},{1,0},{2,3},{3,2},{4,5},{5,4},{6,7},{7,6},{8,9},{9,8},{10,11... | collective-permute-start | bytes 8257544 | tf_op jit(solution)/shard_map/ppermute | solution.py:358
  143.8 11.1 %collective-permute-start.7 = (bf16[4,672,512]{2,1,0:T(8,128)(2,1)}, bf16[4,672,512]{2,1,0:T(8,128)(2,1)S(1)}, u32[]{:S(2)}, u32[]{:S(2)}) collective-permute-start(bf16[4,672,512]{2,1,0:T(8,128)(2,1)} %bitcast.29), channel_id=1, source_target_pairs={{0,1},{1,0},{2,3},{3,2},{4,5},{5,4},{6,7},{7,6},{8,9},{9,8},{10,11... | collective-permute-start | bytes 8257544 | tf_op jit(solution)/shard_map/ppermute | solution.py:358
  154.9 1.8 copy-start
  156.7 1.8 copy-start.2
  158.5 12.1 %copy-start.1 = (bf16[2688,512]{1,0:T(8,128)(2,1)S(1)}, bf16[2688,512]{1,0:T(8,128)(2,1)}, u32[]{:S(2)}) copy-start(bf16[2688,512]{1,0:T(8,128)(2,1)} %all-gather.7.cloned.1.call-done) | copy-start | bytes 8257540
  158.5 12.1 %copy-start.3 = (bf16[2688,512]{1,0:T(8,128)(2,1)S(1)}, bf16[2688,512]{1,0:T(8,128)(2,1)}, u32[]{:S(2)}) copy-start(bf16[2688,512]{1,0:T(8,128)(2,1)} %all-gather.9.cloned.1.call-done) | copy-start | bytes 8257540
  162.5 8.1 %collective-permute-start.8 = (bf16[2,128,224]{2,1,0:T(8,128)(2,1)S(1)}, bf16[2,128,224]{2,1,0:T(8,128)(2,1)S(1)}, u32[]{:S(2)}, u32[]{:S(2)}) collective-permute-start(bf16[2,128,224]{2,1,0:T(8,128)(2,1)S(1)} %get-tuple-element.31.units), channel_id=1, source_target_pairs={{0,2},{1,3},{2,0},{3,1},{4,6},{5,7},{6,4},{7,5},{8,10},{9,11},{10,... | collective-permute-start | bytes 344072 | tf_op jit(solution)/shard_map/ppermute | solution.py:358
  203.5 9.7 %collective-permute-start.9 = (bf16[64,128]{1,0:T(8,128)(2,1)S(1)}, bf16[64,128]{1,0:T(8,128)(2,1)S(1)}, u32[]{:S(2)}, u32[]{:S(2)}) collective-permute-start(bf16[64,128]{1,0:T(8,128)(2,1)S(1)} %get-tuple-element.34), channel_id=1, source_target_pairs={{0,1},{1,0},{2,3},{3,2},{4,5},{5,4},{6,7},{7,6},{8,9},{9,8},{10,11... | collective-permute-start | bytes 49160 | tf_op jit(solution)/shard_map/ppermute | solution.py:358
Sparse Core Ops, SparseCore 0:
  40.7 47.5 all-gather.6
  101.4 42.3 all-gather.8

commit v7 on v6

--- a/solution.py
+++ b/solution.py
@@ -133,7 +133,16 @@
     renorm(got, gain, out)
 
 
-def hidden_kernel(at, near, full, far, gain, mine, mine_lo, core, core_lo, out, kept, normed):
+def multiply(at, near, far, pair, side, totals):
+    for x in range(4):
+        g = jnp.bitwise_xor(at[6], side) * 4 + x
+        rows = jnp.concatenate([near[g], far[g]], axis=0)
+        for i, w in enumerate(pair):
+            totals[2 * i] = totals[2 * i] + nt(rows, w[x, 0:FC, :])
+            totals[2 * i + 1] = totals[2 * i + 1] + nt(rows, w[x, FC : 2 * FC, :])
+
+
+def own_rows_kernel(at, near, full, far, gain, mine, core, out, kept, normed):
     low = at[1] == 0
     lanes = pl.ds(pl.multiple_of(at[1] * 128, 128), 128)
     near_kept, far_kept = full[at[2], :, lanes], far[at[2], :, lanes]
@@ -141,13 +150,15 @@
     kept[HALF : 2 * HALF, :] = jnp.where(low, far_kept, near_kept)
     renorm(far, gain, normed)
     totals = [jnp.zeros((2 * HALF, FC), F32) for _ in range(4)]
-    for x in range(4):
-        for side, pair in enumerate(((mine, core), (mine_lo, core_lo))):
-            g = jnp.bitwise_xor(at[6], side) * 4 + x
-            rows = jnp.concatenate([near[g], normed[g]], axis=0)
-            for i, w in enumerate(pair):
-                totals[2 * i] = totals[2 * i] + nt(rows, w[x, 0:FC, :])
-                totals[2 * i + 1] = totals[2 * i + 1] + nt(rows, w[x, FC : 2 * FC, :])
+    multiply(at, near, normed, (mine, core), 0, totals)
+    for i in range(4):
+        out[i] = totals[i]
+
+
+def partner_rows_kernel(at, near, far, before, mine, core, out):
+    totals = [before[i] for i in range(4)]
+    multiply(at, near, far, (mine, core), 1, totals)
+    low = at[1] == 0
     for i in range(2):
         gate = totals[2 * i]
         units = (gate / (1.0 + jnp.exp(-gate)) * totals[2 * i + 1]).astype(BF)
@@ -318,17 +329,32 @@
     )(got, gain)
 
 
-def hidden_units(at, near, full, far, gain, weights):
-    return pl.pallas_call(
-        hidden_kernel,
-        out_shape=(jax.ShapeDtypeStruct((2, 128, FC), BF), jax.ShapeDtypeStruct((128, 128), BF)),
-        in_specs=[SMEM] + [VMEM] * 8,
-        out_specs=(VMEM, VMEM),
-        scratch_shapes=[pltpu.VMEM((GROUPS, HALF, RUN), BF)],
-        compiler_params=params(16),
-        cost_estimate=cost(4 * HALF * D * 4 * FC, 8 * 2**20),
-        name="hidden",
-    )(at, near, full, far, gain, *weights)
+def own_rows(at, near, full, far, gain, mine, core):
+    return pl.pallas_call(
+        own_rows_kernel,
+        out_shape=(
+            jax.ShapeDtypeStruct((4, 128, FC), F32),
+            jax.ShapeDtypeStruct((128, 128), BF),
+            jax.ShapeDtypeStruct((GROUPS, HALF, RUN), BF),
+        ),
+        in_specs=[SMEM] + [VMEM] * 6,
+        out_specs=(VMEM,) * 3,
+        compiler_params=params(16),
+        cost_estimate=cost(2 * HALF * D * 4 * FC, 4 * 2**20),
+        name="own_rows",
+    )(at, near, full, far, gain, mine, core)
+
+
+def partner_rows(at, near, far, before, mine, core):
+    return pl.pallas_call(
+        partner_rows_kernel,
+        out_shape=jax.ShapeDtypeStruct((2, 128, FC), BF),
+        in_specs=[SMEM] + [VMEM] * 5,
+        out_specs=VMEM,
+        compiler_params=params(16),
+        cost_estimate=cost(2 * HALF * D * 4 * FC, 4 * 2**20),
+        name="partner_rows",
+    )(at, near, far, before, mine, core)
 
 
 def down(at, units, far_units, weights):
@@ -425,11 +451,13 @@
     core_mine = swap(mine, 1)
     full = collect(attended)
     far = swap(full, 2)
-    mine_lo = after(mine_lo, far)
-    weights = (mine, mine_lo, core_mine, swap(mine_lo, 1))
     gain = ffn_gain.reshape(1, D)
     near = near_half(full, gain)
-    units, kept = hidden_units(at, near, full, far, gain, weights)
+    mine_lo = after(mine_lo, (far, near))
+    core_lo = swap(mine_lo, 1)
+    totals, kept, far_normed = own_rows(at, near, full, far, gain, mine, core_mine)
+    units = partner_rows(at, near, far_normed, totals, mine_lo, core_lo)
+    weights = (mine, mine_lo, core_mine, core_lo)
     sums = trade(down(at, units, swap(units, 2), weights), COLUMNS)
     keep, give = finish(at, sums, kept)
     give = swap(give, 1)

time: 222 us -> 218 us (0.982)
  waiting for transfers between devices: 21.8 us -> 15.4 us
  blocking collectives: 101 us -> 104 us
    ppermute x9, waiting for transfers between devices: 12.1 us -> 8.48 us  [swap(): return lax.ppermute(x, 'dev', [(d, d ^ bits) for d in range(MEMBERS)])]
    all_gather x2, blocking collectives: 58.4 us -> 61.8 us  [collect(): return lax.all_gather(x, 'dev', axis=0, axis_index_groups=COLUMNS)]
    all_gather x2, waiting for transfers between devices: 2.79 us -> 0.04 us  [collect_x(): lax.all_gather(x, 'grp', axis=0, axis_index_groups=[[0, 1, 2, 3], [4, 5,...]
    unnamed x32 -> x30, local copies, waits for them, and re-layouts: 6.67 us -> 4.89 us
    pallas_call x1 -> x2, Pallas kernels: 4.01 us -> 4.81 us  [the longest x1 2.93 us: own_rows(): pl.pallas_call(own_rows_kernel, out_shape=(jax.ShapeDtypeStruct((4, 128,...]
  transfers between devices with their start and end apart: 13 -> 13, of which waited for: 6 -> 5; matrix products, arithmetic and copies ran while one was open for 1% -> 1% of each run, Pallas kernels for 4% -> 5%
where the time goes in v7:
time: 218 us; the launch traced here: 217 us
  blocking collectives  104 us (48%)
  starting transfers between devices  55.2 us (25%)
  Pallas kernels  21.1 us (10%)
  waiting for transfers between devices  15.4 us (7%)
  between operations  14.4 us (7%)
  local copies, waits for them, and re-layouts  5.01 us (2%)
    all_gather x2, blocking collectives, collect(): return lax.all_gather(x, 'dev', axis=0, axis_index_groups=COLUMNS)  61.8 us
    ppermute x9, starting transfers between devices, swap(): return lax.ppermute(x, 'dev', [(d, d ^ bits) for d in range(MEMBERS)])  47 us
    all_to_all x2, blocking collectives, trade(): return lax.all_to_all(x, 'dev', 0, 0, axis_index_groups=groups, tiled=True)  41.8 us
    ppermute x9, waiting for transfers between devices, swap(): return lax.ppermute(x, 'dev', [(d, d ^ bits) for d in range(MEMBERS)])  8.48 us
    all_to_all x1, waiting for transfers between devices, on_device(): first = lax.all_to_all(packed, 'grp', 0, 0, tiled=True)  6.84 us
    all_to_all x1, starting transfers between devices, on_device(): first = lax.all_to_all(packed, 'grp', 0, 0, tiled=True)  5.87 us
    unnamed x30, local copies, waits for them, and re-layouts  4.89 us
  transfers between devices with their start and end apart: 13, of which 5 were waited for; matrix products, arithmetic and copies ran while one was open for 1% of the time, Pallas kernels for 5%

profile of v7, /device:TPU:1, one launch (start us, length us, event | category | flops | bytes accessed | tf_op | source)
XLA Modules:
  0.0 216.6 jit_solution(17043038716881011156)
XLA Ops:
  7.2 2.7 %pack.1 = (bf16[8,160,512]{2,1,0:T(8,128)(2,1)}, f32[8,128]{1,0:T(8,128)}) custom-call(bf16[64,512]{1,0:T(8,128)(2,1)} %bitcast.38, bf16[16,512]{1,0:T(8,128)(2,1)} %bitcast.40, bf16[16,512]{1,0:T(8,128)(2,1)} %bitcast.41, bf16[64,512]{1,0:T(8,128)(2,1)} %bitcast.39), custom_call_target="tpu_custom_call" | custom-call | tf_op jit(solution)/shard_map/pack/pallas_call | solution.py:273
  9.9 0.0 copy-start.11
  9.9 5.9 %all-to-all-start = ((bf16[8,160,512]{2,1,0:T(8,128)(2,1)}), bf16[8,160,512]{2,1,0:T(8,128)(2,1)S(1)}, u32[]{:S(2)}, u32[]{:S(2)}) async-start(bf16[8,160,512]{2,1,0:T(8,128)(2,1)} %get-tuple-element.22), calls=%async_computation | async-start | bytes 2621440 | tf_op jit(solution)/shard_map/all_to_all | solution.py:427
  15.7 0.0 all-gather.7.cloned.1.call-start
  15.8 4.5 %collective-permute-start.4 = (bf16[224,512]{1,0:T(8,128)(2,1)}, bf16[224,512]{1,0:T(8,128)(2,1)}, u32[]{:S(2)}, u32[]{:S(2)}) collective-permute-start(bf16[224,512]{1,0:T(8,128)(2,1)} %bitcast.20.narrow), channel_id=1, source_target_pairs={{0,2},{1,3},{2,0},{3,1},{4,6},{5,7},{6,4},{7,5},{8,10},{9,11},{10,... | collective-permute-start | bytes 688136 | tf_op jit(solution)/shard_map/ppermute | solution.py:384
  20.4 0.1 stack.31.at
  20.5 0.1 convert_bitcast_fusion
  20.6 1.2 multiply_sine_fusion
  21.8 0.7 copy-done.10
  22.5 3.4 %norm.1 = (bf16[8,256,512]{2,1,0:T(8,128)(2,1)S(1)}, bf16[64,256]{1,0:T(8,128)(2,1)S(1)}) custom-call(s32[7]{0:T(128)S(1)} %stack.31.at, f32[8,128]{1,0:T(8,128)S(1)} %copy-done.11, f32[256,128]{1,0:T(8,128)S(1)} %get-tuple-element.38.tables.cos, bf16[256,4096]{1,0:T(8,128)(2,1)} %stream.1, f32[1,4096]{1,0:T(1,128)S(1)} %bitcast.37), custom_call_target="tpu_custom_call" | custom-call | tf_op jit(solution)/shard_map/norm/pallas_call | solution.py:229
  25.9 0.0 copy-start.8
  25.9 0.6 copy-done.8
  26.5 6.8 %all-to-all-done.weights = bf16[8,160,512]{2,1,0:T(8,128)(2,1)S(1)} async-done(((bf16[8,160,512]{2,1,0:T(8,128)(2,1)}), bf16[8,160,512]{2,1,0:T(8,128)(2,1)S(1)}, u32[]{:S(2)}, u32[]{:S(2)}) %all-to-all-start) | async-done | bytes 1310752 | tf_op jit(solution)/shard_map/all_to_all | solution.py:427
  33.4 0.9 copy-done.4
  34.3 1.4 project.1
  35.7 2.0 collective-permute-done.4.got
  37.7 2.8 %join.1 = bf16[672,512]{1,0:T(8,128)(2,1)} custom-call(s32[7]{0:T(128)S(1)} %stack.31.at, bf16[8,64,128]{2,1,0:T(8,128)(2,1)S(1)} %get-tuple-element.25.after, bf16[224,512]{1,0:T(8,128)(2,1)S(1)} %bitcast.33, bf16[224,512]{1,0:T(8,128)(2,1)S(1)} %bitcast.34, bf16[224,512]{1,0:T(8,128)(2,1)} %bitcast.20.narrow, bf16[224,512]{1,0:T(8,128)(2,1)} %collective-permute-done.4.got), custom_call_target="tpu_custom_call" | custom-call | tf_op jit(solution)/shard_map/join/pallas_call | solution.py:261
  40.6 0.0 all-gather.7.cloned.1.call-update
  40.6 0.0 all-gather.9.cloned.1.call-start
  40.6 11.9 %all_to_all.15.got = bf16[8,64,128]{2,1,0:T(8,128)(2,1)S(1)} all-to-all(bf16[8,64,128]{2,1,0:T(8,128)(2,1)} %copy-done.3), channel_id=1, replica_groups={{0,1,2,3,4,5,6,7},{8,9,10,11,12,13,14,15},{16,17,18,19,20,21,22,23},{24..., dimensions={0} | all-to-all | bytes 262144 | tf_op jit(solution)/shard_map/all_to_all | solution.py:396
  52.5 2.2 %collective-permute-start.6 = (bf16[672,512]{1,0:T(8,128)(2,1)}, bf16[672,512]{1,0:T(8,128)(2,1)S(1)}, u32[]{:S(2)}, u32[]{:S(2)}) collective-permute-start(bf16[672,512]{1,0:T(8,128)(2,1)} %join.1), channel_id=1, source_target_pairs={{0,256},{64,320},{128,384},{192,448},{256,0},{320,64},{384,128},{4... | collective-permute-start | bytes 2064392 | tf_op jit(solution)/shard_map/ppermute | solution.py:388
  54.8 3.1 %collective-permute-start = (bf16[8,64,512]{2,1,0:T(8,128)(2,1)S(1)}, bf16[8,64,512]{2,1,0:T(8,128)(2,1)S(1)}, u32[]{:S(2)}, u32[]{:S(2)}) collective-permute-start(bf16[8,64,512]{2,1,0:T(8,128)(2,1)S(1)} %slice.4.mine), channel_id=1, source_target_pairs={{0,1},{1,0},{2,3},{3,2},{4,5},{5,4},{6,7},{7,6},{8,9},{9,8},{10,11... | collective-permute-start | bytes 1572872 | tf_op jit(solution)/shard_map/ppermute | solution.py:384
  57.9 3.1 %collective-permute-start.1 = (bf16[8,64,512]{2,1,0:T(8,128)(2,1)S(1)}, bf16[8,64,512]{2,1,0:T(8,128)(2,1)S(1)}, u32[]{:S(2)}, u32[]{:S(2)}) collective-permute-start(bf16[8,64,512]{2,1,0:T(8,128)(2,1)S(1)} %slice.4.mine), channel_id=1, source_target_pairs={{0,2},{1,3},{2,0},{3,1},{4,6},{5,7},{6,4},{7,5},{8,10},{9,11},{10,... | collective-permute-start | bytes 1572872 | tf_op jit(solution)/shard_map/ppermute | solution.py:384
  61.0 3.8 %collective-permute-start.2 = (bf16[8,64,512]{2,1,0:T(8,128)(2,1)S(1)}, bf16[8,64,512]{2,1,0:T(8,128)(2,1)S(1)}, u32[]{:S(2)}, u32[]{:S(2)}) collective-permute-start(bf16[8,64,512]{2,1,0:T(8,128)(2,1)S(1)} %slice.4.mine), channel_id=1, source_target_pairs={{0,3},{1,2},{2,1},{3,0},{4,7},{5,6},{6,5},{7,4},{8,11},{9,10},{10,... | collective-permute-start | bytes 1572872 | tf_op jit(solution)/shard_map/ppermute | solution.py:384
  64.9 1.4 attend.1
  66.3 33.3 %all-gather = bf16[1024,256]{1,0:T(8,128)(2,1)S(1)} all-gather(bf16[64,256]{1,0:T(8,128)(2,1)S(1)} %attend.1), channel_id=2, replica_groups={{0,4,8,12,16,20,24,28,32,36,40,44,48,52,56,60},{1,5,9,13,17,21,25,29,33..., dimensions={0}, use_global_device_ids=true | all-gather | bytes 557056 | tf_op jit(solution)/shard_map/all_gather | solution.py:400
  99.6 1.3 output.1
  100.9 0.8 copy-done.13
  101.8 0.0 all-gather.9.cloned.1.call-update
  101.8 28.5 %all-gather.1 = bf16[1024,256]{1,0:T(8,128)(2,1)} all-gather(bf16[64,256]{1,0:T(8,128)(2,1)S(1)} %output.1), channel_id=3, replica_groups={{0,4,8,12,16,20,24,28,32,36,40,44,48,52,56,60},{1,5,9,13,17,21,25,29,33..., dimensions={0}, use_global_device_ids=true | all-gather | bytes 557056 | tf_op jit(solution)/shard_map/all_gather | solution.py:400
  130.3 4.1 %collective-permute-start.3 = (bf16[16,64,256]{2,1,0:T(8,128)(2,1)}, bf16[16,64,256]{2,1,0:T(8,128)(2,1)}, u32[]{:S(2)}, u32[]{:S(2)}) collective-permute-start(bf16[16,64,256]{2,1,0:T(8,128)(2,1)} %bitcast.16.got.full), channel_id=1, source_target_pairs={{0,2},{1,3},{2,0},{3,1},{4,6},{5,7},{6,4},{7,5},{8,10},{9,11},{10,... | collective-permute-start | bytes 1572872 | tf_op jit(solution)/shard_map/ppermute | solution.py:384
  134.5 0.0 all-gather.7.cloned.1.call-done
  134.5 8.3 %collective-permute-start.5 = (bf16[4,672,512]{2,1,0:T(8,128)(2,1)}, bf16[4,672,512]{2,1,0:T(8,128)(2,1)S(1)}, u32[]{:S(2)}, u32[]{:S(2)}) collective-permute-start(bf16[4,672,512]{2,1,0:T(8,128)(2,1)} %bitcast.26), channel_id=1, source_target_pairs={{0,1},{1,0},{2,3},{3,2},{4,5},{5,4},{6,7},{7,6},{8,9},{9,8},{10,11... | collective-permute-start | bytes 8257544 | tf_op jit(solution)/shard_map/ppermute | solution.py:384
  142.8 1.4 near_half.1.near
  144.2 0.0 all-gather.9.cloned.1.call-done
  144.3 8.5 %collective-permute-start.7 = (bf16[4,672,512]{2,1,0:T(8,128)(2,1)}, bf16[4,672,512]{2,1,0:T(8,128)(2,1)S(1)}, u32[]{:S(2)}, u32[]{:S(2)}) collective-permute-start(bf16[4,672,512]{2,1,0:T(8,128)(2,1)} %bitcast.29), channel_id=1, source_target_pairs={{0,1},{1,0},{2,3},{3,2},{4,5},{5,4},{6,7},{7,6},{8,9},{9,8},{10,11... | collective-permute-start | bytes 8257544 | tf_op jit(solution)/shard_map/ppermute | solution.py:384
  152.8 1.8 copy-done
  154.5 2.9 %own_rows.1 = (f32[4,128,224]{2,1,0:T(8,128)S(1)}, bf16[128,128]{1,0:T(8,128)(2,1)S(1)}, bf16[8,64,512]{2,1,0:T(8,128)(2,1)S(1)}) custom-call(s32[7]{0:T(128)S(1)} %stack.31.at, bf16[8,64,512]{2,1,0:T(8,128)(2,1)S(1)} %near_half.1.near, bf16[16,64,256]{2,1,0:T(8,128)(2,1)} %bitcast.16.got.full, bf16[16,64,256]{2,1,0:T(8,128)(2,1)} %collective-permute-done.3.far, ...), custom_call_target="tpu_custom_call" | custom-call | flops 469762048 | bytes 4194304 | tf_op jit(solution)/shard_map/own_rows/pallas_call | solution.py:333
  157.5 0.2 collective-permute-done.7.core.core_lo
  157.7 1.9 partner_rows.1.units
  159.6 2.6 %collective-permute-start.8 = (bf16[2,128,224]{2,1,0:T(8,128)(2,1)S(1)}, bf16[2,128,224]{2,1,0:T(8,128)(2,1)S(1)}, u32[]{:S(2)}, u32[]{:S(2)}) collective-permute-start(bf16[2,128,224]{2,1,0:T(8,128)(2,1)S(1)} %partner_rows.1.units), channel_id=1, source_target_pairs={{0,2},{1,3},{2,0},{3,1},{4,6},{5,7},{6,4},{7,5},{8,10},{9,11},{10,... | collective-permute-start | bytes 344072 | tf_op jit(solution)/shard_map/ppermute | solution.py:384
  162.2 5.5 %collective-permute-done.8.far_units = bf16[2,128,224]{2,1,0:T(8,128)(2,1)S(1)} collective-permute-done((bf16[2,128,224]{2,1,0:T(8,128)(2,1)S(1)}, bf16[2,128,224]{2,1,0:T(8,128)(2,1)S(1)}, u32[]{:S(2)}, u32[]{:S(2)}) %collective-permute-start.8) | collective-permute-done | bytes 114720 | tf_op jit(solution)/shard_map/ppermute | solution.py:384
  167.7 1.2 down.1
  168.9 29.9 %all_to_all.16.got = bf16[16,128,128]{2,1,0:T(8,128)(2,1)S(1)} all-to-all(bf16[16,128,128]{2,1,0:T(8,128)(2,1)S(1)} %down.1), channel_id=1, replica_groups={{0,4,8,12,16,20,24,28,32,36,40,44,48,52,56,60},{1,5,9,13,17,21,25,29,33..., dimensions={0} | all-to-all | bytes 1048576 | tf_op jit(solution)/shard_map/all_to_all | solution.py:396
  198.8 0.7 finish.1
  199.5 8.9 %collective-permute-start.9 = (bf16[64,128]{1,0:T(8,128)(2,1)S(1)}, bf16[64,128]{1,0:T(8,128)(2,1)S(1)}, u32[]{:S(2)}, u32[]{:S(2)}) collective-permute-start(bf16[64,128]{1,0:T(8,128)(2,1)S(1)} %get-tuple-element.36), channel_id=1, source_target_pairs={{0,1},{1,0},{2,3},{3,2},{4,5},{5,4},{6,7},{7,6},{8,9},{9,8},{10,11... | collective-permute-start | bytes 49160 | tf_op jit(solution)/shard_map/ppermute | solution.py:384
  208.4 0.8 collective-permute-done.9
  209.2 0.6 fusion
  (31 shorter events, 0.1 us)
Async XLA Ops:
  7.2 13.4 %copy-start.14 = (s32[2]{0:T(128)S(1)}, s32[2]{0:T(128)}, u32[]{:S(2)}) copy-start(s32[2]{0:T(128)} %param.14) | copy-start | bytes 28
  9.9 11.9 %copy-start.11 = (f32[8,128]{1,0:T(8,128)S(1)}, f32[8,128]{1,0:T(8,128)}, u32[]{:S(2)}) copy-start(f32[8,128]{1,0:T(8,128)} %get-tuple-element.20.after) | copy-start | bytes 12292
  9.9 23.5 %all-to-all-start = ((bf16[8,160,512]{2,1,0:T(8,128)(2,1)}), bf16[8,160,512]{2,1,0:T(8,128)(2,1)S(1)}, u32[]{:S(2)}, u32[]{:S(2)}) async-start(bf16[8,160,512]{2,1,0:T(8,128)(2,1)} %get-tuple-element.22), calls=%async_computation | async-start | bytes 2621440 | tf_op jit(solution)/shard_map/all_to_all | solution.py:427
  15.7 118.7 %all-gather.7.cloned.1.call-start = ((), (), s32[]{:S(2)}) async-start(), calls=%async_computation.3 | async-start | bytes 3440640 | tf_op jit(solution)/shard_map/all_gather | solution.py:392
  15.8 21.9 %collective-permute-start.4 = (bf16[224,512]{1,0:T(8,128)(2,1)}, bf16[224,512]{1,0:T(8,128)(2,1)}, u32[]{:S(2)}, u32[]{:S(2)}) collective-permute-start(bf16[224,512]{1,0:T(8,128)(2,1)} %bitcast.20.narrow), channel_id=1, source_target_pairs={{0,2},{1,3},{2,0},{3,1},{4,6},{5,7},{6,4},{7,5},{8,10},{9,11},{10,... | collective-permute-start | bytes 688136 | tf_op jit(solution)/shard_map/ppermute | solution.py:384
  21.8 0.7 copy-start.10
  25.9 0.6 copy-start.8
  33.4 0.9 copy-start.4
  34.3 3.5 %copy-start.5 = (bf16[512,224]{0,1:T(8,128)(2,1)S(1)}, bf16[512,224]{0,1:T(8,128)(2,1)}, u32[]{:S(2)}) copy-start(bf16[512,224]{0,1:T(8,128)(2,1)} %param.21) | copy-start | bytes 688132
  34.3 3.5 %copy-start.6 = (bf16[512,224]{0,1:T(8,128)(2,1)S(1)}, bf16[512,224]{0,1:T(8,128)(2,1)}, u32[]{:S(2)}) copy-start(bf16[512,224]{0,1:T(8,128)(2,1)} %param.22) | copy-start | bytes 688132
  35.7 2.0 copy-start.3
  35.7 29.1 %copy-start.12 = (s32[2]{0:T(128)S(1)}, s32[2]{0:T(128)}, u32[]{:S(2)}) copy-start(s32[2]{0:T(128)} %lengths.1) | copy-start | bytes 28
  35.7 63.9 %copy-start.9 = (bf16[64,256]{1,0:T(8,128)(2,1)S(1)}, bf16[64,256]{1,0:T(8,128)(2,1)}, u32[]{:S(2)}) copy-start(bf16[64,256]{1,0:T(8,128)(2,1)} %copy-done.8) | copy-start | bytes 98308
  40.6 103.7 %all-gather.9.cloned.1.call-start = ((), (), s32[]{:S(2)}) async-start(), calls=%async_computation.4 | async-start | bytes 3440640 | tf_op jit(solution)/shard_map/all_gather | solution.py:392
  52.5 90.3 %copy-start.7 = (f32[4096]{0:T(1024)S(1)}, f32[4096]{0:T(1024)}, u32[]{:S(2)}) copy-start(f32[4096]{0:T(1024)} %param.20) | copy-start | bytes 49156
  52.5 48.4 %collective-permute-start.6 = (bf16[672,512]{1,0:T(8,128)(2,1)}, bf16[672,512]{1,0:T(8,128)(2,1)S(1)}, u32[]{:S(2)}, u32[]{:S(2)}) collective-permute-start(bf16[672,512]{1,0:T(8,128)(2,1)} %join.1), channel_id=1, source_target_pairs={{0,256},{64,320},{128,384},{192,448},{256,0},{320,64},{384,128},{4... | collective-permute-start | bytes 2064392 | tf_op jit(solution)/shard_map/ppermute | solution.py:388
  54.8 44.8 %collective-permute-start = (bf16[8,64,512]{2,1,0:T(8,128)(2,1)S(1)}, bf16[8,64,512]{2,1,0:T(8,128)(2,1)S(1)}, u32[]{:S(2)}, u32[]{:S(2)}) collective-permute-start(bf16[8,64,512]{2,1,0:T(8,128)(2,1)S(1)} %slice.4.mine), channel_id=1, source_target_pairs={{0,1},{1,0},{2,3},{3,2},{4,5},{5,4},{6,7},{7,6},{8,9},{9,8},{10,11... | collective-permute-start | bytes 1572872 | tf_op jit(solution)/shard_map/ppermute | solution.py:384
  57.9 41.7 %collective-permute-start.1 = (bf16[8,64,512]{2,1,0:T(8,128)(2,1)S(1)}, bf16[8,64,512]{2,1,0:T(8,128)(2,1)S(1)}, u32[]{:S(2)}, u32[]{:S(2)}) collective-permute-start(bf16[8,64,512]{2,1,0:T(8,128)(2,1)S(1)} %slice.4.mine), channel_id=1, source_target_pairs={{0,2},{1,3},{2,0},{3,1},{4,6},{5,7},{6,4},{7,5},{8,10},{9,11},{10,... | collective-permute-start | bytes 1572872 | tf_op jit(solution)/shard_map/ppermute | solution.py:384
  61.0 38.6 %collective-permute-start.2 = (bf16[8,64,512]{2,1,0:T(8,128)(2,1)S(1)}, bf16[8,64,512]{2,1,0:T(8,128)(2,1)S(1)}, u32[]{:S(2)}, u32[]{:S(2)}) collective-permute-start(bf16[8,64,512]{2,1,0:T(8,128)(2,1)S(1)} %slice.4.mine), channel_id=1, source_target_pairs={{0,3},{1,2},{2,1},{3,0},{4,7},{5,6},{6,5},{7,4},{8,11},{9,10},{10,... | collective-permute-start | bytes 1572872 | tf_op jit(solution)/shard_map/ppermute | solution.py:384
  100.9 0.9 copy-start.13
  130.3 13.9 %collective-permute-start.3 = (bf16[16,64,256]{2,1,0:T(8,128)(2,1)}, bf16[16,64,256]{2,1,0:T(8,128)(2,1)}, u32[]{:S(2)}, u32[]{:S(2)}) collective-permute-start(bf16[16,64,256]{2,1,0:T(8,128)(2,1)} %bitcast.16.got.full), channel_id=1, source_target_pairs={{0,2},{1,3},{2,0},{3,1},{4,6},{5,7},{6,4},{7,5},{8,10},{9,11},{10,... | collective-permute-start | bytes 1572872 | tf_op jit(solution)/shard_map/ppermute | solution.py:384
  134.5 18.3 %collective-permute-start.5 = (bf16[4,672,512]{2,1,0:T(8,128)(2,1)}, bf16[4,672,512]{2,1,0:T(8,128)(2,1)S(1)}, u32[]{:S(2)}, u32[]{:S(2)}) collective-permute-start(bf16[4,672,512]{2,1,0:T(8,128)(2,1)} %bitcast.26), channel_id=1, source_target_pairs={{0,1},{1,0},{2,3},{3,2},{4,5},{5,4},{6,7},{7,6},{8,9},{9,8},{10,11... | collective-permute-start | bytes 8257544 | tf_op jit(solution)/shard_map/ppermute | solution.py:384
  144.3 13.4 %collective-permute-start.7 = (bf16[4,672,512]{2,1,0:T(8,128)(2,1)}, bf16[4,672,512]{2,1,0:T(8,128)(2,1)S(1)}, u32[]{:S(2)}, u32[]{:S(2)}) collective-permute-start(bf16[4,672,512]{2,1,0:T(8,128)(2,1)} %bitcast.29), channel_id=1, source_target_pairs={{0,1},{1,0},{2,3},{3,2},{4,5},{5,4},{6,7},{7,6},{8,9},{9,8},{10,11... | collective-permute-start | bytes 8257544 | tf_op jit(solution)/shard_map/ppermute | solution.py:384
  152.8 1.8 copy-start
  154.5 3.1 %copy-start.2 = (bf16[2688,512]{1,0:T(8,128)(2,1)S(1)}, bf16[2688,512]{1,0:T(8,128)(2,1)}, u32[]{:S(2)}) copy-start(bf16[2688,512]{1,0:T(8,128)(2,1)} %all-gather.9.cloned.1.call-done) | copy-start | bytes 8257540
  157.7 10.0 %copy-start.1 = (bf16[2688,512]{1,0:T(8,128)(2,1)S(1)}, bf16[2688,512]{1,0:T(8,128)(2,1)}, u32[]{:S(2)}) copy-start(bf16[2688,512]{1,0:T(8,128)(2,1)} %all-gather.7.cloned.1.call-done) | copy-start | bytes 8257540
  159.6 8.1 %collective-permute-start.8 = (bf16[2,128,224]{2,1,0:T(8,128)(2,1)S(1)}, bf16[2,128,224]{2,1,0:T(8,128)(2,1)S(1)}, u32[]{:S(2)}, u32[]{:S(2)}) collective-permute-start(bf16[2,128,224]{2,1,0:T(8,128)(2,1)S(1)} %partner_rows.1.units), channel_id=1, source_target_pairs={{0,2},{1,3},{2,0},{3,1},{4,6},{5,7},{6,4},{7,5},{8,10},{9,11},{10,... | collective-permute-start | bytes 344072 | tf_op jit(solution)/shard_map/ppermute | solution.py:384
  199.5 9.7 %collective-permute-start.9 = (bf16[64,128]{1,0:T(8,128)(2,1)S(1)}, bf16[64,128]{1,0:T(8,128)(2,1)S(1)}, u32[]{:S(2)}, u32[]{:S(2)}) collective-permute-start(bf16[64,128]{1,0:T(8,128)(2,1)S(1)} %get-tuple-element.36), channel_id=1, source_target_pairs={{0,1},{1,0},{2,3},{3,2},{4,5},{5,4},{6,7},{7,6},{8,9},{9,8},{10,11... | collective-permute-start | bytes 49160 | tf_op jit(solution)/shard_map/ppermute | solution.py:384
Sparse Core Ops, SparseCore 0:
  40.7 47.5 all-gather.6
  101.9 41.8 all-gather.8

commit v8 on v7

--- a/solution.py
+++ b/solution.py
@@ -25,6 +25,7 @@
 RUN = 512
 
 COLUMNS = [[4 * z + q for z in range(DEPTH)] for q in range(4)]
+PARITIES = [[4 * (2 * i + p) + q for i in range(8)] for p in range(2) for q in range(4)]
 OCTETS = [[8 * z + m for m in range(8)] for z in range(8)]
 
 BF = jnp.bfloat16
@@ -115,22 +116,27 @@
         blocks.append(picked)
     projected = jnp.concatenate(blocks, axis=1)
     attended = (own[...].astype(F32) + projected).astype(BF)
-    out[...] = attended
-
-
-def renorm(got, gain, out):
+    for i in range(8):
+        out[i] = attended
+
+
+def renorm(at, same, other, gain, out):
+    low = at[3] == 0
     squares = jnp.zeros((HALF, 1), F32)
-    for z in range(DEPTH):
-        x = got[z].astype(F32)
-        squares = squares + jnp.sum(x * x, axis=-1, keepdims=True)
+    for got in (same, other):
+        for i in range(8):
+            x = got[i].astype(F32)
+            squares = squares + jnp.sum(x * x, axis=-1, keepdims=True)
     scale = lax.rsqrt(squares * (1.0 / D) + 1e-05)
-    for z in range(DEPTH):
-        x = got[z].astype(F32) * scale * gain[:, z * BAND : (z + 1) * BAND]
-        out[z // 2, :, (z % 2) * BAND : (z % 2 + 1) * BAND] = x.astype(BF)
-
-
-def near_kernel(got, gain, out):
-    renorm(got, gain, out)
+    for i in range(8):
+        one, two = same[i].astype(F32), other[i].astype(F32)
+        for k, x in enumerate((jnp.where(low, one, two), jnp.where(low, two, one))):
+            z = 2 * i + k
+            out[i, :, k * BAND : (k + 1) * BAND] = (x * scale * gain[:, z * BAND : (z + 1) * BAND]).astype(BF)
+
+
+def near_kernel(at, same, other, gain, out):
+    renorm(at, same, other, gain, out)
 
 
 def multiply(at, near, far, pair, side, totals):
@@ -142,13 +148,13 @@
             totals[2 * i + 1] = totals[2 * i + 1] + nt(rows, w[x, FC : 2 * FC, :])
 
 
-def own_rows_kernel(at, near, full, far, gain, mine, core, out, kept, normed):
+def own_rows_kernel(at, near, same, far_same, far_other, gain, mine, core, out, kept, normed):
     low = at[1] == 0
     lanes = pl.ds(pl.multiple_of(at[1] * 128, 128), 128)
-    near_kept, far_kept = full[at[2], :, lanes], far[at[2], :, lanes]
+    near_kept, far_kept = same[at[4], :, lanes], far_same[at[4], :, lanes]
     kept[0:HALF, :] = jnp.where(low, near_kept, far_kept)
     kept[HALF : 2 * HALF, :] = jnp.where(low, far_kept, near_kept)
-    renorm(far, gain, normed)
+    renorm(at, far_same, far_other, gain, normed)
     totals = [jnp.zeros((2 * HALF, FC), F32) for _ in range(4)]
     multiply(at, near, normed, (mine, core), 0, totals)
     for i in range(4):
@@ -167,22 +173,29 @@
         out[i, HALF : 2 * HALF, :] = jnp.where(low, second, first)
 
 
-def down_kernel(at, units, far_units, mine, mine_lo, core, core_lo, out):
+def down_kernel(at, units, far_units, mine, mine_lo, core, core_lo, keep, give):
+    low = at[3] == 0
     for x in range(4):
         for side, pair in enumerate(((mine, core), (mine_lo, core_lo))):
             total = jnp.zeros((128, BAND), F32)
             for i, w in enumerate(pair):
                 total = total + jnp.dot(units[i], w[x, 2 * FC : 3 * FC, 0:BAND], preferred_element_type=F32)
                 total = total + jnp.dot(far_units[i], w[x, 2 * FC : 3 * FC, BAND:RUN], preferred_element_type=F32)
-            z = (jnp.bitwise_xor(at[6], side) * 4 + x) * 2
-            out[z] = total[:, 0:128].astype(BF)
-            out[z + 1] = total[:, 128:256].astype(BF)
+            g = jnp.bitwise_xor(at[6], side) * 4 + x
+            even, odd = total[:, 0:128], total[:, 128:256]
+            keep[g] = jnp.where(low, even, odd)
+            give[g] = jnp.where(low, odd, even).astype(BF)
+
+
+def add_kernel(keep, got, out):
+    for i in range(8):
+        out[i] = (keep[i] + got[i].astype(F32)).astype(BF)
 
 
 def finish_kernel(at, got, kept, keep, give):
     total = kept[...].astype(F32)
-    for z in range(DEPTH):
-        total = total + got[z].astype(F32)
+    for i in range(8):
+        total = total + got[i].astype(F32)
     result = total.T
     head, tail = result[0:QC, :], result[QC : 2 * QC, :]
     keep[...] = jnp.where(at[0] == 0, head, tail).astype(BF)
@@ -310,7 +323,7 @@
 def output(at, got, weights, own):
     return pl.pallas_call(
         output_kernel,
-        out_shape=jax.ShapeDtypeStruct((HALF, BAND), BF),
+        out_shape=jax.ShapeDtypeStruct((8, HALF, BAND), BF),
         in_specs=[SMEM] + [VMEM] * 6,
         out_specs=VMEM,
         compiler_params=params(24),
@@ -318,18 +331,18 @@
     )(at, got, *weights, own)
 
 
-def near_half(got, gain):
+def near_half(at, same, other, gain):
     return pl.pallas_call(
         near_kernel,
         out_shape=jax.ShapeDtypeStruct((GROUPS, HALF, RUN), BF),
-        in_specs=[VMEM] * 2,
+        in_specs=[SMEM] + [VMEM] * 3,
         out_specs=VMEM,
         compiler_params=params(16),
         name="near_half",
-    )(got, gain)
-
-
-def own_rows(at, near, full, far, gain, mine, core):
+    )(at, same, other, gain)
+
+
+def own_rows(at, near, same, far_same, far_other, gain, mine, core):
     return pl.pallas_call(
         own_rows_kernel,
         out_shape=(
@@ -337,12 +350,12 @@
             jax.ShapeDtypeStruct((128, 128), BF),
             jax.ShapeDtypeStruct((GROUPS, HALF, RUN), BF),
         ),
-        in_specs=[SMEM] + [VMEM] * 6,
+        in_specs=[SMEM] + [VMEM] * 7,
         out_specs=(VMEM,) * 3,
         compiler_params=params(16),
         cost_estimate=cost(2 * HALF * D * 4 * FC, 4 * 2**20),
         name="own_rows",
-    )(at, near, full, far, gain, mine, core)
+    )(at, near, same, far_same, far_other, gain, mine, core)
 
 
 def partner_rows(at, near, far, before, mine, core):
@@ -360,13 +373,24 @@
 def down(at, units, far_units, weights):
     return pl.pallas_call(
         down_kernel,
-        out_shape=jax.ShapeDtypeStruct((DEPTH, 128, 128), BF),
+        out_shape=(jax.ShapeDtypeStruct((8, 128, 128), F32), jax.ShapeDtypeStruct((8, 128, 128), BF)),
         in_specs=[SMEM] + [VMEM] * 6,
-        out_specs=VMEM,
+        out_specs=(VMEM, VMEM),
         compiler_params=params(16),
         cost_estimate=cost(4 * HALF * D * 2 * FC, 5 * 2**20),
         name="down",
     )(at, units, far_units, *weights)
+
+
+def add(keep, got):
+    return pl.pallas_call(
+        add_kernel,
+        out_shape=jax.ShapeDtypeStruct((8, 128, 128), BF),
+        in_specs=[VMEM] * 2,
+        out_specs=VMEM,
+        compiler_params=params(16),
+        name="add",
+    )(keep, got)
 
 
 def finish(at, got, kept):
@@ -449,16 +473,17 @@
     mine, mine_lo = collect_x(mine), collect_x(after(mine_lo, attended))
     mine = after(mine, attended)
     core_mine = swap(mine, 1)
-    full = collect(attended)
-    far = swap(full, 2)
+    same = trade(attended, PARITIES)
+    other, far_same, far_other = swap(same, 4), swap(same, 2), swap(same, 6)
     gain = ffn_gain.reshape(1, D)
-    near = near_half(full, gain)
-    mine_lo = after(mine_lo, (far, near))
+    near = near_half(at, same, other, gain)
+    mine_lo = after(mine_lo, (far_same, far_other, near))
     core_lo = swap(mine_lo, 1)
-    totals, kept, far_normed = own_rows(at, near, full, far, gain, mine, core_mine)
+    totals, kept, far_normed = own_rows(at, near, same, far_same, far_other, gain, mine, core_mine)
     units = partner_rows(at, near, far_normed, totals, mine_lo, core_lo)
     weights = (mine, mine_lo, core_mine, core_lo)
-    sums = trade(down(at, units, swap(units, 2), weights), COLUMNS)
+    keep, give = down(at, units, swap(units, 2), weights)
+    sums = trade(add(keep, swap(give, 4)), PARITIES)
     keep, give = finish(at, sums, kept)
     give = swap(give, 1)
     rows = jnp.where(core == 0, jnp.concatenate([keep, give], axis=1), jnp.concatenate([give, keep], axis=1))

time: 218 us -> 219 us (level)
  blocking collectives: 104 us -> 94.4 us
  waiting for transfers between devices: 15.4 us -> 20.4 us
  local copies, waits for them, and re-layouts: 5.01 us -> 9.02 us
  starting transfers between devices: 55.2 us -> 57.4 us
    all_gather x2 -> x1, blocking collectives: 61.8 us -> 32.8 us  [collect(): return lax.all_gather(x, 'dev', axis=0, axis_index_groups=COLUMNS)]
    all_to_all x2 -> x3, blocking collectives: 41.8 us -> 61.6 us  [trade(): return lax.all_to_all(x, 'dev', 0, 0, axis_index_groups=groups, tiled=True)]
    ppermute x9 -> x12, waiting for transfers between devices: 8.48 us -> 13.4 us  [swap(): return lax.ppermute(x, 'dev', [(d, d ^ bits) for d in range(MEMBERS)])]
    unnamed x30 -> x46, local copies, waits for them, and re-layouts: 4.89 us -> 8.9 us
    ppermute x9 -> x12, starting transfers between devices: 47 us -> 49.3 us  [swap(): return lax.ppermute(x, 'dev', [(d, d ^ bits) for d in range(MEMBERS)])]
  transfers between devices with their start and end apart: 13 -> 16, of which waited for: 5 -> 5; matrix products, arithmetic and copies ran while one was open for 1% -> 1% of each run, Pallas kernels for 5% -> 5%
where the time goes in v8:
time: 219 us; the launch traced here: 218 us
  blocking collectives  94.4 us (43%)
  starting transfers between devices  57.4 us (26%)
  Pallas kernels  20.4 us (9%)
  waiting for transfers between devices  20.4 us (9%)
  between operations  14.5 us (7%)
  local copies, waits for them, and re-layouts  9.02 us (4%)
    all_to_all x3, blocking collectives, trade(): return lax.all_to_all(x, 'dev', 0, 0, axis_index_groups=groups, tiled=True)  61.6 us
    ppermute x12, starting transfers between devices, swap(): return lax.ppermute(x, 'dev', [(d, d ^ bits) for d in range(MEMBERS)])  49.3 us
    all_gather x1, blocking collectives, collect(): return lax.all_gather(x, 'dev', axis=0, axis_index_groups=COLUMNS)  32.8 us
    ppermute x12, waiting for transfers between devices, swap(): return lax.ppermute(x, 'dev', [(d, d ^ bits) for d in range(MEMBERS)])  13.4 us
    unnamed x46, local copies, waits for them, and re-layouts  8.9 us
    all_to_all x1, waiting for transfers between devices, on_device(): first = lax.all_to_all(packed, 'grp', 0, 0, tiled=True)  6.84 us
    all_to_all x1, starting transfers between devices, on_device(): first = lax.all_to_all(packed, 'grp', 0, 0, tiled=True)  5.87 us
  transfers between devices with their start and end apart: 16, of which 5 were waited for; matrix products, arithmetic and copies ran while one was open for 1% of the time, Pallas kernels for 5%

profile of v8, /device:TPU:1, one launch (start us, length us, event | category | flops | bytes accessed | tf_op | source)
XLA Modules:
  0.0 218.1 jit_solution(6195289871757535810)
XLA Ops:
  7.2 2.7 %pack.1 = (bf16[8,160,512]{2,1,0:T(8,128)(2,1)}, f32[8,128]{1,0:T(8,128)}) custom-call(bf16[64,512]{1,0:T(8,128)(2,1)} %bitcast.37, bf16[16,512]{1,0:T(8,128)(2,1)} %bitcast.39, bf16[16,512]{1,0:T(8,128)(2,1)} %bitcast.40, bf16[64,512]{1,0:T(8,128)(2,1)} %bitcast.38), custom_call_target="tpu_custom_call" | custom-call | tf_op jit(solution)/shard_map/pack/pallas_call | solution.py:286
  9.9 5.9 %all-to-all-start = ((bf16[8,160,512]{2,1,0:T(8,128)(2,1)}), bf16[8,160,512]{2,1,0:T(8,128)(2,1)S(1)}, u32[]{:S(2)}, u32[]{:S(2)}) async-start(bf16[8,160,512]{2,1,0:T(8,128)(2,1)} %get-tuple-element.24), calls=%async_computation | async-start | bytes 2621440 | tf_op jit(solution)/shard_map/all_to_all | solution.py:451
  15.8 4.5 %collective-permute-start.6 = (bf16[224,512]{1,0:T(8,128)(2,1)}, bf16[224,512]{1,0:T(8,128)(2,1)}, u32[]{:S(2)}, u32[]{:S(2)}) collective-permute-start(bf16[224,512]{1,0:T(8,128)(2,1)} %bitcast.19.narrow), channel_id=1, source_target_pairs={{0,2},{1,3},{2,0},{3,1},{4,6},{5,7},{6,4},{7,5},{8,10},{9,11},{10,... | collective-permute-start | bytes 688136 | tf_op jit(solution)/shard_map/ppermute | solution.py:408
  20.4 0.1 stack.31.at
  20.6 1.2 multiply_sine_fusion
  21.8 0.7 copy-done.18
  22.6 3.4 %norm.1 = (bf16[8,256,512]{2,1,0:T(8,128)(2,1)S(1)}, bf16[64,256]{1,0:T(8,128)(2,1)S(1)}) custom-call(s32[7]{0:T(128)S(1)} %stack.31.at, f32[8,128]{1,0:T(8,128)S(1)} %copy-done.19, f32[256,128]{1,0:T(8,128)S(1)} %get-tuple-element.42.tables.cos, bf16[256,4096]{1,0:T(8,128)(2,1)} %stream.1, f32[1,4096]{1,0:T(1,128)S(1)} %bitcast.36), custom_call_target="tpu_custom_call" | custom-call | tf_op jit(solution)/shard_map/norm/pallas_call | solution.py:242
  26.0 0.6 copy-done.16
  26.6 6.8 %all-to-all-done.weights = bf16[8,160,512]{2,1,0:T(8,128)(2,1)S(1)} async-done(((bf16[8,160,512]{2,1,0:T(8,128)(2,1)}), bf16[8,160,512]{2,1,0:T(8,128)(2,1)S(1)}, u32[]{:S(2)}, u32[]{:S(2)}) %all-to-all-start) | async-done | bytes 1310752 | tf_op jit(solution)/shard_map/all_to_all | solution.py:451
  33.4 0.9 copy-done.4
  34.3 1.4 project.1
  35.8 2.0 collective-permute-done.6.got
  37.8 2.8 %join.1 = bf16[672,512]{1,0:T(8,128)(2,1)} custom-call(s32[7]{0:T(128)S(1)} %stack.31.at, bf16[8,64,128]{2,1,0:T(8,128)(2,1)S(1)} %get-tuple-element.27.after, bf16[224,512]{1,0:T(8,128)(2,1)S(1)} %bitcast.32, bf16[224,512]{1,0:T(8,128)(2,1)S(1)} %bitcast.33, bf16[224,512]{1,0:T(8,128)(2,1)} %bitcast.19.narrow, bf16[224,512]{1,0:T(8,128)(2,1)} %collective-permute-done.6.got), custom_call_target="tpu_custom_call" | custom-call | tf_op jit(solution)/shard_map/join/pallas_call | solution.py:274
  40.7 11.9 %all_to_all.20.got = bf16[8,64,128]{2,1,0:T(8,128)(2,1)S(1)} all-to-all(bf16[8,64,128]{2,1,0:T(8,128)(2,1)} %copy-done.3), channel_id=1, replica_groups={{0,1,2,3,4,5,6,7},{8,9,10,11,12,13,14,15},{16,17,18,19,20,21,22,23},{24..., dimensions={0} | all-to-all | bytes 262144 | tf_op jit(solution)/shard_map/all_to_all | solution.py:420
  52.5 2.2 %collective-permute-start.8 = (bf16[672,512]{1,0:T(8,128)(2,1)}, bf16[672,512]{1,0:T(8,128)(2,1)S(1)}, u32[]{:S(2)}, u32[]{:S(2)}) collective-permute-start(bf16[672,512]{1,0:T(8,128)(2,1)} %join.1), channel_id=1, source_target_pairs={{0,256},{64,320},{128,384},{192,448},{256,0},{320,64},{384,128},{4... | collective-permute-start | bytes 2064392 | tf_op jit(solution)/shard_map/ppermute | solution.py:412
  54.8 3.1 %collective-permute-start = (bf16[8,64,512]{2,1,0:T(8,128)(2,1)S(1)}, bf16[8,64,512]{2,1,0:T(8,128)(2,1)S(1)}, u32[]{:S(2)}, u32[]{:S(2)}) collective-permute-start(bf16[8,64,512]{2,1,0:T(8,128)(2,1)S(1)} %slice.4.mine), channel_id=1, source_target_pairs={{0,1},{1,0},{2,3},{3,2},{4,5},{5,4},{6,7},{7,6},{8,9},{9,8},{10,11... | collective-permute-start | bytes 1572872 | tf_op jit(solution)/shard_map/ppermute | solution.py:408
  57.9 3.1 %collective-permute-start.1 = (bf16[8,64,512]{2,1,0:T(8,128)(2,1)S(1)}, bf16[8,64,512]{2,1,0:T(8,128)(2,1)S(1)}, u32[]{:S(2)}, u32[]{:S(2)}) collective-permute-start(bf16[8,64,512]{2,1,0:T(8,128)(2,1)S(1)} %slice.4.mine), channel_id=1, source_target_pairs={{0,2},{1,3},{2,0},{3,1},{4,6},{5,7},{6,4},{7,5},{8,10},{9,11},{10,... | collective-permute-start | bytes 1572872 | tf_op jit(solution)/shard_map/ppermute | solution.py:408
  61.1 3.8 %collective-permute-start.2 = (bf16[8,64,512]{2,1,0:T(8,128)(2,1)S(1)}, bf16[8,64,512]{2,1,0:T(8,128)(2,1)S(1)}, u32[]{:S(2)}, u32[]{:S(2)}) collective-permute-start(bf16[8,64,512]{2,1,0:T(8,128)(2,1)S(1)} %slice.4.mine), channel_id=1, source_target_pairs={{0,3},{1,2},{2,1},{3,0},{4,7},{5,6},{6,5},{7,4},{8,11},{9,10},{10,... | collective-permute-start | bytes 1572872 | tf_op jit(solution)/shard_map/ppermute | solution.py:408
  64.9 0.6 copy-done.11
  65.5 1.4 attend.1
  66.9 32.8 %all-gather = bf16[1024,256]{1,0:T(8,128)(2,1)S(1)} all-gather(bf16[64,256]{1,0:T(8,128)(2,1)S(1)} %attend.1), channel_id=2, replica_groups={{0,4,8,12,16,20,24,28,32,36,40,44,48,52,56,60},{1,5,9,13,17,21,25,29,33..., dimensions={0}, use_global_device_ids=true | all-gather | bytes 557056 | tf_op jit(solution)/shard_map/all_gather | solution.py:424
  99.7 0.6 copy-done.12
  100.3 1.3 output.1
  101.6 0.8 copy-done.21
  102.5 25.6 %all_to_all.21.same = bf16[8,64,256]{2,1,0:T(8,128)(2,1)S(1)} all-to-all(bf16[8,64,256]{2,1,0:T(8,128)(2,1)S(1)} %output.1), channel_id=1, replica_groups={{0,8,16,24,32,40,48,56},{1,9,17,25,33,41,49,57},{2,10,18,26,34,42,50,58..., dimensions={0} | all-to-all | bytes 524288 | tf_op jit(solution)/shard_map/all_to_all | solution.py:420
  128.0 2.7 %collective-permute-start.3 = (bf16[8,64,256]{2,1,0:T(8,128)(2,1)S(1)}, bf16[8,64,256]{2,1,0:T(8,128)(2,1)S(1)}, u32[]{:S(2)}, u32[]{:S(2)}) collective-permute-start(bf16[8,64,256]{2,1,0:T(8,128)(2,1)S(1)} %all_to_all.21.same), channel_id=1, source_target_pairs={{0,4},{1,5},{2,6},{3,7},{4,0},{5,1},{6,2},{7,3},{8,12},{9,13},{10,... | collective-permute-start | bytes 786440 | tf_op jit(solution)/shard_map/ppermute | solution.py:408
  130.7 4.4 %collective-permute-start.4 = (bf16[8,64,256]{2,1,0:T(8,128)(2,1)S(1)}, bf16[8,64,256]{2,1,0:T(8,128)(2,1)}, u32[]{:S(2)}, u32[]{:S(2)}) collective-permute-start(bf16[8,64,256]{2,1,0:T(8,128)(2,1)S(1)} %all_to_all.21.same), channel_id=1, source_target_pairs={{0,2},{1,3},{2,0},{3,1},{4,6},{5,7},{6,4},{7,5},{8,10},{9,11},{10,... | collective-permute-start | bytes 786440 | tf_op jit(solution)/shard_map/ppermute | solution.py:408
  135.2 2.8 %collective-permute-start.5 = (bf16[8,64,256]{2,1,0:T(8,128)(2,1)S(1)}, bf16[8,64,256]{2,1,0:T(8,128)(2,1)}, u32[]{:S(2)}, u32[]{:S(2)}) collective-permute-start(bf16[8,64,256]{2,1,0:T(8,128)(2,1)S(1)} %all_to_all.21.same), channel_id=1, source_target_pairs={{0,6},{1,7},{2,4},{3,5},{4,2},{5,3},{6,0},{7,1},{8,14},{9,15},{10,... | collective-permute-start | bytes 786440 | tf_op jit(solution)/shard_map/ppermute | solution.py:408
  138.0 8.1 %collective-permute-start.7 = (bf16[4,672,512]{2,1,0:T(8,128)(2,1)}, bf16[4,672,512]{2,1,0:T(8,128)(2,1)S(1)}, u32[]{:S(2)}, u32[]{:S(2)}) collective-permute-start(bf16[4,672,512]{2,1,0:T(8,128)(2,1)} %bitcast.28), channel_id=1, source_target_pairs={{0,1},{1,0},{2,3},{3,2},{4,5},{5,4},{6,7},{7,6},{8,9},{9,8},{10,11... | collective-permute-start | bytes 8257544 | tf_op jit(solution)/shard_map/ppermute | solution.py:408
  146.1 0.7 copy-done.5
  146.8 0.9 copy-done.6
  147.8 0.6 copy-done.13
  148.4 0.9 near_half.1.near
  149.3 3.7 %collective-permute-start.9 = (bf16[4,672,512]{2,1,0:T(8,128)(2,1)}, bf16[4,672,512]{2,1,0:T(8,128)(2,1)S(1)}, u32[]{:S(2)}, u32[]{:S(2)}) collective-permute-start(bf16[4,672,512]{2,1,0:T(8,128)(2,1)} %bitcast.25), channel_id=1, source_target_pairs={{0,1},{1,0},{2,3},{3,2},{4,5},{5,4},{6,7},{7,6},{8,9},{9,8},{10,11... | collective-permute-start | bytes 8257544 | tf_op jit(solution)/shard_map/ppermute | solution.py:408
  153.0 1.8 copy-done.1
  154.8 0.6 copy-done.14
  155.4 2.6 %own_rows.1 = (f32[4,128,224]{2,1,0:T(8,128)S(1)}, bf16[128,128]{1,0:T(8,128)(2,1)S(1)}, bf16[8,64,512]{2,1,0:T(8,128)(2,1)S(1)}) custom-call(s32[7]{0:T(128)S(1)} %copy-done.14, bf16[8,64,512]{2,1,0:T(8,128)(2,1)S(1)} %near_half.1.near, bf16[8,64,256]{2,1,0:T(8,128)(2,1)S(1)} %all_to_all.21.same, bf16[8,64,256]{2,1,0:T(8,128)(2,1)} %collective-permute-done.4.far_same, ...), custom_call_target="tpu_custom_call" | custom-call | flops 469762048 | bytes 4194304 | tf_op jit(solution)/shard_map/own_rows/pallas_call | solution.py:346
  158.0 1.9 partner_rows.1.units
  160.0 3.3 %collective-permute-start.10 = (bf16[2,128,224]{2,1,0:T(8,128)(2,1)S(1)}, bf16[2,128,224]{2,1,0:T(8,128)(2,1)S(1)}, u32[]{:S(2)}, u32[]{:S(2)}) collective-permute-start(bf16[2,128,224]{2,1,0:T(8,128)(2,1)S(1)} %partner_rows.1.units), channel_id=1, source_target_pairs={{0,2},{1,3},{2,0},{3,1},{4,6},{5,7},{6,4},{7,5},{8,10},{9,11},{10,... | collective-permute-start | bytes 344072 | tf_op jit(solution)/shard_map/ppermute | solution.py:408
  163.2 5.0 %collective-permute-done.10.far_units = bf16[2,128,224]{2,1,0:T(8,128)(2,1)S(1)} collective-permute-done((bf16[2,128,224]{2,1,0:T(8,128)(2,1)S(1)}, bf16[2,128,224]{2,1,0:T(8,128)(2,1)S(1)}, u32[]{:S(2)}, u32[]{:S(2)}) %collective-permute-start.10) | collective-permute-done | bytes 114720 | tf_op jit(solution)/shard_map/ppermute | solution.py:408
  168.2 1.3 down.1
  169.5 3.0 %collective-permute-start.11 = (bf16[8,128,128]{2,1,0:T(8,128)(2,1)S(1)}, bf16[8,128,128]{2,1,0:T(8,128)(2,1)S(1)}, u32[]{:S(2)}, u32[]{:S(2)}) collective-permute-start(bf16[8,128,128]{2,1,0:T(8,128)(2,1)S(1)} %get-tuple-element.37), channel_id=1, source_target_pairs={{0,4},{1,5},{2,6},{3,7},{4,0},{5,1},{6,2},{7,3},{8,12},{9,13},{10,... | collective-permute-start | bytes 786440 | tf_op jit(solution)/shard_map/ppermute | solution.py:408
  172.5 5.6 %collective-permute-done.11.got = bf16[8,128,128]{2,1,0:T(8,128)(2,1)S(1)} collective-permute-done((bf16[8,128,128]{2,1,0:T(8,128)(2,1)S(1)}, bf16[8,128,128]{2,1,0:T(8,128)(2,1)S(1)}, u32[]{:S(2)}, u32[]{:S(2)}) %collective-permute-start.11) | collective-permute-done | bytes 262176 | tf_op jit(solution)/shard_map/ppermute | solution.py:408
  178.2 24.2 %all_to_all.22.got = bf16[8,128,128]{2,1,0:T(8,128)(2,1)S(1)} all-to-all(bf16[8,128,128]{2,1,0:T(8,128)(2,1)S(1)} %add.105), channel_id=1, replica_groups={{0,8,16,24,32,40,48,56},{1,9,17,25,33,41,49,57},{2,10,18,26,34,42,50,58..., dimensions={0} | all-to-all | bytes 524288 | tf_op jit(solution)/shard_map/all_to_all | solution.py:420
  202.4 0.6 finish.1
  203.1 6.7 %collective-permute-start.12 = (bf16[64,128]{1,0:T(8,128)(2,1)S(1)}, bf16[64,128]{1,0:T(8,128)(2,1)S(1)}, u32[]{:S(2)}, u32[]{:S(2)}) collective-permute-start(bf16[64,128]{1,0:T(8,128)(2,1)S(1)} %get-tuple-element.40), channel_id=1, source_target_pairs={{0,1},{1,0},{2,3},{3,2},{4,5},{5,4},{6,7},{7,6},{8,9},{9,8},{10,11... | collective-permute-start | bytes 49160 | tf_op jit(solution)/shard_map/ppermute | solution.py:408
  209.8 0.8 collective-permute-done.12
  210.6 0.6 fusion
  (54 shorter events, 0.4 us)
Async XLA Ops:
  7.2 13.4 %copy-start.22 = (s32[2]{0:T(128)S(1)}, s32[2]{0:T(128)}, u32[]{:S(2)}) copy-start(s32[2]{0:T(128)} %param.14) | copy-start | bytes 28
  9.9 11.9 %copy-start.19 = (f32[8,128]{1,0:T(8,128)S(1)}, f32[8,128]{1,0:T(8,128)}, u32[]{:S(2)}) copy-start(f32[8,128]{1,0:T(8,128)} %get-tuple-element.22.after) | copy-start | bytes 12292
  9.9 23.5 %all-to-all-start = ((bf16[8,160,512]{2,1,0:T(8,128)(2,1)}), bf16[8,160,512]{2,1,0:T(8,128)(2,1)S(1)}, u32[]{:S(2)}, u32[]{:S(2)}) async-start(bf16[8,160,512]{2,1,0:T(8,128)(2,1)} %get-tuple-element.24), calls=%async_computation | async-start | bytes 2621440 | tf_op jit(solution)/shard_map/all_to_all | solution.py:451
  15.8 122.2 %all-gather.6.cloned.1.call-start = ((), (), s32[]{:S(2)}) async-start(), calls=%async_computation.4 | async-start | bytes 3440640 | tf_op jit(solution)/shard_map/all_gather | solution.py:416
  15.8 21.9 %collective-permute-start.6 = (bf16[224,512]{1,0:T(8,128)(2,1)}, bf16[224,512]{1,0:T(8,128)(2,1)}, u32[]{:S(2)}, u32[]{:S(2)}) collective-permute-start(bf16[224,512]{1,0:T(8,128)(2,1)} %bitcast.19.narrow), channel_id=1, source_target_pairs={{0,2},{1,3},{2,0},{3,1},{4,6},{5,7},{6,4},{7,5},{8,10},{9,11},{10,... | collective-permute-start | bytes 688136 | tf_op jit(solution)/shard_map/ppermute | solution.py:408
  20.5 17.2 %copy-start.10 = (s32[7]{0:T(128)}, s32[7]{0:T(128)S(1)}, u32[]{:S(2)}) copy-start(s32[7]{0:T(128)S(1)} %stack.31.at) | copy-start | bytes 88
  21.8 0.7 copy-start.18
  26.0 0.6 copy-start.16
  33.4 0.9 copy-start.4
  34.3 3.5 %copy-start.7 = (bf16[512,224]{0,1:T(8,128)(2,1)S(1)}, bf16[512,224]{0,1:T(8,128)(2,1)}, u32[]{:S(2)}) copy-start(bf16[512,224]{0,1:T(8,128)(2,1)} %param.21) | copy-start | bytes 688132
  34.3 3.5 %copy-start.8 = (bf16[512,224]{0,1:T(8,128)(2,1)S(1)}, bf16[512,224]{0,1:T(8,128)(2,1)}, u32[]{:S(2)}) copy-start(bf16[512,224]{0,1:T(8,128)(2,1)} %param.22) | copy-start | bytes 688132
  35.7 2.0 copy-start.3
  35.7 29.1 %copy-start.20 = (s32[2]{0:T(128)S(1)}, s32[2]{0:T(128)}, u32[]{:S(2)}) copy-start(s32[2]{0:T(128)} %lengths.1) | copy-start | bytes 28
  35.8 64.0 %copy-start.17 = (bf16[64,256]{1,0:T(8,128)(2,1)S(1)}, bf16[64,256]{1,0:T(8,128)(2,1)}, u32[]{:S(2)}) copy-start(bf16[64,256]{1,0:T(8,128)(2,1)} %copy-done.16) | copy-start | bytes 98308
  40.6 108.6 %all-gather.8.cloned.1.call-start = ((), (), s32[]{:S(2)}) async-start(), calls=%async_computation.5 | async-start | bytes 3440640 | tf_op jit(solution)/shard_map/all_gather | solution.py:416
  52.5 94.3 %copy-start.9 = (f32[4096]{0:T(1024)S(1)}, f32[4096]{0:T(1024)}, u32[]{:S(2)}) copy-start(f32[4096]{0:T(1024)} %param.20) | copy-start | bytes 49156
  52.5 49.1 %collective-permute-start.8 = (bf16[672,512]{1,0:T(8,128)(2,1)}, bf16[672,512]{1,0:T(8,128)(2,1)S(1)}, u32[]{:S(2)}, u32[]{:S(2)}) collective-permute-start(bf16[672,512]{1,0:T(8,128)(2,1)} %join.1), channel_id=1, source_target_pairs={{0,256},{64,320},{128,384},{192,448},{256,0},{320,64},{384,128},{4... | collective-permute-start | bytes 2064392 | tf_op jit(solution)/shard_map/ppermute | solution.py:412
  54.8 44.9 %collective-permute-start = (bf16[8,64,512]{2,1,0:T(8,128)(2,1)S(1)}, bf16[8,64,512]{2,1,0:T(8,128)(2,1)S(1)}, u32[]{:S(2)}, u32[]{:S(2)}) collective-permute-start(bf16[8,64,512]{2,1,0:T(8,128)(2,1)S(1)} %slice.4.mine), channel_id=1, source_target_pairs={{0,1},{1,0},{2,3},{3,2},{4,5},{5,4},{6,7},{7,6},{8,9},{9,8},{10,11... | collective-permute-start | bytes 1572872 | tf_op jit(solution)/shard_map/ppermute | solution.py:408
  57.9 41.8 %collective-permute-start.1 = (bf16[8,64,512]{2,1,0:T(8,128)(2,1)S(1)}, bf16[8,64,512]{2,1,0:T(8,128)(2,1)S(1)}, u32[]{:S(2)}, u32[]{:S(2)}) collective-permute-start(bf16[8,64,512]{2,1,0:T(8,128)(2,1)S(1)} %slice.4.mine), channel_id=1, source_target_pairs={{0,2},{1,3},{2,0},{3,1},{4,6},{5,7},{6,4},{7,5},{8,10},{9,11},{10,... | collective-permute-start | bytes 1572872 | tf_op jit(solution)/shard_map/ppermute | solution.py:408
  61.1 38.6 %collective-permute-start.2 = (bf16[8,64,512]{2,1,0:T(8,128)(2,1)S(1)}, bf16[8,64,512]{2,1,0:T(8,128)(2,1)S(1)}, u32[]{:S(2)}, u32[]{:S(2)}) collective-permute-start(bf16[8,64,512]{2,1,0:T(8,128)(2,1)S(1)} %slice.4.mine), channel_id=1, source_target_pairs={{0,3},{1,2},{2,1},{3,0},{4,7},{5,6},{6,5},{7,4},{8,11},{9,10},{10,... | collective-permute-start | bytes 1572872 | tf_op jit(solution)/shard_map/ppermute | solution.py:408
  64.9 0.6 copy-start.11
  99.7 0.6 copy-start.12
  101.6 0.8 copy-start.21
  128.0 18.0 %collective-permute-start.3 = (bf16[8,64,256]{2,1,0:T(8,128)(2,1)S(1)}, bf16[8,64,256]{2,1,0:T(8,128)(2,1)S(1)}, u32[]{:S(2)}, u32[]{:S(2)}) collective-permute-start(bf16[8,64,256]{2,1,0:T(8,128)(2,1)S(1)} %all_to_all.21.same), channel_id=1, source_target_pairs={{0,4},{1,5},{2,6},{3,7},{4,0},{5,1},{6,2},{7,3},{8,12},{9,13},{10,... | collective-permute-start | bytes 786440 | tf_op jit(solution)/shard_map/ppermute | solution.py:408
  130.7 18.5 %collective-permute-start.4 = (bf16[8,64,256]{2,1,0:T(8,128)(2,1)S(1)}, bf16[8,64,256]{2,1,0:T(8,128)(2,1)}, u32[]{:S(2)}, u32[]{:S(2)}) collective-permute-start(bf16[8,64,256]{2,1,0:T(8,128)(2,1)S(1)} %all_to_all.21.same), channel_id=1, source_target_pairs={{0,2},{1,3},{2,0},{3,1},{4,6},{5,7},{6,4},{7,5},{8,10},{9,11},{10,... | collective-permute-start | bytes 786440 | tf_op jit(solution)/shard_map/ppermute | solution.py:408
  135.2 14.1 %collective-permute-start.5 = (bf16[8,64,256]{2,1,0:T(8,128)(2,1)S(1)}, bf16[8,64,256]{2,1,0:T(8,128)(2,1)}, u32[]{:S(2)}, u32[]{:S(2)}) collective-permute-start(bf16[8,64,256]{2,1,0:T(8,128)(2,1)S(1)} %all_to_all.21.same), channel_id=1, source_target_pairs={{0,6},{1,7},{2,4},{3,5},{4,2},{5,3},{6,0},{7,1},{8,14},{9,15},{10,... | collective-permute-start | bytes 786440 | tf_op jit(solution)/shard_map/ppermute | solution.py:408
  138.0 15.0 %collective-permute-start.7 = (bf16[4,672,512]{2,1,0:T(8,128)(2,1)}, bf16[4,672,512]{2,1,0:T(8,128)(2,1)S(1)}, u32[]{:S(2)}, u32[]{:S(2)}) collective-permute-start(bf16[4,672,512]{2,1,0:T(8,128)(2,1)} %bitcast.28), channel_id=1, source_target_pairs={{0,1},{1,0},{2,3},{3,2},{4,5},{5,4},{6,7},{7,6},{8,9},{9,8},{10,11... | collective-permute-start | bytes 8257544 | tf_op jit(solution)/shard_map/ppermute | solution.py:408
  146.1 0.7 copy-start.5
  146.8 1.0 copy-start.6
  147.8 0.6 copy-start.13
  149.3 8.8 %copy-start = (bf16[2688,512]{1,0:T(8,128)(2,1)S(1)}, bf16[2688,512]{1,0:T(8,128)(2,1)}, u32[]{:S(2)}) copy-start(bf16[2688,512]{1,0:T(8,128)(2,1)} %all-gather.8.cloned.1.call-done) | copy-start | bytes 8257540
  149.3 8.7 %collective-permute-start.9 = (bf16[4,672,512]{2,1,0:T(8,128)(2,1)}, bf16[4,672,512]{2,1,0:T(8,128)(2,1)S(1)}, u32[]{:S(2)}, u32[]{:S(2)}) collective-permute-start(bf16[4,672,512]{2,1,0:T(8,128)(2,1)} %bitcast.25), channel_id=1, source_target_pairs={{0,1},{1,0},{2,3},{3,2},{4,5},{5,4},{6,7},{7,6},{8,9},{9,8},{10,11... | collective-permute-start | bytes 8257544 | tf_op jit(solution)/shard_map/ppermute | solution.py:408
  153.0 1.8 copy-start.1
  154.8 0.6 copy-start.14
  158.0 10.2 %copy-start.2 = (bf16[2688,512]{1,0:T(8,128)(2,1)S(1)}, bf16[2688,512]{1,0:T(8,128)(2,1)}, u32[]{:S(2)}) copy-start(bf16[2688,512]{1,0:T(8,128)(2,1)} %all-gather.6.cloned.1.call-done) | copy-start | bytes 8257540
  159.9 42.5 %copy-start.15 = (s32[7]{0:T(128)S(1)}, s32[7]{0:T(128)}, u32[]{:S(2)}) copy-start(s32[7]{0:T(128)} %copy-done.10) | copy-start | bytes 88
  160.0 8.3 %collective-permute-start.10 = (bf16[2,128,224]{2,1,0:T(8,128)(2,1)S(1)}, bf16[2,128,224]{2,1,0:T(8,128)(2,1)S(1)}, u32[]{:S(2)}, u32[]{:S(2)}) collective-permute-start(bf16[2,128,224]{2,1,0:T(8,128)(2,1)S(1)} %partner_rows.1.units), channel_id=1, source_target_pairs={{0,2},{1,3},{2,0},{3,1},{4,6},{5,7},{6,4},{7,5},{8,10},{9,11},{10,... | collective-permute-start | bytes 344072 | tf_op jit(solution)/shard_map/ppermute | solution.py:408
  169.5 8.6 %collective-permute-start.11 = (bf16[8,128,128]{2,1,0:T(8,128)(2,1)S(1)}, bf16[8,128,128]{2,1,0:T(8,128)(2,1)S(1)}, u32[]{:S(2)}, u32[]{:S(2)}) collective-permute-start(bf16[8,128,128]{2,1,0:T(8,128)(2,1)S(1)} %get-tuple-element.37), channel_id=1, source_target_pairs={{0,4},{1,5},{2,6},{3,7},{4,0},{5,1},{6,2},{7,3},{8,12},{9,13},{10,... | collective-permute-start | bytes 786440 | tf_op jit(solution)/shard_map/ppermute | solution.py:408
  203.1 7.5 %collective-permute-start.12 = (bf16[64,128]{1,0:T(8,128)(2,1)S(1)}, bf16[64,128]{1,0:T(8,128)(2,1)S(1)}, u32[]{:S(2)}, u32[]{:S(2)}) collective-permute-start(bf16[64,128]{1,0:T(8,128)(2,1)S(1)} %get-tuple-element.40), channel_id=1, source_target_pairs={{0,1},{1,0},{2,3},{3,2},{4,5},{5,4},{6,7},{7,6},{8,9},{9,8},{10,11... | collective-permute-start | bytes 49160 | tf_op jit(solution)/shard_map/ppermute | solution.py:408
Sparse Core Ops, SparseCore 0:
  40.7 47.5 all-gather.5
  102.6 42.4 all-gather.7

commit v9 on v8

--- a/solution.py
+++ b/solution.py
@@ -36,6 +36,11 @@
 SMEM = pl.BlockSpec(memory_space=pltpu.SMEM)
 
 
+def place():
+    d = lax.axis_index("dev")
+    return (d % 2, d // 2 % 2, d // 4, d // 4 % 2, d // 8, d % 4, lax.axis_index("grp") // 4)
+
+
 def nt(a, b):
     return lax.dot_general(a, b, (((1,), (1,)), ((), ())), preferred_element_type=F32)
 
@@ -52,14 +57,19 @@
     return pl.CostEstimate(flops=flops, bytes_accessed=nbytes, transcendentals=0)
 
 
-def project_kernel(normed, weights, cos, sin, send, keys, values):
+def project_kernel(normed, weights, cos, sin, send, keys, values, tables, sems):
+    copies = [pltpu.make_async_copy(ref, tables.at[i], sems.at[i]) for i, ref in enumerate((cos, sin))]
+    for copy in copies:
+        copy.start()
     total = jnp.zeros((256, 96), F32)
     for g in range(GROUPS):
         total = total + nt(normed[g], weights[g, 0:96, :])
     total = jnp.concatenate([total, jnp.zeros((256, 32), F32)], axis=1)
     lane = lax.broadcasted_iota(jnp.int32, (256, 128), 1)
     partner = jnp.where(lane % 2 == 0, -pltpu.roll(total, 127, 1), pltpu.roll(total, 1, 1))
-    turned = jnp.where(lane < QC + KC, total * cos[...] + partner * sin[...], total)
+    for copy in copies:
+        copy.wait()
+    turned = jnp.where(lane < QC + KC, total * tables[0] + partner * tables[1], total)
     turned = turned.astype(BF).astype(F32)
     flipped = turned.T
     keys[...] = flipped[QC : QC + KC, :].astype(BF)
@@ -75,7 +85,8 @@
                 send[zl * 4 + yhi * 2 + c] = chunk.astype(BF)
 
 
-def attend_kernel(at, lengths, got, out):
+def attend_kernel(lengths, got, out):
+    at = place()
     lane = lax.broadcasted_iota(jnp.int32, (HALF, 128), 1)
     pieces = [got[m].astype(F32) for m in range(8)]
 
@@ -101,7 +112,8 @@
         out[:, a * 128 : a * 128 + 128] = mixed
 
 
-def output_kernel(at, got, mine, core, far, cross, own, out):
+def output_kernel(got, mine, core, far, cross, own, out):
+    at = place()
     parts = []
     for w in (mine, core, far, cross):
         total = jnp.zeros((HALF, QC), F32)
@@ -135,7 +147,8 @@
             out[i, :, k * BAND : (k + 1) * BAND] = (x * scale * gain[:, z * BAND : (z + 1) * BAND]).astype(BF)
 
 
-def near_kernel(at, same, other, gain, out):
+def near_kernel(same, other, gain, out):
+    at = place()
     renorm(at, same, other, gain, out)
 
 
@@ -148,7 +161,8 @@
             totals[2 * i + 1] = totals[2 * i + 1] + nt(rows, w[x, FC : 2 * FC, :])
 
 
-def own_rows_kernel(at, near, same, far_same, far_other, gain, mine, core, out, kept, normed):
+def own_rows_kernel(near, same, far_same, far_other, gain, mine, core, out, kept, normed):
+    at = place()
     low = at[1] == 0
     lanes = pl.ds(pl.multiple_of(at[1] * 128, 128), 128)
     near_kept, far_kept = same[at[4], :, lanes], far_same[at[4], :, lanes]
@@ -161,7 +175,8 @@
         out[i] = totals[i]
 
 
-def partner_rows_kernel(at, near, far, before, mine, core, out):
+def partner_rows_kernel(near, far, before, mine, core, out):
+    at = place()
     totals = [before[i] for i in range(4)]
     multiply(at, near, far, (mine, core), 1, totals)
     low = at[1] == 0
@@ -173,7 +188,8 @@
         out[i, HALF : 2 * HALF, :] = jnp.where(low, second, first)
 
 
-def down_kernel(at, units, far_units, mine, mine_lo, core, core_lo, keep, give):
+def down_kernel(units, far_units, mine, mine_lo, core, core_lo, keep, give):
+    at = place()
     low = at[3] == 0
     for x in range(4):
         for side, pair in enumerate(((mine, core), (mine_lo, core_lo))):
@@ -192,7 +208,8 @@
         out[i] = (keep[i] + got[i].astype(F32)).astype(BF)
 
 
-def finish_kernel(at, got, kept, keep, give):
+def finish_kernel(got, kept, keep, give):
+    at = place()
     total = kept[...].astype(F32)
     for i in range(8):
         total = total + got[i].astype(F32)
@@ -220,7 +237,8 @@
         copy.wait()
 
 
-def norm_kernel(at, after, tables, stream, gain, normed, own, held, gains, sems):
+def norm_kernel(after, tables, stream, gain, normed, own, held, gains, sems):
+    at = place()
     copies = [
         pltpu.make_async_copy(stream, held, sems.at[0]),
         pltpu.make_async_copy(gain, gains, sems.at[1]),
@@ -238,19 +256,20 @@
     own[...] = held[rows, pl.ds(pl.multiple_of(at[2] * BAND, BAND), BAND)]
 
 
-def norm(at, after, tables, stream, gain):
+def norm(after, tables, stream, gain):
     return pl.pallas_call(
         norm_kernel,
         out_shape=(jax.ShapeDtypeStruct((GROUPS, 256, RUN), BF), jax.ShapeDtypeStruct((HALF, BAND), BF)),
-        in_specs=[SMEM, ANY, ANY, HBM, HBM],
+        in_specs=[ANY, ANY, HBM, HBM],
         out_specs=(VMEM,) * 2,
         scratch_shapes=[pltpu.VMEM((256, D), BF), pltpu.VMEM((1, D), F32), pltpu.SemaphoreType.DMA((2,))],
-        compiler_params=params(50),
+        compiler_params=params(44),
         name="norm",
-    )(at, after, tables, stream, gain)
-
-
-def join_kernel(at, after, gate, up, narrow, got, out, held, sems):
+    )(after, tables, stream, gain)
+
+
+def join_kernel(after, gate, up, narrow, got, out, held, sems):
+    at = place()
     copies = [
         pltpu.make_async_copy(narrow, held, sems.at[0]),
         pltpu.make_async_copy(gate, out.at[pl.ds(0, FC), :], sems.at[1]),
@@ -270,16 +289,16 @@
     copies[2].wait()
 
 
-def join(at, after, gate, up, narrow, got):
+def join(after, gate, up, narrow, got):
     return pl.pallas_call(
         join_kernel,
         out_shape=jax.ShapeDtypeStruct((3 * FC, RUN), BF),
-        in_specs=[SMEM, ANY, HBM, HBM, HBM, VMEM],
+        in_specs=[ANY, HBM, HBM, HBM, VMEM],
         out_specs=VMEM,
         scratch_shapes=[pltpu.VMEM((FC, RUN), BF), pltpu.SemaphoreType.DMA((3,))],
         compiler_params=params(48),
         name="join",
-    )(at, after, gate, up, narrow, got)
+    )(after, gate, up, narrow, got)
 
 
 def pack(*parts):
@@ -302,47 +321,48 @@
             jax.ShapeDtypeStruct((KC, 256), BF),
             jax.ShapeDtypeStruct((KC, 256), BF),
         ),
-        in_specs=[VMEM] * 4,
+        in_specs=[VMEM] * 2 + [HBM] * 2,
         out_specs=(VMEM,) * 3,
+        scratch_shapes=[pltpu.VMEM((2, 256, 128), F32), pltpu.SemaphoreType.DMA((2,))],
         compiler_params=params(24),
         name="project",
     )(normed, weights, cos, sin)
 
 
-def attend(at, lengths, got):
+def attend(lengths, got):
     return pl.pallas_call(
         attend_kernel,
         out_shape=jax.ShapeDtypeStruct((HALF, BAND), BF),
-        in_specs=[SMEM, SMEM, VMEM],
+        in_specs=[SMEM, VMEM],
         out_specs=VMEM,
         compiler_params=params(16),
         name="attend",
-    )(at, lengths, got)
-
-
-def output(at, got, weights, own):
+    )(lengths, got)
+
+
+def output(got, weights, own):
     return pl.pallas_call(
         output_kernel,
         out_shape=jax.ShapeDtypeStruct((8, HALF, BAND), BF),
-        in_specs=[SMEM] + [VMEM] * 6,
+        in_specs=[VMEM] * 6,
         out_specs=VMEM,
         compiler_params=params(24),
         name="output",
-    )(at, got, *weights, own)
-
-
-def near_half(at, same, other, gain):
+    )(got, *weights, own)
+
+
+def near_half(same, other, gain):
     return pl.pallas_call(
         near_kernel,
         out_shape=jax.ShapeDtypeStruct((GROUPS, HALF, RUN), BF),
-        in_specs=[SMEM] + [VMEM] * 3,
+        in_specs=[VMEM] * 3,
         out_specs=VMEM,
         compiler_params=params(16),
         name="near_half",
-    )(at, same, other, gain)
-
-
-def own_rows(at, near, same, far_same, far_other, gain, mine, core):
+    )(same, other, gain)
+
+
+def own_rows(near, same, far_same, far_other, gain, mine, core):
     return pl.pallas_call(
         own_rows_kernel,
         out_shape=(
@@ -350,36 +370,36 @@
             jax.ShapeDtypeStruct((128, 128), BF),
             jax.ShapeDtypeStruct((GROUPS, HALF, RUN), BF),
         ),
-        in_specs=[SMEM] + [VMEM] * 7,
+        in_specs=[VMEM] * 7,
         out_specs=(VMEM,) * 3,
         compiler_params=params(16),
         cost_estimate=cost(2 * HALF * D * 4 * FC, 4 * 2**20),
         name="own_rows",
-    )(at, near, same, far_same, far_other, gain, mine, core)
-
-
-def partner_rows(at, near, far, before, mine, core):
+    )(near, same, far_same, far_other, gain, mine, core)
+
+
+def partner_rows(near, far, before, mine, core):
     return pl.pallas_call(
         partner_rows_kernel,
         out_shape=jax.ShapeDtypeStruct((2, 128, FC), BF),
-        in_specs=[SMEM] + [VMEM] * 5,
+        in_specs=[VMEM] * 5,
         out_specs=VMEM,
         compiler_params=params(16),
         cost_estimate=cost(2 * HALF * D * 4 * FC, 4 * 2**20),
         name="partner_rows",
-    )(at, near, far, before, mine, core)
-
-
-def down(at, units, far_units, weights):
+    )(near, far, before, mine, core)
+
+
+def down(units, far_units, weights):
     return pl.pallas_call(
         down_kernel,
         out_shape=(jax.ShapeDtypeStruct((8, 128, 128), F32), jax.ShapeDtypeStruct((8, 128, 128), BF)),
-        in_specs=[SMEM] + [VMEM] * 6,
+        in_specs=[VMEM] * 6,
         out_specs=(VMEM, VMEM),
         compiler_params=params(16),
         cost_estimate=cost(4 * HALF * D * 2 * FC, 5 * 2**20),
         name="down",
-    )(at, units, far_units, *weights)
+    )(units, far_units, *weights)
 
 
 def add(keep, got):
@@ -393,15 +413,15 @@
     )(keep, got)
 
 
-def finish(at, got, kept):
+def finish(got, kept):
     return pl.pallas_call(
         finish_kernel,
         out_shape=(jax.ShapeDtypeStruct((QC, 128), BF),) * 2,
-        in_specs=[SMEM] + [VMEM] * 2,
+        in_specs=[VMEM] * 2,
         out_specs=(VMEM, VMEM),
         compiler_params=params(16),
         name="finish",
-    )(at, got, kept)
+    )(got, kept)
 
 
 def swap(x, bits):
@@ -443,9 +463,7 @@
     w_down,
 ):
     member = lax.axis_index("dev")
-    core, yhi, z, quad = member % 2, member // 2 % 2, member // 4, member % 4
-    ylo = lax.axis_index("grp") // 4
-    at = jnp.stack([core, yhi, z, z % 2, z // 2, quad, ylo]).astype(jnp.int32)
+    core = member % 2
 
     packed, token = pack(w_query.T, w_key.T, w_value.T, w_out.T)
     first = lax.all_to_all(packed, "grp", 0, 0, tiled=True)
@@ -458,33 +476,33 @@
     angle = positions.astype(F32)[:, None] * freq[None, :]
     cos, sin = jnp.cos(angle), jnp.sin(angle)
 
-    normed, own = norm(at, token, cos, stream, attn_gain.reshape(1, D))
+    normed, own = norm(token, cos, stream, attn_gain.reshape(1, D))
     narrow = after(w_down.T, token)
     other = swap(narrow, 2)
 
     send, keys, values = project(normed, first, cos, sin)
     got = trade(send, OCTETS)
-    mine = join(at, send, w_gate.T, w_up.T, narrow, other)
+    mine = join(send, w_gate.T, w_up.T, narrow, other)
     mine_lo = swap_groups(after(mine, got))
     out_own = first[:, 96:160, :]
     out_weights = (out_own, swap(out_own, 1), swap(out_own, 2), swap(out_own, 3))
-    mixed = collect(attend(at, row_length, got))
-    attended = output(at, mixed, out_weights, own)
+    mixed = collect(attend(row_length, got))
+    attended = output(mixed, out_weights, own)
     mine, mine_lo = collect_x(mine), collect_x(after(mine_lo, attended))
     mine = after(mine, attended)
     core_mine = swap(mine, 1)
     same = trade(attended, PARITIES)
     other, far_same, far_other = swap(same, 4), swap(same, 2), swap(same, 6)
     gain = ffn_gain.reshape(1, D)
-    near = near_half(at, same, other, gain)
+    near = near_half(same, other, gain)
     mine_lo = after(mine_lo, (far_same, far_other, near))
     core_lo = swap(mine_lo, 1)
-    totals, kept, far_normed = own_rows(at, near, same, far_same, far_other, gain, mine, core_mine)
-    units = partner_rows(at, near, far_normed, totals, mine_lo, core_lo)
+    totals, kept, far_normed = own_rows(near, same, far_same, far_other, gain, mine, core_mine)
+    units = partner_rows(near, far_normed, totals, mine_lo, core_lo)
     weights = (mine, mine_lo, core_mine, core_lo)
-    keep, give = down(at, units, swap(units, 2), weights)
+    keep, give = down(units, swap(units, 2), weights)
     sums = trade(add(keep, swap(give, 4)), PARITIES)
-    keep, give = finish(at, sums, kept)
+    keep, give = finish(sums, kept)
     give = swap(give, 1)
     rows = jnp.where(core == 0, jnp.concatenate([keep, give], axis=1), jnp.concatenate([give, keep], axis=1))
     return (keys.T, values.T, rows.T)

time: 219 us -> 216 us (0.986)
  Pallas kernels: 20.4 us -> 16 us
    unnamed x46 -> x36, local copies, waits for them, and re-layouts: 8.9 us -> 8.72 us
  transfers between devices with their start and end apart: 16 -> 16, of which waited for: 5 -> 6; matrix products, arithmetic and copies ran while one was open for 1% -> 1% of each run, Pallas kernels for 5% -> 4%
where the time goes in v9:
time: 216 us; the launch traced here: 215 us
  blocking collectives  94.5 us (44%)
  starting transfers between devices  59.3 us (27%)
  waiting for transfers between devices  19.8 us (9%)
  Pallas kernels  16 us (7%)
  between operations  14.4 us (7%)
  local copies, waits for them, and re-layouts  8.75 us (4%)
    all_to_all x3, blocking collectives, trade(): return lax.all_to_all(x, 'dev', 0, 0, axis_index_groups=groups, tiled=True)  61.1 us
    ppermute x12, starting transfers between devices, swap(): return lax.ppermute(x, 'dev', [(d, d ^ bits) for d in range(MEMBERS)])  50.9 us
    all_gather x1, blocking collectives, collect(): return lax.all_gather(x, 'dev', axis=0, axis_index_groups=COLUMNS)  33.3 us
    ppermute x12, waiting for transfers between devices, swap(): return lax.ppermute(x, 'dev', [(d, d ^ bits) for d in range(MEMBERS)])  12.3 us
    unnamed x36, local copies, waits for them, and re-layouts  8.72 us
    all_to_all x1, waiting for transfers between devices, on_device(): first = lax.all_to_all(packed, 'grp', 0, 0, tiled=True)  7.42 us
    all_to_all x1, starting transfers between devices, on_device(): first = lax.all_to_all(packed, 'grp', 0, 0, tiled=True)  5.87 us
  transfers between devices with their start and end apart: 16, of which 6 were waited for; matrix products, arithmetic and copies ran while one was open for 1% of the time, Pallas kernels for 4%

profile of v9, /device:TPU:1, one launch (start us, length us, event | category | flops | bytes accessed | tf_op | source)
XLA Modules:
  0.0 214.7 jit_solution(18380748453497424823)
XLA Ops:
  7.2 2.7 %pack.1 = (bf16[8,160,512]{2,1,0:T(8,128)(2,1)}, f32[8,128]{1,0:T(8,128)}) custom-call(bf16[64,512]{1,0:T(8,128)(2,1)} %bitcast.30, bf16[16,512]{1,0:T(8,128)(2,1)} %bitcast.32, bf16[16,512]{1,0:T(8,128)(2,1)} %bitcast.33, bf16[64,512]{1,0:T(8,128)(2,1)} %bitcast.31), custom_call_target="tpu_custom_call" | custom-call | tf_op jit(solution)/shard_map/pack/pallas_call | solution.py:305
  9.9 5.9 %all-to-all-start = ((bf16[8,160,512]{2,1,0:T(8,128)(2,1)}), bf16[8,160,512]{2,1,0:T(8,128)(2,1)S(1)}, u32[]{:S(2)}, u32[]{:S(2)}) async-start(bf16[8,160,512]{2,1,0:T(8,128)(2,1)} %get-tuple-element.24), calls=%async_computation | async-start | bytes 2621440 | tf_op jit(solution)/shard_map/all_to_all | solution.py:469
  15.8 4.5 %collective-permute-start.6 = (bf16[224,512]{1,0:T(8,128)(2,1)}, bf16[224,512]{1,0:T(8,128)(2,1)}, u32[]{:S(2)}, u32[]{:S(2)}) collective-permute-start(bf16[224,512]{1,0:T(8,128)(2,1)} %bitcast.12.narrow), channel_id=1, source_target_pairs={{0,2},{1,3},{2,0},{3,1},{4,6},{5,7},{6,4},{7,5},{8,10},{9,11},{10,... | collective-permute-start | bytes 688136 | tf_op jit(solution)/shard_map/ppermute | solution.py:428
  20.4 0.1 convert_bitcast_fusion
  20.5 1.2 multiply_sine_fusion
  21.7 1.6 copy-done.3
  23.3 0.7 copy-done.14
  24.0 1.4 norm.1
  25.4 0.6 copy-done.11
  26.0 7.4 %all-to-all-done.weights = bf16[8,160,512]{2,1,0:T(8,128)(2,1)S(1)} async-done(((bf16[8,160,512]{2,1,0:T(8,128)(2,1)}), bf16[8,160,512]{2,1,0:T(8,128)(2,1)S(1)}, u32[]{:S(2)}, u32[]{:S(2)}) %all-to-all-start) | async-done | bytes 1310752 | tf_op jit(solution)/shard_map/all_to_all | solution.py:469
  33.4 0.9 copy-done.4
  34.3 1.8 project.1
  36.2 1.6 collective-permute-done.6.got
  37.8 2.8 %join.1 = bf16[672,512]{1,0:T(8,128)(2,1)} custom-call(bf16[8,64,128]{2,1,0:T(8,128)(2,1)S(1)} %get-tuple-element.27.after, bf16[224,512]{1,0:T(8,128)(2,1)S(1)} %bitcast.25, bf16[224,512]{1,0:T(8,128)(2,1)S(1)} %bitcast.26, bf16[224,512]{1,0:T(8,128)(2,1)} %bitcast.12.narrow, bf16[224,512]{1,0:T(8,128)(2,1)} %collective-permute-done.6.got), custom_call_target="tpu_custom_call" | custom-call | tf_op jit(solution)/shard_map/join/pallas_call | solution.py:293
  40.6 0.6 copy-done.5
  41.3 0.0 all-gather.8.cloned.1.call-start
  41.3 11.7 %all_to_all.20.got = bf16[8,64,128]{2,1,0:T(8,128)(2,1)S(1)} all-to-all(bf16[8,64,128]{2,1,0:T(8,128)(2,1)} %copy-done.5), channel_id=1, replica_groups={{0,1,2,3,4,5,6,7},{8,9,10,11,12,13,14,15},{16,17,18,19,20,21,22,23},{24..., dimensions={0} | all-to-all | bytes 262144 | tf_op jit(solution)/shard_map/all_to_all | solution.py:440
  53.0 2.4 %collective-permute-start.8 = (bf16[672,512]{1,0:T(8,128)(2,1)}, bf16[672,512]{1,0:T(8,128)(2,1)S(1)}, u32[]{:S(2)}, u32[]{:S(2)}) collective-permute-start(bf16[672,512]{1,0:T(8,128)(2,1)} %join.1), channel_id=1, source_target_pairs={{0,256},{64,320},{128,384},{192,448},{256,0},{320,64},{384,128},{4... | collective-permute-start | bytes 2064392 | tf_op jit(solution)/shard_map/ppermute | solution.py:432
  55.4 3.1 %collective-permute-start = (bf16[8,64,512]{2,1,0:T(8,128)(2,1)S(1)}, bf16[8,64,512]{2,1,0:T(8,128)(2,1)S(1)}, u32[]{:S(2)}, u32[]{:S(2)}) collective-permute-start(bf16[8,64,512]{2,1,0:T(8,128)(2,1)S(1)} %slice.4.mine), channel_id=1, source_target_pairs={{0,1},{1,0},{2,3},{3,2},{4,5},{5,4},{6,7},{7,6},{8,9},{9,8},{10,11... | collective-permute-start | bytes 1572872 | tf_op jit(solution)/shard_map/ppermute | solution.py:428
  58.5 3.1 %collective-permute-start.1 = (bf16[8,64,512]{2,1,0:T(8,128)(2,1)S(1)}, bf16[8,64,512]{2,1,0:T(8,128)(2,1)S(1)}, u32[]{:S(2)}, u32[]{:S(2)}) collective-permute-start(bf16[8,64,512]{2,1,0:T(8,128)(2,1)S(1)} %slice.4.mine), channel_id=1, source_target_pairs={{0,2},{1,3},{2,0},{3,1},{4,6},{5,7},{6,4},{7,5},{8,10},{9,11},{10,... | collective-permute-start | bytes 1572872 | tf_op jit(solution)/shard_map/ppermute | solution.py:428
  61.7 3.8 %collective-permute-start.2 = (bf16[8,64,512]{2,1,0:T(8,128)(2,1)S(1)}, bf16[8,64,512]{2,1,0:T(8,128)(2,1)S(1)}, u32[]{:S(2)}, u32[]{:S(2)}) collective-permute-start(bf16[8,64,512]{2,1,0:T(8,128)(2,1)S(1)} %slice.4.mine), channel_id=1, source_target_pairs={{0,3},{1,2},{2,1},{3,0},{4,7},{5,6},{6,5},{7,4},{8,11},{9,10},{10,... | collective-permute-start | bytes 1572872 | tf_op jit(solution)/shard_map/ppermute | solution.py:428
  65.5 1.4 attend.1
  66.9 33.3 %all-gather = bf16[1024,256]{1,0:T(8,128)(2,1)S(1)} all-gather(bf16[64,256]{1,0:T(8,128)(2,1)S(1)} %attend.1), channel_id=2, replica_groups={{0,4,8,12,16,20,24,28,32,36,40,44,48,52,56,60},{1,5,9,13,17,21,25,29,33..., dimensions={0}, use_global_device_ids=true | all-gather | bytes 557056 | tf_op jit(solution)/shard_map/all_gather | solution.py:444
  100.3 0.8 output.1
  101.1 0.8 copy-done.16
  101.9 25.7 %all_to_all.21.same = bf16[8,64,256]{2,1,0:T(8,128)(2,1)S(1)} all-to-all(bf16[8,64,256]{2,1,0:T(8,128)(2,1)S(1)} %output.1), channel_id=1, replica_groups={{0,8,16,24,32,40,48,56},{1,9,17,25,33,41,49,57},{2,10,18,26,34,42,50,58..., dimensions={0} | all-to-all | bytes 524288 | tf_op jit(solution)/shard_map/all_to_all | solution.py:440
  127.6 3.1 %collective-permute-start.3 = (bf16[8,64,256]{2,1,0:T(8,128)(2,1)S(1)}, bf16[8,64,256]{2,1,0:T(8,128)(2,1)S(1)}, u32[]{:S(2)}, u32[]{:S(2)}) collective-permute-start(bf16[8,64,256]{2,1,0:T(8,128)(2,1)S(1)} %all_to_all.21.same), channel_id=1, source_target_pairs={{0,4},{1,5},{2,6},{3,7},{4,0},{5,1},{6,2},{7,3},{8,12},{9,13},{10,... | collective-permute-start | bytes 786440 | tf_op jit(solution)/shard_map/ppermute | solution.py:428
  130.7 3.1 %collective-permute-start.4 = (bf16[8,64,256]{2,1,0:T(8,128)(2,1)S(1)}, bf16[8,64,256]{2,1,0:T(8,128)(2,1)}, u32[]{:S(2)}, u32[]{:S(2)}) collective-permute-start(bf16[8,64,256]{2,1,0:T(8,128)(2,1)S(1)} %all_to_all.21.same), channel_id=1, source_target_pairs={{0,2},{1,3},{2,0},{3,1},{4,6},{5,7},{6,4},{7,5},{8,10},{9,11},{10,... | collective-permute-start | bytes 786440 | tf_op jit(solution)/shard_map/ppermute | solution.py:428
  133.8 3.7 %collective-permute-start.5 = (bf16[8,64,256]{2,1,0:T(8,128)(2,1)S(1)}, bf16[8,64,256]{2,1,0:T(8,128)(2,1)}, u32[]{:S(2)}, u32[]{:S(2)}) collective-permute-start(bf16[8,64,256]{2,1,0:T(8,128)(2,1)S(1)} %all_to_all.21.same), channel_id=1, source_target_pairs={{0,6},{1,7},{2,4},{3,5},{4,2},{5,3},{6,0},{7,1},{8,14},{9,15},{10,... | collective-permute-start | bytes 786440 | tf_op jit(solution)/shard_map/ppermute | solution.py:428
  137.5 8.0 %collective-permute-start.7 = (bf16[4,672,512]{2,1,0:T(8,128)(2,1)}, bf16[4,672,512]{2,1,0:T(8,128)(2,1)S(1)}, u32[]{:S(2)}, u32[]{:S(2)}) collective-permute-start(bf16[4,672,512]{2,1,0:T(8,128)(2,1)} %bitcast.21), channel_id=1, source_target_pairs={{0,1},{1,0},{2,3},{3,2},{4,5},{5,4},{6,7},{7,6},{8,9},{9,8},{10,11... | collective-permute-start | bytes 8257544 | tf_op jit(solution)/shard_map/ppermute | solution.py:428
  145.6 0.7 copy-done.6
  146.3 0.9 copy-done.7
  147.2 0.3 near_half.1.near
  147.6 4.7 %collective-permute-start.9 = (bf16[4,672,512]{2,1,0:T(8,128)(2,1)}, bf16[4,672,512]{2,1,0:T(8,128)(2,1)S(1)}, u32[]{:S(2)}, u32[]{:S(2)}) collective-permute-start(bf16[4,672,512]{2,1,0:T(8,128)(2,1)} %bitcast.18), channel_id=1, source_target_pairs={{0,1},{1,0},{2,3},{3,2},{4,5},{5,4},{6,7},{7,6},{8,9},{9,8},{10,11... | collective-permute-start | bytes 8257544 | tf_op jit(solution)/shard_map/ppermute | solution.py:428
  152.3 1.8 copy-done.1
  154.1 2.6 %own_rows.1 = (f32[4,128,224]{2,1,0:T(8,128)S(1)}, bf16[128,128]{1,0:T(8,128)(2,1)S(1)}, bf16[8,64,512]{2,1,0:T(8,128)(2,1)S(1)}) custom-call(bf16[8,64,512]{2,1,0:T(8,128)(2,1)S(1)} %near_half.1.near, bf16[8,64,256]{2,1,0:T(8,128)(2,1)S(1)} %all_to_all.21.same, bf16[8,64,256]{2,1,0:T(8,128)(2,1)} %collective-permute-done.4.far_same, ...), custom_call_target="tpu_custom_call" | custom-call | flops 469762048 | bytes 4194304 | tf_op jit(solution)/shard_map/own_rows/pallas_call | solution.py:366
  156.7 0.5 collective-permute-done.9.core.core_lo
  157.2 1.3 partner_rows.1.units
  158.6 3.9 %collective-permute-start.10 = (bf16[2,128,224]{2,1,0:T(8,128)(2,1)S(1)}, bf16[2,128,224]{2,1,0:T(8,128)(2,1)S(1)}, u32[]{:S(2)}, u32[]{:S(2)}) collective-permute-start(bf16[2,128,224]{2,1,0:T(8,128)(2,1)S(1)} %partner_rows.1.units), channel_id=1, source_target_pairs={{0,2},{1,3},{2,0},{3,1},{4,6},{5,7},{6,4},{7,5},{8,10},{9,11},{10,... | collective-permute-start | bytes 344072 | tf_op jit(solution)/shard_map/ppermute | solution.py:428
  162.5 4.2 %collective-permute-done.10.far_units = bf16[2,128,224]{2,1,0:T(8,128)(2,1)S(1)} collective-permute-done((bf16[2,128,224]{2,1,0:T(8,128)(2,1)S(1)}, bf16[2,128,224]{2,1,0:T(8,128)(2,1)S(1)}, u32[]{:S(2)}, u32[]{:S(2)}) %collective-permute-start.10) | collective-permute-done | bytes 114720 | tf_op jit(solution)/shard_map/ppermute | solution.py:428
  166.7 0.7 down.1
  167.4 3.3 %collective-permute-start.11 = (bf16[8,128,128]{2,1,0:T(8,128)(2,1)S(1)}, bf16[8,128,128]{2,1,0:T(8,128)(2,1)S(1)}, u32[]{:S(2)}, u32[]{:S(2)}) collective-permute-start(bf16[8,128,128]{2,1,0:T(8,128)(2,1)S(1)} %get-tuple-element.37), channel_id=1, source_target_pairs={{0,4},{1,5},{2,6},{3,7},{4,0},{5,1},{6,2},{7,3},{8,12},{9,13},{10,... | collective-permute-start | bytes 786440 | tf_op jit(solution)/shard_map/ppermute | solution.py:428
  170.7 5.2 %collective-permute-done.11.got = bf16[8,128,128]{2,1,0:T(8,128)(2,1)S(1)} collective-permute-done((bf16[8,128,128]{2,1,0:T(8,128)(2,1)S(1)}, bf16[8,128,128]{2,1,0:T(8,128)(2,1)S(1)}, u32[]{:S(2)}, u32[]{:S(2)}) %collective-permute-start.11) | collective-permute-done | bytes 262176 | tf_op jit(solution)/shard_map/ppermute | solution.py:428
  175.9 23.8 %all_to_all.22.got = bf16[8,128,128]{2,1,0:T(8,128)(2,1)S(1)} all-to-all(bf16[8,128,128]{2,1,0:T(8,128)(2,1)S(1)} %add.89), channel_id=1, replica_groups={{0,8,16,24,32,40,48,56},{1,9,17,25,33,41,49,57},{2,10,18,26,34,42,50,58..., dimensions={0} | all-to-all | bytes 524288 | tf_op jit(solution)/shard_map/all_to_all | solution.py:440
  199.7 0.1 finish.1
  199.8 6.6 %collective-permute-start.12 = (bf16[64,128]{1,0:T(8,128)(2,1)S(1)}, bf16[64,128]{1,0:T(8,128)(2,1)S(1)}, u32[]{:S(2)}, u32[]{:S(2)}) collective-permute-start(bf16[64,128]{1,0:T(8,128)(2,1)S(1)} %get-tuple-element.40), channel_id=1, source_target_pairs={{0,1},{1,0},{2,3},{3,2},{4,5},{5,4},{6,7},{7,6},{8,9},{9,8},{10,11... | collective-permute-start | bytes 49160 | tf_op jit(solution)/shard_map/ppermute | solution.py:428
  206.4 0.8 collective-permute-done.12
  207.2 0.6 fusion
  (43 shorter events, 0.3 us)
Async XLA Ops:
  7.2 13.2 %copy-start.17 = (s32[2]{0:T(128)S(1)}, s32[2]{0:T(128)}, u32[]{:S(2)}) copy-start(s32[2]{0:T(128)} %param.14) | copy-start | bytes 28
  7.2 14.5 %copy-start.13 = (f32[4096]{0:T(1024)S(1)}, f32[4096]{0:T(1024)}, u32[]{:S(2)}) copy-start(f32[4096]{0:T(1024)} %param.15) | copy-start | bytes 49156
  9.9 23.5 %all-to-all-start = ((bf16[8,160,512]{2,1,0:T(8,128)(2,1)}), bf16[8,160,512]{2,1,0:T(8,128)(2,1)S(1)}, u32[]{:S(2)}, u32[]{:S(2)}) async-start(bf16[8,160,512]{2,1,0:T(8,128)(2,1)} %get-tuple-element.24), calls=%async_computation | async-start | bytes 2621440 | tf_op jit(solution)/shard_map/all_to_all | solution.py:469
  15.8 121.7 %all-gather.6.cloned.1.call-start = ((), (), s32[]{:S(2)}) async-start(), calls=%async_computation.4 | async-start | bytes 3440640 | tf_op jit(solution)/shard_map/all_gather | solution.py:436
  15.8 21.9 %collective-permute-start.6 = (bf16[224,512]{1,0:T(8,128)(2,1)}, bf16[224,512]{1,0:T(8,128)(2,1)}, u32[]{:S(2)}, u32[]{:S(2)}) collective-permute-start(bf16[224,512]{1,0:T(8,128)(2,1)} %bitcast.12.narrow), channel_id=1, source_target_pairs={{0,2},{1,3},{2,0},{3,1},{4,6},{5,7},{6,4},{7,5},{8,10},{9,11},{10,... | collective-permute-start | bytes 688136 | tf_op jit(solution)/shard_map/ppermute | solution.py:428
  21.7 1.6 copy-start.3
  23.3 0.7 copy-start.14
  25.4 0.6 copy-start.11
  33.4 0.9 copy-start.4
  34.3 3.5 %copy-start.8 = (bf16[512,224]{0,1:T(8,128)(2,1)S(1)}, bf16[512,224]{0,1:T(8,128)(2,1)}, u32[]{:S(2)}) copy-start(bf16[512,224]{0,1:T(8,128)(2,1)} %param.21) | copy-start | bytes 688132
  34.3 3.5 %copy-start.9 = (bf16[512,224]{0,1:T(8,128)(2,1)S(1)}, bf16[512,224]{0,1:T(8,128)(2,1)}, u32[]{:S(2)}) copy-start(bf16[512,224]{0,1:T(8,128)(2,1)} %param.22) | copy-start | bytes 688132
  36.1 29.4 %copy-start.15 = (s32[2]{0:T(128)S(1)}, s32[2]{0:T(128)}, u32[]{:S(2)}) copy-start(s32[2]{0:T(128)} %lengths.1) | copy-start | bytes 28
  36.2 64.1 %copy-start.12 = (bf16[64,256]{1,0:T(8,128)(2,1)S(1)}, bf16[64,256]{1,0:T(8,128)(2,1)}, u32[]{:S(2)}) copy-start(bf16[64,256]{1,0:T(8,128)(2,1)} %copy-done.11) | copy-start | bytes 98308
  40.6 0.6 copy-start.5
  41.3 106.4 %all-gather.8.cloned.1.call-start = ((), (), s32[]{:S(2)}) async-start(), calls=%async_computation.5 | async-start | bytes 3440640 | tf_op jit(solution)/shard_map/all_gather | solution.py:436
  53.0 93.3 %copy-start.10 = (f32[4096]{0:T(1024)S(1)}, f32[4096]{0:T(1024)}, u32[]{:S(2)}) copy-start(f32[4096]{0:T(1024)} %param.20) | copy-start | bytes 49156
  53.0 48.1 %collective-permute-start.8 = (bf16[672,512]{1,0:T(8,128)(2,1)}, bf16[672,512]{1,0:T(8,128)(2,1)S(1)}, u32[]{:S(2)}, u32[]{:S(2)}) collective-permute-start(bf16[672,512]{1,0:T(8,128)(2,1)} %join.1), channel_id=1, source_target_pairs={{0,256},{64,320},{128,384},{192,448},{256,0},{320,64},{384,128},{4... | collective-permute-start | bytes 2064392 | tf_op jit(solution)/shard_map/ppermute | solution.py:432
  55.4 44.8 %collective-permute-start = (bf16[8,64,512]{2,1,0:T(8,128)(2,1)S(1)}, bf16[8,64,512]{2,1,0:T(8,128)(2,1)S(1)}, u32[]{:S(2)}, u32[]{:S(2)}) collective-permute-start(bf16[8,64,512]{2,1,0:T(8,128)(2,1)S(1)} %slice.4.mine), channel_id=1, source_target_pairs={{0,1},{1,0},{2,3},{3,2},{4,5},{5,4},{6,7},{7,6},{8,9},{9,8},{10,11... | collective-permute-start | bytes 1572872 | tf_op jit(solution)/shard_map/ppermute | solution.py:428
  58.5 41.7 %collective-permute-start.1 = (bf16[8,64,512]{2,1,0:T(8,128)(2,1)S(1)}, bf16[8,64,512]{2,1,0:T(8,128)(2,1)S(1)}, u32[]{:S(2)}, u32[]{:S(2)}) collective-permute-start(bf16[8,64,512]{2,1,0:T(8,128)(2,1)S(1)} %slice.4.mine), channel_id=1, source_target_pairs={{0,2},{1,3},{2,0},{3,1},{4,6},{5,7},{6,4},{7,5},{8,10},{9,11},{10,... | collective-permute-start | bytes 1572872 | tf_op jit(solution)/shard_map/ppermute | solution.py:428
  61.7 38.6 %collective-permute-start.2 = (bf16[8,64,512]{2,1,0:T(8,128)(2,1)S(1)}, bf16[8,64,512]{2,1,0:T(8,128)(2,1)S(1)}, u32[]{:S(2)}, u32[]{:S(2)}) collective-permute-start(bf16[8,64,512]{2,1,0:T(8,128)(2,1)S(1)} %slice.4.mine), channel_id=1, source_target_pairs={{0,3},{1,2},{2,1},{3,0},{4,7},{5,6},{6,5},{7,4},{8,11},{9,10},{10,... | collective-permute-start | bytes 1572872 | tf_op jit(solution)/shard_map/ppermute | solution.py:428
  101.1 0.9 copy-start.16
  127.6 18.0 %collective-permute-start.3 = (bf16[8,64,256]{2,1,0:T(8,128)(2,1)S(1)}, bf16[8,64,256]{2,1,0:T(8,128)(2,1)S(1)}, u32[]{:S(2)}, u32[]{:S(2)}) collective-permute-start(bf16[8,64,256]{2,1,0:T(8,128)(2,1)S(1)} %all_to_all.21.same), channel_id=1, source_target_pairs={{0,4},{1,5},{2,6},{3,7},{4,0},{5,1},{6,2},{7,3},{8,12},{9,13},{10,... | collective-permute-start | bytes 786440 | tf_op jit(solution)/shard_map/ppermute | solution.py:428
  130.7 16.9 %collective-permute-start.4 = (bf16[8,64,256]{2,1,0:T(8,128)(2,1)S(1)}, bf16[8,64,256]{2,1,0:T(8,128)(2,1)}, u32[]{:S(2)}, u32[]{:S(2)}) collective-permute-start(bf16[8,64,256]{2,1,0:T(8,128)(2,1)S(1)} %all_to_all.21.same), channel_id=1, source_target_pairs={{0,2},{1,3},{2,0},{3,1},{4,6},{5,7},{6,4},{7,5},{8,10},{9,11},{10,... | collective-permute-start | bytes 786440 | tf_op jit(solution)/shard_map/ppermute | solution.py:428
  133.8 13.8 %collective-permute-start.5 = (bf16[8,64,256]{2,1,0:T(8,128)(2,1)S(1)}, bf16[8,64,256]{2,1,0:T(8,128)(2,1)}, u32[]{:S(2)}, u32[]{:S(2)}) collective-permute-start(bf16[8,64,256]{2,1,0:T(8,128)(2,1)S(1)} %all_to_all.21.same), channel_id=1, source_target_pairs={{0,6},{1,7},{2,4},{3,5},{4,2},{5,3},{6,0},{7,1},{8,14},{9,15},{10,... | collective-permute-start | bytes 786440 | tf_op jit(solution)/shard_map/ppermute | solution.py:428
  137.5 14.8 %collective-permute-start.7 = (bf16[4,672,512]{2,1,0:T(8,128)(2,1)}, bf16[4,672,512]{2,1,0:T(8,128)(2,1)S(1)}, u32[]{:S(2)}, u32[]{:S(2)}) collective-permute-start(bf16[4,672,512]{2,1,0:T(8,128)(2,1)} %bitcast.21), channel_id=1, source_target_pairs={{0,1},{1,0},{2,3},{3,2},{4,5},{5,4},{6,7},{7,6},{8,9},{9,8},{10,11... | collective-permute-start | bytes 8257544 | tf_op jit(solution)/shard_map/ppermute | solution.py:428
  145.6 0.7 copy-start.6
  146.3 1.0 copy-start.7
  147.6 9.6 %copy-start = (bf16[2688,512]{1,0:T(8,128)(2,1)S(1)}, bf16[2688,512]{1,0:T(8,128)(2,1)}, u32[]{:S(2)}) copy-start(bf16[2688,512]{1,0:T(8,128)(2,1)} %all-gather.8.cloned.1.call-done) | copy-start | bytes 8257540
  147.6 9.6 %collective-permute-start.9 = (bf16[4,672,512]{2,1,0:T(8,128)(2,1)}, bf16[4,672,512]{2,1,0:T(8,128)(2,1)S(1)}, u32[]{:S(2)}, u32[]{:S(2)}) collective-permute-start(bf16[4,672,512]{2,1,0:T(8,128)(2,1)} %bitcast.18), channel_id=1, source_target_pairs={{0,1},{1,0},{2,3},{3,2},{4,5},{5,4},{6,7},{7,6},{8,9},{9,8},{10,11... | collective-permute-start | bytes 8257544 | tf_op jit(solution)/shard_map/ppermute | solution.py:428
  152.3 1.8 copy-start.1
  157.2 9.4 %copy-start.2 = (bf16[2688,512]{1,0:T(8,128)(2,1)S(1)}, bf16[2688,512]{1,0:T(8,128)(2,1)}, u32[]{:S(2)}) copy-start(bf16[2688,512]{1,0:T(8,128)(2,1)} %all-gather.6.cloned.1.call-done) | copy-start | bytes 8257540
  158.6 8.1 %collective-permute-start.10 = (bf16[2,128,224]{2,1,0:T(8,128)(2,1)S(1)}, bf16[2,128,224]{2,1,0:T(8,128)(2,1)S(1)}, u32[]{:S(2)}, u32[]{:S(2)}) collective-permute-start(bf16[2,128,224]{2,1,0:T(8,128)(2,1)S(1)} %partner_rows.1.units), channel_id=1, source_target_pairs={{0,2},{1,3},{2,0},{3,1},{4,6},{5,7},{6,4},{7,5},{8,10},{9,11},{10,... | collective-permute-start | bytes 344072 | tf_op jit(solution)/shard_map/ppermute | solution.py:428
  167.4 8.5 %collective-permute-start.11 = (bf16[8,128,128]{2,1,0:T(8,128)(2,1)S(1)}, bf16[8,128,128]{2,1,0:T(8,128)(2,1)S(1)}, u32[]{:S(2)}, u32[]{:S(2)}) collective-permute-start(bf16[8,128,128]{2,1,0:T(8,128)(2,1)S(1)} %get-tuple-element.37), channel_id=1, source_target_pairs={{0,4},{1,5},{2,6},{3,7},{4,0},{5,1},{6,2},{7,3},{8,12},{9,13},{10,... | collective-permute-start | bytes 786440 | tf_op jit(solution)/shard_map/ppermute | solution.py:428
  199.8 7.4 %collective-permute-start.12 = (bf16[64,128]{1,0:T(8,128)(2,1)S(1)}, bf16[64,128]{1,0:T(8,128)(2,1)S(1)}, u32[]{:S(2)}, u32[]{:S(2)}) collective-permute-start(bf16[64,128]{1,0:T(8,128)(2,1)S(1)} %get-tuple-element.40), channel_id=1, source_target_pairs={{0,1},{1,0},{2,3},{3,2},{4,5},{5,4},{6,7},{7,6},{8,9},{9,8},{10,11... | collective-permute-start | bytes 49160 | tf_op jit(solution)/shard_map/ppermute | solution.py:428
Sparse Core Ops, SparseCore 0:
  41.4 47.5 all-gather.5
  102.1 41.8 all-gather.7

commit v10 on v9

--- a/solution.py
+++ b/solution.py
@@ -57,7 +57,7 @@
     return pl.CostEstimate(flops=flops, bytes_accessed=nbytes, transcendentals=0)
 
 
-def project_kernel(normed, weights, cos, sin, send, keys, values, tables, sems):
+def project_kernel(after, normed, weights, cos, sin, send, keys, values, tables, sems):
     copies = [pltpu.make_async_copy(ref, tables.at[i], sems.at[i]) for i, ref in enumerate((cos, sin))]
     for copy in copies:
         copy.start()
@@ -175,37 +175,49 @@
         out[i] = totals[i]
 
 
-def partner_rows_kernel(near, far, before, mine, core, out):
-    at = place()
+def down_kernel(near, far, before, mine, mine_lo, core, core_lo, keep, to_y, to_z, to_both, held, sems):
+    at = place()
+    copies = [
+        pltpu.make_async_copy(w.at[x, pl.ds(2 * FC, FC), :], held.at[i, x], sems.at[i, x])
+        for i, w in enumerate((mine, core))
+        for x in range(4)
+    ]
+    for copy in copies:
+        copy.start()
+    low_y, low_z = at[1] == 0, at[3] == 0
     totals = [before[i] for i in range(4)]
-    multiply(at, near, far, (mine, core), 1, totals)
-    low = at[1] == 0
+    multiply(at, near, far, (mine_lo, core_lo), 1, totals)
+    units = []
     for i in range(2):
         gate = totals[2 * i]
-        units = (gate / (1.0 + jnp.exp(-gate)) * totals[2 * i + 1]).astype(BF)
-        first, second = units[0:HALF, :], units[HALF : 2 * HALF, :]
-        out[i, 0:HALF, :] = jnp.where(low, first, second)
-        out[i, HALF : 2 * HALF, :] = jnp.where(low, second, first)
-
-
-def down_kernel(units, far_units, mine, mine_lo, core, core_lo, keep, give):
-    at = place()
-    low = at[3] == 0
+        part = (gate / (1.0 + jnp.exp(-gate)) * totals[2 * i + 1]).astype(BF)
+        first, second = part[0:HALF, :], part[HALF : 2 * HALF, :]
+        units.append(jnp.concatenate([jnp.where(low_y, first, second), jnp.where(low_y, second, first)], axis=0))
+    for copy in copies:
+        copy.wait()
     for x in range(4):
-        for side, pair in enumerate(((mine, core), (mine_lo, core_lo))):
-            total = jnp.zeros((128, BAND), F32)
-            for i, w in enumerate(pair):
-                total = total + jnp.dot(units[i], w[x, 2 * FC : 3 * FC, 0:BAND], preferred_element_type=F32)
-                total = total + jnp.dot(far_units[i], w[x, 2 * FC : 3 * FC, BAND:RUN], preferred_element_type=F32)
+        for side in range(2):
+            total = jnp.zeros((128, RUN), F32)
+            for i, w in enumerate((mine_lo, core_lo)):
+                block = w[x, 2 * FC : 3 * FC, :] if side else held[i, x]
+                total = total + jnp.dot(units[i], block, preferred_element_type=F32)
             g = jnp.bitwise_xor(at[6], side) * 4 + x
-            even, odd = total[:, 0:128], total[:, 128:256]
-            keep[g] = jnp.where(low, even, odd)
-            give[g] = jnp.where(low, odd, even).astype(BF)
-
-
-def add_kernel(keep, got, out):
+            blocks = [total[:, k * 128 : (k + 1) * 128] for k in range(4)]
+            same = [jnp.where(low_z, blocks[k], blocks[2 + k]) for k in range(2)]
+            other = [jnp.where(low_z, blocks[2 + k], blocks[k]) for k in range(2)]
+            keep[g] = jnp.where(low_y, same[0], same[1])
+            to_y[g] = jnp.where(low_y, same[1], same[0]).astype(BF)
+            to_z[g] = jnp.where(low_y, other[0], other[1]).astype(BF)
+            to_both[g] = jnp.where(low_y, other[1], other[0]).astype(BF)
+
+
+def add_kernel(keep, *refs):
+    out = refs[-1]
     for i in range(8):
-        out[i] = (keep[i] + got[i].astype(F32)).astype(BF)
+        total = keep[i]
+        for got in refs[:-1]:
+            total = total + got[i].astype(F32)
+        out[i] = total.astype(BF)
 
 
 def finish_kernel(got, kept, keep, give):
@@ -263,42 +275,36 @@
         in_specs=[ANY, ANY, HBM, HBM],
         out_specs=(VMEM,) * 2,
         scratch_shapes=[pltpu.VMEM((256, D), BF), pltpu.VMEM((1, D), F32), pltpu.SemaphoreType.DMA((2,))],
-        compiler_params=params(44),
+        compiler_params=params(24),
         name="norm",
     )(after, tables, stream, gain)
 
 
-def join_kernel(after, gate, up, narrow, got, out, held, sems):
-    at = place()
+def join_kernel(after, gate, up, narrow, out, token, held, sems):
+    token[...] = jnp.zeros_like(token)
     copies = [
-        pltpu.make_async_copy(narrow, held, sems.at[0]),
-        pltpu.make_async_copy(gate, out.at[pl.ds(0, FC), :], sems.at[1]),
-        pltpu.make_async_copy(up, out.at[pl.ds(FC, FC), :], sems.at[2]),
+        pltpu.make_async_copy(part, held.at[pl.ds(i * FC, FC), :], sems.at[i])
+        for i, part in enumerate((gate, up, narrow))
     ]
     for copy in copies:
         copy.start()
-    low = at[1] == 0
-    for k, source in ((1, got), (0, held)):
-        if k == 0:
-            copies[0].wait()
-        for i in range(2):
-            even = source[:, 2 * i * 128 : (2 * i + 1) * 128]
-            odd = source[:, (2 * i + 1) * 128 : (2 * i + 2) * 128]
-            out[2 * FC : 3 * FC, k * BAND + i * 128 : k * BAND + (i + 1) * 128] = jnp.where(low, even, odd)
-    copies[1].wait()
-    copies[2].wait()
-
-
-def join(after, gate, up, narrow, got):
+    for copy in copies:
+        copy.wait()
+    whole_copy = pltpu.make_async_copy(held, out, sems.at[3])
+    whole_copy.start()
+    whole_copy.wait()
+
+
+def join(after, *parts):
     return pl.pallas_call(
         join_kernel,
-        out_shape=jax.ShapeDtypeStruct((3 * FC, RUN), BF),
-        in_specs=[ANY, HBM, HBM, HBM, VMEM],
-        out_specs=VMEM,
-        scratch_shapes=[pltpu.VMEM((FC, RUN), BF), pltpu.SemaphoreType.DMA((3,))],
-        compiler_params=params(48),
+        out_shape=(jax.ShapeDtypeStruct((3 * FC, RUN), BF), jax.ShapeDtypeStruct((8, 128), F32)),
+        in_specs=[ANY, HBM, HBM, HBM],
+        out_specs=(HBM, VMEM),
+        scratch_shapes=[pltpu.VMEM((3 * FC, RUN), BF), pltpu.SemaphoreType.DMA((4,))],
+        compiler_params=params(60),
         name="join",
-    )(after, gate, up, narrow, got)
+    )(after, *parts)
 
 
 def pack(*parts):
@@ -313,7 +319,7 @@
     )(*parts)
 
 
-def project(normed, weights, cos, sin):
+def project(after, normed, weights, cos, sin):
     return pl.pallas_call(
         project_kernel,
         out_shape=(
@@ -321,12 +327,12 @@
             jax.ShapeDtypeStruct((KC, 256), BF),
             jax.ShapeDtypeStruct((KC, 256), BF),
         ),
-        in_specs=[VMEM] * 2 + [HBM] * 2,
+        in_specs=[ANY] + [VMEM] * 2 + [HBM] * 2,
         out_specs=(VMEM,) * 3,
         scratch_shapes=[pltpu.VMEM((2, 256, 128), F32), pltpu.SemaphoreType.DMA((2,))],
         compiler_params=params(24),
         name="project",
-    )(normed, weights, cos, sin)
+    )(after, normed, weights, cos, sin)
 
 
 def attend(lengths, got):
@@ -378,39 +384,29 @@
     )(near, same, far_same, far_other, gain, mine, core)
 
 
-def partner_rows(near, far, before, mine, core):
-    return pl.pallas_call(
-        partner_rows_kernel,
-        out_shape=jax.ShapeDtypeStruct((2, 128, FC), BF),
-        in_specs=[VMEM] * 5,
-        out_specs=VMEM,
+def down(near, far, before, weights):
+    part = jax.ShapeDtypeStruct((8, 128, 128), BF)
+    return pl.pallas_call(
+        down_kernel,
+        out_shape=(jax.ShapeDtypeStruct((8, 128, 128), F32), part, part, part),
+        in_specs=[VMEM] * 3 + [HBM, VMEM, ANY, VMEM],
+        out_specs=(VMEM,) * 4,
+        scratch_shapes=[pltpu.VMEM((2, 4, FC, RUN), BF), pltpu.SemaphoreType.DMA((2, 4))],
         compiler_params=params(16),
-        cost_estimate=cost(2 * HALF * D * 4 * FC, 4 * 2**20),
-        name="partner_rows",
-    )(near, far, before, mine, core)
-
-
-def down(units, far_units, weights):
-    return pl.pallas_call(
-        down_kernel,
-        out_shape=(jax.ShapeDtypeStruct((8, 128, 128), F32), jax.ShapeDtypeStruct((8, 128, 128), BF)),
-        in_specs=[VMEM] * 6,
-        out_specs=(VMEM, VMEM),
-        compiler_params=params(16),
-        cost_estimate=cost(4 * HALF * D * 2 * FC, 5 * 2**20),
+        cost_estimate=cost(4 * HALF * D * 4 * FC, 9 * 2**20),
         name="down",
-    )(units, far_units, *weights)
-
-
-def add(keep, got):
+    )(near, far, before, *weights)
+
+
+def add(*parts):
     return pl.pallas_call(
         add_kernel,
         out_shape=jax.ShapeDtypeStruct((8, 128, 128), BF),
-        in_specs=[VMEM] * 2,
+        in_specs=[VMEM] * 4,
         out_specs=VMEM,
         compiler_params=params(16),
         name="add",
-    )(keep, got)
+    )(*parts)
 
 
 def finish(got, kept):
@@ -477,12 +473,10 @@
     cos, sin = jnp.cos(angle), jnp.sin(angle)
 
     normed, own = norm(token, cos, stream, attn_gain.reshape(1, D))
-    narrow = after(w_down.T, token)
-    other = swap(narrow, 2)
-
-    send, keys, values = project(normed, first, cos, sin)
+    mine, token = join(token, w_gate.T, w_up.T, w_down.T)
+    send, keys, values = project(token, normed, first, cos, sin)
     got = trade(send, OCTETS)
-    mine = join(send, w_gate.T, w_up.T, narrow, other)
+    mine = after(mine, send)
     mine_lo = swap_groups(after(mine, got))
     out_own = first[:, 96:160, :]
     out_weights = (out_own, swap(out_own, 1), swap(out_own, 2), swap(out_own, 3))
@@ -498,10 +492,9 @@
     mine_lo = after(mine_lo, (far_same, far_other, near))
     core_lo = swap(mine_lo, 1)
     totals, kept, far_normed = own_rows(near, same, far_same, far_other, gain, mine, core_mine)
-    units = partner_rows(near, far_normed, totals, mine_lo, core_lo)
     weights = (mine, mine_lo, core_mine, core_lo)
-    keep, give = down(units, swap(units, 2), weights)
-    sums = trade(add(keep, swap(give, 4)), PARITIES)
+    keep, to_y, to_z, to_both = down(near, far_normed, totals, weights)
+    sums = trade(add(keep, swap(to_y, 2), swap(to_z, 4), swap(to_both, 6)), PARITIES)
     keep, give = finish(sums, kept)
     give = swap(give, 1)
     rows = jnp.where(core == 0, jnp.concatenate([keep, give], axis=1), jnp.concatenate([give, keep], axis=1))

time: 216 us -> 219 us (1.014)
  Pallas kernels: 16 us -> 18.6 us
    pallas_call x1, Pallas kernels: 0.71 us -> 4.49 us  [down(): pl.pallas_call(down_kernel, out_shape=(jax.ShapeDtypeStruct((8, 128, 128)...]
where the time goes in v10:
time: 219 us; the launch traced here: 218 us
  blocking collectives  94.4 us (43%)
  starting transfers between devices  58.8 us (27%)
  waiting for transfers between devices  20.1 us (9%)
  Pallas kernels  18.6 us (8%)
  between operations  14.4 us (7%)
  local copies, waits for them, and re-layouts  10.1 us (5%)
    all_to_all x3, blocking collectives, trade(): return lax.all_to_all(x, 'dev', 0, 0, axis_index_groups=groups, tiled=True)  62 us
    ppermute x12, starting transfers between devices, swap(): return lax.ppermute(x, 'dev', [(d, d ^ bits) for d in range(MEMBERS)])  50.8 us
    all_gather x1, blocking collectives, collect(): return lax.all_gather(x, 'dev', axis=0, axis_index_groups=COLUMNS)  32.4 us
    ppermute x12, waiting for transfers between devices, swap(): return lax.ppermute(x, 'dev', [(d, d ^ bits) for d in range(MEMBERS)])  10.6 us
    unnamed x36, local copies, waits for them, and re-layouts  10.1 us
    all_to_all x1, waiting for transfers between devices, on_device(): first = lax.all_to_all(packed, 'grp', 0, 0, tiled=True)  9.45 us
    all_to_all x1, starting transfers between devices, on_device(): first = lax.all_to_all(packed, 'grp', 0, 0, tiled=True)  5.87 us
    pallas_call x1, Pallas kernels, down(): pl.pallas_call(down_kernel, out_shape=(jax.ShapeDtypeStruct((8, 128, 128)...  4.49 us
  transfers between devices with their start and end apart: 16, of which 6 were waited for; matrix products, arithmetic and copies ran while one was open for 1% of the time, Pallas kernels for 4%

profile of v10, /device:TPU:1, one launch (start us, length us, event | category | flops | bytes accessed | tf_op | source)
XLA Modules:
  0.0 218.4 jit_solution(12894930652828072220)
XLA Ops:
  7.2 2.8 %pack.1 = (bf16[8,160,512]{2,1,0:T(8,128)(2,1)}, f32[8,128]{1,0:T(8,128)}) custom-call(bf16[64,512]{1,0:T(8,128)(2,1)} %bitcast.30, bf16[16,512]{1,0:T(8,128)(2,1)} %bitcast.32, bf16[16,512]{1,0:T(8,128)(2,1)} %bitcast.33, bf16[64,512]{1,0:T(8,128)(2,1)} %bitcast.31), custom_call_target="tpu_custom_call" | custom-call | tf_op jit(solution)/shard_map/pack/pallas_call | solution.py:311
  10.0 5.9 %all-to-all-start = ((bf16[8,160,512]{2,1,0:T(8,128)(2,1)}), bf16[8,160,512]{2,1,0:T(8,128)(2,1)S(1)}, u32[]{:S(2)}, u32[]{:S(2)}) async-start(bf16[8,160,512]{2,1,0:T(8,128)(2,1)} %get-tuple-element.29), calls=%async_computation | async-start | bytes 2621440 | tf_op jit(solution)/shard_map/all_to_all | solution.py:465
  15.9 2.6 %join.1 = (bf16[672,512]{1,0:T(8,128)(2,1)}, f32[8,128]{1,0:T(8,128)}) custom-call(f32[8,128]{1,0:T(8,128)} %get-tuple-element.26.after, bf16[224,512]{1,0:T(8,128)(2,1)} %bitcast.27, bf16[224,512]{1,0:T(8,128)(2,1)} %bitcast.28, bf16[224,512]{1,0:T(8,128)(2,1)} %bitcast.29), custom_call_target="tpu_custom_call" | custom-call | tf_op jit(solution)/shard_map/join/pallas_call | solution.py:299
  18.6 0.1 convert_bitcast_fusion
  18.7 1.2 multiply_sine_fusion
  19.9 0.7 copy-done.13
  20.6 1.4 norm.1
  22.0 1.3 copy-done.4
  23.3 0.6 copy-done.10
  24.0 9.4 %all-to-all-done.weights = bf16[8,160,512]{2,1,0:T(8,128)(2,1)S(1)} async-done(((bf16[8,160,512]{2,1,0:T(8,128)(2,1)}), bf16[8,160,512]{2,1,0:T(8,128)(2,1)S(1)}, u32[]{:S(2)}, u32[]{:S(2)}) %all-to-all-start) | async-done | bytes 1310752 | tf_op jit(solution)/shard_map/all_to_all | solution.py:465
  33.4 1.6 copy-done.5
  35.0 0.9 copy-done.6
  35.9 0.7 copy-done.14
  36.6 1.8 project.1
  38.5 13.0 %all_to_all.20.got = bf16[8,64,128]{2,1,0:T(8,128)(2,1)S(1)} all-to-all(bf16[8,64,128]{2,1,0:T(8,128)(2,1)S(1)} %get-tuple-element.32), channel_id=1, replica_groups={{0,1,2,3,4,5,6,7},{8,9,10,11,12,13,14,15},{16,17,18,19,20,21,22,23},{24..., dimensions={0} | all-to-all | bytes 262144 | tf_op jit(solution)/shard_map/all_to_all | solution.py:436
  51.5 2.0 collective-permute-start.7
  53.6 3.9 %collective-permute-start.2 = (bf16[8,64,512]{2,1,0:T(8,128)(2,1)S(1)}, bf16[8,64,512]{2,1,0:T(8,128)(2,1)S(1)}, u32[]{:S(2)}, u32[]{:S(2)}) collective-permute-start(bf16[8,64,512]{2,1,0:T(8,128)(2,1)S(1)} %slice.4.mine), channel_id=1, source_target_pairs={{0,3},{1,2},{2,1},{3,0},{4,7},{5,6},{6,5},{7,4},{8,11},{9,10},{10,... | collective-permute-start | bytes 1572872 | tf_op jit(solution)/shard_map/ppermute | solution.py:424
  57.5 3.7 %collective-permute-start.1 = (bf16[8,64,512]{2,1,0:T(8,128)(2,1)S(1)}, bf16[8,64,512]{2,1,0:T(8,128)(2,1)S(1)}, u32[]{:S(2)}, u32[]{:S(2)}) collective-permute-start(bf16[8,64,512]{2,1,0:T(8,128)(2,1)S(1)} %slice.4.mine), channel_id=1, source_target_pairs={{0,2},{1,3},{2,0},{3,1},{4,6},{5,7},{6,4},{7,5},{8,10},{9,11},{10,... | collective-permute-start | bytes 1572872 | tf_op jit(solution)/shard_map/ppermute | solution.py:424
  61.2 1.9 collective-permute-start
  63.2 1.4 attend.1
  64.6 32.4 %all-gather = bf16[1024,256]{1,0:T(8,128)(2,1)S(1)} all-gather(bf16[64,256]{1,0:T(8,128)(2,1)S(1)} %attend.1), channel_id=2, replica_groups={{0,4,8,12,16,20,24,28,32,36,40,44,48,52,56,60},{1,5,9,13,17,21,25,29,33..., dimensions={0}, use_global_device_ids=true | all-gather | bytes 557056 | tf_op jit(solution)/shard_map/all_gather | solution.py:440
  97.0 0.8 output.1
  97.8 0.8 copy-done.16
  98.7 25.4 %all_to_all.21.same = bf16[8,64,256]{2,1,0:T(8,128)(2,1)S(1)} all-to-all(bf16[8,64,256]{2,1,0:T(8,128)(2,1)S(1)} %output.1), channel_id=1, replica_groups={{0,8,16,24,32,40,48,56},{1,9,17,25,33,41,49,57},{2,10,18,26,34,42,50,58..., dimensions={0} | all-to-all | bytes 524288 | tf_op jit(solution)/shard_map/all_to_all | solution.py:436
  124.0 1.9 collective-permute-start.3
  125.9 5.7 %collective-permute-start.5 = (bf16[8,64,256]{2,1,0:T(8,128)(2,1)S(1)}, bf16[8,64,256]{2,1,0:T(8,128)(2,1)}, u32[]{:S(2)}, u32[]{:S(2)}) collective-permute-start(bf16[8,64,256]{2,1,0:T(8,128)(2,1)S(1)} %all_to_all.21.same), channel_id=1, source_target_pairs={{0,6},{1,7},{2,4},{3,5},{4,2},{5,3},{6,0},{7,1},{8,14},{9,15},{10,... | collective-permute-start | bytes 786440 | tf_op jit(solution)/shard_map/ppermute | solution.py:424
  131.7 2.2 %collective-permute-start.4 = (bf16[8,64,256]{2,1,0:T(8,128)(2,1)S(1)}, bf16[8,64,256]{2,1,0:T(8,128)(2,1)}, u32[]{:S(2)}, u32[]{:S(2)}) collective-permute-start(bf16[8,64,256]{2,1,0:T(8,128)(2,1)S(1)} %all_to_all.21.same), channel_id=1, source_target_pairs={{0,2},{1,3},{2,0},{3,1},{4,6},{5,7},{6,4},{7,5},{8,10},{9,11},{10,... | collective-permute-start | bytes 786440 | tf_op jit(solution)/shard_map/ppermute | solution.py:424
  134.0 8.4 %collective-permute-start.6 = (bf16[4,672,512]{2,1,0:T(8,128)(2,1)}, bf16[4,672,512]{2,1,0:T(8,128)(2,1)S(1)}, u32[]{:S(2)}, u32[]{:S(2)}) collective-permute-start(bf16[4,672,512]{2,1,0:T(8,128)(2,1)} %bitcast.18), channel_id=1, source_target_pairs={{0,1},{1,0},{2,3},{3,2},{4,5},{5,4},{6,7},{7,6},{8,9},{9,8},{10,11... | collective-permute-start | bytes 8257544 | tf_op jit(solution)/shard_map/ppermute | solution.py:424
  142.3 0.7 copy-done.7
  143.1 0.9 copy-done.8
  144.0 0.3 near_half.1.near
  144.4 5.1 %collective-permute-start.8 = (bf16[4,672,512]{2,1,0:T(8,128)(2,1)}, bf16[4,672,512]{2,1,0:T(8,128)(2,1)S(1)}, u32[]{:S(2)}, u32[]{:S(2)}) collective-permute-start(bf16[4,672,512]{2,1,0:T(8,128)(2,1)} %bitcast.21), channel_id=1, source_target_pairs={{0,1},{1,0},{2,3},{3,2},{4,5},{5,4},{6,7},{7,6},{8,9},{9,8},{10,11... | collective-permute-start | bytes 8257544 | tf_op jit(solution)/shard_map/ppermute | solution.py:424
  149.5 1.8 copy-done
  151.3 2.7 %own_rows.1 = (f32[4,128,224]{2,1,0:T(8,128)S(1)}, bf16[128,128]{1,0:T(8,128)(2,1)S(1)}, bf16[8,64,512]{2,1,0:T(8,128)(2,1)S(1)}) custom-call(bf16[8,64,512]{2,1,0:T(8,128)(2,1)S(1)} %near_half.1.near, bf16[8,64,256]{2,1,0:T(8,128)(2,1)S(1)} %all_to_all.21.same, bf16[8,64,256]{2,1,0:T(8,128)(2,1)} %collective-permute-done.4.far_same, ...), custom_call_target="tpu_custom_call" | custom-call | flops 469762048 | bytes 4194304 | tf_op jit(solution)/shard_map/own_rows/pallas_call | solution.py:372
  154.1 0.4 collective-permute-done.8.core_lo
  154.4 4.5 %down.1 = (f32[8,128,128]{2,1,0:T(8,128)S(1)}, bf16[8,128,128]{2,1,0:T(8,128)(2,1)S(1)}, bf16[8,128,128]{2,1,0:T(8,128)(2,1)S(1)}, bf16[8,128,128]{2,1,0:T(8,128)(2,1)S(1)}) custom-call(bf16[8,64,512]{2,1,0:T(8,128)(2,1)S(1)} %near_half.1.near, bf16[8,64,512]{2,1,0:T(8,128)(2,1)S(1)} %get-tuple-element.37.far, f32[4,128,224]{2,1,0:T(8,128)S(1)} %get-tuple-element.38.before, ...), custom_call_target="tpu_custom_call" | custom-call | flops 939524096 | bytes 9437184 | tf_op jit(solution)/shard_map/down/pallas_call | solution.py:389
  158.9 3.5 %collective-permute-start.9 = (bf16[8,128,128]{2,1,0:T(8,128)(2,1)S(1)}, bf16[8,128,128]{2,1,0:T(8,128)(2,1)S(1)}, u32[]{:S(2)}, u32[]{:S(2)}) collective-permute-start(bf16[8,128,128]{2,1,0:T(8,128)(2,1)S(1)} %get-tuple-element.43), channel_id=1, source_target_pairs={{0,2},{1,3},{2,0},{3,1},{4,6},{5,7},{6,4},{7,5},{8,10},{9,11},{10,... | collective-permute-start | bytes 786440 | tf_op jit(solution)/shard_map/ppermute | solution.py:424
  162.4 2.6 %collective-permute-start.10 = (bf16[8,128,128]{2,1,0:T(8,128)(2,1)S(1)}, bf16[8,128,128]{2,1,0:T(8,128)(2,1)S(1)}, u32[]{:S(2)}, u32[]{:S(2)}) collective-permute-start(bf16[8,128,128]{2,1,0:T(8,128)(2,1)S(1)} %get-tuple-element.44), channel_id=1, source_target_pairs={{0,4},{1,5},{2,6},{3,7},{4,0},{5,1},{6,2},{7,3},{8,12},{9,13},{10,... | collective-permute-start | bytes 786440 | tf_op jit(solution)/shard_map/ppermute | solution.py:424
  165.1 3.8 %collective-permute-start.11 = (bf16[8,128,128]{2,1,0:T(8,128)(2,1)S(1)}, bf16[8,128,128]{2,1,0:T(8,128)(2,1)S(1)}, u32[]{:S(2)}, u32[]{:S(2)}) collective-permute-start(bf16[8,128,128]{2,1,0:T(8,128)(2,1)S(1)} %get-tuple-element.45), channel_id=1, source_target_pairs={{0,6},{1,7},{2,4},{3,5},{4,2},{5,3},{6,0},{7,1},{8,14},{9,15},{10,... | collective-permute-start | bytes 786440 | tf_op jit(solution)/shard_map/ppermute | solution.py:424
  168.8 1.0 collective-permute-done.9.refs_0_
  169.8 1.6 collective-permute-done.10.refs_1_
  171.5 6.8 %collective-permute-done.11.refs_2_ = bf16[8,128,128]{2,1,0:T(8,128)(2,1)S(1)} collective-permute-done((bf16[8,128,128]{2,1,0:T(8,128)(2,1)S(1)}, bf16[8,128,128]{2,1,0:T(8,128)(2,1)S(1)}, u32[]{:S(2)}, u32[]{:S(2)}) %collective-permute-start.11) | collective-permute-done | bytes 262176 | tf_op jit(solution)/shard_map/ppermute | solution.py:424
  178.2 0.1 add.89
  178.4 23.6 %all_to_all.22.got = bf16[8,128,128]{2,1,0:T(8,128)(2,1)S(1)} all-to-all(bf16[8,128,128]{2,1,0:T(8,128)(2,1)S(1)} %add.89), channel_id=1, replica_groups={{0,8,16,24,32,40,48,56},{1,9,17,25,33,41,49,57},{2,10,18,26,34,42,50,58..., dimensions={0} | all-to-all | bytes 524288 | tf_op jit(solution)/shard_map/all_to_all | solution.py:436
  202.0 0.1 finish.1
  202.1 8.1 %collective-permute-start.12 = (bf16[64,128]{1,0:T(8,128)(2,1)S(1)}, bf16[64,128]{1,0:T(8,128)(2,1)S(1)}, u32[]{:S(2)}, u32[]{:S(2)}) collective-permute-start(bf16[64,128]{1,0:T(8,128)(2,1)S(1)} %get-tuple-element.48), channel_id=1, source_target_pairs={{0,1},{1,0},{2,3},{3,2},{4,5},{5,4},{6,7},{7,6},{8,9},{9,8},{10,11... | collective-permute-start | bytes 49160 | tf_op jit(solution)/shard_map/ppermute | solution.py:424
  210.2 0.8 collective-permute-done.12
  211.0 0.6 fusion
  (42 shorter events, 0.3 us)
Async XLA Ops:
  7.2 11.4 %copy-start.17 = (s32[2]{0:T(128)S(1)}, s32[2]{0:T(128)}, u32[]{:S(2)}) copy-start(s32[2]{0:T(128)} %param.14) | copy-start | bytes 28
  7.2 12.7 %copy-start.12 = (f32[4096]{0:T(1024)S(1)}, f32[4096]{0:T(1024)}, u32[]{:S(2)}) copy-start(f32[4096]{0:T(1024)} %param.15) | copy-start | bytes 49156
  7.2 12.7 %copy-start.3 = (bf16[256,4096]{1,0:T(8,128)(2,1)S(1)}, bf16[256,4096]{1,0:T(8,128)(2,1)}, u32[]{:S(2)}) copy-start(bf16[256,4096]{1,0:T(8,128)(2,1)} %stream.1) | copy-start | bytes 6291460
  10.0 23.4 %all-to-all-start = ((bf16[8,160,512]{2,1,0:T(8,128)(2,1)}), bf16[8,160,512]{2,1,0:T(8,128)(2,1)S(1)}, u32[]{:S(2)}, u32[]{:S(2)}) async-start(bf16[8,160,512]{2,1,0:T(8,128)(2,1)} %get-tuple-element.29), calls=%async_computation | async-start | bytes 2621440 | tf_op jit(solution)/shard_map/all_to_all | solution.py:465
  15.9 118.1 %all-gather.6.cloned.1.call-start = ((), (), s32[]{:S(2)}) async-start(), calls=%async_computation.4 | async-start | bytes 3440640 | tf_op jit(solution)/shard_map/all_gather | solution.py:432
  19.9 0.7 copy-start.13
  22.0 1.3 copy-start.4
  23.3 0.6 copy-start.10
  33.4 1.6 copy-start.5
  35.0 0.9 copy-start.6
  35.9 0.7 copy-start.14
  36.6 26.6 %copy-start.15 = (s32[2]{0:T(128)S(1)}, s32[2]{0:T(128)}, u32[]{:S(2)}) copy-start(s32[2]{0:T(128)} %lengths.1) | copy-start | bytes 28
  36.6 60.4 %copy-start.11 = (bf16[64,256]{1,0:T(8,128)(2,1)S(1)}, bf16[64,256]{1,0:T(8,128)(2,1)}, u32[]{:S(2)}) copy-start(bf16[64,256]{1,0:T(8,128)(2,1)} %copy-done.10) | copy-start | bytes 98308
  38.4 105.9 %all-gather.8.cloned.1.call-start = ((), (), s32[]{:S(2)}) async-start(), calls=%async_computation.5 | async-start | bytes 3440640 | tf_op jit(solution)/shard_map/all_gather | solution.py:432
  51.5 91.5 %copy-start.9 = (f32[4096]{0:T(1024)S(1)}, f32[4096]{0:T(1024)}, u32[]{:S(2)}) copy-start(f32[4096]{0:T(1024)} %param.20) | copy-start | bytes 49156
  51.5 46.3 %collective-permute-start.7 = (bf16[672,512]{1,0:T(8,128)(2,1)}, bf16[672,512]{1,0:T(8,128)(2,1)S(1)}, u32[]{:S(2)}, u32[]{:S(2)}) collective-permute-start(bf16[672,512]{1,0:T(8,128)(2,1)} %get-tuple-element.39), channel_id=1, source_target_pairs={{0,256},{64,320},{128,384},{192,448},{256,0},{320,64},{384,128},{4... | collective-permute-start | bytes 2064392 | tf_op jit(solution)/shard_map/ppermute | solution.py:428
  53.6 43.4 %collective-permute-start.2 = (bf16[8,64,512]{2,1,0:T(8,128)(2,1)S(1)}, bf16[8,64,512]{2,1,0:T(8,128)(2,1)S(1)}, u32[]{:S(2)}, u32[]{:S(2)}) collective-permute-start(bf16[8,64,512]{2,1,0:T(8,128)(2,1)S(1)} %slice.4.mine), channel_id=1, source_target_pairs={{0,3},{1,2},{2,1},{3,0},{4,7},{5,6},{6,5},{7,4},{8,11},{9,10},{10,... | collective-permute-start | bytes 1572872 | tf_op jit(solution)/shard_map/ppermute | solution.py:424
  57.5 39.5 %collective-permute-start.1 = (bf16[8,64,512]{2,1,0:T(8,128)(2,1)S(1)}, bf16[8,64,512]{2,1,0:T(8,128)(2,1)S(1)}, u32[]{:S(2)}, u32[]{:S(2)}) collective-permute-start(bf16[8,64,512]{2,1,0:T(8,128)(2,1)S(1)} %slice.4.mine), channel_id=1, source_target_pairs={{0,2},{1,3},{2,0},{3,1},{4,6},{5,7},{6,4},{7,5},{8,10},{9,11},{10,... | collective-permute-start | bytes 1572872 | tf_op jit(solution)/shard_map/ppermute | solution.py:424
  61.2 35.8 %collective-permute-start = (bf16[8,64,512]{2,1,0:T(8,128)(2,1)S(1)}, bf16[8,64,512]{2,1,0:T(8,128)(2,1)S(1)}, u32[]{:S(2)}, u32[]{:S(2)}) collective-permute-start(bf16[8,64,512]{2,1,0:T(8,128)(2,1)S(1)} %slice.4.mine), channel_id=1, source_target_pairs={{0,1},{1,0},{2,3},{3,2},{4,5},{5,4},{6,7},{7,6},{8,9},{9,8},{10,11... | collective-permute-start | bytes 1572872 | tf_op jit(solution)/shard_map/ppermute | solution.py:424
  97.8 0.8 copy-start.16
  124.0 18.3 %collective-permute-start.3 = (bf16[8,64,256]{2,1,0:T(8,128)(2,1)S(1)}, bf16[8,64,256]{2,1,0:T(8,128)(2,1)S(1)}, u32[]{:S(2)}, u32[]{:S(2)}) collective-permute-start(bf16[8,64,256]{2,1,0:T(8,128)(2,1)S(1)} %all_to_all.21.same), channel_id=1, source_target_pairs={{0,4},{1,5},{2,6},{3,7},{4,0},{5,1},{6,2},{7,3},{8,12},{9,13},{10,... | collective-permute-start | bytes 786440 | tf_op jit(solution)/shard_map/ppermute | solution.py:424
  125.9 18.4 %collective-permute-start.5 = (bf16[8,64,256]{2,1,0:T(8,128)(2,1)S(1)}, bf16[8,64,256]{2,1,0:T(8,128)(2,1)}, u32[]{:S(2)}, u32[]{:S(2)}) collective-permute-start(bf16[8,64,256]{2,1,0:T(8,128)(2,1)S(1)} %all_to_all.21.same), channel_id=1, source_target_pairs={{0,6},{1,7},{2,4},{3,5},{4,2},{5,3},{6,0},{7,1},{8,14},{9,15},{10,... | collective-permute-start | bytes 786440 | tf_op jit(solution)/shard_map/ppermute | solution.py:424
  131.7 12.6 %collective-permute-start.4 = (bf16[8,64,256]{2,1,0:T(8,128)(2,1)S(1)}, bf16[8,64,256]{2,1,0:T(8,128)(2,1)}, u32[]{:S(2)}, u32[]{:S(2)}) collective-permute-start(bf16[8,64,256]{2,1,0:T(8,128)(2,1)S(1)} %all_to_all.21.same), channel_id=1, source_target_pairs={{0,2},{1,3},{2,0},{3,1},{4,6},{5,7},{6,4},{7,5},{8,10},{9,11},{10,... | collective-permute-start | bytes 786440 | tf_op jit(solution)/shard_map/ppermute | solution.py:424
  134.0 15.6 %collective-permute-start.6 = (bf16[4,672,512]{2,1,0:T(8,128)(2,1)}, bf16[4,672,512]{2,1,0:T(8,128)(2,1)S(1)}, u32[]{:S(2)}, u32[]{:S(2)}) collective-permute-start(bf16[4,672,512]{2,1,0:T(8,128)(2,1)} %bitcast.18), channel_id=1, source_target_pairs={{0,1},{1,0},{2,3},{3,2},{4,5},{5,4},{6,7},{7,6},{8,9},{9,8},{10,11... | collective-permute-start | bytes 8257544 | tf_op jit(solution)/shard_map/ppermute | solution.py:424
  142.3 0.7 copy-start.7
  143.0 1.0 copy-start.8
  144.4 10.1 %collective-permute-start.8 = (bf16[4,672,512]{2,1,0:T(8,128)(2,1)}, bf16[4,672,512]{2,1,0:T(8,128)(2,1)S(1)}, u32[]{:S(2)}, u32[]{:S(2)}) collective-permute-start(bf16[4,672,512]{2,1,0:T(8,128)(2,1)} %bitcast.21), channel_id=1, source_target_pairs={{0,1},{1,0},{2,3},{3,2},{4,5},{5,4},{6,7},{7,6},{8,9},{9,8},{10,11... | collective-permute-start | bytes 8257544 | tf_op jit(solution)/shard_map/ppermute | solution.py:424
  149.5 1.8 copy-start
  151.3 3.1 %copy-start.1 = (bf16[2688,512]{1,0:T(8,128)(2,1)S(1)}, bf16[2688,512]{1,0:T(8,128)(2,1)}, u32[]{:S(2)}) copy-start(bf16[2688,512]{1,0:T(8,128)(2,1)} %all-gather.6.cloned.1.call-done) | copy-start | bytes 8257540
  151.3 3.1 %copy-start.2 = (bf16[2688,512]{1,0:T(8,128)(2,1)S(1)}, bf16[2688,512]{1,0:T(8,128)(2,1)}, u32[]{:S(2)}) copy-start(bf16[2688,512]{1,0:T(8,128)(2,1)} %all-gather.8.cloned.1.call-done) | copy-start | bytes 8257540
  158.9 10.9 %collective-permute-start.9 = (bf16[8,128,128]{2,1,0:T(8,128)(2,1)S(1)}, bf16[8,128,128]{2,1,0:T(8,128)(2,1)S(1)}, u32[]{:S(2)}, u32[]{:S(2)}) collective-permute-start(bf16[8,128,128]{2,1,0:T(8,128)(2,1)S(1)} %get-tuple-element.43), channel_id=1, source_target_pairs={{0,2},{1,3},{2,0},{3,1},{4,6},{5,7},{6,4},{7,5},{8,10},{9,11},{10,... | collective-permute-start | bytes 786440 | tf_op jit(solution)/shard_map/ppermute | solution.py:424
  162.4 9.1 %collective-permute-start.10 = (bf16[8,128,128]{2,1,0:T(8,128)(2,1)S(1)}, bf16[8,128,128]{2,1,0:T(8,128)(2,1)S(1)}, u32[]{:S(2)}, u32[]{:S(2)}) collective-permute-start(bf16[8,128,128]{2,1,0:T(8,128)(2,1)S(1)} %get-tuple-element.44), channel_id=1, source_target_pairs={{0,4},{1,5},{2,6},{3,7},{4,0},{5,1},{6,2},{7,3},{8,12},{9,13},{10,... | collective-permute-start | bytes 786440 | tf_op jit(solution)/shard_map/ppermute | solution.py:424
  165.1 13.2 %collective-permute-start.11 = (bf16[8,128,128]{2,1,0:T(8,128)(2,1)S(1)}, bf16[8,128,128]{2,1,0:T(8,128)(2,1)S(1)}, u32[]{:S(2)}, u32[]{:S(2)}) collective-permute-start(bf16[8,128,128]{2,1,0:T(8,128)(2,1)S(1)} %get-tuple-element.45), channel_id=1, source_target_pairs={{0,6},{1,7},{2,4},{3,5},{4,2},{5,3},{6,0},{7,1},{8,14},{9,15},{10,... | collective-permute-start | bytes 786440 | tf_op jit(solution)/shard_map/ppermute | solution.py:424
  202.1 8.9 %collective-permute-start.12 = (bf16[64,128]{1,0:T(8,128)(2,1)S(1)}, bf16[64,128]{1,0:T(8,128)(2,1)S(1)}, u32[]{:S(2)}, u32[]{:S(2)}) collective-permute-start(bf16[64,128]{1,0:T(8,128)(2,1)S(1)} %get-tuple-element.48), channel_id=1, source_target_pairs={{0,1},{1,0},{2,3},{3,2},{4,5},{5,4},{6,7},{7,6},{8,9},{9,8},{10,11... | collective-permute-start | bytes 49160 | tf_op jit(solution)/shard_map/ppermute | solution.py:424
Sparse Core Ops, SparseCore 0:
  38.6 47.1 all-gather.5
  98.8 41.1 all-gather.7

commit v11 on v10

--- a/solution.py
+++ b/solution.py
@@ -57,13 +57,13 @@
     return pl.CostEstimate(flops=flops, bytes_accessed=nbytes, transcendentals=0)
 
 
-def project_kernel(after, normed, weights, cos, sin, send, keys, values, tables, sems):
+def project_kernel(after, core_out, far_out, cross_out, normed, weights, cos, sin, send, keys, values, tables, sems):
     copies = [pltpu.make_async_copy(ref, tables.at[i], sems.at[i]) for i, ref in enumerate((cos, sin))]
     for copy in copies:
         copy.start()
     total = jnp.zeros((256, 96), F32)
     for g in range(GROUPS):
-        total = total + nt(normed[g], weights[g, 0:96, :])
+        total = total + nt(normed[g], weights[g])
     total = jnp.concatenate([total, jnp.zeros((256, 32), F32)], axis=1)
     lane = lax.broadcasted_iota(jnp.int32, (256, 128), 1)
     partner = jnp.where(lane % 2 == 0, -pltpu.roll(total, 127, 1), pltpu.roll(total, 1, 1))
@@ -112,21 +112,10 @@
         out[:, a * 128 : a * 128 + 128] = mixed
 
 
-def output_kernel(got, mine, core, far, cross, own, out):
-    at = place()
-    parts = []
-    for w in (mine, core, far, cross):
-        total = jnp.zeros((HALF, QC), F32)
-        for g in range(GROUPS):
-            total = total + nt(got[2 * g], w[g, :, 0:BAND]) + nt(got[2 * g + 1], w[g, :, BAND:RUN])
-        parts.append(total)
-    blocks = []
-    for j in range(4):
-        picked = parts[0]
-        for k in range(1, 4):
-            picked = jnp.where(jnp.bitwise_xor(at[5], j) == k, parts[k], picked)
-        blocks.append(picked)
-    projected = jnp.concatenate(blocks, axis=1)
+def output_kernel(got, weights, own, out):
+    projected = jnp.zeros((HALF, BAND), F32)
+    for g in range(GROUPS):
+        projected = projected + nt(got[2 * g], weights[g, :, 0:BAND]) + nt(got[2 * g + 1], weights[g, :, BAND:RUN])
     attended = (own[...].astype(F32) + projected).astype(BF)
     for i in range(8):
         out[i] = attended
@@ -175,15 +164,8 @@
         out[i] = totals[i]
 
 
-def down_kernel(near, far, before, mine, mine_lo, core, core_lo, keep, to_y, to_z, to_both, held, sems):
+def down_kernel(near, far, before, mine, mine_lo, core, core_lo, keep, to_y, to_z, to_both):
     at = place()
-    copies = [
-        pltpu.make_async_copy(w.at[x, pl.ds(2 * FC, FC), :], held.at[i, x], sems.at[i, x])
-        for i, w in enumerate((mine, core))
-        for x in range(4)
-    ]
-    for copy in copies:
-        copy.start()
     low_y, low_z = at[1] == 0, at[3] == 0
     totals = [before[i] for i in range(4)]
     multiply(at, near, far, (mine_lo, core_lo), 1, totals)
@@ -193,14 +175,11 @@
         part = (gate / (1.0 + jnp.exp(-gate)) * totals[2 * i + 1]).astype(BF)
         first, second = part[0:HALF, :], part[HALF : 2 * HALF, :]
         units.append(jnp.concatenate([jnp.where(low_y, first, second), jnp.where(low_y, second, first)], axis=0))
-    for copy in copies:
-        copy.wait()
     for x in range(4):
-        for side in range(2):
+        for side, pair in enumerate(((mine, core), (mine_lo, core_lo))):
             total = jnp.zeros((128, RUN), F32)
-            for i, w in enumerate((mine_lo, core_lo)):
-                block = w[x, 2 * FC : 3 * FC, :] if side else held[i, x]
-                total = total + jnp.dot(units[i], block, preferred_element_type=F32)
+            for i, w in enumerate(pair):
+                total = total + jnp.dot(units[i], w[x, 2 * FC : 3 * FC, :], preferred_element_type=F32)
             g = jnp.bitwise_xor(at[6], side) * 4 + x
             blocks = [total[:, k * 128 : (k + 1) * 128] for k in range(4)]
             same = [jnp.where(low_z, blocks[k], blocks[2 + k]) for k in range(2)]
@@ -231,22 +210,45 @@
     give[...] = jnp.where(at[0] == 0, tail, head).astype(BF)
 
 
-def pack_kernel(query, key, value, out_part, out, token, held, sems):
+def spread(reads, held, out, sems):
+    for copy in reads:
+        copy.start()
+    for copy in reads:
+        copy.wait()
+    writes = [pltpu.make_async_copy(held, out.at[g], sems.at[len(reads) + g]) for g in range(GROUPS)]
+    for copy in writes:
+        copy.start()
+    for copy in writes:
+        copy.wait()
+
+
+def pack_kernel(query, key, value, out, token, held, sems):
     token[...] = jnp.zeros_like(token)
-    spans = ((query, 0, QC), (key, QC, KC), (value, QC + KC, KC), (out_part, 96, QC))
+    spans = ((query, 0, QC), (key, QC, KC), (value, QC + KC, KC))
     reads = [
         pltpu.make_async_copy(ref, held.at[pl.ds(start, rows), :], sems.at[i])
         for i, (ref, start, rows) in enumerate(spans)
     ]
-    for copy in reads:
-        copy.start()
-    for copy in reads:
-        copy.wait()
-    writes = [pltpu.make_async_copy(held, out.at[g], sems.at[4 + g]) for g in range(GROUPS)]
-    for copy in writes:
-        copy.start()
-    for copy in writes:
-        copy.wait()
+    spread(reads, held, out, sems)
+
+
+def pack_out_kernel(after, mine, core, far, cross, out):
+    quad = place()[5]
+    for k, ref in enumerate((mine, core, far, cross)):
+        rows = pl.ds(pl.multiple_of(jnp.bitwise_xor(quad, k) * QC, QC), QC)
+        for g in range(GROUPS):
+            out[g, rows, :] = ref[...]
+
+
+def pack_out(after, *parts):
+    return pl.pallas_call(
+        pack_out_kernel,
+        out_shape=jax.ShapeDtypeStruct((GROUPS, BAND, RUN), BF),
+        in_specs=[ANY] + [VMEM] * 4,
+        out_specs=VMEM,
+        compiler_params=params(16),
+        name="pack_out",
+    )(after, *parts)
 
 
 def norm_kernel(after, tables, stream, gain, normed, own, held, gains, sems):
@@ -310,16 +312,16 @@
 def pack(*parts):
     return pl.pallas_call(
         pack_kernel,
-        out_shape=(jax.ShapeDtypeStruct((GROUPS, 160, RUN), BF), jax.ShapeDtypeStruct((8, 128), F32)),
-        in_specs=[HBM] * 4,
+        out_shape=(jax.ShapeDtypeStruct((GROUPS, 96, RUN), BF), jax.ShapeDtypeStruct((8, 128), F32)),
+        in_specs=[HBM] * 3,
         out_specs=(HBM, VMEM),
-        scratch_shapes=[pltpu.VMEM((160, RUN), BF), pltpu.SemaphoreType.DMA((4 + GROUPS,))],
+        scratch_shapes=[pltpu.VMEM((96, RUN), BF), pltpu.SemaphoreType.DMA((3 + GROUPS,))],
         compiler_params=params(60),
         name="pack",
     )(*parts)
 
 
-def project(after, normed, weights, cos, sin):
+def project(after, traded, normed, weights, cos, sin):
     return pl.pallas_call(
         project_kernel,
         out_shape=(
@@ -327,12 +329,12 @@
             jax.ShapeDtypeStruct((KC, 256), BF),
             jax.ShapeDtypeStruct((KC, 256), BF),
         ),
-        in_specs=[ANY] + [VMEM] * 2 + [HBM] * 2,
+        in_specs=[ANY] * 4 + [VMEM] * 2 + [HBM] * 2,
         out_specs=(VMEM,) * 3,
         scratch_shapes=[pltpu.VMEM((2, 256, 128), F32), pltpu.SemaphoreType.DMA((2,))],
         compiler_params=params(24),
         name="project",
-    )(after, normed, weights, cos, sin)
+    )(after, *traded, normed, weights, cos, sin)
 
 
 def attend(lengths, got):
@@ -350,11 +352,11 @@
     return pl.pallas_call(
         output_kernel,
         out_shape=jax.ShapeDtypeStruct((8, HALF, BAND), BF),
-        in_specs=[VMEM] * 6,
+        in_specs=[VMEM] * 3,
         out_specs=VMEM,
         compiler_params=params(24),
         name="output",
-    )(got, *weights, own)
+    )(got, weights, own)
 
 
 def near_half(same, other, gain):
@@ -389,9 +391,8 @@
     return pl.pallas_call(
         down_kernel,
         out_shape=(jax.ShapeDtypeStruct((8, 128, 128), F32), part, part, part),
-        in_specs=[VMEM] * 3 + [HBM, VMEM, ANY, VMEM],
+        in_specs=[VMEM] * 7,
         out_specs=(VMEM,) * 4,
-        scratch_shapes=[pltpu.VMEM((2, 4, FC, RUN), BF), pltpu.SemaphoreType.DMA((2, 4))],
         compiler_params=params(16),
         cost_estimate=cost(4 * HALF * D * 4 * FC, 9 * 2**20),
         name="down",
@@ -461,7 +462,7 @@
     member = lax.axis_index("dev")
     core = member % 2
 
-    packed, token = pack(w_query.T, w_key.T, w_value.T, w_out.T)
+    packed, token = pack(w_query.T, w_key.T, w_value.T)
     first = lax.all_to_all(packed, "grp", 0, 0, tiled=True)
 
     lane = jnp.arange(128, dtype=jnp.int32)
@@ -473,13 +474,15 @@
     cos, sin = jnp.cos(angle), jnp.sin(angle)
 
     normed, own = norm(token, cos, stream, attn_gain.reshape(1, D))
+    own_out = after(w_out.T, token)
+    traded = (swap(own_out, 1), swap(own_out, 2), swap(own_out, 3))
     mine, token = join(token, w_gate.T, w_up.T, w_down.T)
-    send, keys, values = project(token, normed, first, cos, sin)
+    send, keys, values = project(token, traded, normed, first, cos, sin)
     got = trade(send, OCTETS)
     mine = after(mine, send)
+    out_weights = pack_out(got, own_out, *traded)
+    out_weights = lax.all_to_all(out_weights, "grp", 0, 0, tiled=True)
     mine_lo = swap_groups(after(mine, got))
-    out_own = first[:, 96:160, :]
-    out_weights = (out_own, swap(out_own, 1), swap(out_own, 2), swap(out_own, 3))
     mixed = collect(attend(row_length, got))
     attended = output(mixed, out_weights, own)
     mine, mine_lo = collect_x(mine), collect_x(after(mine_lo, attended))

time: 219 us -> 224 us (1.023)
  starting transfers between devices: 58.8 us -> 66 us
  blocking collectives: 94.4 us -> 99.2 us
  waiting for transfers between devices: 20.1 us -> 16.9 us
  Pallas kernels: 18.6 us -> 15.9 us
    all_to_all x1, waiting for transfers between devices: 9.45 us -> 0.01 us  [on_device(): first = lax.all_to_all(packed, 'grp', 0, 0, tiled=True)]
    all_gather x2, waiting for transfers between devices: 0.04 us -> 6.02 us  [collect_x(): lax.all_gather(x, 'grp', axis=0, axis_index_groups=[[0, 1, 2, 3], [4, 5,...]
    all_to_all x0 -> x1, starting transfers between devices: none -> 5.43 us  [on_device(): out_weights = lax.all_to_all(out_weights, 'grp', 0, 0, tiled=True)]
    all_to_all x3, blocking collectives: 62 us -> 66.8 us  [trade(): return lax.all_to_all(x, 'dev', 0, 0, axis_index_groups=groups, tiled=True)]
    pallas_call x1, Pallas kernels: 4.49 us -> 2.03 us  [down(): pl.pallas_call(down_kernel, out_shape=(jax.ShapeDtypeStruct((8, 128, 128)...]
    unnamed x36 -> x30, local copies, waits for them, and re-layouts: 10.1 us -> 9.07 us
  transfers between devices with their start and end apart: 16 -> 17, of which waited for: 6 -> 7; matrix products, arithmetic and copies ran while one was open for 1% -> 1% of each run, Pallas kernels for 4% -> 4%
where the time goes in v11:
time: 224 us; the launch traced here: 223 us
  blocking collectives  99.2 us (44%)
  starting transfers between devices  66 us (29%)
  waiting for transfers between devices  16.9 us (8%)
  Pallas kernels  15.9 us (7%)
  between operations  14.4 us (6%)
  local copies, waits for them, and re-layouts  9.07 us (4%)
    all_to_all x3, blocking collectives, trade(): return lax.all_to_all(x, 'dev', 0, 0, axis_index_groups=groups, tiled=True)  66.8 us
    ppermute x12, starting transfers between devices, swap(): return lax.ppermute(x, 'dev', [(d, d ^ bits) for d in range(MEMBERS)])  51.1 us
    all_gather x1, blocking collectives, collect(): return lax.all_gather(x, 'dev', axis=0, axis_index_groups=COLUMNS)  32.4 us
    ppermute x12, waiting for transfers between devices, swap(): return lax.ppermute(x, 'dev', [(d, d ^ bits) for d in range(MEMBERS)])  10.3 us
    unnamed x30, local copies, waits for them, and re-layouts  9.07 us
    all_gather x2, waiting for transfers between devices, collect_x(): lax.all_gather(x, 'grp', axis=0, axis_index_groups=[[0, 1, 2, 3], [4, 5,...  6.02 us
    all_to_all x1, starting transfers between devices, on_device(): first = lax.all_to_all(packed, 'grp', 0, 0, tiled=True)  5.87 us
    all_to_all x1, starting transfers between devices, on_device(): out_weights = lax.all_to_all(out_weights, 'grp', 0, 0, tiled=True)  5.43 us
  transfers between devices with their start and end apart: 17, of which 7 were waited for; matrix products, arithmetic and copies ran while one was open for 1% of the time, Pallas kernels for 4%

profile of v11, /device:TPU:1, one launch (start us, length us, event | category | flops | bytes accessed | tf_op | source)
XLA Modules:
  0.0 223.3 jit_solution(9181876783252476903)
XLA Ops:
  7.2 2.4 %pack.1 = (bf16[8,96,512]{2,1,0:T(8,128)(2,1)}, f32[8,128]{1,0:T(8,128)}) custom-call(bf16[64,512]{1,0:T(8,128)(2,1)} %bitcast.34, bf16[16,512]{1,0:T(8,128)(2,1)} %bitcast.35, bf16[16,512]{1,0:T(8,128)(2,1)} %bitcast.36), custom_call_target="tpu_custom_call" | custom-call | tf_op jit(solution)/shard_map/pack/pallas_call | solution.py:313
  9.6 5.9 %all-to-all-start = ((bf16[8,96,512]{2,1,0:T(8,128)(2,1)}), bf16[8,96,512]{2,1,0:T(8,128)(2,1)S(1)}, u32[]{:S(2)}, u32[]{:S(2)}) async-start(bf16[8,96,512]{2,1,0:T(8,128)(2,1)} %get-tuple-element.31), calls=%async_computation | async-start | bytes 1572864 | tf_op jit(solution)/shard_map/all_to_all | solution.py:466
  15.5 5.4 %collective-permute-start.2 = (bf16[64,512]{1,0:T(8,128)(2,1)}, bf16[64,512]{1,0:T(8,128)(2,1)S(1)}, u32[]{:S(2)}, u32[]{:S(2)}) collective-permute-start(bf16[64,512]{1,0:T(8,128)(2,1)} %bitcast.26), channel_id=1, source_target_pairs={{0,3},{1,2},{2,1},{3,0},{4,7},{5,6},{6,5},{7,4},{8,11},{9,10},{10,... | collective-permute-start | bytes 196616 | tf_op jit(solution)/shard_map/ppermute | solution.py:425
  20.9 5.9 %collective-permute-start.1 = (bf16[64,512]{1,0:T(8,128)(2,1)}, bf16[64,512]{1,0:T(8,128)(2,1)S(1)}, u32[]{:S(2)}, u32[]{:S(2)}) collective-permute-start(bf16[64,512]{1,0:T(8,128)(2,1)} %bitcast.27), channel_id=1, source_target_pairs={{0,2},{1,3},{2,0},{3,1},{4,6},{5,7},{6,4},{7,5},{8,10},{9,11},{10,... | collective-permute-start | bytes 196616 | tf_op jit(solution)/shard_map/ppermute | solution.py:425
  26.8 1.9 collective-permute-start
  28.7 0.7 convert_bitcast_fusion
  29.5 0.5 multiply_sine_fusion
  30.0 2.6 %join.1 = (bf16[672,512]{1,0:T(8,128)(2,1)}, f32[8,128]{1,0:T(8,128)}) custom-call(f32[8,128]{1,0:T(8,128)} %get-tuple-element.27.after, bf16[224,512]{1,0:T(8,128)(2,1)} %bitcast.31, bf16[224,512]{1,0:T(8,128)(2,1)} %bitcast.32, bf16[224,512]{1,0:T(8,128)(2,1)} %bitcast.33), custom_call_target="tpu_custom_call" | custom-call | tf_op jit(solution)/shard_map/join/pallas_call | solution.py:301
  32.7 1.6 copy-done.4
  34.3 0.7 copy-done.11
  35.0 0.7 copy-done.12
  35.7 1.4 norm.1
  37.1 0.6 copy-done.9
  37.7 0.7 copy-done.13
  38.4 1.8 project.1
  40.2 8.7 %all_to_all.25.got.after = bf16[8,64,128]{2,1,0:T(8,128)(2,1)S(1)} all-to-all(bf16[8,64,128]{2,1,0:T(8,128)(2,1)S(1)} %get-tuple-element.34), channel_id=1, replica_groups={{0,1,2,3,4,5,6,7},{8,9,10,11,12,13,14,15},{16,17,18,19,20,21,22,23},{24..., dimensions={0} | all-to-all | bytes 262144 | tf_op jit(solution)/shard_map/all_to_all | solution.py:437
  48.9 0.1 pack_out.1
  49.1 1.3 copy-done.2
  50.4 5.4 %all-to-all-start.2 = ((bf16[8,256,512]{2,1,0:T(8,128)(2,1)}), bf16[8,256,512]{2,1,0:T(8,128)(2,1)S(1)}, u32[]{:S(2)}, u32[]{:S(2)}) async-start(bf16[8,256,512]{2,1,0:T(8,128)(2,1)} %copy-done.2), calls=%async_computation.2 | async-start | bytes 4194304 | tf_op jit(solution)/shard_map/all_to_all | solution.py:484
  55.9 3.5 %collective-permute-start.7 = (bf16[672,512]{1,0:T(8,128)(2,1)}, bf16[672,512]{1,0:T(8,128)(2,1)}, u32[]{:S(2)}, u32[]{:S(2)}) collective-permute-start(bf16[672,512]{1,0:T(8,128)(2,1)} %get-tuple-element.41), channel_id=1, source_target_pairs={{0,256},{64,320},{128,384},{192,448},{256,0},{320,64},{384,128},{4... | collective-permute-start | bytes 2064392 | tf_op jit(solution)/shard_map/ppermute | solution.py:429
  59.4 1.4 attend.1
  60.8 32.4 %all-gather = bf16[1024,256]{1,0:T(8,128)(2,1)S(1)} all-gather(bf16[64,256]{1,0:T(8,128)(2,1)S(1)} %attend.1), channel_id=2, replica_groups={{0,4,8,12,16,20,24,28,32,36,40,44,48,52,56,60},{1,5,9,13,17,21,25,29,33..., dimensions={0}, use_global_device_ids=true | all-gather | bytes 557056 | tf_op jit(solution)/shard_map/all_gather | solution.py:441
  93.2 0.5 all-to-all-done.2.weights
  93.7 0.7 output.1
  94.5 28.3 %all_to_all.26.same = bf16[8,64,256]{2,1,0:T(8,128)(2,1)S(1)} all-to-all(bf16[8,64,256]{2,1,0:T(8,128)(2,1)S(1)} %output.1), channel_id=1, replica_groups={{0,8,16,24,32,40,48,56},{1,9,17,25,33,41,49,57},{2,10,18,26,34,42,50,58..., dimensions={0} | all-to-all | bytes 524288 | tf_op jit(solution)/shard_map/all_to_all | solution.py:437
  122.8 2.3 %collective-permute-start.3 = (bf16[8,64,256]{2,1,0:T(8,128)(2,1)S(1)}, bf16[8,64,256]{2,1,0:T(8,128)(2,1)S(1)}, u32[]{:S(2)}, u32[]{:S(2)}) collective-permute-start(bf16[8,64,256]{2,1,0:T(8,128)(2,1)S(1)} %all_to_all.26.same), channel_id=1, source_target_pairs={{0,4},{1,5},{2,6},{3,7},{4,0},{5,1},{6,2},{7,3},{8,12},{9,13},{10,... | collective-permute-start | bytes 786440 | tf_op jit(solution)/shard_map/ppermute | solution.py:425
  125.1 4.4 %collective-permute-start.5 = (bf16[8,64,256]{2,1,0:T(8,128)(2,1)S(1)}, bf16[8,64,256]{2,1,0:T(8,128)(2,1)}, u32[]{:S(2)}, u32[]{:S(2)}) collective-permute-start(bf16[8,64,256]{2,1,0:T(8,128)(2,1)S(1)} %all_to_all.26.same), channel_id=1, source_target_pairs={{0,6},{1,7},{2,4},{3,5},{4,2},{5,3},{6,0},{7,1},{8,14},{9,15},{10,... | collective-permute-start | bytes 786440 | tf_op jit(solution)/shard_map/ppermute | solution.py:425
  129.5 3.2 %collective-permute-start.4 = (bf16[8,64,256]{2,1,0:T(8,128)(2,1)S(1)}, bf16[8,64,256]{2,1,0:T(8,128)(2,1)}, u32[]{:S(2)}, u32[]{:S(2)}) collective-permute-start(bf16[8,64,256]{2,1,0:T(8,128)(2,1)S(1)} %all_to_all.26.same), channel_id=1, source_target_pairs={{0,2},{1,3},{2,0},{3,1},{4,6},{5,7},{6,4},{7,5},{8,10},{9,11},{10,... | collective-permute-start | bytes 786440 | tf_op jit(solution)/shard_map/ppermute | solution.py:425
  132.7 9.6 %collective-permute-start.6 = (bf16[4,672,512]{2,1,0:T(8,128)(2,1)}, bf16[4,672,512]{2,1,0:T(8,128)(2,1)S(1)}, u32[]{:S(2)}, u32[]{:S(2)}) collective-permute-start(bf16[4,672,512]{2,1,0:T(8,128)(2,1)} %bitcast.18), channel_id=1, source_target_pairs={{0,1},{1,0},{2,3},{3,2},{4,5},{5,4},{6,7},{7,6},{8,9},{9,8},{10,11... | collective-permute-start | bytes 8257544 | tf_op jit(solution)/shard_map/ppermute | solution.py:425
  142.4 0.7 copy-done.5
  143.1 1.0 copy-done.6
  144.0 0.3 near_half.1.near
  144.4 6.0 %all-gather.8.cloned.1.call-done = bf16[2688,512]{1,0:T(8,128)(2,1)} async-done(((bf16[672,512]{1,0:T(8,128)(2,1)}), bf16[2688,512]{1,0:T(8,128)(2,1)}) %all-gather.8.cloned.1.call-update) | async-done | bytes 2752528 | tf_op jit(solution)/shard_map/all_gather | solution.py:433
  150.4 2.6 %collective-permute-start.8 = (bf16[4,672,512]{2,1,0:T(8,128)(2,1)}, bf16[4,672,512]{2,1,0:T(8,128)(2,1)S(1)}, u32[]{:S(2)}, u32[]{:S(2)}) collective-permute-start(bf16[4,672,512]{2,1,0:T(8,128)(2,1)} %bitcast.21), channel_id=1, source_target_pairs={{0,1},{1,0},{2,3},{3,2},{4,5},{5,4},{6,7},{7,6},{8,9},{9,8},{10,11... | collective-permute-start | bytes 8257544 | tf_op jit(solution)/shard_map/ppermute | solution.py:425
  153.0 1.8 copy-done
  154.8 2.7 %own_rows.1 = (f32[4,128,224]{2,1,0:T(8,128)S(1)}, bf16[128,128]{1,0:T(8,128)(2,1)S(1)}, bf16[8,64,512]{2,1,0:T(8,128)(2,1)S(1)}) custom-call(bf16[8,64,512]{2,1,0:T(8,128)(2,1)S(1)} %near_half.1.near, bf16[8,64,256]{2,1,0:T(8,128)(2,1)S(1)} %all_to_all.26.same, bf16[8,64,256]{2,1,0:T(8,128)(2,1)} %collective-permute-done.4.far_same, ...), custom_call_target="tpu_custom_call" | custom-call | flops 469762048 | bytes 4194304 | tf_op jit(solution)/shard_map/own_rows/pallas_call | solution.py:374
  157.5 0.4 collective-permute-done.8.core_lo
  157.9 2.0 down.1
  159.9 4.6 %collective-permute-start.9 = (bf16[8,128,128]{2,1,0:T(8,128)(2,1)S(1)}, bf16[8,128,128]{2,1,0:T(8,128)(2,1)S(1)}, u32[]{:S(2)}, u32[]{:S(2)}) collective-permute-start(bf16[8,128,128]{2,1,0:T(8,128)(2,1)S(1)} %get-tuple-element.45), channel_id=1, source_target_pairs={{0,2},{1,3},{2,0},{3,1},{4,6},{5,7},{6,4},{7,5},{8,10},{9,11},{10,... | collective-permute-start | bytes 786440 | tf_op jit(solution)/shard_map/ppermute | solution.py:425
  164.6 3.2 %collective-permute-start.10 = (bf16[8,128,128]{2,1,0:T(8,128)(2,1)S(1)}, bf16[8,128,128]{2,1,0:T(8,128)(2,1)S(1)}, u32[]{:S(2)}, u32[]{:S(2)}) collective-permute-start(bf16[8,128,128]{2,1,0:T(8,128)(2,1)S(1)} %get-tuple-element.46), channel_id=1, source_target_pairs={{0,4},{1,5},{2,6},{3,7},{4,0},{5,1},{6,2},{7,3},{8,12},{9,13},{10,... | collective-permute-start | bytes 786440 | tf_op jit(solution)/shard_map/ppermute | solution.py:425
  167.7 2.1 collective-permute-start.11
  169.8 1.0 collective-permute-done.9.refs_0_
  170.9 2.8 %collective-permute-done.10.refs_1_ = bf16[8,128,128]{2,1,0:T(8,128)(2,1)S(1)} collective-permute-done((bf16[8,128,128]{2,1,0:T(8,128)(2,1)S(1)}, bf16[8,128,128]{2,1,0:T(8,128)(2,1)S(1)}, u32[]{:S(2)}, u32[]{:S(2)}) %collective-permute-start.10) | collective-permute-done | bytes 262176 | tf_op jit(solution)/shard_map/ppermute | solution.py:425
  173.7 5.3 %collective-permute-done.11.refs_2_ = bf16[8,128,128]{2,1,0:T(8,128)(2,1)S(1)} collective-permute-done((bf16[8,128,128]{2,1,0:T(8,128)(2,1)S(1)}, bf16[8,128,128]{2,1,0:T(8,128)(2,1)S(1)}, u32[]{:S(2)}, u32[]{:S(2)}) %collective-permute-start.11) | collective-permute-done | bytes 262176 | tf_op jit(solution)/shard_map/ppermute | solution.py:425
  179.0 29.8 %all_to_all.27.got = bf16[8,128,128]{2,1,0:T(8,128)(2,1)S(1)} all-to-all(bf16[8,128,128]{2,1,0:T(8,128)(2,1)S(1)} %add.89), channel_id=1, replica_groups={{0,8,16,24,32,40,48,56},{1,9,17,25,33,41,49,57},{2,10,18,26,34,42,50,58..., dimensions={0} | all-to-all | bytes 524288 | tf_op jit(solution)/shard_map/all_to_all | solution.py:437
  209.0 6.0 %collective-permute-start.12 = (bf16[64,128]{1,0:T(8,128)(2,1)S(1)}, bf16[64,128]{1,0:T(8,128)(2,1)S(1)}, u32[]{:S(2)}, u32[]{:S(2)}) collective-permute-start(bf16[64,128]{1,0:T(8,128)(2,1)S(1)} %get-tuple-element.50), channel_id=1, source_target_pairs={{0,1},{1,0},{2,3},{3,2},{4,5},{5,4},{6,7},{7,6},{8,9},{9,8},{10,11... | collective-permute-start | bytes 49160 | tf_op jit(solution)/shard_map/ppermute | solution.py:425
  215.0 0.8 collective-permute-done.12
  215.8 0.6 fusion
  (38 shorter events, 0.4 us)
Async XLA Ops:
  9.6 28.1 %all-to-all-start = ((bf16[8,96,512]{2,1,0:T(8,128)(2,1)}), bf16[8,96,512]{2,1,0:T(8,128)(2,1)S(1)}, u32[]{:S(2)}, u32[]{:S(2)}) async-start(bf16[8,96,512]{2,1,0:T(8,128)(2,1)} %get-tuple-element.31), calls=%async_computation | async-start | bytes 1572864 | tf_op jit(solution)/shard_map/all_to_all | solution.py:466
  15.5 117.3 %all-gather.6.cloned.1.call-start = ((), (), s32[]{:S(2)}) async-start(), calls=%async_computation.5 | async-start | bytes 3440640 | tf_op jit(solution)/shard_map/all_gather | solution.py:433
  15.5 22.2 %collective-permute-start.2 = (bf16[64,512]{1,0:T(8,128)(2,1)}, bf16[64,512]{1,0:T(8,128)(2,1)S(1)}, u32[]{:S(2)}, u32[]{:S(2)}) collective-permute-start(bf16[64,512]{1,0:T(8,128)(2,1)} %bitcast.26), channel_id=1, source_target_pairs={{0,3},{1,2},{2,1},{3,0},{4,7},{5,6},{6,5},{7,4},{8,11},{9,10},{10,... | collective-permute-start | bytes 196616 | tf_op jit(solution)/shard_map/ppermute | solution.py:425
  20.9 16.8 %collective-permute-start.1 = (bf16[64,512]{1,0:T(8,128)(2,1)}, bf16[64,512]{1,0:T(8,128)(2,1)S(1)}, u32[]{:S(2)}, u32[]{:S(2)}) collective-permute-start(bf16[64,512]{1,0:T(8,128)(2,1)} %bitcast.27), channel_id=1, source_target_pairs={{0,2},{1,3},{2,0},{3,1},{4,6},{5,7},{6,4},{7,5},{8,10},{9,11},{10,... | collective-permute-start | bytes 196616 | tf_op jit(solution)/shard_map/ppermute | solution.py:425
  26.8 10.9 %collective-permute-start = (bf16[64,512]{1,0:T(8,128)(2,1)}, bf16[64,512]{1,0:T(8,128)(2,1)S(1)}, u32[]{:S(2)}, u32[]{:S(2)}) collective-permute-start(bf16[64,512]{1,0:T(8,128)(2,1)} %bitcast.28), channel_id=1, source_target_pairs={{0,1},{1,0},{2,3},{3,2},{4,5},{5,4},{6,7},{7,6},{8,9},{9,8},{10,11... | collective-permute-start | bytes 196616 | tf_op jit(solution)/shard_map/ppermute | solution.py:425
  32.7 1.6 copy-start.4
  34.3 0.7 copy-start.11
  35.0 0.7 copy-start.12
  35.7 13.2 %copy-start.8 = (bf16[512,64]{0,1:T(8,128)(2,1)S(1)}, bf16[512,64]{0,1:T(8,128)(2,1)}, u32[]{:S(2)}) copy-start(bf16[512,64]{0,1:T(8,128)(2,1)} %param.19) | copy-start | bytes 196612
  37.1 0.6 copy-start.9
  37.7 0.7 copy-start.13
  48.9 10.5 %copy-start.14 = (s32[2]{0:T(128)S(1)}, s32[2]{0:T(128)}, u32[]{:S(2)}) copy-start(s32[2]{0:T(128)} %lengths.1) | copy-start | bytes 28
  49.1 1.4 copy-start.2
  50.4 43.3 %copy-start.10 = (bf16[64,256]{1,0:T(8,128)(2,1)S(1)}, bf16[64,256]{1,0:T(8,128)(2,1)}, u32[]{:S(2)}) copy-start(bf16[64,256]{1,0:T(8,128)(2,1)} %copy-done.9) | copy-start | bytes 98308
  50.4 43.3 %all-to-all-start.2 = ((bf16[8,256,512]{2,1,0:T(8,128)(2,1)}), bf16[8,256,512]{2,1,0:T(8,128)(2,1)S(1)}, u32[]{:S(2)}, u32[]{:S(2)}) async-start(bf16[8,256,512]{2,1,0:T(8,128)(2,1)} %copy-done.2), calls=%async_computation.2 | async-start | bytes 4194304 | tf_op jit(solution)/shard_map/all_to_all | solution.py:484
  55.8 87.2 %copy-start.7 = (f32[4096]{0:T(1024)S(1)}, f32[4096]{0:T(1024)}, u32[]{:S(2)}) copy-start(f32[4096]{0:T(1024)} %param.20) | copy-start | bytes 49156
  55.8 94.5 %all-gather.8.cloned.1.call-start = ((), (), s32[]{:S(2)}) async-start(), calls=%async_computation.6 | async-start | bytes 3440640 | tf_op jit(solution)/shard_map/all_gather | solution.py:433
  55.9 38.6 %collective-permute-start.7 = (bf16[672,512]{1,0:T(8,128)(2,1)}, bf16[672,512]{1,0:T(8,128)(2,1)}, u32[]{:S(2)}, u32[]{:S(2)}) collective-permute-start(bf16[672,512]{1,0:T(8,128)(2,1)} %get-tuple-element.41), channel_id=1, source_target_pairs={{0,256},{64,320},{128,384},{192,448},{256,0},{320,64},{384,128},{4... | collective-permute-start | bytes 2064392 | tf_op jit(solution)/shard_map/ppermute | solution.py:429
  122.8 19.6 %collective-permute-start.3 = (bf16[8,64,256]{2,1,0:T(8,128)(2,1)S(1)}, bf16[8,64,256]{2,1,0:T(8,128)(2,1)S(1)}, u32[]{:S(2)}, u32[]{:S(2)}) collective-permute-start(bf16[8,64,256]{2,1,0:T(8,128)(2,1)S(1)} %all_to_all.26.same), channel_id=1, source_target_pairs={{0,4},{1,5},{2,6},{3,7},{4,0},{5,1},{6,2},{7,3},{8,12},{9,13},{10,... | collective-permute-start | bytes 786440 | tf_op jit(solution)/shard_map/ppermute | solution.py:425
  125.1 19.2 %collective-permute-start.5 = (bf16[8,64,256]{2,1,0:T(8,128)(2,1)S(1)}, bf16[8,64,256]{2,1,0:T(8,128)(2,1)}, u32[]{:S(2)}, u32[]{:S(2)}) collective-permute-start(bf16[8,64,256]{2,1,0:T(8,128)(2,1)S(1)} %all_to_all.26.same), channel_id=1, source_target_pairs={{0,6},{1,7},{2,4},{3,5},{4,2},{5,3},{6,0},{7,1},{8,14},{9,15},{10,... | collective-permute-start | bytes 786440 | tf_op jit(solution)/shard_map/ppermute | solution.py:425
  129.5 14.9 %collective-permute-start.4 = (bf16[8,64,256]{2,1,0:T(8,128)(2,1)S(1)}, bf16[8,64,256]{2,1,0:T(8,128)(2,1)}, u32[]{:S(2)}, u32[]{:S(2)}) collective-permute-start(bf16[8,64,256]{2,1,0:T(8,128)(2,1)S(1)} %all_to_all.26.same), channel_id=1, source_target_pairs={{0,2},{1,3},{2,0},{3,1},{4,6},{5,7},{6,4},{7,5},{8,10},{9,11},{10,... | collective-permute-start | bytes 786440 | tf_op jit(solution)/shard_map/ppermute | solution.py:425
  132.7 20.2 %collective-permute-start.6 = (bf16[4,672,512]{2,1,0:T(8,128)(2,1)}, bf16[4,672,512]{2,1,0:T(8,128)(2,1)S(1)}, u32[]{:S(2)}, u32[]{:S(2)}) collective-permute-start(bf16[4,672,512]{2,1,0:T(8,128)(2,1)} %bitcast.18), channel_id=1, source_target_pairs={{0,1},{1,0},{2,3},{3,2},{4,5},{5,4},{6,7},{7,6},{8,9},{9,8},{10,11... | collective-permute-start | bytes 8257544 | tf_op jit(solution)/shard_map/ppermute | solution.py:425
  142.4 0.7 copy-start.5
  143.1 1.0 copy-start.6
  150.4 7.5 %collective-permute-start.8 = (bf16[4,672,512]{2,1,0:T(8,128)(2,1)}, bf16[4,672,512]{2,1,0:T(8,128)(2,1)S(1)}, u32[]{:S(2)}, u32[]{:S(2)}) collective-permute-start(bf16[4,672,512]{2,1,0:T(8,128)(2,1)} %bitcast.21), channel_id=1, source_target_pairs={{0,1},{1,0},{2,3},{3,2},{4,5},{5,4},{6,7},{7,6},{8,9},{9,8},{10,11... | collective-permute-start | bytes 8257544 | tf_op jit(solution)/shard_map/ppermute | solution.py:425
  153.0 1.8 copy-start
  154.8 3.1 %copy-start.1 = (bf16[2688,512]{1,0:T(8,128)(2,1)S(1)}, bf16[2688,512]{1,0:T(8,128)(2,1)}, u32[]{:S(2)}) copy-start(bf16[2688,512]{1,0:T(8,128)(2,1)} %all-gather.6.cloned.1.call-done) | copy-start | bytes 8257540
  154.8 3.1 %copy-start.3 = (bf16[2688,512]{1,0:T(8,128)(2,1)S(1)}, bf16[2688,512]{1,0:T(8,128)(2,1)}, u32[]{:S(2)}) copy-start(bf16[2688,512]{1,0:T(8,128)(2,1)} %all-gather.8.cloned.1.call-done) | copy-start | bytes 8257540
  159.9 10.9 %collective-permute-start.9 = (bf16[8,128,128]{2,1,0:T(8,128)(2,1)S(1)}, bf16[8,128,128]{2,1,0:T(8,128)(2,1)S(1)}, u32[]{:S(2)}, u32[]{:S(2)}) collective-permute-start(bf16[8,128,128]{2,1,0:T(8,128)(2,1)S(1)} %get-tuple-element.45), channel_id=1, source_target_pairs={{0,2},{1,3},{2,0},{3,1},{4,6},{5,7},{6,4},{7,5},{8,10},{9,11},{10,... | collective-permute-start | bytes 786440 | tf_op jit(solution)/shard_map/ppermute | solution.py:425
  164.6 9.1 %collective-permute-start.10 = (bf16[8,128,128]{2,1,0:T(8,128)(2,1)S(1)}, bf16[8,128,128]{2,1,0:T(8,128)(2,1)S(1)}, u32[]{:S(2)}, u32[]{:S(2)}) collective-permute-start(bf16[8,128,128]{2,1,0:T(8,128)(2,1)S(1)} %get-tuple-element.46), channel_id=1, source_target_pairs={{0,4},{1,5},{2,6},{3,7},{4,0},{5,1},{6,2},{7,3},{8,12},{9,13},{10,... | collective-permute-start | bytes 786440 | tf_op jit(solution)/shard_map/ppermute | solution.py:425
  167.7 11.2 %collective-permute-start.11 = (bf16[8,128,128]{2,1,0:T(8,128)(2,1)S(1)}, bf16[8,128,128]{2,1,0:T(8,128)(2,1)S(1)}, u32[]{:S(2)}, u32[]{:S(2)}) collective-permute-start(bf16[8,128,128]{2,1,0:T(8,128)(2,1)S(1)} %get-tuple-element.47), channel_id=1, source_target_pairs={{0,6},{1,7},{2,4},{3,5},{4,2},{5,3},{6,0},{7,1},{8,14},{9,15},{10,... | collective-permute-start | bytes 786440 | tf_op jit(solution)/shard_map/ppermute | solution.py:425
  209.0 6.8 %collective-permute-start.12 = (bf16[64,128]{1,0:T(8,128)(2,1)S(1)}, bf16[64,128]{1,0:T(8,128)(2,1)S(1)}, u32[]{:S(2)}, u32[]{:S(2)}) collective-permute-start(bf16[64,128]{1,0:T(8,128)(2,1)S(1)} %get-tuple-element.50), channel_id=1, source_target_pairs={{0,1},{1,0},{2,3},{3,2},{4,5},{5,4},{6,7},{7,6},{8,9},{9,8},{10,11... | collective-permute-start | bytes 49160 | tf_op jit(solution)/shard_map/ppermute | solution.py:425
Sparse Core Ops, SparseCore 0:
  40.4 64.4 all-gather.5
  107.0 43.3 all-gather.7

commit v12 on v10

--- a/solution.py
+++ b/solution.py
@@ -57,17 +57,24 @@
     return pl.CostEstimate(flops=flops, bytes_accessed=nbytes, transcendentals=0)
 
 
-def project_kernel(after, normed, weights, cos, sin, send, keys, values, tables, sems):
-    copies = [pltpu.make_async_copy(ref, tables.at[i], sems.at[i]) for i, ref in enumerate((cos, sin))]
+def project_kernel(normed, weights, cos, sin, send, keys, values, rows, cols, tables, sems):
+    copies = []
+    for g in range(GROUPS):
+        copies.append(pltpu.make_async_copy(normed.at[g], rows.at[g], sems.at[2 * g]))
+        copies.append(pltpu.make_async_copy(weights.at[g, pl.ds(0, 96), :], cols.at[g], sems.at[2 * g + 1]))
+    for i, ref in enumerate((cos, sin)):
+        copies.append(pltpu.make_async_copy(ref, tables.at[i], sems.at[2 * GROUPS + i]))
     for copy in copies:
         copy.start()
     total = jnp.zeros((256, 96), F32)
     for g in range(GROUPS):
-        total = total + nt(normed[g], weights[g, 0:96, :])
+        copies[2 * g].wait()
+        copies[2 * g + 1].wait()
+        total = total + nt(rows[g], cols[g])
     total = jnp.concatenate([total, jnp.zeros((256, 32), F32)], axis=1)
     lane = lax.broadcasted_iota(jnp.int32, (256, 128), 1)
     partner = jnp.where(lane % 2 == 0, -pltpu.roll(total, 127, 1), pltpu.roll(total, 1, 1))
-    for copy in copies:
+    for copy in copies[2 * GROUPS :]:
         copy.wait()
     turned = jnp.where(lane < QC + KC, total * tables[0] + partner * tables[1], total)
     turned = turned.astype(BF).astype(F32)
@@ -175,15 +182,8 @@
         out[i] = totals[i]
 
 
-def down_kernel(near, far, before, mine, mine_lo, core, core_lo, keep, to_y, to_z, to_both, held, sems):
-    at = place()
-    copies = [
-        pltpu.make_async_copy(w.at[x, pl.ds(2 * FC, FC), :], held.at[i, x], sems.at[i, x])
-        for i, w in enumerate((mine, core))
-        for x in range(4)
-    ]
-    for copy in copies:
-        copy.start()
+def down_kernel(near, far, before, mine, mine_lo, core, core_lo, keep, to_y, to_z, to_both):
+    at = place()
     low_y, low_z = at[1] == 0, at[3] == 0
     totals = [before[i] for i in range(4)]
     multiply(at, near, far, (mine_lo, core_lo), 1, totals)
@@ -193,14 +193,11 @@
         part = (gate / (1.0 + jnp.exp(-gate)) * totals[2 * i + 1]).astype(BF)
         first, second = part[0:HALF, :], part[HALF : 2 * HALF, :]
         units.append(jnp.concatenate([jnp.where(low_y, first, second), jnp.where(low_y, second, first)], axis=0))
-    for copy in copies:
-        copy.wait()
     for x in range(4):
-        for side in range(2):
+        for side, pair in enumerate(((mine, core), (mine_lo, core_lo))):
             total = jnp.zeros((128, RUN), F32)
-            for i, w in enumerate((mine_lo, core_lo)):
-                block = w[x, 2 * FC : 3 * FC, :] if side else held[i, x]
-                total = total + jnp.dot(units[i], block, preferred_element_type=F32)
+            for i, w in enumerate(pair):
+                total = total + jnp.dot(units[i], w[x, 2 * FC : 3 * FC, :], preferred_element_type=F32)
             g = jnp.bitwise_xor(at[6], side) * 4 + x
             blocks = [total[:, k * 128 : (k + 1) * 128] for k in range(4)]
             same = [jnp.where(low_z, blocks[k], blocks[2 + k]) for k in range(2)]
@@ -319,7 +316,7 @@
     )(*parts)
 
 
-def project(after, normed, weights, cos, sin):
+def project(normed, weights, cos, sin):
     return pl.pallas_call(
         project_kernel,
         out_shape=(
@@ -327,12 +324,17 @@
             jax.ShapeDtypeStruct((KC, 256), BF),
             jax.ShapeDtypeStruct((KC, 256), BF),
         ),
-        in_specs=[ANY] + [VMEM] * 2 + [HBM] * 2,
+        in_specs=[HBM] * 4,
         out_specs=(VMEM,) * 3,
-        scratch_shapes=[pltpu.VMEM((2, 256, 128), F32), pltpu.SemaphoreType.DMA((2,))],
-        compiler_params=params(24),
+        scratch_shapes=[
+            pltpu.VMEM((GROUPS, 256, RUN), BF),
+            pltpu.VMEM((GROUPS, 96, RUN), BF),
+            pltpu.VMEM((2, 256, 128), F32),
+            pltpu.SemaphoreType.DMA((2 * GROUPS + 2,)),
+        ],
+        compiler_params=params(58),
         name="project",
-    )(after, normed, weights, cos, sin)
+    )(normed, weights, cos, sin)
 
 
 def attend(lengths, got):
@@ -389,9 +391,8 @@
     return pl.pallas_call(
         down_kernel,
         out_shape=(jax.ShapeDtypeStruct((8, 128, 128), F32), part, part, part),
-        in_specs=[VMEM] * 3 + [HBM, VMEM, ANY, VMEM],
+        in_specs=[VMEM] * 7,
         out_specs=(VMEM,) * 4,
-        scratch_shapes=[pltpu.VMEM((2, 4, FC, RUN), BF), pltpu.SemaphoreType.DMA((2, 4))],
         compiler_params=params(16),
         cost_estimate=cost(4 * HALF * D * 4 * FC, 9 * 2**20),
         name="down",
@@ -472,9 +473,9 @@
     angle = positions.astype(F32)[:, None] * freq[None, :]
     cos, sin = jnp.cos(angle), jnp.sin(angle)
 
+    mine, token = join(token, w_gate.T, w_up.T, w_down.T)
     normed, own = norm(token, cos, stream, attn_gain.reshape(1, D))
-    mine, token = join(token, w_gate.T, w_up.T, w_down.T)
-    send, keys, values = project(token, normed, first, cos, sin)
+    send, keys, values = project(normed, first, cos, sin)
     got = trade(send, OCTETS)
     mine = after(mine, send)
     mine_lo = swap_groups(after(mine, got))

time: 219 us -> 214 us (0.977)
  local copies, waits for them, and re-layouts: 10.1 us -> 7.43 us
    unnamed x36 -> x30, local copies, waits for them, and re-layouts: 10.1 us -> 6.35 us
    pallas_call x1, Pallas kernels: 4.49 us -> 2.03 us  [down(): pl.pallas_call(down_kernel, out_shape=(jax.ShapeDtypeStruct((8, 128, 128)...]
where the time goes in v12:
time: 214 us; the launch traced here: 213 us
  blocking collectives  93 us (43%)
  starting transfers between devices  58.8 us (27%)
  waiting for transfers between devices  19.9 us (9%)
  Pallas kernels  18 us (8%)
  between operations  14.4 us (7%)
  local copies, waits for them, and re-layouts  7.43 us (3%)
    all_to_all x3, blocking collectives, trade(): return lax.all_to_all(x, 'dev', 0, 0, axis_index_groups=groups, tiled=True)  60.2 us
    ppermute x12, starting transfers between devices, swap(): return lax.ppermute(x, 'dev', [(d, d ^ bits) for d in range(MEMBERS)])  50.8 us
    all_gather x1, blocking collectives, collect(): return lax.all_gather(x, 'dev', axis=0, axis_index_groups=COLUMNS)  32.8 us
    ppermute x12, waiting for transfers between devices, swap(): return lax.ppermute(x, 'dev', [(d, d ^ bits) for d in range(MEMBERS)])  10.6 us
    all_to_all x1, waiting for transfers between devices, on_device(): first = lax.all_to_all(packed, 'grp', 0, 0, tiled=True)  9.17 us
    unnamed x30, local copies, waits for them, and re-layouts  6.35 us
    all_to_all x1, starting transfers between devices, on_device(): first = lax.all_to_all(packed, 'grp', 0, 0, tiled=True)  5.87 us
  transfers between devices with their start and end apart: 16, of which 6 were waited for; matrix products, arithmetic and copies ran while one was open for 1% of the time, Pallas kernels for 4%

profile of v12, /device:TPU:1, one launch (start us, length us, event | category | flops | bytes accessed | tf_op | source)
XLA Modules:
  0.0 213.4 jit_solution(6242465404080175603)
XLA Ops:
  7.2 2.9 %pack.1 = (bf16[8,160,512]{2,1,0:T(8,128)(2,1)}, f32[8,128]{1,0:T(8,128)}) custom-call(bf16[64,512]{1,0:T(8,128)(2,1)} %bitcast.30, bf16[16,512]{1,0:T(8,128)(2,1)} %bitcast.32, bf16[16,512]{1,0:T(8,128)(2,1)} %bitcast.33, bf16[64,512]{1,0:T(8,128)(2,1)} %bitcast.31), custom_call_target="tpu_custom_call" | custom-call | tf_op jit(solution)/shard_map/pack/pallas_call | solution.py:308
  10.1 5.9 %all-to-all-start = ((bf16[8,160,512]{2,1,0:T(8,128)(2,1)}), bf16[8,160,512]{2,1,0:T(8,128)(2,1)}, u32[]{:S(2)}, u32[]{:S(2)}) async-start(bf16[8,160,512]{2,1,0:T(8,128)(2,1)} %get-tuple-element.29), calls=%async_computation | async-start | bytes 2621440 | tf_op jit(solution)/shard_map/all_to_all | solution.py:466
  16.0 0.0 all-gather.6.cloned.1.call-start
  16.0 2.6 %join.1 = (bf16[672,512]{1,0:T(8,128)(2,1)}, f32[8,128]{1,0:T(8,128)}) custom-call(f32[8,128]{1,0:T(8,128)} %get-tuple-element.26.after, bf16[224,512]{1,0:T(8,128)(2,1)} %bitcast.27, bf16[224,512]{1,0:T(8,128)(2,1)} %bitcast.28, bf16[224,512]{1,0:T(8,128)(2,1)} %bitcast.29), custom_call_target="tpu_custom_call" | custom-call | tf_op jit(solution)/shard_map/join/pallas_call | solution.py:296
  18.7 0.1 convert_bitcast_fusion
  18.8 1.2 multiply_sine_fusion
  20.0 0.7 copy-done.10
  20.7 1.4 norm.1
  22.1 1.4 copy-done.3
  23.5 9.2 %all-to-all-done.weights = bf16[8,160,512]{2,1,0:T(8,128)(2,1)} async-done(((bf16[8,160,512]{2,1,0:T(8,128)(2,1)}), bf16[8,160,512]{2,1,0:T(8,128)(2,1)}, u32[]{:S(2)}, u32[]{:S(2)}) %all-to-all-start) | async-done | bytes 1310752 | tf_op jit(solution)/shard_map/all_to_all | solution.py:466
  32.6 3.6 %project.1 = (bf16[8,64,128]{2,1,0:T(8,128)(2,1)}, bf16[16,256]{1,0:T(8,128)(2,1)}, bf16[16,256]{1,0:T(8,128)(2,1)}) custom-call(bf16[8,256,512]{2,1,0:T(8,128)(2,1)} %copy-done.3, bf16[8,160,512]{2,1,0:T(8,128)(2,1)} %all-to-all-done.weights, f32[256,128]{1,0:T(8,128)} %copy-done.5, f32[256,128]{1,0:T(8,128)} %get-tuple-element.49.sin), custom_call_target="tpu_custom_call" | custom-call | tf_op jit(solution)/shard_map/project/pallas_call | solution.py:320
  36.2 0.0 all-gather.8.cloned.1.call-start
  36.3 14.2 %all_to_all.20.got = bf16[8,64,128]{2,1,0:T(8,128)(2,1)S(1)} all-to-all(bf16[8,64,128]{2,1,0:T(8,128)(2,1)} %get-tuple-element.32), channel_id=1, replica_groups={{0,1,2,3,4,5,6,7},{8,9,10,11,12,13,14,15},{16,17,18,19,20,21,22,23},{24..., dimensions={0} | all-to-all | bytes 262144 | tf_op jit(solution)/shard_map/all_to_all | solution.py:437
  50.5 2.0 collective-permute-start.7
  52.5 1.1 slice.4.mine
  53.6 3.9 %collective-permute-start.2 = (bf16[8,64,512]{2,1,0:T(8,128)(2,1)S(1)}, bf16[8,64,512]{2,1,0:T(8,128)(2,1)S(1)}, u32[]{:S(2)}, u32[]{:S(2)}) collective-permute-start(bf16[8,64,512]{2,1,0:T(8,128)(2,1)S(1)} %slice.4.mine), channel_id=1, source_target_pairs={{0,3},{1,2},{2,1},{3,0},{4,7},{5,6},{6,5},{7,4},{8,11},{9,10},{10,... | collective-permute-start | bytes 1572872 | tf_op jit(solution)/shard_map/ppermute | solution.py:425
  57.5 3.7 %collective-permute-start.1 = (bf16[8,64,512]{2,1,0:T(8,128)(2,1)S(1)}, bf16[8,64,512]{2,1,0:T(8,128)(2,1)S(1)}, u32[]{:S(2)}, u32[]{:S(2)}) collective-permute-start(bf16[8,64,512]{2,1,0:T(8,128)(2,1)S(1)} %slice.4.mine), channel_id=1, source_target_pairs={{0,2},{1,3},{2,0},{3,1},{4,6},{5,7},{6,4},{7,5},{8,10},{9,11},{10,... | collective-permute-start | bytes 1572872 | tf_op jit(solution)/shard_map/ppermute | solution.py:425
  61.2 1.9 collective-permute-start
  63.2 1.4 attend.1
  64.6 32.8 %all-gather = bf16[1024,256]{1,0:T(8,128)(2,1)S(1)} all-gather(bf16[64,256]{1,0:T(8,128)(2,1)S(1)} %attend.1), channel_id=2, replica_groups={{0,4,8,12,16,20,24,28,32,36,40,44,48,52,56,60},{1,5,9,13,17,21,25,29,33..., dimensions={0}, use_global_device_ids=true | all-gather | bytes 557056 | tf_op jit(solution)/shard_map/all_gather | solution.py:441
  97.4 0.8 output.1
  98.2 0.8 copy-done.13
  99.0 22.8 %all_to_all.21.same = bf16[8,64,256]{2,1,0:T(8,128)(2,1)S(1)} all-to-all(bf16[8,64,256]{2,1,0:T(8,128)(2,1)S(1)} %output.1), channel_id=1, replica_groups={{0,8,16,24,32,40,48,56},{1,9,17,25,33,41,49,57},{2,10,18,26,34,42,50,58..., dimensions={0} | all-to-all | bytes 524288 | tf_op jit(solution)/shard_map/all_to_all | solution.py:437
  121.8 2.9 %collective-permute-start.3 = (bf16[8,64,256]{2,1,0:T(8,128)(2,1)S(1)}, bf16[8,64,256]{2,1,0:T(8,128)(2,1)S(1)}, u32[]{:S(2)}, u32[]{:S(2)}) collective-permute-start(bf16[8,64,256]{2,1,0:T(8,128)(2,1)S(1)} %all_to_all.21.same), channel_id=1, source_target_pairs={{0,4},{1,5},{2,6},{3,7},{4,0},{5,1},{6,2},{7,3},{8,12},{9,13},{10,... | collective-permute-start | bytes 786440 | tf_op jit(solution)/shard_map/ppermute | solution.py:425
  124.8 5.0 %collective-permute-start.5 = (bf16[8,64,256]{2,1,0:T(8,128)(2,1)S(1)}, bf16[8,64,256]{2,1,0:T(8,128)(2,1)}, u32[]{:S(2)}, u32[]{:S(2)}) collective-permute-start(bf16[8,64,256]{2,1,0:T(8,128)(2,1)S(1)} %all_to_all.21.same), channel_id=1, source_target_pairs={{0,6},{1,7},{2,4},{3,5},{4,2},{5,3},{6,0},{7,1},{8,14},{9,15},{10,... | collective-permute-start | bytes 786440 | tf_op jit(solution)/shard_map/ppermute | solution.py:425
  129.8 1.9 collective-permute-start.4
  131.7 0.0 all-gather.6.cloned.1.call-done
  131.7 9.5 %collective-permute-start.6 = (bf16[4,672,512]{2,1,0:T(8,128)(2,1)}, bf16[4,672,512]{2,1,0:T(8,128)(2,1)S(1)}, u32[]{:S(2)}, u32[]{:S(2)}) collective-permute-start(bf16[4,672,512]{2,1,0:T(8,128)(2,1)} %bitcast.18), channel_id=1, source_target_pairs={{0,1},{1,0},{2,3},{3,2},{4,5},{5,4},{6,7},{7,6},{8,9},{9,8},{10,11... | collective-permute-start | bytes 8257544 | tf_op jit(solution)/shard_map/ppermute | solution.py:425
  141.3 0.7 copy-done.6
  142.0 0.9 copy-done.7
  142.9 0.3 near_half.1.near
  143.3 5.1 %collective-permute-start.8 = (bf16[4,672,512]{2,1,0:T(8,128)(2,1)}, bf16[4,672,512]{2,1,0:T(8,128)(2,1)S(1)}, u32[]{:S(2)}, u32[]{:S(2)}) collective-permute-start(bf16[4,672,512]{2,1,0:T(8,128)(2,1)} %bitcast.21), channel_id=1, source_target_pairs={{0,1},{1,0},{2,3},{3,2},{4,5},{5,4},{6,7},{7,6},{8,9},{9,8},{10,11... | collective-permute-start | bytes 8257544 | tf_op jit(solution)/shard_map/ppermute | solution.py:425
  148.4 1.8 copy-done
  150.2 2.7 %own_rows.1 = (f32[4,128,224]{2,1,0:T(8,128)S(1)}, bf16[128,128]{1,0:T(8,128)(2,1)S(1)}, bf16[8,64,512]{2,1,0:T(8,128)(2,1)S(1)}) custom-call(bf16[8,64,512]{2,1,0:T(8,128)(2,1)S(1)} %near_half.1.near, bf16[8,64,256]{2,1,0:T(8,128)(2,1)S(1)} %all_to_all.21.same, bf16[8,64,256]{2,1,0:T(8,128)(2,1)} %collective-permute-done.4.far_same, ...), custom_call_target="tpu_custom_call" | custom-call | flops 469762048 | bytes 4194304 | tf_op jit(solution)/shard_map/own_rows/pallas_call | solution.py:374
  153.0 0.4 collective-permute-done.8.core_lo
  153.3 2.0 down.1
  155.4 2.4 %collective-permute-start.9 = (bf16[8,128,128]{2,1,0:T(8,128)(2,1)S(1)}, bf16[8,128,128]{2,1,0:T(8,128)(2,1)S(1)}, u32[]{:S(2)}, u32[]{:S(2)}) collective-permute-start(bf16[8,128,128]{2,1,0:T(8,128)(2,1)S(1)} %get-tuple-element.43), channel_id=1, source_target_pairs={{0,2},{1,3},{2,0},{3,1},{4,6},{5,7},{6,4},{7,5},{8,10},{9,11},{10,... | collective-permute-start | bytes 786440 | tf_op jit(solution)/shard_map/ppermute | solution.py:425
  157.8 3.2 %collective-permute-start.10 = (bf16[8,128,128]{2,1,0:T(8,128)(2,1)S(1)}, bf16[8,128,128]{2,1,0:T(8,128)(2,1)S(1)}, u32[]{:S(2)}, u32[]{:S(2)}) collective-permute-start(bf16[8,128,128]{2,1,0:T(8,128)(2,1)S(1)} %get-tuple-element.44), channel_id=1, source_target_pairs={{0,4},{1,5},{2,6},{3,7},{4,0},{5,1},{6,2},{7,3},{8,12},{9,13},{10,... | collective-permute-start | bytes 786440 | tf_op jit(solution)/shard_map/ppermute | solution.py:425
  161.0 4.3 %collective-permute-start.11 = (bf16[8,128,128]{2,1,0:T(8,128)(2,1)S(1)}, bf16[8,128,128]{2,1,0:T(8,128)(2,1)S(1)}, u32[]{:S(2)}, u32[]{:S(2)}) collective-permute-start(bf16[8,128,128]{2,1,0:T(8,128)(2,1)S(1)} %get-tuple-element.45), channel_id=1, source_target_pairs={{0,6},{1,7},{2,4},{3,5},{4,2},{5,3},{6,0},{7,1},{8,14},{9,15},{10,... | collective-permute-start | bytes 786440 | tf_op jit(solution)/shard_map/ppermute | solution.py:425
  165.3 1.0 collective-permute-done.9.refs_0_
  166.3 0.6 collective-permute-done.10.refs_1_
  166.8 7.8 %collective-permute-done.11.refs_2_ = bf16[8,128,128]{2,1,0:T(8,128)(2,1)S(1)} collective-permute-done((bf16[8,128,128]{2,1,0:T(8,128)(2,1)S(1)}, bf16[8,128,128]{2,1,0:T(8,128)(2,1)S(1)}, u32[]{:S(2)}, u32[]{:S(2)}) %collective-permute-start.11) | collective-permute-done | bytes 262176 | tf_op jit(solution)/shard_map/ppermute | solution.py:425
  174.7 0.1 add.89
  174.8 23.2 %all_to_all.22.got = bf16[8,128,128]{2,1,0:T(8,128)(2,1)S(1)} all-to-all(bf16[8,128,128]{2,1,0:T(8,128)(2,1)S(1)} %add.89), channel_id=1, replica_groups={{0,8,16,24,32,40,48,56},{1,9,17,25,33,41,49,57},{2,10,18,26,34,42,50,58..., dimensions={0} | all-to-all | bytes 524288 | tf_op jit(solution)/shard_map/all_to_all | solution.py:437
  198.0 0.1 finish.1
  198.2 7.0 %collective-permute-start.12 = (bf16[64,128]{1,0:T(8,128)(2,1)S(1)}, bf16[64,128]{1,0:T(8,128)(2,1)S(1)}, u32[]{:S(2)}, u32[]{:S(2)}) collective-permute-start(bf16[64,128]{1,0:T(8,128)(2,1)S(1)} %get-tuple-element.48), channel_id=1, source_target_pairs={{0,1},{1,0},{2,3},{3,2},{4,5},{5,4},{6,7},{7,6},{8,9},{9,8},{10,11... | collective-permute-start | bytes 49160 | tf_op jit(solution)/shard_map/ppermute | solution.py:425
  205.1 0.8 collective-permute-done.12
  205.9 0.6 fusion
  (36 shorter events, 0.1 us)
Async XLA Ops:
  7.2 11.5 %copy-start.14 = (s32[2]{0:T(128)S(1)}, s32[2]{0:T(128)}, u32[]{:S(2)}) copy-start(s32[2]{0:T(128)} %param.14) | copy-start | bytes 28
  7.2 12.8 %copy-start.9 = (f32[4096]{0:T(1024)S(1)}, f32[4096]{0:T(1024)}, u32[]{:S(2)}) copy-start(f32[4096]{0:T(1024)} %param.15) | copy-start | bytes 49156
  7.2 12.8 %copy-start.4 = (bf16[256,4096]{1,0:T(8,128)(2,1)S(1)}, bf16[256,4096]{1,0:T(8,128)(2,1)}, u32[]{:S(2)}) copy-start(bf16[256,4096]{1,0:T(8,128)(2,1)} %stream.1) | copy-start | bytes 6291460
  10.1 22.6 %all-to-all-start = ((bf16[8,160,512]{2,1,0:T(8,128)(2,1)}), bf16[8,160,512]{2,1,0:T(8,128)(2,1)}, u32[]{:S(2)}, u32[]{:S(2)}) async-start(bf16[8,160,512]{2,1,0:T(8,128)(2,1)} %get-tuple-element.29), calls=%async_computation | async-start | bytes 2621440 | tf_op jit(solution)/shard_map/all_to_all | solution.py:466
  16.0 115.8 %all-gather.6.cloned.1.call-start = ((), (), s32[]{:S(2)}) async-start(), calls=%async_computation.4 | async-start | bytes 3440640 | tf_op jit(solution)/shard_map/all_gather | solution.py:433
  20.0 12.7 %copy-start.5 = (f32[256,128]{1,0:T(8,128)}, f32[256,128]{1,0:T(8,128)S(1)}, u32[]{:S(2)}) copy-start(f32[256,128]{1,0:T(8,128)S(1)} %get-tuple-element.50.tables.cos) | copy-start | bytes 393220
  20.0 0.7 copy-start.10
  22.1 1.4 copy-start.3
  23.5 27.0 %copy-start.12 = (bf16[672,512]{1,0:T(8,128)(2,1)S(1)}, bf16[672,512]{1,0:T(8,128)(2,1)}, u32[]{:S(2)}) copy-start(bf16[672,512]{1,0:T(8,128)(2,1)} %get-tuple-element.39) | copy-start | bytes 2064388
  32.6 30.5 %copy-start.11 = (s32[2]{0:T(128)S(1)}, s32[2]{0:T(128)}, u32[]{:S(2)}) copy-start(s32[2]{0:T(128)} %lengths.1) | copy-start | bytes 28
  36.2 107.0 %all-gather.8.cloned.1.call-start = ((), (), s32[]{:S(2)}) async-start(), calls=%async_computation.5 | async-start | bytes 3440640 | tf_op jit(solution)/shard_map/all_gather | solution.py:433
  50.5 91.5 %copy-start.8 = (f32[4096]{0:T(1024)S(1)}, f32[4096]{0:T(1024)}, u32[]{:S(2)}) copy-start(f32[4096]{0:T(1024)} %param.20) | copy-start | bytes 49156
  50.5 47.7 %collective-permute-start.7 = (bf16[672,512]{1,0:T(8,128)(2,1)S(1)}, bf16[672,512]{1,0:T(8,128)(2,1)S(1)}, u32[]{:S(2)}, u32[]{:S(2)}) collective-permute-start(bf16[672,512]{1,0:T(8,128)(2,1)S(1)} %copy-done.12), channel_id=1, source_target_pairs={{0,256},{64,320},{128,384},{192,448},{256,0},{320,64},{384,128},{4... | collective-permute-start | bytes 2064392 | tf_op jit(solution)/shard_map/ppermute | solution.py:429
  53.6 43.8 %collective-permute-start.2 = (bf16[8,64,512]{2,1,0:T(8,128)(2,1)S(1)}, bf16[8,64,512]{2,1,0:T(8,128)(2,1)S(1)}, u32[]{:S(2)}, u32[]{:S(2)}) collective-permute-start(bf16[8,64,512]{2,1,0:T(8,128)(2,1)S(1)} %slice.4.mine), channel_id=1, source_target_pairs={{0,3},{1,2},{2,1},{3,0},{4,7},{5,6},{6,5},{7,4},{8,11},{9,10},{10,... | collective-permute-start | bytes 1572872 | tf_op jit(solution)/shard_map/ppermute | solution.py:425
  57.5 39.9 %collective-permute-start.1 = (bf16[8,64,512]{2,1,0:T(8,128)(2,1)S(1)}, bf16[8,64,512]{2,1,0:T(8,128)(2,1)S(1)}, u32[]{:S(2)}, u32[]{:S(2)}) collective-permute-start(bf16[8,64,512]{2,1,0:T(8,128)(2,1)S(1)} %slice.4.mine), channel_id=1, source_target_pairs={{0,2},{1,3},{2,0},{3,1},{4,6},{5,7},{6,4},{7,5},{8,10},{9,11},{10,... | collective-permute-start | bytes 1572872 | tf_op jit(solution)/shard_map/ppermute | solution.py:425
  61.2 36.1 %collective-permute-start = (bf16[8,64,512]{2,1,0:T(8,128)(2,1)S(1)}, bf16[8,64,512]{2,1,0:T(8,128)(2,1)S(1)}, u32[]{:S(2)}, u32[]{:S(2)}) collective-permute-start(bf16[8,64,512]{2,1,0:T(8,128)(2,1)S(1)} %slice.4.mine), channel_id=1, source_target_pairs={{0,1},{1,0},{2,3},{3,2},{4,5},{5,4},{6,7},{7,6},{8,9},{9,8},{10,11... | collective-permute-start | bytes 1572872 | tf_op jit(solution)/shard_map/ppermute | solution.py:425
  98.2 0.9 copy-start.13
  121.8 19.5 %collective-permute-start.3 = (bf16[8,64,256]{2,1,0:T(8,128)(2,1)S(1)}, bf16[8,64,256]{2,1,0:T(8,128)(2,1)S(1)}, u32[]{:S(2)}, u32[]{:S(2)}) collective-permute-start(bf16[8,64,256]{2,1,0:T(8,128)(2,1)S(1)} %all_to_all.21.same), channel_id=1, source_target_pairs={{0,4},{1,5},{2,6},{3,7},{4,0},{5,1},{6,2},{7,3},{8,12},{9,13},{10,... | collective-permute-start | bytes 786440 | tf_op jit(solution)/shard_map/ppermute | solution.py:425
  124.8 18.5 %collective-permute-start.5 = (bf16[8,64,256]{2,1,0:T(8,128)(2,1)S(1)}, bf16[8,64,256]{2,1,0:T(8,128)(2,1)}, u32[]{:S(2)}, u32[]{:S(2)}) collective-permute-start(bf16[8,64,256]{2,1,0:T(8,128)(2,1)S(1)} %all_to_all.21.same), channel_id=1, source_target_pairs={{0,6},{1,7},{2,4},{3,5},{4,2},{5,3},{6,0},{7,1},{8,14},{9,15},{10,... | collective-permute-start | bytes 786440 | tf_op jit(solution)/shard_map/ppermute | solution.py:425
  129.8 13.5 %collective-permute-start.4 = (bf16[8,64,256]{2,1,0:T(8,128)(2,1)S(1)}, bf16[8,64,256]{2,1,0:T(8,128)(2,1)}, u32[]{:S(2)}, u32[]{:S(2)}) collective-permute-start(bf16[8,64,256]{2,1,0:T(8,128)(2,1)S(1)} %all_to_all.21.same), channel_id=1, source_target_pairs={{0,2},{1,3},{2,0},{3,1},{4,6},{5,7},{6,4},{7,5},{8,10},{9,11},{10,... | collective-permute-start | bytes 786440 | tf_op jit(solution)/shard_map/ppermute | solution.py:425
  131.7 16.7 %collective-permute-start.6 = (bf16[4,672,512]{2,1,0:T(8,128)(2,1)}, bf16[4,672,512]{2,1,0:T(8,128)(2,1)S(1)}, u32[]{:S(2)}, u32[]{:S(2)}) collective-permute-start(bf16[4,672,512]{2,1,0:T(8,128)(2,1)} %bitcast.18), channel_id=1, source_target_pairs={{0,1},{1,0},{2,3},{3,2},{4,5},{5,4},{6,7},{7,6},{8,9},{9,8},{10,11... | collective-permute-start | bytes 8257544 | tf_op jit(solution)/shard_map/ppermute | solution.py:425
  141.3 0.7 copy-start.6
  142.0 1.0 copy-start.7
  143.3 10.0 %collective-permute-start.8 = (bf16[4,672,512]{2,1,0:T(8,128)(2,1)}, bf16[4,672,512]{2,1,0:T(8,128)(2,1)S(1)}, u32[]{:S(2)}, u32[]{:S(2)}) collective-permute-start(bf16[4,672,512]{2,1,0:T(8,128)(2,1)} %bitcast.21), channel_id=1, source_target_pairs={{0,1},{1,0},{2,3},{3,2},{4,5},{5,4},{6,7},{7,6},{8,9},{9,8},{10,11... | collective-permute-start | bytes 8257544 | tf_op jit(solution)/shard_map/ppermute | solution.py:425
  148.4 1.8 copy-start
  150.2 3.1 %copy-start.1 = (bf16[2688,512]{1,0:T(8,128)(2,1)S(1)}, bf16[2688,512]{1,0:T(8,128)(2,1)}, u32[]{:S(2)}) copy-start(bf16[2688,512]{1,0:T(8,128)(2,1)} %all-gather.6.cloned.1.call-done) | copy-start | bytes 8257540
  150.2 3.1 %copy-start.2 = (bf16[2688,512]{1,0:T(8,128)(2,1)S(1)}, bf16[2688,512]{1,0:T(8,128)(2,1)}, u32[]{:S(2)}) copy-start(bf16[2688,512]{1,0:T(8,128)(2,1)} %all-gather.8.cloned.1.call-done) | copy-start | bytes 8257540
  155.4 10.9 %collective-permute-start.9 = (bf16[8,128,128]{2,1,0:T(8,128)(2,1)S(1)}, bf16[8,128,128]{2,1,0:T(8,128)(2,1)S(1)}, u32[]{:S(2)}, u32[]{:S(2)}) collective-permute-start(bf16[8,128,128]{2,1,0:T(8,128)(2,1)S(1)} %get-tuple-element.43), channel_id=1, source_target_pairs={{0,2},{1,3},{2,0},{3,1},{4,6},{5,7},{6,4},{7,5},{8,10},{9,11},{10,... | collective-permute-start | bytes 786440 | tf_op jit(solution)/shard_map/ppermute | solution.py:425
  157.8 9.1 %collective-permute-start.10 = (bf16[8,128,128]{2,1,0:T(8,128)(2,1)S(1)}, bf16[8,128,128]{2,1,0:T(8,128)(2,1)S(1)}, u32[]{:S(2)}, u32[]{:S(2)}) collective-permute-start(bf16[8,128,128]{2,1,0:T(8,128)(2,1)S(1)} %get-tuple-element.44), channel_id=1, source_target_pairs={{0,4},{1,5},{2,6},{3,7},{4,0},{5,1},{6,2},{7,3},{8,12},{9,13},{10,... | collective-permute-start | bytes 786440 | tf_op jit(solution)/shard_map/ppermute | solution.py:425
  161.0 13.7 %collective-permute-start.11 = (bf16[8,128,128]{2,1,0:T(8,128)(2,1)S(1)}, bf16[8,128,128]{2,1,0:T(8,128)(2,1)S(1)}, u32[]{:S(2)}, u32[]{:S(2)}) collective-permute-start(bf16[8,128,128]{2,1,0:T(8,128)(2,1)S(1)} %get-tuple-element.45), channel_id=1, source_target_pairs={{0,6},{1,7},{2,4},{3,5},{4,2},{5,3},{6,0},{7,1},{8,14},{9,15},{10,... | collective-permute-start | bytes 786440 | tf_op jit(solution)/shard_map/ppermute | solution.py:425
  198.2 7.8 %collective-permute-start.12 = (bf16[64,128]{1,0:T(8,128)(2,1)S(1)}, bf16[64,128]{1,0:T(8,128)(2,1)S(1)}, u32[]{:S(2)}, u32[]{:S(2)}) collective-permute-start(bf16[64,128]{1,0:T(8,128)(2,1)S(1)} %get-tuple-element.48), channel_id=1, source_target_pairs={{0,1},{1,0},{2,3},{3,2},{4,5},{5,4},{6,7},{7,6},{8,9},{9,8},{10,11... | collective-permute-start | bytes 49160 | tf_op jit(solution)/shard_map/ppermute | solution.py:425
Sparse Core Ops, SparseCore 0:
  36.4 48.1 all-gather.5
  99.2 40.9 all-gather.7

commit v13 on v12

--- a/solution.py
+++ b/solution.py
@@ -57,13 +57,16 @@
     return pl.CostEstimate(flops=flops, bytes_accessed=nbytes, transcendentals=0)
 
 
-def project_kernel(normed, weights, cos, sin, send, keys, values, rows, cols, tables, sems):
+def project_kernel(normed, weights, cos, sin, send, keys, values, out_own, rows, cols, tables, sems):
     copies = []
     for g in range(GROUPS):
         copies.append(pltpu.make_async_copy(normed.at[g], rows.at[g], sems.at[2 * g]))
         copies.append(pltpu.make_async_copy(weights.at[g, pl.ds(0, 96), :], cols.at[g], sems.at[2 * g + 1]))
     for i, ref in enumerate((cos, sin)):
         copies.append(pltpu.make_async_copy(ref, tables.at[i], sems.at[2 * GROUPS + i]))
+    for g in range(GROUPS):
+        source = weights.at[g, pl.ds(96, QC), :]
+        copies.append(pltpu.make_async_copy(source, out_own.at[g], sems.at[2 * GROUPS + 2 + g]))
     for copy in copies:
         copy.start()
     total = jnp.zeros((256, 96), F32)
@@ -323,14 +326,15 @@
             jax.ShapeDtypeStruct((8, HALF, 128), BF),
             jax.ShapeDtypeStruct((KC, 256), BF),
             jax.ShapeDtypeStruct((KC, 256), BF),
+            jax.ShapeDtypeStruct((GROUPS, QC, RUN), BF),
         ),
         in_specs=[HBM] * 4,
-        out_specs=(VMEM,) * 3,
+        out_specs=(VMEM,) * 4,
         scratch_shapes=[
             pltpu.VMEM((GROUPS, 256, RUN), BF),
             pltpu.VMEM((GROUPS, 96, RUN), BF),
             pltpu.VMEM((2, 256, 128), F32),
-            pltpu.SemaphoreType.DMA((2 * GROUPS + 2,)),
+            pltpu.SemaphoreType.DMA((3 * GROUPS + 2,)),
         ],
         compiler_params=params(58),
         name="project",
@@ -475,11 +479,10 @@
 
     mine, token = join(token, w_gate.T, w_up.T, w_down.T)
     normed, own = norm(token, cos, stream, attn_gain.reshape(1, D))
-    send, keys, values = project(normed, first, cos, sin)
+    send, keys, values, out_own = project(normed, first, cos, sin)
     got = trade(send, OCTETS)
     mine = after(mine, send)
     mine_lo = swap_groups(after(mine, got))
-    out_own = first[:, 96:160, :]
     out_weights = (out_own, swap(out_own, 1), swap(out_own, 2), swap(out_own, 3))
     mixed = collect(attend(row_length, got))
     attended = output(mixed, out_weights, own)
@@ -490,7 +493,7 @@
     other, far_same, far_other = swap(same, 4), swap(same, 2), swap(same, 6)
     gain = ffn_gain.reshape(1, D)
     near = near_half(same, other, gain)
-    mine_lo = after(mine_lo, (far_same, far_other, near))
+    mine_lo = after(mine_lo, (far_same, far_other, other))
     core_lo = swap(mine_lo, 1)
     totals, kept, far_normed = own_rows(near, same, far_same, far_other, gain, mine, core_mine)
     weights = (mine, mine_lo, core_mine, core_lo)

time: 214 us -> 214 us (level)
  blocking collectives: 93 us -> 96.3 us
    all_to_all x3, blocking collectives: 60.2 us -> 63.9 us  [trade(): return lax.all_to_all(x, 'dev', 0, 0, axis_index_groups=groups, tiled=True)]
    unnamed x30 -> x28, local copies, waits for them, and re-layouts: 6.35 us -> 5.74 us
  transfers between devices with their start and end apart: 16 -> 16, of which waited for: 6 -> 7; matrix products, arithmetic and copies ran while one was open for 1% -> 1% of each run, Pallas kernels for 4% -> 4%
where the time goes in v13:
time: 214 us; the launch traced here: 213 us
  blocking collectives  96.3 us (45%)
  starting transfers between devices  57.1 us (27%)
  waiting for transfers between devices  19.4 us (9%)
  Pallas kernels  18 us (8%)
  between operations  14.4 us (7%)
  local copies, waits for them, and re-layouts  5.74 us (3%)
    all_to_all x3, blocking collectives, trade(): return lax.all_to_all(x, 'dev', 0, 0, axis_index_groups=groups, tiled=True)  63.9 us
    ppermute x12, starting transfers between devices, swap(): return lax.ppermute(x, 'dev', [(d, d ^ bits) for d in range(MEMBERS)])  49.2 us
    all_gather x1, blocking collectives, collect(): return lax.all_gather(x, 'dev', axis=0, axis_index_groups=COLUMNS)  32.4 us
    ppermute x12, waiting for transfers between devices, swap(): return lax.ppermute(x, 'dev', [(d, d ^ bits) for d in range(MEMBERS)])  10.2 us
    all_to_all x1, waiting for transfers between devices, on_device(): first = lax.all_to_all(packed, 'grp', 0, 0, tiled=True)  9.17 us
    all_to_all x1, starting transfers between devices, on_device(): first = lax.all_to_all(packed, 'grp', 0, 0, tiled=True)  5.87 us
    unnamed x28, local copies, waits for them, and re-layouts  5.74 us
  transfers between devices with their start and end apart: 16, of which 7 were waited for; matrix products, arithmetic and copies ran while one was open for 1% of the time, Pallas kernels for 4%

profile of v13, /device:TPU:1, one launch (start us, length us, event | category | flops | bytes accessed | tf_op | source)
XLA Modules:
  0.0 212.8 jit_solution(12262229227668457586)
XLA Ops:
  7.2 2.8 %pack.1 = (bf16[8,160,512]{2,1,0:T(8,128)(2,1)}, f32[8,128]{1,0:T(8,128)}) custom-call(bf16[64,512]{1,0:T(8,128)(2,1)} %bitcast.30, bf16[16,512]{1,0:T(8,128)(2,1)} %bitcast.32, bf16[16,512]{1,0:T(8,128)(2,1)} %bitcast.33, bf16[64,512]{1,0:T(8,128)(2,1)} %bitcast.31), custom_call_target="tpu_custom_call" | custom-call | tf_op jit(solution)/shard_map/pack/pallas_call | solution.py:311
  10.0 5.9 %all-to-all-start = ((bf16[8,160,512]{2,1,0:T(8,128)(2,1)}), bf16[8,160,512]{2,1,0:T(8,128)(2,1)}, u32[]{:S(2)}, u32[]{:S(2)}) async-start(bf16[8,160,512]{2,1,0:T(8,128)(2,1)} %get-tuple-element.30), calls=%async_computation | async-start | bytes 2621440 | tf_op jit(solution)/shard_map/all_to_all | solution.py:470
  15.9 0.0 all-gather.6.cloned.1.call-start
  15.9 2.6 %join.1 = (bf16[672,512]{1,0:T(8,128)(2,1)}, f32[8,128]{1,0:T(8,128)}) custom-call(f32[8,128]{1,0:T(8,128)} %get-tuple-element.27.after, bf16[224,512]{1,0:T(8,128)(2,1)} %bitcast.27, bf16[224,512]{1,0:T(8,128)(2,1)} %bitcast.28, bf16[224,512]{1,0:T(8,128)(2,1)} %bitcast.29), custom_call_target="tpu_custom_call" | custom-call | tf_op jit(solution)/shard_map/join/pallas_call | solution.py:299
  18.6 0.1 convert_bitcast_fusion
  18.7 1.2 multiply_sine_fusion
  19.9 0.7 copy-done.9
  20.6 1.4 norm.1
  22.0 1.4 copy-done.3
  23.4 9.2 %all-to-all-done.weights = bf16[8,160,512]{2,1,0:T(8,128)(2,1)} async-done(((bf16[8,160,512]{2,1,0:T(8,128)(2,1)}), bf16[8,160,512]{2,1,0:T(8,128)(2,1)}, u32[]{:S(2)}, u32[]{:S(2)}) %all-to-all-start) | async-done | bytes 1310752 | tf_op jit(solution)/shard_map/all_to_all | solution.py:470
  32.6 3.8 %project.1 = (bf16[8,64,128]{2,1,0:T(8,128)(2,1)}, bf16[16,256]{1,0:T(8,128)(2,1)}, bf16[16,256]{1,0:T(8,128)(2,1)}, bf16[8,64,512]{2,1,0:T(8,128)(2,1)}) custom-call(bf16[8,256,512]{2,1,0:T(8,128)(2,1)} %copy-done.3, bf16[8,160,512]{2,1,0:T(8,128)(2,1)} %all-to-all-done.weights, f32[256,128]{1,0:T(8,128)} %copy-done.5, f32[256,128]{1,0:T(8,128)} %get-tuple-element.51.sin), custom_call_target="tpu_custom_call" | custom-call | tf_op jit(solution)/shard_map/project/pallas_call | solution.py:323
  36.3 0.0 all-gather.6.cloned.1.call-update
  36.4 0.0 all-gather.8.cloned.1.call-start
  36.4 14.2 %all_to_all.20.got = bf16[8,64,128]{2,1,0:T(8,128)(2,1)S(1)} all-to-all(bf16[8,64,128]{2,1,0:T(8,128)(2,1)} %get-tuple-element.33), channel_id=1, replica_groups={{0,1,2,3,4,5,6,7},{8,9,10,11,12,13,14,15},{16,17,18,19,20,21,22,23},{24..., dimensions={0} | all-to-all | bytes 262144 | tf_op jit(solution)/shard_map/all_to_all | solution.py:441
  50.6 1.9 collective-permute-start.7
  52.5 3.9 %collective-permute-start.2 = (bf16[8,64,512]{2,1,0:T(8,128)(2,1)}, bf16[8,64,512]{2,1,0:T(8,128)(2,1)S(1)}, u32[]{:S(2)}, u32[]{:S(2)}) collective-permute-start(bf16[8,64,512]{2,1,0:T(8,128)(2,1)} %get-tuple-element.34.mine), channel_id=1, source_target_pairs={{0,3},{1,2},{2,1},{3,0},{4,7},{5,6},{6,5},{7,4},{8,11},{9,10},{10,... | collective-permute-start | bytes 1572872 | tf_op jit(solution)/shard_map/ppermute | solution.py:429
  56.4 3.7 %collective-permute-start.1 = (bf16[8,64,512]{2,1,0:T(8,128)(2,1)}, bf16[8,64,512]{2,1,0:T(8,128)(2,1)S(1)}, u32[]{:S(2)}, u32[]{:S(2)}) collective-permute-start(bf16[8,64,512]{2,1,0:T(8,128)(2,1)} %get-tuple-element.34.mine), channel_id=1, source_target_pairs={{0,2},{1,3},{2,0},{3,1},{4,6},{5,7},{6,4},{7,5},{8,10},{9,11},{10,... | collective-permute-start | bytes 1572872 | tf_op jit(solution)/shard_map/ppermute | solution.py:429
  60.1 1.9 collective-permute-start
  62.1 1.4 attend.1
  63.5 32.4 %all-gather = bf16[1024,256]{1,0:T(8,128)(2,1)S(1)} all-gather(bf16[64,256]{1,0:T(8,128)(2,1)S(1)} %attend.1), channel_id=2, replica_groups={{0,4,8,12,16,20,24,28,32,36,40,44,48,52,56,60},{1,5,9,13,17,21,25,29,33..., dimensions={0}, use_global_device_ids=true | all-gather | bytes 557056 | tf_op jit(solution)/shard_map/all_gather | solution.py:445
  95.9 1.0 copy-done.6
  97.0 0.8 output.1
  97.8 0.8 copy-done.12
  98.6 24.1 %all_to_all.21.same = bf16[8,64,256]{2,1,0:T(8,128)(2,1)S(1)} all-to-all(bf16[8,64,256]{2,1,0:T(8,128)(2,1)S(1)} %output.1), channel_id=1, replica_groups={{0,8,16,24,32,40,48,56},{1,9,17,25,33,41,49,57},{2,10,18,26,34,42,50,58..., dimensions={0} | all-to-all | bytes 524288 | tf_op jit(solution)/shard_map/all_to_all | solution.py:441
  122.7 6.7 %collective-permute-start.5 = (bf16[8,64,256]{2,1,0:T(8,128)(2,1)S(1)}, bf16[8,64,256]{2,1,0:T(8,128)(2,1)S(1)}, u32[]{:S(2)}, u32[]{:S(2)}) collective-permute-start(bf16[8,64,256]{2,1,0:T(8,128)(2,1)S(1)} %all_to_all.21.same), channel_id=1, source_target_pairs={{0,6},{1,7},{2,4},{3,5},{4,2},{5,3},{6,0},{7,1},{8,14},{9,15},{10,... | collective-permute-start | bytes 786440 | tf_op jit(solution)/shard_map/ppermute | solution.py:429
  129.4 1.9 collective-permute-start.4
  131.4 2.2 %collective-permute-start.3 = (bf16[8,64,256]{2,1,0:T(8,128)(2,1)S(1)}, bf16[8,64,256]{2,1,0:T(8,128)(2,1)S(1)}, u32[]{:S(2)}, u32[]{:S(2)}) collective-permute-start(bf16[8,64,256]{2,1,0:T(8,128)(2,1)S(1)} %all_to_all.21.same), channel_id=1, source_target_pairs={{0,4},{1,5},{2,6},{3,7},{4,0},{5,1},{6,2},{7,3},{8,12},{9,13},{10,... | collective-permute-start | bytes 786440 | tf_op jit(solution)/shard_map/ppermute | solution.py:429
  133.6 0.0 all-gather.6.cloned.1.call-done
  133.6 8.5 %collective-permute-start.6 = (bf16[4,672,512]{2,1,0:T(8,128)(2,1)}, bf16[4,672,512]{2,1,0:T(8,128)(2,1)S(1)}, u32[]{:S(2)}, u32[]{:S(2)}) collective-permute-start(bf16[4,672,512]{2,1,0:T(8,128)(2,1)} %bitcast.18), channel_id=1, source_target_pairs={{0,1},{1,0},{2,3},{3,2},{4,5},{5,4},{6,7},{7,6},{8,9},{9,8},{10,11... | collective-permute-start | bytes 8257544 | tf_op jit(solution)/shard_map/ppermute | solution.py:429
  142.1 0.2 collective-permute-done.4.far_same
  142.3 4.4 %collective-permute-start.8 = (bf16[4,672,512]{2,1,0:T(8,128)(2,1)}, bf16[4,672,512]{2,1,0:T(8,128)(2,1)S(1)}, u32[]{:S(2)}, u32[]{:S(2)}) collective-permute-start(bf16[4,672,512]{2,1,0:T(8,128)(2,1)} %bitcast.21), channel_id=1, source_target_pairs={{0,1},{1,0},{2,3},{3,2},{4,5},{5,4},{6,7},{7,6},{8,9},{9,8},{10,11... | collective-permute-start | bytes 8257544 | tf_op jit(solution)/shard_map/ppermute | solution.py:429
  146.7 0.3 near_half.1.near
  147.1 1.8 copy-done
  148.8 2.7 %own_rows.1 = (f32[4,128,224]{2,1,0:T(8,128)S(1)}, bf16[128,128]{1,0:T(8,128)(2,1)S(1)}, bf16[8,64,512]{2,1,0:T(8,128)(2,1)S(1)}) custom-call(bf16[8,64,512]{2,1,0:T(8,128)(2,1)S(1)} %near_half.1.near, bf16[8,64,256]{2,1,0:T(8,128)(2,1)S(1)} %all_to_all.21.same, bf16[8,64,256]{2,1,0:T(8,128)(2,1)} %collective-permute-done.4.far_same, ...), custom_call_target="tpu_custom_call" | custom-call | flops 469762048 | bytes 4194304 | tf_op jit(solution)/shard_map/own_rows/pallas_call | solution.py:378
  151.5 0.1 collective-permute-done.8.core_lo
  151.6 2.0 down.1
  153.7 4.4 %collective-permute-start.9 = (bf16[8,128,128]{2,1,0:T(8,128)(2,1)S(1)}, bf16[8,128,128]{2,1,0:T(8,128)(2,1)S(1)}, u32[]{:S(2)}, u32[]{:S(2)}) collective-permute-start(bf16[8,128,128]{2,1,0:T(8,128)(2,1)S(1)} %get-tuple-element.45), channel_id=1, source_target_pairs={{0,2},{1,3},{2,0},{3,1},{4,6},{5,7},{6,4},{7,5},{8,10},{9,11},{10,... | collective-permute-start | bytes 786440 | tf_op jit(solution)/shard_map/ppermute | solution.py:429
  158.1 3.5 %collective-permute-start.10 = (bf16[8,128,128]{2,1,0:T(8,128)(2,1)S(1)}, bf16[8,128,128]{2,1,0:T(8,128)(2,1)S(1)}, u32[]{:S(2)}, u32[]{:S(2)}) collective-permute-start(bf16[8,128,128]{2,1,0:T(8,128)(2,1)S(1)} %get-tuple-element.46), channel_id=1, source_target_pairs={{0,4},{1,5},{2,6},{3,7},{4,0},{5,1},{6,2},{7,3},{8,12},{9,13},{10,... | collective-permute-start | bytes 786440 | tf_op jit(solution)/shard_map/ppermute | solution.py:429
  161.5 2.0 collective-permute-start.11
  163.6 1.0 collective-permute-done.9.refs_0_
  164.6 2.8 %collective-permute-done.10.refs_1_ = bf16[8,128,128]{2,1,0:T(8,128)(2,1)S(1)} collective-permute-done((bf16[8,128,128]{2,1,0:T(8,128)(2,1)S(1)}, bf16[8,128,128]{2,1,0:T(8,128)(2,1)S(1)}, u32[]{:S(2)}, u32[]{:S(2)}) %collective-permute-start.10) | collective-permute-done | bytes 262176 | tf_op jit(solution)/shard_map/ppermute | solution.py:429
  167.3 5.4 %collective-permute-done.11.refs_2_ = bf16[8,128,128]{2,1,0:T(8,128)(2,1)S(1)} collective-permute-done((bf16[8,128,128]{2,1,0:T(8,128)(2,1)S(1)}, bf16[8,128,128]{2,1,0:T(8,128)(2,1)S(1)}, u32[]{:S(2)}, u32[]{:S(2)}) %collective-permute-start.11) | collective-permute-done | bytes 262176 | tf_op jit(solution)/shard_map/ppermute | solution.py:429
  172.7 0.1 add.89
  172.8 25.5 %all_to_all.22.got = bf16[8,128,128]{2,1,0:T(8,128)(2,1)S(1)} all-to-all(bf16[8,128,128]{2,1,0:T(8,128)(2,1)S(1)} %add.89), channel_id=1, replica_groups={{0,8,16,24,32,40,48,56},{1,9,17,25,33,41,49,57},{2,10,18,26,34,42,50,58..., dimensions={0} | all-to-all | bytes 524288 | tf_op jit(solution)/shard_map/all_to_all | solution.py:441
  198.4 0.1 finish.1
  198.5 6.1 %collective-permute-start.12 = (bf16[64,128]{1,0:T(8,128)(2,1)S(1)}, bf16[64,128]{1,0:T(8,128)(2,1)S(1)}, u32[]{:S(2)}, u32[]{:S(2)}) collective-permute-start(bf16[64,128]{1,0:T(8,128)(2,1)S(1)} %get-tuple-element.50), channel_id=1, source_target_pairs={{0,1},{1,0},{2,3},{3,2},{4,5},{5,4},{6,7},{7,6},{8,9},{9,8},{10,11... | collective-permute-start | bytes 49160 | tf_op jit(solution)/shard_map/ppermute | solution.py:429
  204.6 0.8 collective-permute-done.12
  205.4 0.6 fusion
  (33 shorter events, 0.1 us)
Async XLA Ops:
  7.2 11.4 %copy-start.13 = (s32[2]{0:T(128)S(1)}, s32[2]{0:T(128)}, u32[]{:S(2)}) copy-start(s32[2]{0:T(128)} %param.14) | copy-start | bytes 28
  7.2 12.7 %copy-start.8 = (f32[4096]{0:T(1024)S(1)}, f32[4096]{0:T(1024)}, u32[]{:S(2)}) copy-start(f32[4096]{0:T(1024)} %param.15) | copy-start | bytes 49156
  7.2 12.7 %copy-start.4 = (bf16[256,4096]{1,0:T(8,128)(2,1)S(1)}, bf16[256,4096]{1,0:T(8,128)(2,1)}, u32[]{:S(2)}) copy-start(bf16[256,4096]{1,0:T(8,128)(2,1)} %stream.1) | copy-start | bytes 6291460
  10.0 22.6 %all-to-all-start = ((bf16[8,160,512]{2,1,0:T(8,128)(2,1)}), bf16[8,160,512]{2,1,0:T(8,128)(2,1)}, u32[]{:S(2)}, u32[]{:S(2)}) async-start(bf16[8,160,512]{2,1,0:T(8,128)(2,1)} %get-tuple-element.30), calls=%async_computation | async-start | bytes 2621440 | tf_op jit(solution)/shard_map/all_to_all | solution.py:470
  15.9 117.7 %all-gather.6.cloned.1.call-start = ((), (), s32[]{:S(2)}) async-start(), calls=%async_computation.4 | async-start | bytes 3440640 | tf_op jit(solution)/shard_map/all_gather | solution.py:437
  19.9 12.7 %copy-start.5 = (f32[256,128]{1,0:T(8,128)}, f32[256,128]{1,0:T(8,128)S(1)}, u32[]{:S(2)}) copy-start(f32[256,128]{1,0:T(8,128)S(1)} %get-tuple-element.52.tables.cos) | copy-start | bytes 393220
  19.9 0.7 copy-start.9
  22.0 1.4 copy-start.3
  23.4 27.2 %copy-start.11 = (bf16[672,512]{1,0:T(8,128)(2,1)S(1)}, bf16[672,512]{1,0:T(8,128)(2,1)}, u32[]{:S(2)}) copy-start(bf16[672,512]{1,0:T(8,128)(2,1)} %get-tuple-element.41) | copy-start | bytes 2064388
  23.4 38.7 %copy-start.10 = (s32[2]{0:T(128)S(1)}, s32[2]{0:T(128)}, u32[]{:S(2)}) copy-start(s32[2]{0:T(128)} %lengths.1) | copy-start | bytes 28
  36.3 110.4 %copy-start.7 = (f32[4096]{0:T(1024)S(1)}, f32[4096]{0:T(1024)}, u32[]{:S(2)}) copy-start(f32[4096]{0:T(1024)} %param.20) | copy-start | bytes 49156
  36.4 105.9 %all-gather.8.cloned.1.call-start = ((), (), s32[]{:S(2)}) async-start(), calls=%async_computation.5 | async-start | bytes 3440640 | tf_op jit(solution)/shard_map/all_gather | solution.py:437
  50.6 47.1 %collective-permute-start.7 = (bf16[672,512]{1,0:T(8,128)(2,1)S(1)}, bf16[672,512]{1,0:T(8,128)(2,1)S(1)}, u32[]{:S(2)}, u32[]{:S(2)}) collective-permute-start(bf16[672,512]{1,0:T(8,128)(2,1)S(1)} %copy-done.11), channel_id=1, source_target_pairs={{0,256},{64,320},{128,384},{192,448},{256,0},{320,64},{384,128},{4... | collective-permute-start | bytes 2064392 | tf_op jit(solution)/shard_map/ppermute | solution.py:433
  52.5 43.4 %collective-permute-start.2 = (bf16[8,64,512]{2,1,0:T(8,128)(2,1)}, bf16[8,64,512]{2,1,0:T(8,128)(2,1)S(1)}, u32[]{:S(2)}, u32[]{:S(2)}) collective-permute-start(bf16[8,64,512]{2,1,0:T(8,128)(2,1)} %get-tuple-element.34.mine), channel_id=1, source_target_pairs={{0,3},{1,2},{2,1},{3,0},{4,7},{5,6},{6,5},{7,4},{8,11},{9,10},{10,... | collective-permute-start | bytes 1572872 | tf_op jit(solution)/shard_map/ppermute | solution.py:429
  56.4 39.5 %collective-permute-start.1 = (bf16[8,64,512]{2,1,0:T(8,128)(2,1)}, bf16[8,64,512]{2,1,0:T(8,128)(2,1)S(1)}, u32[]{:S(2)}, u32[]{:S(2)}) collective-permute-start(bf16[8,64,512]{2,1,0:T(8,128)(2,1)} %get-tuple-element.34.mine), channel_id=1, source_target_pairs={{0,2},{1,3},{2,0},{3,1},{4,6},{5,7},{6,4},{7,5},{8,10},{9,11},{10,... | collective-permute-start | bytes 1572872 | tf_op jit(solution)/shard_map/ppermute | solution.py:429
  60.1 35.8 %collective-permute-start = (bf16[8,64,512]{2,1,0:T(8,128)(2,1)}, bf16[8,64,512]{2,1,0:T(8,128)(2,1)S(1)}, u32[]{:S(2)}, u32[]{:S(2)}) collective-permute-start(bf16[8,64,512]{2,1,0:T(8,128)(2,1)} %get-tuple-element.34.mine), channel_id=1, source_target_pairs={{0,1},{1,0},{2,3},{3,2},{4,5},{5,4},{6,7},{7,6},{8,9},{9,8},{10,11... | collective-permute-start | bytes 1572872 | tf_op jit(solution)/shard_map/ppermute | solution.py:429
  95.9 1.0 copy-start.6
  97.7 0.8 copy-start.12
  122.7 19.4 %collective-permute-start.5 = (bf16[8,64,256]{2,1,0:T(8,128)(2,1)S(1)}, bf16[8,64,256]{2,1,0:T(8,128)(2,1)S(1)}, u32[]{:S(2)}, u32[]{:S(2)}) collective-permute-start(bf16[8,64,256]{2,1,0:T(8,128)(2,1)S(1)} %all_to_all.21.same), channel_id=1, source_target_pairs={{0,6},{1,7},{2,4},{3,5},{4,2},{5,3},{6,0},{7,1},{8,14},{9,15},{10,... | collective-permute-start | bytes 786440 | tf_op jit(solution)/shard_map/ppermute | solution.py:429
  129.4 12.8 %collective-permute-start.4 = (bf16[8,64,256]{2,1,0:T(8,128)(2,1)S(1)}, bf16[8,64,256]{2,1,0:T(8,128)(2,1)}, u32[]{:S(2)}, u32[]{:S(2)}) collective-permute-start(bf16[8,64,256]{2,1,0:T(8,128)(2,1)S(1)} %all_to_all.21.same), channel_id=1, source_target_pairs={{0,2},{1,3},{2,0},{3,1},{4,6},{5,7},{6,4},{7,5},{8,10},{9,11},{10,... | collective-permute-start | bytes 786440 | tf_op jit(solution)/shard_map/ppermute | solution.py:429
  131.4 10.9 %collective-permute-start.3 = (bf16[8,64,256]{2,1,0:T(8,128)(2,1)S(1)}, bf16[8,64,256]{2,1,0:T(8,128)(2,1)S(1)}, u32[]{:S(2)}, u32[]{:S(2)}) collective-permute-start(bf16[8,64,256]{2,1,0:T(8,128)(2,1)S(1)} %all_to_all.21.same), channel_id=1, source_target_pairs={{0,4},{1,5},{2,6},{3,7},{4,0},{5,1},{6,2},{7,3},{8,12},{9,13},{10,... | collective-permute-start | bytes 786440 | tf_op jit(solution)/shard_map/ppermute | solution.py:429
  133.6 13.4 %collective-permute-start.6 = (bf16[4,672,512]{2,1,0:T(8,128)(2,1)}, bf16[4,672,512]{2,1,0:T(8,128)(2,1)S(1)}, u32[]{:S(2)}, u32[]{:S(2)}) collective-permute-start(bf16[4,672,512]{2,1,0:T(8,128)(2,1)} %bitcast.18), channel_id=1, source_target_pairs={{0,1},{1,0},{2,3},{3,2},{4,5},{5,4},{6,7},{7,6},{8,9},{9,8},{10,11... | collective-permute-start | bytes 8257544 | tf_op jit(solution)/shard_map/ppermute | solution.py:429
  142.3 9.3 %collective-permute-start.8 = (bf16[4,672,512]{2,1,0:T(8,128)(2,1)}, bf16[4,672,512]{2,1,0:T(8,128)(2,1)S(1)}, u32[]{:S(2)}, u32[]{:S(2)}) collective-permute-start(bf16[4,672,512]{2,1,0:T(8,128)(2,1)} %bitcast.21), channel_id=1, source_target_pairs={{0,1},{1,0},{2,3},{3,2},{4,5},{5,4},{6,7},{7,6},{8,9},{9,8},{10,11... | collective-permute-start | bytes 8257544 | tf_op jit(solution)/shard_map/ppermute | solution.py:429
  147.1 1.8 copy-start
  148.8 2.8 %copy-start.1 = (bf16[2688,512]{1,0:T(8,128)(2,1)S(1)}, bf16[2688,512]{1,0:T(8,128)(2,1)}, u32[]{:S(2)}) copy-start(bf16[2688,512]{1,0:T(8,128)(2,1)} %all-gather.6.cloned.1.call-done) | copy-start | bytes 8257540
  148.8 2.8 %copy-start.2 = (bf16[2688,512]{1,0:T(8,128)(2,1)S(1)}, bf16[2688,512]{1,0:T(8,128)(2,1)}, u32[]{:S(2)}) copy-start(bf16[2688,512]{1,0:T(8,128)(2,1)} %all-gather.8.cloned.1.call-done) | copy-start | bytes 8257540
  153.7 10.9 %collective-permute-start.9 = (bf16[8,128,128]{2,1,0:T(8,128)(2,1)S(1)}, bf16[8,128,128]{2,1,0:T(8,128)(2,1)S(1)}, u32[]{:S(2)}, u32[]{:S(2)}) collective-permute-start(bf16[8,128,128]{2,1,0:T(8,128)(2,1)S(1)} %get-tuple-element.45), channel_id=1, source_target_pairs={{0,2},{1,3},{2,0},{3,1},{4,6},{5,7},{6,4},{7,5},{8,10},{9,11},{10,... | collective-permute-start | bytes 786440 | tf_op jit(solution)/shard_map/ppermute | solution.py:429
  158.1 9.3 %collective-permute-start.10 = (bf16[8,128,128]{2,1,0:T(8,128)(2,1)S(1)}, bf16[8,128,128]{2,1,0:T(8,128)(2,1)S(1)}, u32[]{:S(2)}, u32[]{:S(2)}) collective-permute-start(bf16[8,128,128]{2,1,0:T(8,128)(2,1)S(1)} %get-tuple-element.46), channel_id=1, source_target_pairs={{0,4},{1,5},{2,6},{3,7},{4,0},{5,1},{6,2},{7,3},{8,12},{9,13},{10,... | collective-permute-start | bytes 786440 | tf_op jit(solution)/shard_map/ppermute | solution.py:429
  161.5 11.2 %collective-permute-start.11 = (bf16[8,128,128]{2,1,0:T(8,128)(2,1)S(1)}, bf16[8,128,128]{2,1,0:T(8,128)(2,1)S(1)}, u32[]{:S(2)}, u32[]{:S(2)}) collective-permute-start(bf16[8,128,128]{2,1,0:T(8,128)(2,1)S(1)} %get-tuple-element.47), channel_id=1, source_target_pairs={{0,6},{1,7},{2,4},{3,5},{4,2},{5,3},{6,0},{7,1},{8,14},{9,15},{10,... | collective-permute-start | bytes 786440 | tf_op jit(solution)/shard_map/ppermute | solution.py:429
  198.5 6.9 %collective-permute-start.12 = (bf16[64,128]{1,0:T(8,128)(2,1)S(1)}, bf16[64,128]{1,0:T(8,128)(2,1)S(1)}, u32[]{:S(2)}, u32[]{:S(2)}) collective-permute-start(bf16[64,128]{1,0:T(8,128)(2,1)S(1)} %get-tuple-element.50), channel_id=1, source_target_pairs={{0,1},{1,0},{2,3},{3,2},{4,5},{5,4},{6,7},{7,6},{8,9},{9,8},{10,11... | collective-permute-start | bytes 49160 | tf_op jit(solution)/shard_map/ppermute | solution.py:429
Sparse Core Ops, SparseCore 0:
  36.5 48.1 all-gather.5
  98.7 41.1 all-gather.7

commit v14 on v13

--- a/solution.py
+++ b/solution.py
@@ -498,7 +498,7 @@
     totals, kept, far_normed = own_rows(near, same, far_same, far_other, gain, mine, core_mine)
     weights = (mine, mine_lo, core_mine, core_lo)
     keep, to_y, to_z, to_both = down(near, far_normed, totals, weights)
-    sums = trade(add(keep, swap(to_y, 2), swap(to_z, 4), swap(to_both, 6)), PARITIES)
+    sums = trade(add(keep, swap(to_both, 6), swap(to_y, 2), swap(to_z, 4)), PARITIES)
     keep, give = finish(sums, kept)
     give = swap(give, 1)
     rows = jnp.where(core == 0, jnp.concatenate([keep, give], axis=1), jnp.concatenate([give, keep], axis=1))

time: 214 us -> 213 us (level)
  transfers between devices with their start and end apart: 16 -> 16, of which waited for: 7 -> 6; matrix products, arithmetic and copies ran while one was open for 1% -> 1% of each run, Pallas kernels for 4% -> 4%
where the time goes in v14:
time: 213 us; the launch traced here: 212 us
  blocking collectives  95.9 us (45%)
  starting transfers between devices  57.4 us (27%)
  waiting for transfers between devices  18.4 us (9%)
  Pallas kernels  18 us (8%)
  between operations  14.4 us (7%)
  local copies, waits for them, and re-layouts  5.74 us (3%)
    all_to_all x3, blocking collectives, trade(): return lax.all_to_all(x, 'dev', 0, 0, axis_index_groups=groups, tiled=True)  63.4 us
    ppermute x12, starting transfers between devices, swap(): return lax.ppermute(x, 'dev', [(d, d ^ bits) for d in range(MEMBERS)])  49.5 us
    all_gather x1, blocking collectives, collect(): return lax.all_gather(x, 'dev', axis=0, axis_index_groups=COLUMNS)  32.4 us
    ppermute x12, waiting for transfers between devices, swap(): return lax.ppermute(x, 'dev', [(d, d ^ bits) for d in range(MEMBERS)])  9.2 us
    all_to_all x1, waiting for transfers between devices, on_device(): first = lax.all_to_all(packed, 'grp', 0, 0, tiled=True)  9.17 us
    all_to_all x1, starting transfers between devices, on_device(): first = lax.all_to_all(packed, 'grp', 0, 0, tiled=True)  5.87 us
    unnamed x28, local copies, waits for them, and re-layouts  5.74 us
  transfers between devices with their start and end apart: 16, of which 6 were waited for; matrix products, arithmetic and copies ran while one was open for 1% of the time, Pallas kernels for 4%

profile of v14, /device:TPU:1, one launch (start us, length us, event | category | flops | bytes accessed | tf_op | source)
XLA Modules:
  0.0 211.7 jit_solution(13166937877736794529)
XLA Ops:
  7.2 2.8 %pack.1 = (bf16[8,160,512]{2,1,0:T(8,128)(2,1)}, f32[8,128]{1,0:T(8,128)}) custom-call(bf16[64,512]{1,0:T(8,128)(2,1)} %bitcast.30, bf16[16,512]{1,0:T(8,128)(2,1)} %bitcast.32, bf16[16,512]{1,0:T(8,128)(2,1)} %bitcast.33, bf16[64,512]{1,0:T(8,128)(2,1)} %bitcast.31), custom_call_target="tpu_custom_call" | custom-call | tf_op jit(solution)/shard_map/pack/pallas_call | solution.py:311
  10.0 5.9 %all-to-all-start = ((bf16[8,160,512]{2,1,0:T(8,128)(2,1)}), bf16[8,160,512]{2,1,0:T(8,128)(2,1)}, u32[]{:S(2)}, u32[]{:S(2)}) async-start(bf16[8,160,512]{2,1,0:T(8,128)(2,1)} %get-tuple-element.30), calls=%async_computation | async-start | bytes 2621440 | tf_op jit(solution)/shard_map/all_to_all | solution.py:470
  15.9 0.0 all-gather.6.cloned.1.call-start
  15.9 2.6 %join.1 = (bf16[672,512]{1,0:T(8,128)(2,1)}, f32[8,128]{1,0:T(8,128)}) custom-call(f32[8,128]{1,0:T(8,128)} %get-tuple-element.27.after, bf16[224,512]{1,0:T(8,128)(2,1)} %bitcast.27, bf16[224,512]{1,0:T(8,128)(2,1)} %bitcast.28, bf16[224,512]{1,0:T(8,128)(2,1)} %bitcast.29), custom_call_target="tpu_custom_call" | custom-call | tf_op jit(solution)/shard_map/join/pallas_call | solution.py:299
  18.6 0.1 convert_bitcast_fusion
  18.7 1.2 multiply_sine_fusion
  19.9 0.7 copy-done.9
  20.6 1.4 norm.1
  22.0 1.4 copy-done.3
  23.4 9.2 %all-to-all-done.weights = bf16[8,160,512]{2,1,0:T(8,128)(2,1)} async-done(((bf16[8,160,512]{2,1,0:T(8,128)(2,1)}), bf16[8,160,512]{2,1,0:T(8,128)(2,1)}, u32[]{:S(2)}, u32[]{:S(2)}) %all-to-all-start) | async-done | bytes 1310752 | tf_op jit(solution)/shard_map/all_to_all | solution.py:470
  32.6 3.8 %project.1 = (bf16[8,64,128]{2,1,0:T(8,128)(2,1)}, bf16[16,256]{1,0:T(8,128)(2,1)}, bf16[16,256]{1,0:T(8,128)(2,1)}, bf16[8,64,512]{2,1,0:T(8,128)(2,1)}) custom-call(bf16[8,256,512]{2,1,0:T(8,128)(2,1)} %copy-done.3, bf16[8,160,512]{2,1,0:T(8,128)(2,1)} %all-to-all-done.weights, f32[256,128]{1,0:T(8,128)} %copy-done.5, f32[256,128]{1,0:T(8,128)} %get-tuple-element.51.sin), custom_call_target="tpu_custom_call" | custom-call | tf_op jit(solution)/shard_map/project/pallas_call | solution.py:323
  36.3 0.0 all-gather.6.cloned.1.call-update
  36.4 0.0 all-gather.8.cloned.1.call-start
  36.4 14.2 %all_to_all.20.got = bf16[8,64,128]{2,1,0:T(8,128)(2,1)S(1)} all-to-all(bf16[8,64,128]{2,1,0:T(8,128)(2,1)} %get-tuple-element.33), channel_id=1, replica_groups={{0,1,2,3,4,5,6,7},{8,9,10,11,12,13,14,15},{16,17,18,19,20,21,22,23},{24..., dimensions={0} | all-to-all | bytes 262144 | tf_op jit(solution)/shard_map/all_to_all | solution.py:441
  50.6 1.9 collective-permute-start.7
  52.5 3.9 %collective-permute-start.2 = (bf16[8,64,512]{2,1,0:T(8,128)(2,1)}, bf16[8,64,512]{2,1,0:T(8,128)(2,1)S(1)}, u32[]{:S(2)}, u32[]{:S(2)}) collective-permute-start(bf16[8,64,512]{2,1,0:T(8,128)(2,1)} %get-tuple-element.34.mine), channel_id=1, source_target_pairs={{0,3},{1,2},{2,1},{3,0},{4,7},{5,6},{6,5},{7,4},{8,11},{9,10},{10,... | collective-permute-start | bytes 1572872 | tf_op jit(solution)/shard_map/ppermute | solution.py:429
  56.4 3.7 %collective-permute-start.1 = (bf16[8,64,512]{2,1,0:T(8,128)(2,1)}, bf16[8,64,512]{2,1,0:T(8,128)(2,1)S(1)}, u32[]{:S(2)}, u32[]{:S(2)}) collective-permute-start(bf16[8,64,512]{2,1,0:T(8,128)(2,1)} %get-tuple-element.34.mine), channel_id=1, source_target_pairs={{0,2},{1,3},{2,0},{3,1},{4,6},{5,7},{6,4},{7,5},{8,10},{9,11},{10,... | collective-permute-start | bytes 1572872 | tf_op jit(solution)/shard_map/ppermute | solution.py:429
  60.1 1.9 collective-permute-start
  62.1 1.4 attend.1
  63.5 32.4 %all-gather = bf16[1024,256]{1,0:T(8,128)(2,1)S(1)} all-gather(bf16[64,256]{1,0:T(8,128)(2,1)S(1)} %attend.1), channel_id=2, replica_groups={{0,4,8,12,16,20,24,28,32,36,40,44,48,52,56,60},{1,5,9,13,17,21,25,29,33..., dimensions={0}, use_global_device_ids=true | all-gather | bytes 557056 | tf_op jit(solution)/shard_map/all_gather | solution.py:445
  95.9 1.0 copy-done.6
  97.0 0.8 output.1
  97.8 0.8 copy-done.12
  98.6 0.0 all-gather.8.cloned.1.call-update
  98.6 24.1 %all_to_all.21.same = bf16[8,64,256]{2,1,0:T(8,128)(2,1)S(1)} all-to-all(bf16[8,64,256]{2,1,0:T(8,128)(2,1)S(1)} %output.1), channel_id=1, replica_groups={{0,8,16,24,32,40,48,56},{1,9,17,25,33,41,49,57},{2,10,18,26,34,42,50,58..., dimensions={0} | all-to-all | bytes 524288 | tf_op jit(solution)/shard_map/all_to_all | solution.py:441
  122.7 6.7 %collective-permute-start.5 = (bf16[8,64,256]{2,1,0:T(8,128)(2,1)S(1)}, bf16[8,64,256]{2,1,0:T(8,128)(2,1)S(1)}, u32[]{:S(2)}, u32[]{:S(2)}) collective-permute-start(bf16[8,64,256]{2,1,0:T(8,128)(2,1)S(1)} %all_to_all.21.same), channel_id=1, source_target_pairs={{0,6},{1,7},{2,4},{3,5},{4,2},{5,3},{6,0},{7,1},{8,14},{9,15},{10,... | collective-permute-start | bytes 786440 | tf_op jit(solution)/shard_map/ppermute | solution.py:429
  129.4 1.9 collective-permute-start.4
  131.4 2.2 %collective-permute-start.3 = (bf16[8,64,256]{2,1,0:T(8,128)(2,1)S(1)}, bf16[8,64,256]{2,1,0:T(8,128)(2,1)S(1)}, u32[]{:S(2)}, u32[]{:S(2)}) collective-permute-start(bf16[8,64,256]{2,1,0:T(8,128)(2,1)S(1)} %all_to_all.21.same), channel_id=1, source_target_pairs={{0,4},{1,5},{2,6},{3,7},{4,0},{5,1},{6,2},{7,3},{8,12},{9,13},{10,... | collective-permute-start | bytes 786440 | tf_op jit(solution)/shard_map/ppermute | solution.py:429
  133.6 0.0 all-gather.6.cloned.1.call-done
  133.6 8.5 %collective-permute-start.6 = (bf16[4,672,512]{2,1,0:T(8,128)(2,1)}, bf16[4,672,512]{2,1,0:T(8,128)(2,1)S(1)}, u32[]{:S(2)}, u32[]{:S(2)}) collective-permute-start(bf16[4,672,512]{2,1,0:T(8,128)(2,1)} %bitcast.18), channel_id=1, source_target_pairs={{0,1},{1,0},{2,3},{3,2},{4,5},{5,4},{6,7},{7,6},{8,9},{9,8},{10,11... | collective-permute-start | bytes 8257544 | tf_op jit(solution)/shard_map/ppermute | solution.py:429
  142.1 0.2 collective-permute-done.4.far_same
  142.3 4.4 %collective-permute-start.8 = (bf16[4,672,512]{2,1,0:T(8,128)(2,1)}, bf16[4,672,512]{2,1,0:T(8,128)(2,1)S(1)}, u32[]{:S(2)}, u32[]{:S(2)}) collective-permute-start(bf16[4,672,512]{2,1,0:T(8,128)(2,1)} %bitcast.21), channel_id=1, source_target_pairs={{0,1},{1,0},{2,3},{3,2},{4,5},{5,4},{6,7},{7,6},{8,9},{9,8},{10,11... | collective-permute-start | bytes 8257544 | tf_op jit(solution)/shard_map/ppermute | solution.py:429
  146.7 0.3 near_half.1.near
  147.1 1.8 copy-done
  148.8 2.7 %own_rows.1 = (f32[4,128,224]{2,1,0:T(8,128)S(1)}, bf16[128,128]{1,0:T(8,128)(2,1)S(1)}, bf16[8,64,512]{2,1,0:T(8,128)(2,1)S(1)}) custom-call(bf16[8,64,512]{2,1,0:T(8,128)(2,1)S(1)} %near_half.1.near, bf16[8,64,256]{2,1,0:T(8,128)(2,1)S(1)} %all_to_all.21.same, bf16[8,64,256]{2,1,0:T(8,128)(2,1)} %collective-permute-done.4.far_same, ...), custom_call_target="tpu_custom_call" | custom-call | flops 469762048 | bytes 4194304 | tf_op jit(solution)/shard_map/own_rows/pallas_call | solution.py:378
  151.5 0.1 collective-permute-done.8.core_lo
  151.6 2.0 down.1
  153.7 5.6 %collective-permute-start.9 = (bf16[8,128,128]{2,1,0:T(8,128)(2,1)S(1)}, bf16[8,128,128]{2,1,0:T(8,128)(2,1)S(1)}, u32[]{:S(2)}, u32[]{:S(2)}) collective-permute-start(bf16[8,128,128]{2,1,0:T(8,128)(2,1)S(1)} %get-tuple-element.45), channel_id=1, source_target_pairs={{0,6},{1,7},{2,4},{3,5},{4,2},{5,3},{6,0},{7,1},{8,14},{9,15},{10,... | collective-permute-start | bytes 786440 | tf_op jit(solution)/shard_map/ppermute | solution.py:429
  159.3 2.3 %collective-permute-start.10 = (bf16[8,128,128]{2,1,0:T(8,128)(2,1)S(1)}, bf16[8,128,128]{2,1,0:T(8,128)(2,1)S(1)}, u32[]{:S(2)}, u32[]{:S(2)}) collective-permute-start(bf16[8,128,128]{2,1,0:T(8,128)(2,1)S(1)} %get-tuple-element.46), channel_id=1, source_target_pairs={{0,2},{1,3},{2,0},{3,1},{4,6},{5,7},{6,4},{7,5},{8,10},{9,11},{10,... | collective-permute-start | bytes 786440 | tf_op jit(solution)/shard_map/ppermute | solution.py:429
  161.6 2.0 collective-permute-start.11
  163.6 1.9 collective-permute-done.9.refs_0_
  165.5 6.2 %collective-permute-done.10.refs_1_ = bf16[8,128,128]{2,1,0:T(8,128)(2,1)S(1)} collective-permute-done((bf16[8,128,128]{2,1,0:T(8,128)(2,1)S(1)}, bf16[8,128,128]{2,1,0:T(8,128)(2,1)S(1)}, u32[]{:S(2)}, u32[]{:S(2)}) %collective-permute-start.10) | collective-permute-done | bytes 262176 | tf_op jit(solution)/shard_map/ppermute | solution.py:429
  171.7 0.1 add.89
  171.8 25.1 %all_to_all.22.got = bf16[8,128,128]{2,1,0:T(8,128)(2,1)S(1)} all-to-all(bf16[8,128,128]{2,1,0:T(8,128)(2,1)S(1)} %add.89), channel_id=1, replica_groups={{0,8,16,24,32,40,48,56},{1,9,17,25,33,41,49,57},{2,10,18,26,34,42,50,58..., dimensions={0} | all-to-all | bytes 524288 | tf_op jit(solution)/shard_map/all_to_all | solution.py:441
  196.9 0.1 finish.1
  197.0 6.4 %collective-permute-start.12 = (bf16[64,128]{1,0:T(8,128)(2,1)S(1)}, bf16[64,128]{1,0:T(8,128)(2,1)S(1)}, u32[]{:S(2)}, u32[]{:S(2)}) collective-permute-start(bf16[64,128]{1,0:T(8,128)(2,1)S(1)} %get-tuple-element.50), channel_id=1, source_target_pairs={{0,1},{1,0},{2,3},{3,2},{4,5},{5,4},{6,7},{7,6},{8,9},{9,8},{10,11... | collective-permute-start | bytes 49160 | tf_op jit(solution)/shard_map/ppermute | solution.py:429
  203.5 0.8 collective-permute-done.12
  204.3 0.6 fusion
  (33 shorter events, 0.1 us)
Async XLA Ops:
  7.2 11.4 %copy-start.13 = (s32[2]{0:T(128)S(1)}, s32[2]{0:T(128)}, u32[]{:S(2)}) copy-start(s32[2]{0:T(128)} %param.14) | copy-start | bytes 28
  7.2 12.7 %copy-start.8 = (f32[4096]{0:T(1024)S(1)}, f32[4096]{0:T(1024)}, u32[]{:S(2)}) copy-start(f32[4096]{0:T(1024)} %param.15) | copy-start | bytes 49156
  7.2 12.7 %copy-start.4 = (bf16[256,4096]{1,0:T(8,128)(2,1)S(1)}, bf16[256,4096]{1,0:T(8,128)(2,1)}, u32[]{:S(2)}) copy-start(bf16[256,4096]{1,0:T(8,128)(2,1)} %stream.1) | copy-start | bytes 6291460
  10.0 22.6 %all-to-all-start = ((bf16[8,160,512]{2,1,0:T(8,128)(2,1)}), bf16[8,160,512]{2,1,0:T(8,128)(2,1)}, u32[]{:S(2)}, u32[]{:S(2)}) async-start(bf16[8,160,512]{2,1,0:T(8,128)(2,1)} %get-tuple-element.30), calls=%async_computation | async-start | bytes 2621440 | tf_op jit(solution)/shard_map/all_to_all | solution.py:470
  15.9 117.7 %all-gather.6.cloned.1.call-start = ((), (), s32[]{:S(2)}) async-start(), calls=%async_computation.4 | async-start | bytes 3440640 | tf_op jit(solution)/shard_map/all_gather | solution.py:437
  19.9 12.7 %copy-start.5 = (f32[256,128]{1,0:T(8,128)}, f32[256,128]{1,0:T(8,128)S(1)}, u32[]{:S(2)}) copy-start(f32[256,128]{1,0:T(8,128)S(1)} %get-tuple-element.52.tables.cos) | copy-start | bytes 393220
  19.9 0.7 copy-start.9
  22.0 1.4 copy-start.3
  23.4 27.2 %copy-start.11 = (bf16[672,512]{1,0:T(8,128)(2,1)S(1)}, bf16[672,512]{1,0:T(8,128)(2,1)}, u32[]{:S(2)}) copy-start(bf16[672,512]{1,0:T(8,128)(2,1)} %get-tuple-element.41) | copy-start | bytes 2064388
  23.4 38.7 %copy-start.10 = (s32[2]{0:T(128)S(1)}, s32[2]{0:T(128)}, u32[]{:S(2)}) copy-start(s32[2]{0:T(128)} %lengths.1) | copy-start | bytes 28
  36.3 110.4 %copy-start.7 = (f32[4096]{0:T(1024)S(1)}, f32[4096]{0:T(1024)}, u32[]{:S(2)}) copy-start(f32[4096]{0:T(1024)} %param.20) | copy-start | bytes 49156
  36.4 105.9 %all-gather.8.cloned.1.call-start = ((), (), s32[]{:S(2)}) async-start(), calls=%async_computation.5 | async-start | bytes 3440640 | tf_op jit(solution)/shard_map/all_gather | solution.py:437
  50.6 47.1 %collective-permute-start.7 = (bf16[672,512]{1,0:T(8,128)(2,1)S(1)}, bf16[672,512]{1,0:T(8,128)(2,1)S(1)}, u32[]{:S(2)}, u32[]{:S(2)}) collective-permute-start(bf16[672,512]{1,0:T(8,128)(2,1)S(1)} %copy-done.11), channel_id=1, source_target_pairs={{0,256},{64,320},{128,384},{192,448},{256,0},{320,64},{384,128},{4... | collective-permute-start | bytes 2064392 | tf_op jit(solution)/shard_map/ppermute | solution.py:433
  52.5 43.4 %collective-permute-start.2 = (bf16[8,64,512]{2,1,0:T(8,128)(2,1)}, bf16[8,64,512]{2,1,0:T(8,128)(2,1)S(1)}, u32[]{:S(2)}, u32[]{:S(2)}) collective-permute-start(bf16[8,64,512]{2,1,0:T(8,128)(2,1)} %get-tuple-element.34.mine), channel_id=1, source_target_pairs={{0,3},{1,2},{2,1},{3,0},{4,7},{5,6},{6,5},{7,4},{8,11},{9,10},{10,... | collective-permute-start | bytes 1572872 | tf_op jit(solution)/shard_map/ppermute | solution.py:429
  56.4 39.5 %collective-permute-start.1 = (bf16[8,64,512]{2,1,0:T(8,128)(2,1)}, bf16[8,64,512]{2,1,0:T(8,128)(2,1)S(1)}, u32[]{:S(2)}, u32[]{:S(2)}) collective-permute-start(bf16[8,64,512]{2,1,0:T(8,128)(2,1)} %get-tuple-element.34.mine), channel_id=1, source_target_pairs={{0,2},{1,3},{2,0},{3,1},{4,6},{5,7},{6,4},{7,5},{8,10},{9,11},{10,... | collective-permute-start | bytes 1572872 | tf_op jit(solution)/shard_map/ppermute | solution.py:429
  60.1 35.8 %collective-permute-start = (bf16[8,64,512]{2,1,0:T(8,128)(2,1)}, bf16[8,64,512]{2,1,0:T(8,128)(2,1)S(1)}, u32[]{:S(2)}, u32[]{:S(2)}) collective-permute-start(bf16[8,64,512]{2,1,0:T(8,128)(2,1)} %get-tuple-element.34.mine), channel_id=1, source_target_pairs={{0,1},{1,0},{2,3},{3,2},{4,5},{5,4},{6,7},{7,6},{8,9},{9,8},{10,11... | collective-permute-start | bytes 1572872 | tf_op jit(solution)/shard_map/ppermute | solution.py:429
  95.9 1.0 copy-start.6
  97.7 0.8 copy-start.12
  122.7 19.4 %collective-permute-start.5 = (bf16[8,64,256]{2,1,0:T(8,128)(2,1)S(1)}, bf16[8,64,256]{2,1,0:T(8,128)(2,1)S(1)}, u32[]{:S(2)}, u32[]{:S(2)}) collective-permute-start(bf16[8,64,256]{2,1,0:T(8,128)(2,1)S(1)} %all_to_all.21.same), channel_id=1, source_target_pairs={{0,6},{1,7},{2,4},{3,5},{4,2},{5,3},{6,0},{7,1},{8,14},{9,15},{10,... | collective-permute-start | bytes 786440 | tf_op jit(solution)/shard_map/ppermute | solution.py:429
  129.4 12.8 %collective-permute-start.4 = (bf16[8,64,256]{2,1,0:T(8,128)(2,1)S(1)}, bf16[8,64,256]{2,1,0:T(8,128)(2,1)}, u32[]{:S(2)}, u32[]{:S(2)}) collective-permute-start(bf16[8,64,256]{2,1,0:T(8,128)(2,1)S(1)} %all_to_all.21.same), channel_id=1, source_target_pairs={{0,2},{1,3},{2,0},{3,1},{4,6},{5,7},{6,4},{7,5},{8,10},{9,11},{10,... | collective-permute-start | bytes 786440 | tf_op jit(solution)/shard_map/ppermute | solution.py:429
  131.4 10.9 %collective-permute-start.3 = (bf16[8,64,256]{2,1,0:T(8,128)(2,1)S(1)}, bf16[8,64,256]{2,1,0:T(8,128)(2,1)S(1)}, u32[]{:S(2)}, u32[]{:S(2)}) collective-permute-start(bf16[8,64,256]{2,1,0:T(8,128)(2,1)S(1)} %all_to_all.21.same), channel_id=1, source_target_pairs={{0,4},{1,5},{2,6},{3,7},{4,0},{5,1},{6,2},{7,3},{8,12},{9,13},{10,... | collective-permute-start | bytes 786440 | tf_op jit(solution)/shard_map/ppermute | solution.py:429
  133.6 13.4 %collective-permute-start.6 = (bf16[4,672,512]{2,1,0:T(8,128)(2,1)}, bf16[4,672,512]{2,1,0:T(8,128)(2,1)S(1)}, u32[]{:S(2)}, u32[]{:S(2)}) collective-permute-start(bf16[4,672,512]{2,1,0:T(8,128)(2,1)} %bitcast.18), channel_id=1, source_target_pairs={{0,1},{1,0},{2,3},{3,2},{4,5},{5,4},{6,7},{7,6},{8,9},{9,8},{10,11... | collective-permute-start | bytes 8257544 | tf_op jit(solution)/shard_map/ppermute | solution.py:429
  142.3 9.3 %collective-permute-start.8 = (bf16[4,672,512]{2,1,0:T(8,128)(2,1)}, bf16[4,672,512]{2,1,0:T(8,128)(2,1)S(1)}, u32[]{:S(2)}, u32[]{:S(2)}) collective-permute-start(bf16[4,672,512]{2,1,0:T(8,128)(2,1)} %bitcast.21), channel_id=1, source_target_pairs={{0,1},{1,0},{2,3},{3,2},{4,5},{5,4},{6,7},{7,6},{8,9},{9,8},{10,11... | collective-permute-start | bytes 8257544 | tf_op jit(solution)/shard_map/ppermute | solution.py:429
  147.1 1.8 copy-start
  148.8 2.8 %copy-start.1 = (bf16[2688,512]{1,0:T(8,128)(2,1)S(1)}, bf16[2688,512]{1,0:T(8,128)(2,1)}, u32[]{:S(2)}) copy-start(bf16[2688,512]{1,0:T(8,128)(2,1)} %all-gather.6.cloned.1.call-done) | copy-start | bytes 8257540
  148.8 2.8 %copy-start.2 = (bf16[2688,512]{1,0:T(8,128)(2,1)S(1)}, bf16[2688,512]{1,0:T(8,128)(2,1)}, u32[]{:S(2)}) copy-start(bf16[2688,512]{1,0:T(8,128)(2,1)} %all-gather.8.cloned.1.call-done) | copy-start | bytes 8257540
  153.7 11.8 %collective-permute-start.9 = (bf16[8,128,128]{2,1,0:T(8,128)(2,1)S(1)}, bf16[8,128,128]{2,1,0:T(8,128)(2,1)S(1)}, u32[]{:S(2)}, u32[]{:S(2)}) collective-permute-start(bf16[8,128,128]{2,1,0:T(8,128)(2,1)S(1)} %get-tuple-element.45), channel_id=1, source_target_pairs={{0,6},{1,7},{2,4},{3,5},{4,2},{5,3},{6,0},{7,1},{8,14},{9,15},{10,... | collective-permute-start | bytes 786440 | tf_op jit(solution)/shard_map/ppermute | solution.py:429
  159.3 12.4 %collective-permute-start.10 = (bf16[8,128,128]{2,1,0:T(8,128)(2,1)S(1)}, bf16[8,128,128]{2,1,0:T(8,128)(2,1)S(1)}, u32[]{:S(2)}, u32[]{:S(2)}) collective-permute-start(bf16[8,128,128]{2,1,0:T(8,128)(2,1)S(1)} %get-tuple-element.46), channel_id=1, source_target_pairs={{0,2},{1,3},{2,0},{3,1},{4,6},{5,7},{6,4},{7,5},{8,10},{9,11},{10,... | collective-permute-start | bytes 786440 | tf_op jit(solution)/shard_map/ppermute | solution.py:429
  161.6 10.1 %collective-permute-start.11 = (bf16[8,128,128]{2,1,0:T(8,128)(2,1)S(1)}, bf16[8,128,128]{2,1,0:T(8,128)(2,1)S(1)}, u32[]{:S(2)}, u32[]{:S(2)}) collective-permute-start(bf16[8,128,128]{2,1,0:T(8,128)(2,1)S(1)} %get-tuple-element.47), channel_id=1, source_target_pairs={{0,4},{1,5},{2,6},{3,7},{4,0},{5,1},{6,2},{7,3},{8,12},{9,13},{10,... | collective-permute-start | bytes 786440 | tf_op jit(solution)/shard_map/ppermute | solution.py:429
  197.0 7.2 %collective-permute-start.12 = (bf16[64,128]{1,0:T(8,128)(2,1)S(1)}, bf16[64,128]{1,0:T(8,128)(2,1)S(1)}, u32[]{:S(2)}, u32[]{:S(2)}) collective-permute-start(bf16[64,128]{1,0:T(8,128)(2,1)S(1)} %get-tuple-element.50), channel_id=1, source_target_pairs={{0,1},{1,0},{2,3},{3,2},{4,5},{5,4},{6,7},{7,6},{8,9},{9,8},{10,11... | collective-permute-start | bytes 49160 | tf_op jit(solution)/shard_map/ppermute | solution.py:429
Sparse Core Ops, SparseCore 0:
  36.5 48.1 all-gather.5
  98.7 41.1 all-gather.7
